TPU v7x, 32 devices: a whole 2x2x4 slice. The times are simulated.
32 devices in a mesh: group: 2 (over x), seq: 16 (over z, y, core).
Axes of the slice: x: 2, y: 2, z: 4, core: 2. Of those that a mesh axis runs over, the one named last changes fastest.
Arguments:
- x_rows: bfloat16 [32, 8192], P('group', 'seq'), parts along dimension 0, may hold values from -0.59765625 to 0.59765625
- attn_gain: bfloat16 [8192], replicated, may hold values from 0.5 to 1.5
- q_weight: bfloat16 [8192, 8192], P(None, 'seq'), may hold values from -0.0625 to 0.0625
- o_weight: bfloat16 [8192, 8192], P('seq'), may hold values from -0.0625 to 0.0625
- mlp_gain: bfloat16 [8192], replicated, may hold values from 0.5 to 1.5
- gate_weight: bfloat16 [8192, 14336], P(None, 'seq'), may hold values from -0.0625 to 0.0625
- up_weight: bfloat16 [8192, 14336], P(None, 'seq'), may hold values from -0.0625 to 0.0625
- down_weight: bfloat16 [14336, 8192], P('seq'), may hold values from -0.046875 to 0.046875
- kv_cache: bfloat16 [2, 4096, 1024], P(None, ('group', 'seq')), parts along dimension 1, may hold values from -250 to 250, as said below
- block_mask: int32 [32, 8, 16], P('group', None, 'seq'), parts along dimension 0, may hold values from 0 to 1, as said below
Outputs:
- y_rows: bfloat16 [32, 8192], P('group', 'seq'), parts along dimension 0
There are 2 independent parts, one for each index of `group`. A program takes and returns all parts, laid end to end along the dimension named above; an argument that names none is the same for every part. Nothing has to cross between parts.
Inputs may be any that keep to these rules, and one draw needn't show every extreme that they name: `kv_cache`: document keys and values; they differ from document to document. `block_mask`: 1 where the row may attend to that block of 128 document tokens for that key-value head, else 0; the document's last block is 1 for every row and key-value head.
All inputs are finite; a program needn't handle non-finite values.
Results may differ from a plain program's by a relative error of at most 0.013.
The roundings to bfloat16 on the way count: a program that leaves them out, or rounds other values in their place, can miss the bound.
Values may be sent and summed in bfloat16 or wider, within the bound.
No kernel may reach another device: no remote copies, remote signals or barrier semaphores. Data moves between devices by JAX's collectives and lax.ppermute only.
A program may use at most 192 MiB of HBM per device.

v0:
```python
import jax
import jax.numpy as jnp
from jax import lax
from jax.sharding import PartitionSpec as P

HEADS = 64
KV_HEADS = 8
HEAD_DIM = 128
BLOCK = 128


eps = 1e-05
floor_score = -1e30


def combined_all(x, axis, combine):
    everything = jax.tree.map(lambda part: lax.all_gather(part, axis), x)
    initial = jax.tree.map(lambda part: part[0], everything)

    def turn(k, so_far):
        return combine(so_far, jax.tree.map(lambda part: part[k], everything))

    return lax.fori_loop(1, lax.axis_size(axis), turn, initial)


def rms_norm(values, gain):
    wide = values.astype(jnp.float32)
    inverse = lax.rsqrt(jnp.mean(wide * wide, axis=-1, keepdims=True) + eps)
    return (wide * inverse * gain.astype(jnp.float32)).astype(jnp.bfloat16)


def combine_states(first, second):
    top_a, total_a, accum_a = first
    top_b, total_b, accum_b = second
    top = jnp.maximum(top_a, top_b)
    factor_a = jnp.exp(top_a - top)
    factor_b = jnp.exp(top_b - top)
    return (
        top,
        total_a * factor_a + total_b * factor_b,
        accum_a * factor_a[..., None] + accum_b * factor_b[..., None],
    )


def local(
    x_rows,
    attn_gain,
    q_weight,
    o_weight,
    mlp_gain,
    gate_weight,
    up_weight,
    down_weight,
    kv_cache,
    block_mask,
):
    rows = x_rows.shape[0]
    group = HEADS // KV_HEADS
    key_len = kv_cache.shape[1]
    spans = key_len // BLOCK
    scale = 1.0 / HEAD_DIM**0.5
    whole = lax.all_gather(x_rows, "seq", axis=1, tiled=True)
    normed = rms_norm(whole, attn_gain)
    query_part = jnp.dot(normed, q_weight, preferred_element_type=jnp.float32).astype(jnp.bfloat16)
    queries = lax.all_gather(query_part, "seq", axis=1, tiled=True)
    doc_keys = kv_cache[0]
    doc_values = kv_cache[1]

    def one_group(index):
        query_group = lax.dynamic_slice_in_dim(
            queries, index * (group * HEAD_DIM), group * HEAD_DIM, 1
        ).reshape(rows, group, HEAD_DIM)
        key_group = lax.dynamic_slice_in_dim(doc_keys, index * HEAD_DIM, HEAD_DIM, 1)
        value_group = lax.dynamic_slice_in_dim(doc_values, index * HEAD_DIM, HEAD_DIM, 1)
        mask_group = lax.dynamic_slice_in_dim(block_mask, index, 1, 1)[:, 0, :]
        scores = (
            jnp.einsum("rhd,kd->rhk", query_group, key_group, preferred_element_type=jnp.float32)
            * scale
        )
        scores = scores.reshape(rows, group, spans, BLOCK)
        live = (mask_group == 1)[:, None, :, None]
        masked = jnp.where(live, scores, floor_score)
        local_top = jnp.max(masked, axis=(2, 3))
        weights = jnp.where(live, jnp.exp(masked - local_top[..., None, None]), 0.0)
        local_total = jnp.sum(weights, axis=(2, 3))
        rounded = weights.astype(jnp.bfloat16).reshape(rows, group, key_len)
        local_accum = jnp.einsum(
            "rhk,kd->rhd", rounded, value_group, preferred_element_type=jnp.float32
        )
        return (local_top, local_total, local_accum)

    tops, totals, accums = lax.map(one_group, jnp.arange(KV_HEADS, dtype=jnp.int32))
    local_top = jnp.moveaxis(tops, 0, 1)
    local_total = jnp.moveaxis(totals, 0, 1)
    local_accum = jnp.moveaxis(accums, 0, 1)
    columns = q_weight.shape[1]
    col_start = lax.axis_index("seq") * columns
    top, total, accum = combined_all((local_top, local_total, local_accum), "seq", combine_states)
    attended = accum / total[..., None]
    attended = attended.reshape(rows, HEADS * HEAD_DIM).astype(jnp.bfloat16)
    attn_cols = lax.dynamic_slice_in_dim(attended, col_start, columns, 1)
    weight_cols = o_weight
    attn_out = lax.psum_scatter(
        lax.dot_general(
            weight_cols, attn_cols, (((0,), (1,)), ((), ())), preferred_element_type=jnp.float32
        ),
        "seq",
        scatter_dimension=0,
        tiled=True,
    )
    stream = (x_rows.astype(jnp.float32) + attn_out.T).astype(jnp.bfloat16)
    stream_whole = lax.all_gather(stream, "seq", axis=1, tiled=True)
    normed_two = rms_norm(stream_whole, mlp_gain)
    gate = jnp.dot(normed_two, gate_weight, preferred_element_type=jnp.float32)
    upward = jnp.dot(normed_two, up_weight, preferred_element_type=jnp.float32)
    hidden = (jax.nn.silu(gate) * upward).astype(jnp.bfloat16)
    weight_cols = down_weight
    down_out = lax.psum_scatter(
        lax.dot_general(
            weight_cols, hidden, (((0,), (1,)), ((), ())), preferred_element_type=jnp.float32
        ),
        "seq",
        scatter_dimension=0,
        tiled=True,
    )
    return (stream.astype(jnp.float32) + down_out.T).astype(jnp.bfloat16)


def solution(mesh):
    return jax.shard_map(
        local,
        mesh=mesh,
        in_specs=(
            P("group", "seq"),
            P(),
            P(None, "seq"),
            P("seq", None),
            P(),
            P(None, "seq"),
            P(None, "seq"),
            P("seq", None),
            P(None, ("group", "seq"), None),
            P("group", None, "seq"),
        ),
        out_specs=P("group", "seq"),
        check_vma=False,
    )
```

profile of v0, /device:TPU:0, one launch (start us, length us, event | category | flops | bytes accessed | tf_op | source)
XLA Modules:
  0.0 377.5 jit_solution(1394457069898761389)
XLA Ops:
  6.5 24.0 %all_gather.27 = bf16[16,8192]{1,0:T(8,128)(2,1)S(1)} all-gather(bf16[16,512]{1,0:T(8,128)(2,1)} %param.14), channel_id=1, replica_groups=mesh['group'=2,'seq'=16] {'seq'}, dimensions={1}, use_global_device_ids=true | all-gather | bytes 278528 | tf_op jit(solution)/shard_map/all_gather | solution.py:62
  31.5 4.6 %convolution_convert_fusion = bf16[16,512]{1,0:T(8,128)(2,1)S(1)} fusion(bf16[8192,512]{1,0:T(8,128)(2,1)} %param.16, bf16[16,8192]{1,0:T(8,128)(2,1)S(1)} %all_gather.27, f32[8192]{0:T(1024)S(1)} %convert_element_type.48, f32[16]{0:T(128)S(1)} %add_rsqrt_fusion.1), kind=kOutput, calls=%fused_computation.34 | convolution fusion | flops 134750208 | bytes 8699968 | tf_op jit(solution)/shard_map/dot_general | solution.py:64
  36.1 18.1 %all_gather.28 = bf16[16,8192]{1,0:T(8,128)(2,1)S(1)} all-gather(bf16[16,512]{1,0:T(8,128)(2,1)S(1)} %convolution_convert_fusion), channel_id=1, replica_groups=mesh['group'=2,'seq'=16] {'seq'}, dimensions={1}, use_global_device_ids=true | all-gather | bytes 278528 | tf_op jit(solution)/shard_map/all_gather | solution.py:65
  55.3 50.1 %while.33 = (s32[]{:T(128)}, f32[8,16,8]{1,2,0:T(8,128)S(1)}, f32[8,16,8]{1,2,0:T(8,128)S(1)}, f32[8,16,8,128]{3,2,0,1:T(8,128)}, s32[8]{0:T(128)S(1)}, /*index=...) while((s32[]{:T(128)}, f32[8,16,8]{1,2,0:T(8,128)S(1)}, ...), condition=%wide.region_4.5_spmd, body=%wide.region_1.4_spmd.sunk | while | flops 8535837 | bytes 521611 | solution.py:92
  105.6 25.8 %all-gather = f32[256,8,8]{2,1,0:T(8,128)S(1)} all-gather(f32[16,8,8]{2,1,0:T(8,128)S(1)} %bitcast.101), channel_id=2, replica_groups=mesh['group'=2,'seq'=16] {'seq'}, dimensions={0}, use_global_device_ids=true | all-gather | bytes 69632 | tf_op jit(solution)/shard_map/all_gather | solution.py:17
  131.8 25.2 %all-gather.1 = f32[256,8,8]{2,1,0:T(8,128)S(1)} all-gather(f32[16,8,8]{2,1,0:T(8,128)S(1)} %bitcast.102), channel_id=3, replica_groups=mesh['group'=2,'seq'=16] {'seq'}, dimensions={0}, use_global_device_ids=true | all-gather | bytes 69632 | tf_op jit(solution)/shard_map/all_gather | solution.py:17
  157.5 28.1 %all-gather.5.cloned.1.call-done = f32[256,8,8,128]{3,2,1,0:T(8,128)} async-done(((f32[16,8,8,128]{3,2,1,0:T(8,128)}), f32[256,8,8,128]{3,2,1,0:T(8,128)}) %all-gather.5.cloned.1.call-update) | async-done | bytes 8388624 | tf_op jit(solution)/shard_map/all_gather | solution.py:17
  186.6 25.3 %while.34 = (s32[]{:T(128)}, f32[16,8,8]{0,2,1:T(8,128)S(1)}, f32[16,8,8]{0,2,1:T(8,128)S(1)}, f32[16,8,8,128]{3,2,1,0:T(8,128)S(1)}, f32[16,16,8,8]{1,3,2,0:T(8...) while((s32[]{:T(128)}, f32[16,8,8]{0,2,1:T(8,128)S(1)}, ...), condition=%wide.region_6.7_spmd, body=%wide.region_5.6_spmd.sunk | while | flops 399365 | bytes 1630359 | solution.py:23
  186.9 1.4 fusion.66
  188.6 1.4 fusion.66
  190.3 1.4 fusion.66
  191.9 1.4 fusion.66
  193.6 1.4 fusion.66
  195.3 1.4 fusion.66
  197.0 1.4 fusion.66
  198.7 1.4 fusion.66
  200.4 1.4 fusion.66
  205.5 1.4 fusion.66
  212.5 5.4 %convolution_bitcast_fusion.2 = f32[8192,16]{0,1:T(8,128)} fusion(bf16[512,8192]{1,0:T(8,128)(2,1)} %param.17, bf16[16,8192]{1,0:T(8,128)(2,1)S(1)} %bitcast.100, s32[]{:T(128)S(6)} %select_n.34), kind=kOutput, calls=%fused_computation.31 | convolution fusion | flops 134217728 | bytes 8929284 | tf_op jit(solution)/shard_map/dot_general | solution.py:104
  217.9 55.6 %reduce-scatter.3.cloned.1.call-done = f32[512,16]{0,1:T(8,128)} async-done(((f32[8192,16]{0,1:T(8,128)}), f32[512,16]{0,1:T(8,128)}) %reduce-scatter.3.cloned.1.call-update) | async-done | bytes 32784 | tf_op jit(solution)/shard_map/reduce_scatter | solution.py:103
  274.3 20.1 %all_gather.35 = bf16[16,8192]{1,0:T(8,128)(2,1)S(1)} all-gather(bf16[16,512]{1,0:T(8,128)(2,1)S(1)} %fusion.38), channel_id=1, replica_groups=mesh['group'=2,'seq'=16] {'seq'}, dimensions={1}, use_global_device_ids=true | all-gather | bytes 278528 | tf_op jit(solution)/shard_map/all_gather | solution.py:112
  294.6 7.2 %fusion.30 = f32[16,896]{1,0:T(8,128)S(1)} fusion(bf16[8192,896]{1,0:T(8,128)(2,1)} %param.19, bf16[16,8192]{1,0:T(8,128)(2,1)S(1)} %all_gather.35, f32[8192]{0:T(1024)S(1)} %convert_element_type.56, f32[16]{0:T(128)S(1)} %add_rsqrt_fusion), kind=kOutput, calls=%fused_computation.51 | convolution fusion | flops 235405312 | bytes 15032384 | tf_op jit(solution)/shard_map/dot_general | solution.py:114
  301.8 14.6 %convolution_bitcast_fusion.1 = f32[8192,16]{0,1:T(8,128)} fusion(bf16[896,8192]{1,0:T(8,128)(2,1)} %param.21, bf16[8192,896]{1,0:T(8,128)(2,1)} %param.20, bf16[16,8192]{1,0:T(8,128)(2,1)S(1)} %all_gather.35, f32[8192]{0:T(1024)S(1)} %convert_element_type.56, f32[16]{0:T(128)S(1)} %add_rsqrt_fusion, f32[16,896]{1,0:T(8,128)S(1)} %fusion.30), kind=kOutput, calls=%fused_computation.30 | convolution fusion | flops 470372352 | bytes 30236736 | tf_op jit(solution)/shard_map/dot_general | solution.py:119
  316.5 53.1 %reduce-scatter.5.cloned.1.call-done = f32[512,16]{0,1:T(8,128)} async-done(((f32[8192,16]{0,1:T(8,128)}), f32[512,16]{0,1:T(8,128)}) %reduce-scatter.5.cloned.1.call-update) | async-done | bytes 32784 | tf_op jit(solution)/shard_map/reduce_scatter | solution.py:118
  (165 shorter events, 39.4 us)
Async XLA Ops:
  6.5 179.0 %all-gather.5.cloned.1.call-start = ((), (), s32[]{:S(2)}) async-start(), calls=%async_computation.4 | async-start | bytes 8912896 | tf_op jit(solution)/shard_map/all_gather | solution.py:17
  105.4 168.1 %reduce-scatter.3.cloned.1.call-start = ((), (), s32[]{:S(2)}) async-start(), calls=%async_computation.2 | async-start | bytes 557056 | tf_op jit(solution)/shard_map/reduce_scatter | solution.py:103
  157.0 61.0 %copy-start.1 = (bf16[8192]{0:T(1024)(128)(2,1)S(1)}, bf16[8192]{0:T(1024)(128)(2,1)}, u32[]{:S(2)}) copy-start(bf16[8192]{0:T(1024)(128)(2,1)} %param.18) | copy-start | bytes 49156
  157.0 116.6 %copy-start = (bf16[16,512]{1,0:T(8,128)(2,1)S(1)}, bf16[16,512]{1,0:T(8,128)(2,1)}, u32[]{:S(2)}) copy-start(bf16[16,512]{1,0:T(8,128)(2,1)} %param.14) | copy-start | bytes 49156
  217.9 151.7 %reduce-scatter.5.cloned.1.call-start = ((), (), s32[]{:S(2)}) async-start(), calls=%async_computation.3 | async-start | bytes 557056 | tf_op jit(solution)/shard_map/reduce_scatter | solution.py:118
Sparse Core Ops, SparseCore 0:
  105.5 79.9 all-gather.4
  218.0 55.4 reduce-scatter.2
  316.6 52.9 reduce-scatter.4
where the time goes:
time: 379 us; the launch traced here: 378 us
  waiting for transfers between devices  137 us (36%)
  blocking collectives  113 us (30%)
  matrix products  40.6 us (11%)
  other arithmetic  32.3 us (9%)
  loops' own time  28.6 us (8%)
  between operations  13.2 us (3%)
  local copies, waits for them, and re-layouts  12.6 us (3%)
    reduce_scatter x1, waiting for transfers between devices, local(): lax.psum_scatter(lax.dot_general(weight_cols, attn_cols, (((0,), (1,)), (...  55.6 us
    reduce_scatter x1, waiting for transfers between devices, local(): lax.psum_scatter(lax.dot_general(weight_cols, hidden, (((0,), (1,)), ((),...  53.1 us
    all_gather x2, blocking collectives, combined_all(): everything = jax.tree.map(lambda part: lax.all_gather(part, axis), x)  51 us
    all_gather x1, waiting for transfers between devices, combined_all(): everything = jax.tree.map(lambda part: lax.all_gather(part, axis), x)  28.1 us
    another operation x1, loops' own time, local(): lax.map(one_group, jnp.arange(KV_HEADS, dtype=jnp.int32))  28 us
    all_gather x1, blocking collectives, local(): whole = lax.all_gather(x_rows, 'seq', axis=1, tiled=True)  24 us
    add x15, other arithmetic, combine_states(): accum_a * factor_a[..., None] + accum_b * factor_b[..., None]  21.6 us
    all_gather x1, blocking collectives, local(): stream_whole = lax.all_gather(stream, 'seq', axis=1, tiled=True)  20.1 us
  transfers between devices with their start and end apart: 3, of which 3 were waited for; matrix products, arithmetic and copies ran while one was open for 0% of the time, Pallas kernels for 0%

commit v1 on v0

v1 whole, which is shorter than its diff:
```python
import functools

import jax
import jax.numpy as jnp
from jax import lax
from jax.experimental import pallas as pl
from jax.experimental.pallas import tpu as pltpu
from jax.sharding import PartitionSpec as P

HEADS = 64
KV_HEADS = 8
HEAD_DIM = 128
BLOCK = 128
QUAD = 4

eps = 1e-05
floor_score = -1e30

bf16 = jnp.bfloat16
f32 = jnp.float32
VMEM = pl.BlockSpec(memory_space=pltpu.VMEM)


def call(body, outs, ins, scratch=(), limit=16 * 2**20, cost=None):
    return pl.pallas_call(
        body,
        out_shape=outs,
        in_specs=[VMEM] * len(ins),
        out_specs=jax.tree.map(lambda _: VMEM, outs),
        scratch_shapes=list(scratch),
        compiler_params=pltpu.CompilerParams(vmem_limit_bytes=limit),
        cost_estimate=cost,
    )(*ins)


def like(shape, dtype):
    return jax.ShapeDtypeStruct(shape, dtype)


def swap(x, distance):
    size = lax.axis_size("seq")
    return lax.ppermute(x, "seq", [(i, i ^ distance) for i in range(size)])


def pack_kernel(outer, kv_ref, mask_ref, *out_refs):
    quad = lax.axis_index("seq") // QUAD
    keys = kv_ref.shape[1]
    rows = mask_ref.shape[0]
    wide = kv_ref.shape[2] // outer
    mask = mask_ref[...]
    lane = lax.broadcasted_iota(jnp.int32, mask.shape, 1)
    for k in range(outer):
        peer = jnp.bitwise_xor(quad, k)
        cols = pl.ds(pl.multiple_of(peer * wide, wide), wide)
        out = out_refs[k]
        out[0:keys, :] = kv_ref[0, :, cols]
        out[keys : 2 * keys, :] = kv_ref[1, :, cols]
        for h in range(wide // HEAD_DIM):
            head = peer * (wide // HEAD_DIM) + h
            live = jnp.sum(
                jnp.where((lane == head) & (mask == 1), 1.0, 0.0).astype(f32), axis=1, keepdims=True
            )
            out[2 * keys : 2 * keys + rows, h * HEAD_DIM : (h + 1) * HEAD_DIM] = jnp.broadcast_to(
                live, (rows, HEAD_DIM)
            ).astype(bf16)


def split_kernel(outer, *refs):
    ins, (mine, other) = refs[:outer], refs[outer:]
    high = (lax.axis_index("seq") // 2) % 2
    size = ins[0].shape[0]
    for k in range(outer):
        span = pl.ds(k * size, size)
        mine[span, :] = ins[k][:, pl.ds(pl.multiple_of(high * HEAD_DIM, HEAD_DIM), HEAD_DIM)]
        other[span, :] = ins[k][:, pl.ds(pl.multiple_of((1 - high) * HEAD_DIM, HEAD_DIM), HEAD_DIM)]


def normed_chunks(outer, wide, part_refs, gain_ref):
    me = lax.axis_index("seq")
    width = QUAD * outer * wide
    squares = None
    for ref in part_refs:
        v = ref[...].astype(f32)
        s = jnp.sum(v * v, axis=1, keepdims=True)
        squares = s if squares is None else squares + s
    inverse = lax.rsqrt(squares / width + eps)
    for j in range(QUAD):
        for k in range(outer):
            source = jnp.bitwise_xor(me, QUAD * k + j)
            at = pl.ds(pl.multiple_of(source * wide, wide), wide)
            v = part_refs[j][:, k * wide : (k + 1) * wide].astype(f32)
            yield at, (v * inverse * gain_ref[:, at].astype(f32)).astype(bf16)


def query_kernel(outer, wide, *refs):
    parts, gain_ref, w_ref, out_ref = refs[:QUAD], refs[QUAD], refs[QUAD + 1], refs[QUAD + 2]
    total = None
    for at, chunk in normed_chunks(outer, wide, parts, gain_ref):
        term = jnp.dot(chunk, w_ref[at, :], preferred_element_type=f32)
        total = term if total is None else total + term
    out_ref[...] = total.astype(bf16)


def scatter_dot(outer, wide, left, w_ref, out_refs):
    me = lax.axis_index("seq")
    for j in (3, 2, 1, 0):
        for k in range(outer):
            target = jnp.bitwise_xor(me, QUAD * k + j)
            at = pl.ds(pl.multiple_of(target * wide, wide), wide)
            term = jnp.dot(left, w_ref[:, at], preferred_element_type=f32)
            out_refs[j][:, k * wide : (k + 1) * wide] = term.astype(out_refs[j].dtype)


def attend_kernel(outer, wide, q_ref, *refs):
    cache, w_ref, outs = refs[:QUAD], refs[QUAD], refs[QUAD + 1 :]
    rows = q_ref.shape[0]
    heads = q_ref.shape[1] // HEAD_DIM
    scale = 1.0 / HEAD_DIM**0.5
    size = cache[0].shape[0] // outer
    keys = (size - rows) // 2
    queries = jnp.concatenate(
        [q_ref[:, h * HEAD_DIM : (h + 1) * HEAD_DIM] for h in range(heads)], axis=0
    )
    states = []
    for ref in cache:
        for k in range(outer):
            at = k * size
            live = ref[at + 2 * keys : at + size, :].astype(f32) > 0.5
            live = jnp.concatenate([live.astype(f32)] * heads, axis=0) > 0.5
            score = (
                lax.dot_general(
                    queries,
                    ref[at : at + keys, :],
                    (((1,), (1,)), ((), ())),
                    preferred_element_type=f32,
                )
                * scale
            )
            masked = jnp.where(live, score, floor_score)
            top = jnp.max(masked, axis=1, keepdims=True)
            weight = jnp.where(live, jnp.exp(masked - top), 0.0)
            total = jnp.sum(weight, axis=1, keepdims=True)
            accum = jnp.dot(
                weight.astype(bf16), ref[at + keys : at + 2 * keys, :], preferred_element_type=f32
            )
            states.append((top, total, accum))
    top = functools.reduce(jnp.maximum, [s[0] for s in states])
    total = accum = None
    for t, s, a in states:
        factor = jnp.exp(t - top)
        total = s * factor if total is None else total + s * factor
        accum = a * factor if accum is None else accum + a * factor
    attended = (accum / total).astype(bf16)
    attended = jnp.concatenate([attended[h * rows : (h + 1) * rows] for h in range(heads)], axis=1)
    scatter_dot(outer, wide, attended, w_ref, outs)


def hidden_kernel(outer, wide, *refs):
    parts, gain_ref = refs[:QUAD], refs[QUAD]
    gate_ref, up_ref, down_ref = refs[QUAD + 1 : QUAD + 4]
    outs = refs[QUAD + 4 :]
    gate = up = None
    for at, chunk in normed_chunks(outer, wide, parts, gain_ref):
        g = jnp.dot(chunk, gate_ref[at, :], preferred_element_type=f32)
        u = jnp.dot(chunk, up_ref[at, :], preferred_element_type=f32)
        gate = g if gate is None else gate + g
        up = u if up is None else up + u
    hidden = (gate / (1.0 + jnp.exp(-gate)) * up).astype(bf16)
    scatter_dot(outer, wide, hidden, down_ref, outs)


def fold_kernel(outer, wide, own_ref, *refs):
    recv, keep_ref, sends = refs[: QUAD - 1], refs[QUAD - 1], refs[QUAD:]
    for k in range(outer):
        at = slice(k * wide, (k + 1) * wide)
        total = own_ref[:, at]
        for r in recv:
            total = total + r[:, at].astype(f32)
        if k == 0:
            keep_ref[...] = total
        else:
            sends[k - 1][...] = total.astype(bf16)


def final_kernel(base_ref, keep_ref, *refs):
    total = keep_ref[...]
    for r in refs[:-1]:
        total = total + r[...].astype(f32)
    refs[-1][...] = (base_ref[...].astype(f32) + total).astype(bf16)


def gathered(x, outer):
    line = jnp.concatenate([x] + [swap(x, QUAD * k) for k in range(1, outer)], axis=1)
    return [line] + [swap(line, j) for j in range(1, QUAD)]


def scattered(base, partials, outer, wide):
    rows = base.shape[0]
    recv = [swap(partials[j], j) for j in range(1, QUAD)]
    outs = [like((rows, wide), f32)] + [like((rows, wide), bf16)] * (outer - 1)
    keep, *sends = call(
        functools.partial(fold_kernel, outer, wide), outs, [partials[0], *recv]
    )
    arrived = [swap(s, QUAD * (k + 1)) for k, s in enumerate(sends)]
    return call(final_kernel, like((rows, wide), bf16), [base, keep, *arrived])


def local_pairs(
    x_rows, attn_gain, q_weight, o_weight, mlp_gain, gate_weight, up_weight, down_weight, kv_cache, block_mask
):
    rows, wide = x_rows.shape
    outer = lax.axis_size("seq") // QUAD
    columns = q_weight.shape[1]
    attn_gain = attn_gain.reshape(1, -1)
    mlp_gain = mlp_gain.reshape(1, -1)
    x_parts = gathered(x_rows, outer)

    size = 2 * kv_cache.shape[1] + rows
    across = kv_cache.shape[2] // outer
    packed = call(
        functools.partial(pack_kernel, outer),
        [like((size, across), bf16)] * outer,
        [kv_cache, block_mask[:, :, 0]],
    )
    line = [packed[0]] + [swap(packed[k], QUAD * k) for k in range(1, outer)]
    mine, other = call(
        functools.partial(split_kernel, outer), [like((size * outer, HEAD_DIM), bf16)] * 2, line
    )
    across_y = swap(other, 2)
    cache = [mine, across_y, swap(mine, 1), swap(across_y, 1)]

    queries = call(
        functools.partial(query_kernel, outer, wide),
        like((rows, columns), bf16),
        [*x_parts, attn_gain, q_weight],
    )
    partial_outs = [like((rows, outer * wide), f32)] + [like((rows, outer * wide), bf16)] * (QUAD - 1)
    partials = call(
        functools.partial(attend_kernel, outer, wide), partial_outs, [queries, *cache, o_weight]
    )
    stream = scattered(x_rows, partials, outer, wide)
    stream_parts = gathered(stream, outer)
    partials = call(
        functools.partial(hidden_kernel, outer, wide),
        partial_outs,
        [*stream_parts, mlp_gain, gate_weight, up_weight, down_weight],
    )
    return scattered(stream, partials, outer, wide)


def rms_norm(values, gain):
    wide = values.astype(f32)
    inverse = lax.rsqrt(jnp.mean(wide * wide, axis=-1, keepdims=True) + eps)
    return (wide * inverse * gain.astype(f32)).astype(bf16)


def combine_states(first, second):
    top_a, total_a, accum_a = first
    top_b, total_b, accum_b = second
    top = jnp.maximum(top_a, top_b)
    factor_a = jnp.exp(top_a - top)
    factor_b = jnp.exp(top_b - top)
    return (
        top,
        total_a * factor_a + total_b * factor_b,
        accum_a * factor_a[..., None] + accum_b * factor_b[..., None],
    )


def combined_all(x, axis, combine):
    everything = jax.tree.map(lambda part: lax.all_gather(part, axis), x)
    initial = jax.tree.map(lambda part: part[0], everything)

    def turn(k, so_far):
        return combine(so_far, jax.tree.map(lambda part: part[k], everything))

    return lax.fori_loop(1, lax.axis_size(axis), turn, initial)


def summed(weight, left):
    product = lax.dot_general(weight, left, (((0,), (1,)), ((), ())), preferred_element_type=f32)
    return lax.psum_scatter(product, "seq", scatter_dimension=0, tiled=True).T


def local_tokens(
    x_rows, attn_gain, q_weight, o_weight, mlp_gain, gate_weight, up_weight, down_weight, kv_cache, block_mask
):
    rows = x_rows.shape[0]
    group = HEADS // KV_HEADS
    key_len = kv_cache.shape[1]
    spans = key_len // BLOCK
    scale = 1.0 / HEAD_DIM**0.5
    normed = rms_norm(lax.all_gather(x_rows, "seq", axis=1, tiled=True), attn_gain)
    query_part = jnp.dot(normed, q_weight, preferred_element_type=f32).astype(bf16)
    queries = lax.all_gather(query_part, "seq", axis=1, tiled=True)

    def one_group(index):
        def cut(array, width):
            return lax.dynamic_slice_in_dim(array, index * width, width, 1)

        query_group = cut(queries, group * HEAD_DIM).reshape(rows, group, HEAD_DIM)
        scores = (
            jnp.einsum("rhd,kd->rhk", query_group, cut(kv_cache[0], HEAD_DIM), preferred_element_type=f32)
            * scale
        )
        scores = scores.reshape(rows, group, spans, BLOCK)
        live = (cut(block_mask, 1)[:, 0, :] == 1)[:, None, :, None]
        masked = jnp.where(live, scores, floor_score)
        top = jnp.max(masked, axis=(2, 3))
        weights = jnp.where(live, jnp.exp(masked - top[..., None, None]), 0.0)
        rounded = weights.astype(bf16).reshape(rows, group, key_len)
        accum = jnp.einsum("rhk,kd->rhd", rounded, cut(kv_cache[1], HEAD_DIM), preferred_element_type=f32)
        return (top, jnp.sum(weights, axis=(2, 3)), accum)

    states = lax.map(one_group, jnp.arange(KV_HEADS, dtype=jnp.int32))
    states = jax.tree.map(lambda part: jnp.moveaxis(part, 0, 1), states)
    columns = q_weight.shape[1]
    top, total, accum = combined_all(states, "seq", combine_states)
    attended = (accum / total[..., None]).reshape(rows, HEADS * HEAD_DIM).astype(bf16)
    attn_cols = lax.dynamic_slice_in_dim(attended, lax.axis_index("seq") * columns, columns, 1)
    stream = (x_rows.astype(f32) + summed(o_weight, attn_cols)).astype(bf16)
    normed_two = rms_norm(lax.all_gather(stream, "seq", axis=1, tiled=True), mlp_gain)
    gate = jnp.dot(normed_two, gate_weight, preferred_element_type=f32)
    upward = jnp.dot(normed_two, up_weight, preferred_element_type=f32)
    hidden = (jax.nn.silu(gate) * upward).astype(bf16)
    return (stream.astype(f32) + summed(down_weight, hidden)).astype(bf16)


def solution(mesh):
    pairs = mesh.shape["seq"] == 2 * KV_HEADS
    return jax.shard_map(
        local_pairs if pairs else local_tokens,
        mesh=mesh,
        in_specs=(
            P("group", "seq"),
            P(),
            P(None, "seq"),
            P("seq", None),
            P(),
            P(None, "seq"),
            P(None, "seq"),
            P("seq", None),
            P(None, ("group", "seq"), None),
            P("group", None, "seq"),
        ),
        out_specs=P("group", "seq"),
        check_vma=False,
    )
```

time: 379 us -> 106 us (0.28)
  blocking collectives: 113 us -> 0 us
  waiting for transfers between devices: 137 us -> 37.4 us
  matrix products: 40.6 us -> 0 us
  starting transfers between devices: 0.09 us -> 33.1 us
  other arithmetic: 32.3 us -> 0.01 us
  loops' own time: 28.6 us -> 0 us
  Pallas kernels: 0 us -> 18.4 us
  between operations: 13.2 us -> 0.13 us
  local copies, waits for them, and re-layouts: 12.6 us -> 16.7 us
    all_gather x5 -> x0, blocking collectives: 113 us -> none  [the longest x2 51 us: combined_all(): everything = jax.tree.map(lambda part: lax.all_gather(part, axis), x)]
    reduce_scatter x2 -> x0, waiting for transfers between devices: 109 us -> none  [the longest x1 55.6 us: local(): lax.psum_scatter(lax.dot_general(weight_cols, attn_cols, (((0,), (1,)), (...]
    dot_general x20 -> x0, matrix products: 40.6 us -> none  [the longest x1 14.6 us: local(): lax.dot_general(weight_cols, hidden, (((0,), (1,)), ((), ())), preferred_...]
    ppermute x0 -> x30, waiting for transfers between devices: none -> 37.4 us  [swap(): return lax.ppermute(x, 'seq', [(i, i ^ distance) for i in range(size)])]
    ppermute x0 -> x30, starting transfers between devices: none -> 33.1 us  [swap(): return lax.ppermute(x, 'seq', [(i, i ^ distance) for i in range(size)])]
    another operation x2 -> x0, loops' own time: 28.6 us -> none  [the longest x1 28 us: local(): lax.map(one_group, jnp.arange(KV_HEADS, dtype=jnp.int32))]
    all_gather x1 -> x0, waiting for transfers between devices: 28.1 us -> none  [combined_all(): everything = jax.tree.map(lambda part: lax.all_gather(part, axis), x)]
    add x30 -> x0, other arithmetic: 22.1 us -> none  [the longest x15 21.6 us: combine_states(): accum_a * factor_a[..., None] + accum_b * factor_b[..., None]]
  transfers between devices with their start and end apart: 3 -> 30, of which waited for: 3 -> 18; matrix products, arithmetic and copies ran while one was open for 0% -> 2% of each run, Pallas kernels for 0% -> 1%
where the time goes in v1:
time: 106 us
  waiting for transfers between devices  37.4 us (35%)
  starting transfers between devices  33.1 us (31%)
  Pallas kernels  18.4 us (17%)
  local copies, waits for them, and re-layouts  16.7 us (16%)
    ppermute x30, waiting for transfers between devices, swap(): return lax.ppermute(x, 'seq', [(i, i ^ distance) for i in range(size)])  37.4 us
    ppermute x30, starting transfers between devices, swap(): return lax.ppermute(x, 'seq', [(i, i ^ distance) for i in range(size)])  33.1 us
    pallas_call x9, Pallas kernels, call(): pl.pallas_call(body, out_shape=outs, in_specs=[VMEM] * len(ins), out_spec...  18.4 us
    unnamed x15, local copies, waits for them, and re-layouts  14.4 us
  transfers between devices with their start and end apart: 30, of which 18 were waited for; matrix products, arithmetic and copies ran while one was open for 2% of the time, Pallas kernels for 1%

profile of v1, /device:TPU:0, one launch (start us, length us, event | category | flops | bytes accessed | tf_op | source)
XLA Modules:
  0.0 105.7 jit_solution(7296678435268704074)
XLA Ops:
  1.9 3.1 %collective-permute-start.6 = (bf16[272,256]{1,0:T(8,128)(2,1)S(1)}, bf16[272,256]{1,0:T(8,128)(2,1)S(1)}, u32[]{:S(2)}, u32[]{:S(2)}) collective-permute-start(bf16[272,256]{1,0:T(8,128)(2,1)S(1)} %get-tuple-element.28), channel_id=1, source_target_pairs={{0,4},{1,5},{2,6},{3,7},{4,0},{5,1},{6,2},{7,3},{8,12},{9,13},{10,... | collective-permute-start | bytes 417800 | tf_op jit(solution)/shard_map/ppermute | solution.py:42
  5.0 2.6 %collective-permute-start.7 = (bf16[272,256]{1,0:T(8,128)(2,1)S(1)}, bf16[272,256]{1,0:T(8,128)(2,1)S(1)}, u32[]{:S(2)}, u32[]{:S(2)}) collective-permute-start(bf16[272,256]{1,0:T(8,128)(2,1)S(1)} %get-tuple-element.29), channel_id=1, source_target_pairs={{0,8},{1,9},{2,10},{3,11},{4,12},{5,13},{6,14},{7,15},{8,0},{9,1},... | collective-permute-start | bytes 417800 | tf_op jit(solution)/shard_map/ppermute | solution.py:42
  7.6 2.9 %collective-permute-done.6.refs_1_ = bf16[272,256]{1,0:T(8,128)(2,1)S(1)} collective-permute-done((bf16[272,256]{1,0:T(8,128)(2,1)S(1)}, bf16[272,256]{1,0:T(8,128)(2,1)S(1)}, u32[]{:S(2)}, u32[]{:S(2)}) %collective-permute-start.6) | collective-permute-done | bytes 139296 | tf_op jit(solution)/shard_map/ppermute | solution.py:42
  10.4 8.0 %collective-permute-done.7.refs_2_ = bf16[272,256]{1,0:T(8,128)(2,1)S(1)} collective-permute-done((bf16[272,256]{1,0:T(8,128)(2,1)S(1)}, bf16[272,256]{1,0:T(8,128)(2,1)S(1)}, u32[]{:S(2)}, u32[]{:S(2)}) %collective-permute-start.7) | collective-permute-done | bytes 139296 | tf_op jit(solution)/shard_map/ppermute | solution.py:42
  18.6 1.6 %collective-permute-start.9 = (bf16[1088,128]{1,0:T(8,128)(2,1)S(1)}, bf16[1088,128]{1,0:T(8,128)(2,1)S(1)}, u32[]{:S(2)}, u32[]{:S(2)}) collective-permute-start(bf16[1088,128]{1,0:T(8,128)(2,1)S(1)} %get-tuple-element.32), channel_id=1, source_target_pairs={{0,2},{1,3},{2,0},{3,1},{4,6},{5,7},{6,4},{7,5},{8,10},{9,11},{10,... | collective-permute-start | bytes 835592 | tf_op jit(solution)/shard_map/ppermute | solution.py:42
  20.1 2.1 %collective-permute-start = (bf16[16,512]{1,0:T(8,128)(2,1)}, bf16[16,512]{1,0:T(8,128)(2,1)S(1)}, u32[]{:S(2)}, u32[]{:S(2)}) collective-permute-start(bf16[16,512]{1,0:T(8,128)(2,1)} %base_ref.1), channel_id=1, source_target_pairs={{0,4},{1,5},{2,6},{3,7},{4,0},{5,1},{6,2},{7,3},{8,12},{9,13},{10,... | collective-permute-start | bytes 49160 | tf_op jit(solution)/shard_map/ppermute | solution.py:42
  27.1 1.9 %collective-permute-done.2 = bf16[16,512]{1,0:T(8,128)(2,1)S(1)} collective-permute-done((bf16[16,512]{1,0:T(8,128)(2,1)}, bf16[16,512]{1,0:T(8,128)(2,1)S(1)}, u32[]{:S(2)}, u32[]{:S(2)}) %collective-permute-start.2) | collective-permute-done | bytes 16416 | tf_op jit(solution)/shard_map/ppermute | solution.py:42
  31.6 2.3 %collective-permute-done.4.refs_2_ = bf16[16,2048]{1,0:T(8,128)(2,1)S(1)} collective-permute-done((bf16[16,2048]{1,0:T(8,128)(2,1)S(1)}, bf16[16,2048]{1,0:T(8,128)(2,1)S(1)}, u32[]{:S(2)}, u32[]{:S(2)}) %collective-permute-start.4) | collective-permute-done | bytes 65568 | tf_op jit(solution)/shard_map/ppermute | solution.py:42
  34.6 3.4 %copy-done.3 = bf16[8192,512]{1,0:T(8,128)(2,1)S(1)} copy-done((bf16[8192,512]{1,0:T(8,128)(2,1)S(1)}, bf16[8192,512]{1,0:T(8,128)(2,1)}, u32[]{:S(2)}) %copy-start.3) | copy-done | bytes 8388632
  39.3 3.4 %copy-done.2 = bf16[512,8192]{1,0:T(8,128)(2,1)S(1)} copy-done((bf16[512,8192]{1,0:T(8,128)(2,1)S(1)}, bf16[512,8192]{1,0:T(8,128)(2,1)}, u32[]{:S(2)}) %copy-start.2) | copy-done | bytes 8388632
  42.6 5.1 %shard_map.103 = (f32[16,2048]{1,0:T(8,128)S(1)}, bf16[16,2048]{1,0:T(8,128)(2,1)S(1)}, bf16[16,2048]{1,0:T(8,128)(2,1)S(1)}, bf16[16,2048]{1,0:T(8,128)(2,1)S(1)}) custom-call(bf16[16,512]{1,0:T(8,128)(2,1)S(1)} %shard_map.100.q_ref, bf16[1088,128]{1,0:T(8,128)(2,1)S(1)} %get-tuple-element.31.refs_0_, bf16[1088,128]{1,0:T(8,128)(2,1)S(1)} %collective-permute-done.9.refs_1_, ...), custom_call_target="tpu_custom_call" | custom-call | tf_op jit(solution)/shard_map/pallas_call | solution.py:25
  49.6 3.3 %collective-permute-done.13.refs_1_ = bf16[16,2048]{1,0:T(8,128)(2,1)S(1)} collective-permute-done((bf16[16,2048]{1,0:T(8,128)(2,1)S(1)}, bf16[16,2048]{1,0:T(8,128)(2,1)S(1)}, u32[]{:S(2)}, u32[]{:S(2)}) %collective-permute-start.13) | collective-permute-done | bytes 65568 | tf_op jit(solution)/shard_map/ppermute | solution.py:42
  53.4 1.8 %collective-permute-start.16 = (bf16[16,512]{1,0:T(8,128)(2,1)S(1)}, bf16[16,512]{1,0:T(8,128)(2,1)S(1)}, u32[]{:S(2)}, u32[]{:S(2)}) collective-permute-start(bf16[16,512]{1,0:T(8,128)(2,1)S(1)} %get-tuple-element.39), channel_id=1, source_target_pairs={{0,8},{1,9},{2,10},{3,11},{4,12},{5,13},{6,14},{7,15},{8,0},{9,1},... | collective-permute-start | bytes 49160 | tf_op jit(solution)/shard_map/ppermute | solution.py:42
  55.2 2.4 %collective-permute-start.17 = (bf16[16,512]{1,0:T(8,128)(2,1)S(1)}, bf16[16,512]{1,0:T(8,128)(2,1)S(1)}, u32[]{:S(2)}, u32[]{:S(2)}) collective-permute-start(bf16[16,512]{1,0:T(8,128)(2,1)S(1)} %get-tuple-element.40), channel_id=1, source_target_pairs={{0,12},{1,13},{2,14},{3,15},{4,8},{5,9},{6,10},{7,11},{8,4},{9,5},... | collective-permute-start | bytes 49160 | tf_op jit(solution)/shard_map/ppermute | solution.py:42
  58.0 2.7 %collective-permute-done.17.refs_2_ = bf16[16,512]{1,0:T(8,128)(2,1)S(1)} collective-permute-done((bf16[16,512]{1,0:T(8,128)(2,1)S(1)}, bf16[16,512]{1,0:T(8,128)(2,1)S(1)}, u32[]{:S(2)}, u32[]{:S(2)}) %collective-permute-start.17) | collective-permute-done | bytes 16416 | tf_op jit(solution)/shard_map/ppermute | solution.py:42
  61.5 2.9 %collective-permute-start.19 = (bf16[16,512]{1,0:T(8,128)(2,1)S(1)}, bf16[16,512]{1,0:T(8,128)(2,1)S(1)}, u32[]{:S(2)}, u32[]{:S(2)}) collective-permute-start(bf16[16,512]{1,0:T(8,128)(2,1)S(1)} %shard_map.105.base_ref), channel_id=1, source_target_pairs={{0,8},{1,9},{2,10},{3,11},{4,12},{5,13},{6,14},{7,15},{8,0},{9,1},... | collective-permute-start | bytes 49160 | tf_op jit(solution)/shard_map/ppermute | solution.py:42
  66.2 3.7 %collective-permute-done.20 = bf16[16,512]{1,0:T(8,128)(2,1)S(1)} collective-permute-done((bf16[16,512]{1,0:T(8,128)(2,1)S(1)}, bf16[16,512]{1,0:T(8,128)(2,1)S(1)}, u32[]{:S(2)}, u32[]{:S(2)}) %collective-permute-start.20) | collective-permute-done | bytes 16416 | tf_op jit(solution)/shard_map/ppermute | solution.py:42
  72.6 2.3 %collective-permute-done.22.refs_2_ = bf16[16,2048]{1,0:T(8,128)(2,1)S(1)} collective-permute-done((bf16[16,2048]{1,0:T(8,128)(2,1)S(1)}, bf16[16,2048]{1,0:T(8,128)(2,1)S(1)}, u32[]{:S(2)}, u32[]{:S(2)}) %collective-permute-start.22) | collective-permute-done | bytes 65568 | tf_op jit(solution)/shard_map/ppermute | solution.py:42
  75.5 5.2 %copy-done.1 = bf16[8192,896]{1,0:T(8,128)(2,1)S(1)} copy-done((bf16[8192,896]{1,0:T(8,128)(2,1)S(1)}, bf16[8192,896]{1,0:T(8,128)(2,1)}, u32[]{:S(2)}) %copy-start.1) | copy-done | bytes 14680088
  80.7 11.1 %shard_map.106 = (f32[16,2048]{1,0:T(8,128)S(1)}, bf16[16,2048]{1,0:T(8,128)(2,1)S(1)}, bf16[16,2048]{1,0:T(8,128)(2,1)S(1)}, bf16[16,2048]{1,0:T(8,128)(2,1)S(1)}) custom-call(bf16[16,2048]{1,0:T(8,128)(2,1)S(1)} %pad_maximum_fusion.refs_0_, bf16[16,2048]{1,0:T(8,128)(2,1)S(1)} %collective-permute-done.21.refs_1_, ...), custom_call_target="tpu_custom_call" | custom-call | tf_op jit(solution)/shard_map/pallas_call | solution.py:25
  93.7 2.9 %collective-permute-done.25.refs_1_ = bf16[16,2048]{1,0:T(8,128)(2,1)S(1)} collective-permute-done((bf16[16,2048]{1,0:T(8,128)(2,1)S(1)}, bf16[16,2048]{1,0:T(8,128)(2,1)S(1)}, u32[]{:S(2)}, u32[]{:S(2)}) %collective-permute-start.25) | collective-permute-done | bytes 65568 | tf_op jit(solution)/shard_map/ppermute | solution.py:42
  97.6 2.0 %collective-permute-start.28 = (bf16[16,512]{1,0:T(8,128)(2,1)S(1)}, bf16[16,512]{1,0:T(8,128)(2,1)S(1)}, u32[]{:S(2)}, u32[]{:S(2)}) collective-permute-start(bf16[16,512]{1,0:T(8,128)(2,1)S(1)} %get-tuple-element.47), channel_id=1, source_target_pairs={{0,8},{1,9},{2,10},{3,11},{4,12},{5,13},{6,14},{7,15},{8,0},{9,1},... | collective-permute-start | bytes 49160 | tf_op jit(solution)/shard_map/ppermute | solution.py:42
  99.6 2.4 %collective-permute-start.29 = (bf16[16,512]{1,0:T(8,128)(2,1)S(1)}, bf16[16,512]{1,0:T(8,128)(2,1)S(1)}, u32[]{:S(2)}, u32[]{:S(2)}) collective-permute-start(bf16[16,512]{1,0:T(8,128)(2,1)S(1)} %get-tuple-element.48), channel_id=1, source_target_pairs={{0,12},{1,13},{2,14},{3,15},{4,8},{5,9},{6,10},{7,11},{8,4},{9,5},... | collective-permute-start | bytes 49160 | tf_op jit(solution)/shard_map/ppermute | solution.py:42
  102.3 2.8 %collective-permute-done.29.refs_2_ = bf16[16,512]{1,0:T(8,128)(2,1)S(1)} collective-permute-done((bf16[16,512]{1,0:T(8,128)(2,1)S(1)}, bf16[16,512]{1,0:T(8,128)(2,1)S(1)}, u32[]{:S(2)}, u32[]{:S(2)}) %collective-permute-start.29) | collective-permute-done | bytes 16416 | tf_op jit(solution)/shard_map/ppermute | solution.py:42
  (65 shorter events, 23.8 us)
Async XLA Ops:
  1.9 8.5 %collective-permute-start.6 = (bf16[272,256]{1,0:T(8,128)(2,1)S(1)}, bf16[272,256]{1,0:T(8,128)(2,1)S(1)}, u32[]{:S(2)}, u32[]{:S(2)}) collective-permute-start(bf16[272,256]{1,0:T(8,128)(2,1)S(1)} %get-tuple-element.28), channel_id=1, source_target_pairs={{0,4},{1,5},{2,6},{3,7},{4,0},{5,1},{6,2},{7,3},{8,12},{9,13},{10,... | collective-permute-start | bytes 417800 | tf_op jit(solution)/shard_map/ppermute | solution.py:42
  5.0 13.5 %collective-permute-start.7 = (bf16[272,256]{1,0:T(8,128)(2,1)S(1)}, bf16[272,256]{1,0:T(8,128)(2,1)S(1)}, u32[]{:S(2)}, u32[]{:S(2)}) collective-permute-start(bf16[272,256]{1,0:T(8,128)(2,1)S(1)} %get-tuple-element.29), channel_id=1, source_target_pairs={{0,8},{1,9},{2,10},{3,11},{4,12},{5,13},{6,14},{7,15},{8,0},{9,1},... | collective-permute-start | bytes 417800 | tf_op jit(solution)/shard_map/ppermute | solution.py:42
  7.6 10.9 %collective-permute-start.8 = (bf16[272,256]{1,0:T(8,128)(2,1)S(1)}, bf16[272,256]{1,0:T(8,128)(2,1)S(1)}, u32[]{:S(2)}, u32[]{:S(2)}) collective-permute-start(bf16[272,256]{1,0:T(8,128)(2,1)S(1)} %get-tuple-element.30), channel_id=1, source_target_pairs={{0,12},{1,13},{2,14},{3,15},{4,8},{5,9},{6,10},{7,11},{8,4},{9,5},... | collective-permute-start | bytes 417800 | tf_op jit(solution)/shard_map/ppermute | solution.py:42
  18.6 7.0 %collective-permute-start.9 = (bf16[1088,128]{1,0:T(8,128)(2,1)S(1)}, bf16[1088,128]{1,0:T(8,128)(2,1)S(1)}, u32[]{:S(2)}, u32[]{:S(2)}) collective-permute-start(bf16[1088,128]{1,0:T(8,128)(2,1)S(1)} %get-tuple-element.32), channel_id=1, source_target_pairs={{0,2},{1,3},{2,0},{3,1},{4,6},{5,7},{6,4},{7,5},{8,10},{9,11},{10,... | collective-permute-start | bytes 835592 | tf_op jit(solution)/shard_map/ppermute | solution.py:42
  20.1 5.4 %collective-permute-start = (bf16[16,512]{1,0:T(8,128)(2,1)}, bf16[16,512]{1,0:T(8,128)(2,1)S(1)}, u32[]{:S(2)}, u32[]{:S(2)}) collective-permute-start(bf16[16,512]{1,0:T(8,128)(2,1)} %base_ref.1), channel_id=1, source_target_pairs={{0,4},{1,5},{2,6},{3,7},{4,0},{5,1},{6,2},{7,3},{8,12},{9,13},{10,... | collective-permute-start | bytes 49160 | tf_op jit(solution)/shard_map/ppermute | solution.py:42
  22.3 4.8 %collective-permute-start.1 = (bf16[16,512]{1,0:T(8,128)(2,1)}, bf16[16,512]{1,0:T(8,128)(2,1)S(1)}, u32[]{:S(2)}, u32[]{:S(2)}) collective-permute-start(bf16[16,512]{1,0:T(8,128)(2,1)} %base_ref.1), channel_id=1, source_target_pairs={{0,8},{1,9},{2,10},{3,11},{4,12},{5,13},{6,14},{7,15},{8,0},{9,1},... | collective-permute-start | bytes 49160 | tf_op jit(solution)/shard_map/ppermute | solution.py:42
  23.3 5.7 %collective-permute-start.2 = (bf16[16,512]{1,0:T(8,128)(2,1)}, bf16[16,512]{1,0:T(8,128)(2,1)S(1)}, u32[]{:S(2)}, u32[]{:S(2)}) collective-permute-start(bf16[16,512]{1,0:T(8,128)(2,1)} %base_ref.1), channel_id=1, source_target_pairs={{0,12},{1,13},{2,14},{3,15},{4,8},{5,9},{6,10},{7,11},{8,4},{9,5},... | collective-permute-start | bytes 49160 | tf_op jit(solution)/shard_map/ppermute | solution.py:42
  25.5 13.7 %collective-permute-start.10 = (bf16[1088,128]{1,0:T(8,128)(2,1)S(1)}, bf16[1088,128]{1,0:T(8,128)(2,1)S(1)}, u32[]{:S(2)}, u32[]{:S(2)}) collective-permute-start(bf16[1088,128]{1,0:T(8,128)(2,1)S(1)} %get-tuple-element.31.refs_0_), channel_id=1, source_target_pairs={{0,1},{1,0},{2,3},{3,2},{4,5},{5,4},{6,7},{7,6},{8,9},{9,8},{10,11... | collective-permute-start | bytes 835592 | tf_op jit(solution)/shard_map/ppermute | solution.py:42
  25.5 13.7 %collective-permute-start.11 = (bf16[1088,128]{1,0:T(8,128)(2,1)S(1)}, bf16[1088,128]{1,0:T(8,128)(2,1)S(1)}, u32[]{:S(2)}, u32[]{:S(2)}) collective-permute-start(bf16[1088,128]{1,0:T(8,128)(2,1)S(1)} %collective-permute-done.9.refs_1_), channel_id=1, source_target_pairs={{0,1},{1,0},{2,3},{3,2},{4,5},{5,4},{6,7},{7,6},{8,9},{9,8},{10,11... | collective-permute-start | bytes 835592 | tf_op jit(solution)/shard_map/ppermute | solution.py:42
  29.0 4.9 %collective-permute-start.4 = (bf16[16,2048]{1,0:T(8,128)(2,1)S(1)}, bf16[16,2048]{1,0:T(8,128)(2,1)S(1)}, u32[]{:S(2)}, u32[]{:S(2)}) collective-permute-start(bf16[16,2048]{1,0:T(8,128)(2,1)S(1)} %constant_dynamic-update-slice_fusion.refs_0_), channel_id=1, source_target_pairs={{0,2},{1,3},{2,0},{3,1},{4,6},{5,7},{6,4},{7,5},{8,10},{9,11},{10,... | collective-permute-start | bytes 196616 | tf_op jit(solution)/shard_map/ppermute | solution.py:42
  29.5 5.0 %collective-permute-start.5 = (bf16[16,2048]{1,0:T(8,128)(2,1)S(1)}, bf16[16,2048]{1,0:T(8,128)(2,1)S(1)}, u32[]{:S(2)}, u32[]{:S(2)}) collective-permute-start(bf16[16,2048]{1,0:T(8,128)(2,1)S(1)} %constant_dynamic-update-slice_fusion.refs_0_), channel_id=1, source_target_pairs={{0,3},{1,2},{2,1},{3,0},{4,7},{5,6},{6,5},{7,4},{8,11},{9,10},{10,... | collective-permute-start | bytes 196616 | tf_op jit(solution)/shard_map/ppermute | solution.py:42
  47.9 4.9 %collective-permute-start.13 = (bf16[16,2048]{1,0:T(8,128)(2,1)S(1)}, bf16[16,2048]{1,0:T(8,128)(2,1)S(1)}, u32[]{:S(2)}, u32[]{:S(2)}) collective-permute-start(bf16[16,2048]{1,0:T(8,128)(2,1)S(1)} %get-tuple-element.35), channel_id=1, source_target_pairs={{0,2},{1,3},{2,0},{3,1},{4,6},{5,7},{6,4},{7,5},{8,10},{9,11},{10,... | collective-permute-start | bytes 196616 | tf_op jit(solution)/shard_map/ppermute | solution.py:42
  48.5 4.6 %collective-permute-start.14 = (bf16[16,2048]{1,0:T(8,128)(2,1)S(1)}, bf16[16,2048]{1,0:T(8,128)(2,1)S(1)}, u32[]{:S(2)}, u32[]{:S(2)}) collective-permute-start(bf16[16,2048]{1,0:T(8,128)(2,1)S(1)} %get-tuple-element.36), channel_id=1, source_target_pairs={{0,3},{1,2},{2,1},{3,0},{4,7},{5,6},{6,5},{7,4},{8,11},{9,10},{10,... | collective-permute-start | bytes 196616 | tf_op jit(solution)/shard_map/ppermute | solution.py:42
  53.1 4.5 %collective-permute-start.15 = (bf16[16,512]{1,0:T(8,128)(2,1)S(1)}, bf16[16,512]{1,0:T(8,128)(2,1)S(1)}, u32[]{:S(2)}, u32[]{:S(2)}) collective-permute-start(bf16[16,512]{1,0:T(8,128)(2,1)S(1)} %get-tuple-element.38), channel_id=1, source_target_pairs={{0,4},{1,5},{2,6},{3,7},{4,0},{5,1},{6,2},{7,3},{8,12},{9,13},{10,... | collective-permute-start | bytes 49160 | tf_op jit(solution)/shard_map/ppermute | solution.py:42
  53.4 4.6 %collective-permute-start.16 = (bf16[16,512]{1,0:T(8,128)(2,1)S(1)}, bf16[16,512]{1,0:T(8,128)(2,1)S(1)}, u32[]{:S(2)}, u32[]{:S(2)}) collective-permute-start(bf16[16,512]{1,0:T(8,128)(2,1)S(1)} %get-tuple-element.39), channel_id=1, source_target_pairs={{0,8},{1,9},{2,10},{3,11},{4,12},{5,13},{6,14},{7,15},{8,0},{9,1},... | collective-permute-start | bytes 49160 | tf_op jit(solution)/shard_map/ppermute | solution.py:42
  55.2 5.5 %collective-permute-start.17 = (bf16[16,512]{1,0:T(8,128)(2,1)S(1)}, bf16[16,512]{1,0:T(8,128)(2,1)S(1)}, u32[]{:S(2)}, u32[]{:S(2)}) collective-permute-start(bf16[16,512]{1,0:T(8,128)(2,1)S(1)} %get-tuple-element.40), channel_id=1, source_target_pairs={{0,12},{1,13},{2,14},{3,15},{4,8},{5,9},{6,10},{7,11},{8,4},{9,5},... | collective-permute-start | bytes 49160 | tf_op jit(solution)/shard_map/ppermute | solution.py:42
  61.4 4.5 %collective-permute-start.18 = (bf16[16,512]{1,0:T(8,128)(2,1)S(1)}, bf16[16,512]{1,0:T(8,128)(2,1)S(1)}, u32[]{:S(2)}, u32[]{:S(2)}) collective-permute-start(bf16[16,512]{1,0:T(8,128)(2,1)S(1)} %shard_map.105.base_ref), channel_id=1, source_target_pairs={{0,4},{1,5},{2,6},{3,7},{4,0},{5,1},{6,2},{7,3},{8,12},{9,13},{10,... | collective-permute-start | bytes 49160 | tf_op jit(solution)/shard_map/ppermute | solution.py:42
  61.5 4.7 %collective-permute-start.19 = (bf16[16,512]{1,0:T(8,128)(2,1)S(1)}, bf16[16,512]{1,0:T(8,128)(2,1)S(1)}, u32[]{:S(2)}, u32[]{:S(2)}) collective-permute-start(bf16[16,512]{1,0:T(8,128)(2,1)S(1)} %shard_map.105.base_ref), channel_id=1, source_target_pairs={{0,8},{1,9},{2,10},{3,11},{4,12},{5,13},{6,14},{7,15},{8,0},{9,1},... | collective-permute-start | bytes 49160 | tf_op jit(solution)/shard_map/ppermute | solution.py:42
  64.4 5.5 %collective-permute-start.20 = (bf16[16,512]{1,0:T(8,128)(2,1)S(1)}, bf16[16,512]{1,0:T(8,128)(2,1)S(1)}, u32[]{:S(2)}, u32[]{:S(2)}) collective-permute-start(bf16[16,512]{1,0:T(8,128)(2,1)S(1)} %shard_map.105.base_ref), channel_id=1, source_target_pairs={{0,12},{1,13},{2,14},{3,15},{4,8},{5,9},{6,10},{7,11},{8,4},{9,5},... | collective-permute-start | bytes 49160 | tf_op jit(solution)/shard_map/ppermute | solution.py:42
  70.0 4.9 %collective-permute-start.22 = (bf16[16,2048]{1,0:T(8,128)(2,1)S(1)}, bf16[16,2048]{1,0:T(8,128)(2,1)S(1)}, u32[]{:S(2)}, u32[]{:S(2)}) collective-permute-start(bf16[16,2048]{1,0:T(8,128)(2,1)S(1)} %pad_maximum_fusion.refs_0_), channel_id=1, source_target_pairs={{0,2},{1,3},{2,0},{3,1},{4,6},{5,7},{6,4},{7,5},{8,10},{9,11},{10,... | collective-permute-start | bytes 196616 | tf_op jit(solution)/shard_map/ppermute | solution.py:42
  92.0 4.5 %collective-permute-start.25 = (bf16[16,2048]{1,0:T(8,128)(2,1)S(1)}, bf16[16,2048]{1,0:T(8,128)(2,1)S(1)}, u32[]{:S(2)}, u32[]{:S(2)}) collective-permute-start(bf16[16,2048]{1,0:T(8,128)(2,1)S(1)} %get-tuple-element.43), channel_id=1, source_target_pairs={{0,2},{1,3},{2,0},{3,1},{4,6},{5,7},{6,4},{7,5},{8,10},{9,11},{10,... | collective-permute-start | bytes 196616 | tf_op jit(solution)/shard_map/ppermute | solution.py:42
  97.5 4.5 %collective-permute-start.27 = (bf16[16,512]{1,0:T(8,128)(2,1)S(1)}, bf16[16,512]{1,0:T(8,128)(2,1)S(1)}, u32[]{:S(2)}, u32[]{:S(2)}) collective-permute-start(bf16[16,512]{1,0:T(8,128)(2,1)S(1)} %get-tuple-element.46), channel_id=1, source_target_pairs={{0,4},{1,5},{2,6},{3,7},{4,0},{5,1},{6,2},{7,3},{8,12},{9,13},{10,... | collective-permute-start | bytes 49160 | tf_op jit(solution)/shard_map/ppermute | solution.py:42
  97.6 4.7 %collective-permute-start.28 = (bf16[16,512]{1,0:T(8,128)(2,1)S(1)}, bf16[16,512]{1,0:T(8,128)(2,1)S(1)}, u32[]{:S(2)}, u32[]{:S(2)}) collective-permute-start(bf16[16,512]{1,0:T(8,128)(2,1)S(1)} %get-tuple-element.47), channel_id=1, source_target_pairs={{0,8},{1,9},{2,10},{3,11},{4,12},{5,13},{6,14},{7,15},{8,0},{9,1},... | collective-permute-start | bytes 49160 | tf_op jit(solution)/shard_map/ppermute | solution.py:42
  99.6 5.5 %collective-permute-start.29 = (bf16[16,512]{1,0:T(8,128)(2,1)S(1)}, bf16[16,512]{1,0:T(8,128)(2,1)S(1)}, u32[]{:S(2)}, u32[]{:S(2)}) collective-permute-start(bf16[16,512]{1,0:T(8,128)(2,1)S(1)} %get-tuple-element.48), channel_id=1, source_target_pairs={{0,12},{1,13},{2,14},{3,15},{4,8},{5,9},{6,10},{7,11},{8,4},{9,5},... | collective-permute-start | bytes 49160 | tf_op jit(solution)/shard_map/ppermute | solution.py:42
  (12 other events, 105.0 us)

commit v2 on v1

--- a/solution.py
+++ b/solution.py
@@ -21,16 +21,27 @@
 VMEM = pl.BlockSpec(memory_space=pltpu.VMEM)
 
 
-def call(body, outs, ins, scratch=(), limit=16 * 2**20, cost=None):
+def call(body, outs, ins, beside=(), limit=4 * 2**20):
+    count, extra = len(ins), len(beside)
+
+    def kernel(*refs):
+        body(*refs[:count], *refs[count + extra :])
+
     return pl.pallas_call(
-        body,
+        kernel,
         out_shape=outs,
-        in_specs=[VMEM] * len(ins),
+        in_specs=[VMEM] * count + [pl.BlockSpec(memory_space=pl.ANY)] * extra,
         out_specs=jax.tree.map(lambda _: VMEM, outs),
-        scratch_shapes=list(scratch),
         compiler_params=pltpu.CompilerParams(vmem_limit_bytes=limit),
-        cost_estimate=cost,
-    )(*ins)
+    )(*ins, *beside)
+
+
+def room(size):
+    return pl.pallas_call(
+        lambda out: None,
+        out_shape=like((size, 1024), f32),
+        out_specs=pl.BlockSpec(memory_space=pl.ANY),
+    )()
 
 
 def like(shape, dtype):
@@ -42,91 +53,116 @@
     return lax.ppermute(x, "seq", [(i, i ^ distance) for i in range(size)])
 
 
-def pack_kernel(outer, kv_ref, mask_ref, *out_refs):
-    quad = lax.axis_index("seq") // QUAD
+def live_lanes(mask, head, rows):
+    lane = lax.broadcasted_iota(jnp.int32, mask.shape, 1)
+    live = jnp.where((lane == head) & (mask == 1), 1.0, 0.0).astype(f32)
+    return jnp.broadcast_to(jnp.sum(live, axis=1, keepdims=True), (rows, HEAD_DIM)).astype(bf16)
+
+
+def pack_kernel(outer, kv_ref, mask_ref, own_ref, send_ref):
+    y = (lax.axis_index("seq") // 2) % 2
     keys = kv_ref.shape[1]
     rows = mask_ref.shape[0]
-    wide = kv_ref.shape[2] // outer
     mask = mask_ref[...]
-    lane = lax.broadcasted_iota(jnp.int32, mask.shape, 1)
+    for out, parity in ((send_ref, 1 - y), (own_ref, y)):
+        for z in range(outer):
+            head = 2 * z + parity
+            cols = pl.ds(pl.multiple_of(head * HEAD_DIM, HEAD_DIM), HEAD_DIM)
+            at = slice(z * HEAD_DIM, (z + 1) * HEAD_DIM)
+            out[0:keys, at] = kv_ref[0, :, cols]
+            out[keys : 2 * keys, at] = kv_ref[1, :, cols]
+            out[2 * keys : 2 * keys + rows, at] = live_lanes(mask, head, rows)
+
+
+def route_kernel(outer, own_ref, other_ref, order_ref, *outs):
+    z = lax.axis_index("seq") // QUAD
+    size = own_ref.shape[0]
     for k in range(outer):
-        peer = jnp.bitwise_xor(quad, k)
-        cols = pl.ds(pl.multiple_of(peer * wide, wide), wide)
-        out = out_refs[k]
-        out[0:keys, :] = kv_ref[0, :, cols]
-        out[keys : 2 * keys, :] = kv_ref[1, :, cols]
-        for h in range(wide // HEAD_DIM):
-            head = peer * (wide // HEAD_DIM) + h
-            live = jnp.sum(
-                jnp.where((lane == head) & (mask == 1), 1.0, 0.0).astype(f32), axis=1, keepdims=True
-            )
-            out[2 * keys : 2 * keys + rows, h * HEAD_DIM : (h + 1) * HEAD_DIM] = jnp.broadcast_to(
-                live, (rows, HEAD_DIM)
-            ).astype(bf16)
-
-
-def split_kernel(outer, *refs):
-    ins, (mine, other) = refs[:outer], refs[outer:]
-    high = (lax.axis_index("seq") // 2) % 2
-    size = ins[0].shape[0]
-    for k in range(outer):
-        span = pl.ds(k * size, size)
-        mine[span, :] = ins[k][:, pl.ds(pl.multiple_of(high * HEAD_DIM, HEAD_DIM), HEAD_DIM)]
-        other[span, :] = ins[k][:, pl.ds(pl.multiple_of((1 - high) * HEAD_DIM, HEAD_DIM), HEAD_DIM)]
+        peer = jnp.bitwise_xor(z, k)
+        cols = pl.ds(pl.multiple_of(peer * HEAD_DIM, HEAD_DIM), HEAD_DIM)
+        outs[k][0:size, :] = own_ref[:, cols]
+        outs[k][size : 2 * size, :] = other_ref[:, cols]
+
+
+def stack_kernel(axis, *refs):
+    at = 0
+    for ref in refs[:-1]:
+        size = ref.shape[axis]
+        if axis == 0:
+            refs[-1][at : at + size, :] = ref[...]
+        else:
+            refs[-1][:, at : at + size] = ref[...]
+        at += size
+
+
+def stacked(parts, axis, beside=()):
+    shape = list(parts[0].shape)
+    shape[axis] = sum(p.shape[axis] for p in parts)
+    return call(functools.partial(stack_kernel, axis), like(tuple(shape), parts[0].dtype), parts, beside)
 
 
 def normed_chunks(outer, wide, part_refs, gain_ref):
     me = lax.axis_index("seq")
     width = QUAD * outer * wide
     squares = None
-    for ref in part_refs:
+    for ref, _ in part_refs:
         v = ref[...].astype(f32)
         s = jnp.sum(v * v, axis=1, keepdims=True)
         squares = s if squares is None else squares + s
     inverse = lax.rsqrt(squares / width + eps)
-    for j in range(QUAD):
-        for k in range(outer):
-            source = jnp.bitwise_xor(me, QUAD * k + j)
+    for ref, distances in part_refs:
+        for i, distance in enumerate(distances):
+            source = jnp.bitwise_xor(me, distance)
             at = pl.ds(pl.multiple_of(source * wide, wide), wide)
-            v = part_refs[j][:, k * wide : (k + 1) * wide].astype(f32)
+            v = ref[:, i * wide : (i + 1) * wide].astype(f32)
             yield at, (v * inverse * gain_ref[:, at].astype(f32)).astype(bf16)
 
 
+def line_of(outer, *nears):
+    return [QUAD * k + j for j in nears for k in range(outer)]
+
+
+def part_list(outer, refs):
+    return list(zip(refs, (line_of(outer, 0), line_of(outer, 2), line_of(outer, 1, 3))))
+
+
 def query_kernel(outer, wide, *refs):
-    parts, gain_ref, w_ref, out_ref = refs[:QUAD], refs[QUAD], refs[QUAD + 1], refs[QUAD + 2]
+    gain_ref, w_ref, out_ref = refs[3:]
     total = None
-    for at, chunk in normed_chunks(outer, wide, parts, gain_ref):
+    for at, chunk in normed_chunks(outer, wide, part_list(outer, refs[:3]), gain_ref):
         term = jnp.dot(chunk, w_ref[at, :], preferred_element_type=f32)
         total = term if total is None else total + term
     out_ref[...] = total.astype(bf16)
 
 
-def scatter_dot(outer, wide, left, w_ref, out_refs):
+def scatter_dot(wide, left, w_ref, out_ref, distances):
     me = lax.axis_index("seq")
-    for j in (3, 2, 1, 0):
-        for k in range(outer):
-            target = jnp.bitwise_xor(me, QUAD * k + j)
-            at = pl.ds(pl.multiple_of(target * wide, wide), wide)
-            term = jnp.dot(left, w_ref[:, at], preferred_element_type=f32)
-            out_refs[j][:, k * wide : (k + 1) * wide] = term.astype(out_refs[j].dtype)
-
-
-def attend_kernel(outer, wide, q_ref, *refs):
-    cache, w_ref, outs = refs[:QUAD], refs[QUAD], refs[QUAD + 1 :]
+    for i, distance in enumerate(distances):
+        target = jnp.bitwise_xor(me, distance)
+        at = pl.ds(pl.multiple_of(target * wide, wide), wide)
+        out_ref[:, i * wide : (i + 1) * wide] = jnp.dot(left, w_ref[:, at], preferred_element_type=f32)
+
+
+def scatter_kernel(wide, distances, left_ref, w_ref, out_ref):
+    scatter_dot(wide, left_ref[...], w_ref, out_ref, distances)
+
+
+def attend_kernel(wide, distances, spans, q_ref, *refs):
+    cache, w_ref, left_ref, send_ref = refs[:-3], *refs[-3:]
     rows = q_ref.shape[0]
     heads = q_ref.shape[1] // HEAD_DIM
     scale = 1.0 / HEAD_DIM**0.5
-    size = cache[0].shape[0] // outer
-    keys = (size - rows) // 2
     queries = jnp.concatenate(
         [q_ref[:, h * HEAD_DIM : (h + 1) * HEAD_DIM] for h in range(heads)], axis=0
     )
     states = []
-    for ref in cache:
-        for k in range(outer):
+    for ref, count in zip(cache, spans):
+        size = ref.shape[0] // count
+        keys = (size - rows) // 2
+        for k in range(count):
             at = k * size
-            live = ref[at + 2 * keys : at + size, :].astype(f32) > 0.5
-            live = jnp.concatenate([live.astype(f32)] * heads, axis=0) > 0.5
+            live = ref[at + 2 * keys : at + size, :].astype(f32)
+            live = jnp.concatenate([live] * heads, axis=0) > 0.5
             score = (
                 lax.dot_general(
                     queries,
@@ -152,34 +188,33 @@
         accum = a * factor if accum is None else accum + a * factor
     attended = (accum / total).astype(bf16)
     attended = jnp.concatenate([attended[h * rows : (h + 1) * rows] for h in range(heads)], axis=1)
-    scatter_dot(outer, wide, attended, w_ref, outs)
-
-
-def hidden_kernel(outer, wide, *refs):
-    parts, gain_ref = refs[:QUAD], refs[QUAD]
-    gate_ref, up_ref, down_ref = refs[QUAD + 1 : QUAD + 4]
-    outs = refs[QUAD + 4 :]
+    left_ref[...] = attended
+    scatter_dot(wide, attended, w_ref, send_ref, distances)
+
+
+def hidden_kernel(outer, wide, distances, *refs):
+    gain_ref, gate_ref, up_ref, down_ref, left_ref, send_ref = refs[3:]
     gate = up = None
-    for at, chunk in normed_chunks(outer, wide, parts, gain_ref):
+    for at, chunk in normed_chunks(outer, wide, part_list(outer, refs[:3]), gain_ref):
         g = jnp.dot(chunk, gate_ref[at, :], preferred_element_type=f32)
         u = jnp.dot(chunk, up_ref[at, :], preferred_element_type=f32)
         gate = g if gate is None else gate + g
         up = u if up is None else up + u
     hidden = (gate / (1.0 + jnp.exp(-gate)) * up).astype(bf16)
-    scatter_dot(outer, wide, hidden, down_ref, outs)
-
-
-def fold_kernel(outer, wide, own_ref, *refs):
-    recv, keep_ref, sends = refs[: QUAD - 1], refs[QUAD - 1], refs[QUAD:]
-    for k in range(outer):
+    left_ref[...] = hidden
+    scatter_dot(wide, hidden, down_ref, send_ref, distances)
+
+
+def half_kernel(own_ref, recv_ref, keep_ref, send_ref):
+    half = own_ref.shape[1] // 2
+    keep_ref[...] = own_ref[:, :half] + recv_ref[:, :half]
+    send_ref[...] = (own_ref[:, half:] + recv_ref[:, half:]).astype(send_ref.dtype)
+
+
+def fold_kernel(wide, own_ref, recv_ref, keep_ref, *sends):
+    for k, out in enumerate((keep_ref, *sends)):
         at = slice(k * wide, (k + 1) * wide)
-        total = own_ref[:, at]
-        for r in recv:
-            total = total + r[:, at].astype(f32)
-        if k == 0:
-            keep_ref[...] = total
-        else:
-            sends[k - 1][...] = total.astype(bf16)
+        out[...] = (own_ref[:, at] + recv_ref[:, at].astype(f32)).astype(out.dtype)
 
 
 def final_kernel(base_ref, keep_ref, *refs):
@@ -189,18 +224,28 @@
     refs[-1][...] = (base_ref[...].astype(f32) + total).astype(bf16)
 
 
-def gathered(x, outer):
-    line = jnp.concatenate([x] + [swap(x, QUAD * k) for k in range(1, outer)], axis=1)
-    return [line] + [swap(line, j) for j in range(1, QUAD)]
-
-
-def scattered(base, partials, outer, wide):
+def z_gathered(x, outer):
+    return stacked([x] + [swap(x, QUAD * k) for k in range(1, outer)], 1)
+
+
+def near_gathered(line):
+    other = swap(line, 2)
+    return [line, other, swap(stacked([line, other], 1), 1)]
+
+
+def scattered(base, send, left, weight, outer, wide, y_type, z_type, beside=()):
     rows = base.shape[0]
-    recv = [swap(partials[j], j) for j in range(1, QUAD)]
-    outs = [like((rows, wide), f32)] + [like((rows, wide), bf16)] * (outer - 1)
-    keep, *sends = call(
-        functools.partial(fold_kernel, outer, wide), outs, [partials[0], *recv]
-    )
+    far = swap(send, 1)
+    keep = call(
+        functools.partial(scatter_kernel, wide, line_of(outer, 0, 2)),
+        like((rows, 2 * outer * wide), f32),
+        [left, weight],
+    )
+    keep, send = call(
+        half_kernel, [like((rows, outer * wide), f32), like((rows, outer * wide), y_type)], [keep, far], beside
+    )
+    outs = [like((rows, wide), f32)] + [like((rows, wide), z_type)] * (outer - 1)
+    keep, *sends = call(functools.partial(fold_kernel, wide), outs, [keep, swap(send, 2)], beside)
     arrived = [swap(s, QUAD * (k + 1)) for k, s in enumerate(sends)]
     return call(final_kernel, like((rows, wide), bf16), [base, keep, *arrived])
 
@@ -211,41 +256,48 @@
     rows, wide = x_rows.shape
     outer = lax.axis_size("seq") // QUAD
     columns = q_weight.shape[1]
+    beside = [room(18432)]
     attn_gain = attn_gain.reshape(1, -1)
     mlp_gain = mlp_gain.reshape(1, -1)
-    x_parts = gathered(x_rows, outer)
+    near = line_of(outer, 1, 3)
 
     size = 2 * kv_cache.shape[1] + rows
-    across = kv_cache.shape[2] // outer
-    packed = call(
+    own, send = call(
         functools.partial(pack_kernel, outer),
-        [like((size, across), bf16)] * outer,
+        [like((size, outer * HEAD_DIM), bf16)] * 2,
         [kv_cache, block_mask[:, :, 0]],
-    )
-    line = [packed[0]] + [swap(packed[k], QUAD * k) for k in range(1, outer)]
-    mine, other = call(
-        functools.partial(split_kernel, outer), [like((size * outer, HEAD_DIM), bf16)] * 2, line
-    )
-    across_y = swap(other, 2)
-    cache = [mine, across_y, swap(mine, 1), swap(across_y, 1)]
-
+        beside,
+    )
+    other = swap(send, 2)
+    line = z_gathered(x_rows, outer)
+    routed = call(
+        functools.partial(route_kernel, outer),
+        [like((2 * size, HEAD_DIM), bf16)] * outer,
+        [own, other, line],
+        beside,
+    )
+    x_parts = near_gathered(line)
     queries = call(
         functools.partial(query_kernel, outer, wide),
         like((rows, columns), bf16),
         [*x_parts, attn_gain, q_weight],
     )
-    partial_outs = [like((rows, outer * wide), f32)] + [like((rows, outer * wide), bf16)] * (QUAD - 1)
-    partials = call(
-        functools.partial(attend_kernel, outer, wide), partial_outs, [queries, *cache, o_weight]
-    )
-    stream = scattered(x_rows, partials, outer, wide)
-    stream_parts = gathered(stream, outer)
-    partials = call(
-        functools.partial(hidden_kernel, outer, wide),
-        partial_outs,
-        [*stream_parts, mlp_gain, gate_weight, up_weight, down_weight],
-    )
-    return scattered(stream, partials, outer, wide)
+    arrived = [swap(routed[k], QUAD * k) for k in range(1, outer)]
+    mine = stacked([routed[0], *arrived], 0, [queries])
+    cache = [mine, swap(mine, 1)]
+    left, send = call(
+        functools.partial(attend_kernel, wide, near, [2 * outer] * 2),
+        [like((rows, columns), bf16), like((rows, 2 * outer * wide), f32)],
+        [queries, *cache, o_weight],
+    )
+    stream = scattered(x_rows, send, left, o_weight, outer, wide, f32, f32, beside)
+    parts = near_gathered(z_gathered(stream, outer))
+    left, send = call(
+        functools.partial(hidden_kernel, outer, wide, near),
+        [like((rows, gate_weight.shape[1]), bf16), like((rows, 2 * outer * wide), f32)],
+        [*parts, mlp_gain, gate_weight, up_weight, down_weight],
+    )
+    return scattered(stream, send, left, down_weight, outer, wide, bf16, f32)
 
 
 def rms_norm(values, gain):

time: 106 us -> 82.4 us (0.78)
  local copies, waits for them, and re-layouts: 16.7 us -> 1.18 us
  Pallas kernels: 18.4 us -> 13.7 us
  starting transfers between devices: 33.1 us -> 30.2 us
    unnamed x15 -> x42, local copies, waits for them, and re-layouts: 14.4 us -> 1.07 us
    pallas_call x9 -> x19, Pallas kernels: 18.4 us -> 13.7 us  [the longest x18 13.7 us: call(): pl.pallas_call(kernel, out_shape=outs, in_specs=[VMEM] * count + [pl.Bloc...]
    ppermute x30 -> x25, starting transfers between devices: 33.1 us -> 30.2 us  [swap(): return lax.ppermute(x, 'seq', [(i, i ^ distance) for i in range(size)])]
    ppermute x30 -> x25, waiting for transfers between devices: 37.4 us -> 36.7 us  [swap(): return lax.ppermute(x, 'seq', [(i, i ^ distance) for i in range(size)])]
  transfers between devices with their start and end apart: 30 -> 25, of which waited for: 18 -> 17; matrix products, arithmetic and copies ran while one was open for 2% -> 0% of each run, Pallas kernels for 1% -> 4%
where the time goes in v2:
time: 82.4 us; the launch traced here: 82.2 us
  waiting for transfers between devices  36.7 us (45%)
  starting transfers between devices  30.2 us (37%)
  Pallas kernels  13.7 us (17%)
  local copies, waits for them, and re-layouts  1.18 us (1%)
    ppermute x25, waiting for transfers between devices, swap(): return lax.ppermute(x, 'seq', [(i, i ^ distance) for i in range(size)])  36.7 us
    ppermute x25, starting transfers between devices, swap(): return lax.ppermute(x, 'seq', [(i, i ^ distance) for i in range(size)])  30.2 us
    pallas_call x18, Pallas kernels, call(): pl.pallas_call(kernel, out_shape=outs, in_specs=[VMEM] * count + [pl.Bloc...  13.7 us
  transfers between devices with their start and end apart: 25, of which 17 were waited for; matrix products, arithmetic and copies ran while one was open for 0% of the time, Pallas kernels for 4%

profile of v2, /device:TPU:0, one launch (start us, length us, event | category | flops | bytes accessed | tf_op | source)
XLA Modules:
  0.0 82.2 jit_solution(13397433333237811641)
XLA Ops:
  1.3 3.0 %collective-permute-start.5 = (bf16[272,512]{1,0:T(8,128)(2,1)S(1)}, bf16[272,512]{1,0:T(8,128)(2,1)S(1)}, u32[]{:S(2)}, u32[]{:S(2)}) collective-permute-start(bf16[272,512]{1,0:T(8,128)(2,1)S(1)} %get-tuple-element.28), channel_id=1, source_target_pairs={{0,2},{1,3},{2,0},{3,1},{4,6},{5,7},{6,4},{7,5},{8,10},{9,11},{10,... | collective-permute-start | bytes 835592 | tf_op jit(solution)/shard_map/ppermute | solution.py:53
  4.3 1.6 %collective-permute-start = (bf16[16,512]{1,0:T(8,128)(2,1)S(1)}, bf16[16,512]{1,0:T(8,128)(2,1)S(1)}, u32[]{:S(2)}, u32[]{:S(2)}) collective-permute-start(bf16[16,512]{1,0:T(8,128)(2,1)S(1)} %copy-done.1), channel_id=1, source_target_pairs={{0,4},{1,5},{2,6},{3,7},{4,0},{5,1},{6,2},{7,3},{8,12},{9,13},{10,... | collective-permute-start | bytes 49160 | tf_op jit(solution)/shard_map/ppermute | solution.py:53
  5.8 2.6 %collective-permute-start.1 = (bf16[16,512]{1,0:T(8,128)(2,1)S(1)}, bf16[16,512]{1,0:T(8,128)(2,1)S(1)}, u32[]{:S(2)}, u32[]{:S(2)}) collective-permute-start(bf16[16,512]{1,0:T(8,128)(2,1)S(1)} %copy-done.1), channel_id=1, source_target_pairs={{0,8},{1,9},{2,10},{3,11},{4,12},{5,13},{6,14},{7,15},{8,0},{9,1},... | collective-permute-start | bytes 49160 | tf_op jit(solution)/shard_map/ppermute | solution.py:53
  8.7 1.9 %collective-permute-done.1.refs_2_ = bf16[16,512]{1,0:T(8,128)(2,1)S(1)} collective-permute-done((bf16[16,512]{1,0:T(8,128)(2,1)S(1)}, bf16[16,512]{1,0:T(8,128)(2,1)S(1)}, u32[]{:S(2)}, u32[]{:S(2)}) %collective-permute-start.1) | collective-permute-done | bytes 16416 | tf_op jit(solution)/shard_map/ppermute | solution.py:53
  10.5 3.4 %collective-permute-done.2.refs_3_ = bf16[16,512]{1,0:T(8,128)(2,1)S(1)} collective-permute-done((bf16[16,512]{1,0:T(8,128)(2,1)S(1)}, bf16[16,512]{1,0:T(8,128)(2,1)S(1)}, u32[]{:S(2)}, u32[]{:S(2)}) %collective-permute-start.2) | collective-permute-done | bytes 16416 | tf_op jit(solution)/shard_map/ppermute | solution.py:53
  15.5 3.6 %collective-permute-start.8 = (bf16[544,128]{1,0:T(8,128)(2,1)S(1)}, bf16[544,128]{1,0:T(8,128)(2,1)S(1)}, u32[]{:S(2)}, u32[]{:S(2)}) collective-permute-start(bf16[544,128]{1,0:T(8,128)(2,1)S(1)} %get-tuple-element.32), channel_id=1, source_target_pairs={{0,12},{1,13},{2,14},{3,15},{4,8},{5,9},{6,10},{7,11},{8,4},{9,5},... | collective-permute-start | bytes 417800 | tf_op jit(solution)/shard_map/ppermute | solution.py:53
  21.8 4.7 %collective-permute-done.7.refs_2_ = bf16[544,128]{1,0:T(8,128)(2,1)S(1)} collective-permute-done((bf16[544,128]{1,0:T(8,128)(2,1)S(1)}, bf16[544,128]{1,0:T(8,128)(2,1)S(1)}, u32[]{:S(2)}, u32[]{:S(2)}) %collective-permute-start.7) | collective-permute-done | bytes 139296 | tf_op jit(solution)/shard_map/ppermute | solution.py:53
  26.7 1.9 %collective-permute-done.9.refs_2_ = bf16[2176,128]{1,0:T(8,128)(2,1)S(1)} collective-permute-done((bf16[2176,128]{1,0:T(8,128)(2,1)S(1)}, bf16[2176,128]{1,0:T(8,128)(2,1)S(1)}, u32[]{:S(2)}, u32[]{:S(2)}) %collective-permute-start.9) | collective-permute-done | bytes 557088 | tf_op jit(solution)/shard_map/ppermute | solution.py:53
  28.7 4.5 %shard_map.107 = (bf16[16,512]{1,0:T(8,128)(2,1)S(1)}, f32[16,4096]{1,0:T(8,128)S(1)}) custom-call(bf16[16,512]{1,0:T(8,128)(2,1)S(1)} %shard_map.102.refs_4_.refs_0_, bf16[2176,128]{1,0:T(8,128)(2,1)S(1)} %shard_map.106.refs_1_, bf16[2176,128]{1,0:T(8,128)(2,1)S(1)} %collective-permute-done.9.refs_2_, bf16[512,8192]{1,0:T(8,128)(2,1)S(1)} %bitcast.4), custom_call_target="tpu_custom_call" | custom-call | tf_op jit(solution)/shard_map/pallas_call | solution.py:30
  34.8 1.3 %collective-permute-start.11 = (f32[16,2048]{1,0:T(8,128)S(1)}, f32[16,2048]{1,0:T(8,128)S(1)}, u32[]{:S(2)}, u32[]{:S(2)}) collective-permute-start(f32[16,2048]{1,0:T(8,128)S(1)} %get-tuple-element.36), channel_id=1, source_target_pairs={{0,2},{1,3},{2,0},{3,1},{4,6},{5,7},{6,4},{7,5},{8,10},{9,11},{10,... | collective-permute-start | bytes 393224 | tf_op jit(solution)/shard_map/ppermute | solution.py:53
  36.2 4.3 %collective-permute-done.11.refs_1_ = f32[16,2048]{1,0:T(8,128)S(1)} collective-permute-done((f32[16,2048]{1,0:T(8,128)S(1)}, f32[16,2048]{1,0:T(8,128)S(1)}, u32[]{:S(2)}, u32[]{:S(2)}) %collective-permute-start.11) | collective-permute-done | bytes 131104 | tf_op jit(solution)/shard_map/ppermute | solution.py:53
  40.5 2.1 %collective-permute-start.12 = (f32[16,512]{1,0:T(8,128)S(1)}, f32[16,512]{1,0:T(8,128)S(1)}, u32[]{:S(2)}, u32[]{:S(2)}) collective-permute-start(f32[16,512]{1,0:T(8,128)S(1)} %get-tuple-element.38), channel_id=1, source_target_pairs={{0,4},{1,5},{2,6},{3,7},{4,0},{5,1},{6,2},{7,3},{8,12},{9,13},{10,... | collective-permute-start | bytes 98312 | tf_op jit(solution)/shard_map/ppermute | solution.py:53
  42.7 2.3 %collective-permute-start.14 = (f32[16,512]{1,0:T(8,128)S(1)}, f32[16,512]{1,0:T(8,128)S(1)}, u32[]{:S(2)}, u32[]{:S(2)}) collective-permute-start(f32[16,512]{1,0:T(8,128)S(1)} %get-tuple-element.40), channel_id=1, source_target_pairs={{0,12},{1,13},{2,14},{3,15},{4,8},{5,9},{6,10},{7,11},{8,4},{9,5},... | collective-permute-start | bytes 98312 | tf_op jit(solution)/shard_map/ppermute | solution.py:53
  45.0 2.4 %collective-permute-done.13.refs_3_ = f32[16,512]{1,0:T(8,128)S(1)} collective-permute-done((f32[16,512]{1,0:T(8,128)S(1)}, f32[16,512]{1,0:T(8,128)S(1)}, u32[]{:S(2)}, u32[]{:S(2)}) %collective-permute-start.13) | collective-permute-done | bytes 32800 | tf_op jit(solution)/shard_map/ppermute | solution.py:53
  48.6 2.8 %collective-permute-start.16 = (bf16[16,512]{1,0:T(8,128)(2,1)S(1)}, bf16[16,512]{1,0:T(8,128)(2,1)S(1)}, u32[]{:S(2)}, u32[]{:S(2)}) collective-permute-start(bf16[16,512]{1,0:T(8,128)(2,1)S(1)} %shard_map.111.refs_0_), channel_id=1, source_target_pairs={{0,8},{1,9},{2,10},{3,11},{4,12},{5,13},{6,14},{7,15},{8,0},{9,1},... | collective-permute-start | bytes 49160 | tf_op jit(solution)/shard_map/ppermute | solution.py:53
  51.4 1.5 %collective-permute-start.17 = (bf16[16,512]{1,0:T(8,128)(2,1)S(1)}, bf16[16,512]{1,0:T(8,128)(2,1)S(1)}, u32[]{:S(2)}, u32[]{:S(2)}) collective-permute-start(bf16[16,512]{1,0:T(8,128)(2,1)S(1)} %shard_map.111.refs_0_), channel_id=1, source_target_pairs={{0,12},{1,13},{2,14},{3,15},{4,8},{5,9},{6,10},{7,11},{8,4},{9,5},... | collective-permute-start | bytes 49160 | tf_op jit(solution)/shard_map/ppermute | solution.py:53
  53.3 3.7 %collective-permute-done.17.refs_3_ = bf16[16,512]{1,0:T(8,128)(2,1)S(1)} collective-permute-done((bf16[16,512]{1,0:T(8,128)(2,1)S(1)}, bf16[16,512]{1,0:T(8,128)(2,1)S(1)}, u32[]{:S(2)}, u32[]{:S(2)}) %collective-permute-start.17) | collective-permute-done | bytes 16416 | tf_op jit(solution)/shard_map/ppermute | solution.py:53
  58.2 3.0 %collective-permute-done.18.refs_1_ = bf16[16,2048]{1,0:T(8,128)(2,1)S(1)} collective-permute-done((bf16[16,2048]{1,0:T(8,128)(2,1)S(1)}, bf16[16,2048]{1,0:T(8,128)(2,1)S(1)}, u32[]{:S(2)}, u32[]{:S(2)}) %collective-permute-start.18) | collective-permute-done | bytes 65568 | tf_op jit(solution)/shard_map/ppermute | solution.py:53
  62.8 5.1 %shard_map.114 = (bf16[16,896]{1,0:T(8,128)(2,1)S(1)}, f32[16,4096]{1,0:T(8,128)S(1)}) custom-call(bf16[16,2048]{1,0:T(8,128)(2,1)S(1)} %shard_map.112.refs_0_, bf16[16,2048]{1,0:T(8,128)(2,1)S(1)} %collective-permute-done.18.refs_1_, bf16[16,4096]{1,0:T(8,128)(2,1)S(1)} %collective-permute-done.19.refs_2_, bf16[1,8192]{1,0:T(2,128)(2,1)S(1)} %reshape.7.refs_3_, ...), custom_call_target="tpu_custom_call" | custom-call | tf_op jit(solution)/shard_map/pallas_call | solution.py:30
  69.4 1.3 %collective-permute-start.21 = (bf16[16,2048]{1,0:T(8,128)(2,1)S(1)}, bf16[16,2048]{1,0:T(8,128)(2,1)S(1)}, u32[]{:S(2)}, u32[]{:S(2)}) collective-permute-start(bf16[16,2048]{1,0:T(8,128)(2,1)S(1)} %get-tuple-element.44), channel_id=1, source_target_pairs={{0,2},{1,3},{2,0},{3,1},{4,6},{5,7},{6,4},{7,5},{8,10},{9,11},{10,... | collective-permute-start | bytes 196616 | tf_op jit(solution)/shard_map/ppermute | solution.py:53
  70.8 3.0 %collective-permute-done.21.refs_1_ = bf16[16,2048]{1,0:T(8,128)(2,1)S(1)} collective-permute-done((bf16[16,2048]{1,0:T(8,128)(2,1)S(1)}, bf16[16,2048]{1,0:T(8,128)(2,1)S(1)}, u32[]{:S(2)}, u32[]{:S(2)}) %collective-permute-start.21) | collective-permute-done | bytes 65568 | tf_op jit(solution)/shard_map/ppermute | solution.py:53
  73.8 2.0 %collective-permute-start.23 = (f32[16,512]{1,0:T(8,128)S(1)}, f32[16,512]{1,0:T(8,128)S(1)}, u32[]{:S(2)}, u32[]{:S(2)}) collective-permute-start(f32[16,512]{1,0:T(8,128)S(1)} %get-tuple-element.47), channel_id=1, source_target_pairs={{0,8},{1,9},{2,10},{3,11},{4,12},{5,13},{6,14},{7,15},{8,0},{9,1},... | collective-permute-start | bytes 98312 | tf_op jit(solution)/shard_map/ppermute | solution.py:53
  75.9 2.3 %collective-permute-start.24 = (f32[16,512]{1,0:T(8,128)S(1)}, f32[16,512]{1,0:T(8,128)S(1)}, u32[]{:S(2)}, u32[]{:S(2)}) collective-permute-start(f32[16,512]{1,0:T(8,128)S(1)} %get-tuple-element.48), channel_id=1, source_target_pairs={{0,12},{1,13},{2,14},{3,15},{4,8},{5,9},{6,10},{7,11},{8,4},{9,5},... | collective-permute-start | bytes 98312 | tf_op jit(solution)/shard_map/ppermute | solution.py:53
  78.7 2.8 %collective-permute-done.24.refs_4_ = f32[16,512]{1,0:T(8,128)S(1)} collective-permute-done((f32[16,512]{1,0:T(8,128)S(1)}, f32[16,512]{1,0:T(8,128)S(1)}, u32[]{:S(2)}, u32[]{:S(2)}) %collective-permute-start.24) | collective-permute-done | bytes 32800 | tf_op jit(solution)/shard_map/ppermute | solution.py:53
  (95 shorter events, 14.6 us)
Async XLA Ops:
  1.3 13.2 %collective-permute-start.5 = (bf16[272,512]{1,0:T(8,128)(2,1)S(1)}, bf16[272,512]{1,0:T(8,128)(2,1)S(1)}, u32[]{:S(2)}, u32[]{:S(2)}) collective-permute-start(bf16[272,512]{1,0:T(8,128)(2,1)S(1)} %get-tuple-element.28), channel_id=1, source_target_pairs={{0,2},{1,3},{2,0},{3,1},{4,6},{5,7},{6,4},{7,5},{8,10},{9,11},{10,... | collective-permute-start | bytes 835592 | tf_op jit(solution)/shard_map/ppermute | solution.py:53
  4.3 4.4 %collective-permute-start = (bf16[16,512]{1,0:T(8,128)(2,1)S(1)}, bf16[16,512]{1,0:T(8,128)(2,1)S(1)}, u32[]{:S(2)}, u32[]{:S(2)}) collective-permute-start(bf16[16,512]{1,0:T(8,128)(2,1)S(1)} %copy-done.1), channel_id=1, source_target_pairs={{0,4},{1,5},{2,6},{3,7},{4,0},{5,1},{6,2},{7,3},{8,12},{9,13},{10,... | collective-permute-start | bytes 49160 | tf_op jit(solution)/shard_map/ppermute | solution.py:53
  5.8 4.7 %collective-permute-start.1 = (bf16[16,512]{1,0:T(8,128)(2,1)S(1)}, bf16[16,512]{1,0:T(8,128)(2,1)S(1)}, u32[]{:S(2)}, u32[]{:S(2)}) collective-permute-start(bf16[16,512]{1,0:T(8,128)(2,1)S(1)} %copy-done.1), channel_id=1, source_target_pairs={{0,8},{1,9},{2,10},{3,11},{4,12},{5,13},{6,14},{7,15},{8,0},{9,1},... | collective-permute-start | bytes 49160 | tf_op jit(solution)/shard_map/ppermute | solution.py:53
  8.4 5.5 %collective-permute-start.2 = (bf16[16,512]{1,0:T(8,128)(2,1)S(1)}, bf16[16,512]{1,0:T(8,128)(2,1)S(1)}, u32[]{:S(2)}, u32[]{:S(2)}) collective-permute-start(bf16[16,512]{1,0:T(8,128)(2,1)S(1)} %copy-done.1), channel_id=1, source_target_pairs={{0,12},{1,13},{2,14},{3,15},{4,8},{5,9},{6,10},{7,11},{8,4},{9,5},... | collective-permute-start | bytes 49160 | tf_op jit(solution)/shard_map/ppermute | solution.py:53
  14.0 5.1 %collective-permute-start.3 = (bf16[16,2048]{1,0:T(8,128)(2,1)S(1)}, bf16[16,2048]{1,0:T(8,128)(2,1)S(1)}, u32[]{:S(2)}, u32[]{:S(2)}) collective-permute-start(bf16[16,2048]{1,0:T(8,128)(2,1)S(1)} %shard_map.100.refs_0_.refs_2_), channel_id=1, source_target_pairs={{0,2},{1,3},{2,0},{3,1},{4,6},{5,7},{6,4},{7,5},{8,10},{9,11},{10,... | collective-permute-start | bytes 196616 | tf_op jit(solution)/shard_map/ppermute | solution.py:53
  14.6 7.2 %collective-permute-start.6 = (bf16[544,128]{1,0:T(8,128)(2,1)S(1)}, bf16[544,128]{1,0:T(8,128)(2,1)S(1)}, u32[]{:S(2)}, u32[]{:S(2)}) collective-permute-start(bf16[544,128]{1,0:T(8,128)(2,1)S(1)} %get-tuple-element.30), channel_id=1, source_target_pairs={{0,4},{1,5},{2,6},{3,7},{4,0},{5,1},{6,2},{7,3},{8,12},{9,13},{10,... | collective-permute-start | bytes 417800 | tf_op jit(solution)/shard_map/ppermute | solution.py:53
  14.7 11.9 %collective-permute-start.7 = (bf16[544,128]{1,0:T(8,128)(2,1)S(1)}, bf16[544,128]{1,0:T(8,128)(2,1)S(1)}, u32[]{:S(2)}, u32[]{:S(2)}) collective-permute-start(bf16[544,128]{1,0:T(8,128)(2,1)S(1)} %get-tuple-element.31), channel_id=1, source_target_pairs={{0,8},{1,9},{2,10},{3,11},{4,12},{5,13},{6,14},{7,15},{8,0},{9,1},... | collective-permute-start | bytes 417800 | tf_op jit(solution)/shard_map/ppermute | solution.py:53
  15.5 11.1 %collective-permute-start.8 = (bf16[544,128]{1,0:T(8,128)(2,1)S(1)}, bf16[544,128]{1,0:T(8,128)(2,1)S(1)}, u32[]{:S(2)}, u32[]{:S(2)}) collective-permute-start(bf16[544,128]{1,0:T(8,128)(2,1)S(1)} %get-tuple-element.32), channel_id=1, source_target_pairs={{0,12},{1,13},{2,14},{3,15},{4,8},{5,9},{6,10},{7,11},{8,4},{9,5},... | collective-permute-start | bytes 417800 | tf_op jit(solution)/shard_map/ppermute | solution.py:53
  19.1 1.4 %collective-permute-start.4 = (bf16[16,4096]{1,0:T(8,128)(2,1)S(1)}, bf16[16,4096]{1,0:T(8,128)(2,1)S(1)}, u32[]{:S(2)}, u32[]{:S(2)}) collective-permute-start(bf16[16,4096]{1,0:T(8,128)(2,1)S(1)} %shard_map.101), channel_id=1, source_target_pairs={{0,1},{1,0},{2,3},{3,2},{4,5},{5,4},{6,7},{7,6},{8,9},{9,8},{10,11... | collective-permute-start | bytes 393224 | tf_op jit(solution)/shard_map/ppermute | solution.py:53
  26.6 2.0 %collective-permute-start.9 = (bf16[2176,128]{1,0:T(8,128)(2,1)S(1)}, bf16[2176,128]{1,0:T(8,128)(2,1)S(1)}, u32[]{:S(2)}, u32[]{:S(2)}) collective-permute-start(bf16[2176,128]{1,0:T(8,128)(2,1)S(1)} %shard_map.106.refs_1_), channel_id=1, source_target_pairs={{0,1},{1,0},{2,3},{3,2},{4,5},{5,4},{6,7},{7,6},{8,9},{9,8},{10,11... | collective-permute-start | bytes 1671176 | tf_op jit(solution)/shard_map/ppermute | solution.py:53
  33.2 1.5 %collective-permute-start.10 = (f32[16,4096]{1,0:T(8,128)S(1)}, f32[16,4096]{1,0:T(8,128)S(1)}, u32[]{:S(2)}, u32[]{:S(2)}) collective-permute-start(f32[16,4096]{1,0:T(8,128)S(1)} %get-tuple-element.34), channel_id=1, source_target_pairs={{0,1},{1,0},{2,3},{3,2},{4,5},{5,4},{6,7},{7,6},{8,9},{9,8},{10,11... | collective-permute-start | bytes 786440 | tf_op jit(solution)/shard_map/ppermute | solution.py:53
  34.8 5.6 %collective-permute-start.11 = (f32[16,2048]{1,0:T(8,128)S(1)}, f32[16,2048]{1,0:T(8,128)S(1)}, u32[]{:S(2)}, u32[]{:S(2)}) collective-permute-start(f32[16,2048]{1,0:T(8,128)S(1)} %get-tuple-element.36), channel_id=1, source_target_pairs={{0,2},{1,3},{2,0},{3,1},{4,6},{5,7},{6,4},{7,5},{8,10},{9,11},{10,... | collective-permute-start | bytes 393224 | tf_op jit(solution)/shard_map/ppermute | solution.py:53
  40.5 4.6 %collective-permute-start.12 = (f32[16,512]{1,0:T(8,128)S(1)}, f32[16,512]{1,0:T(8,128)S(1)}, u32[]{:S(2)}, u32[]{:S(2)}) collective-permute-start(f32[16,512]{1,0:T(8,128)S(1)} %get-tuple-element.38), channel_id=1, source_target_pairs={{0,4},{1,5},{2,6},{3,7},{4,0},{5,1},{6,2},{7,3},{8,12},{9,13},{10,... | collective-permute-start | bytes 98312 | tf_op jit(solution)/shard_map/ppermute | solution.py:53
  42.6 4.8 %collective-permute-start.13 = (f32[16,512]{1,0:T(8,128)S(1)}, f32[16,512]{1,0:T(8,128)S(1)}, u32[]{:S(2)}, u32[]{:S(2)}) collective-permute-start(f32[16,512]{1,0:T(8,128)S(1)} %get-tuple-element.39), channel_id=1, source_target_pairs={{0,8},{1,9},{2,10},{3,11},{4,12},{5,13},{6,14},{7,15},{8,0},{9,1},... | collective-permute-start | bytes 98312 | tf_op jit(solution)/shard_map/ppermute | solution.py:53
  42.7 5.7 %collective-permute-start.14 = (f32[16,512]{1,0:T(8,128)S(1)}, f32[16,512]{1,0:T(8,128)S(1)}, u32[]{:S(2)}, u32[]{:S(2)}) collective-permute-start(f32[16,512]{1,0:T(8,128)S(1)} %get-tuple-element.40), channel_id=1, source_target_pairs={{0,12},{1,13},{2,14},{3,15},{4,8},{5,9},{6,10},{7,11},{8,4},{9,5},... | collective-permute-start | bytes 98312 | tf_op jit(solution)/shard_map/ppermute | solution.py:53
  48.4 4.5 %collective-permute-start.15 = (bf16[16,512]{1,0:T(8,128)(2,1)S(1)}, bf16[16,512]{1,0:T(8,128)(2,1)S(1)}, u32[]{:S(2)}, u32[]{:S(2)}) collective-permute-start(bf16[16,512]{1,0:T(8,128)(2,1)S(1)} %shard_map.111.refs_0_), channel_id=1, source_target_pairs={{0,4},{1,5},{2,6},{3,7},{4,0},{5,1},{6,2},{7,3},{8,12},{9,13},{10,... | collective-permute-start | bytes 49160 | tf_op jit(solution)/shard_map/ppermute | solution.py:53
  48.6 4.6 %collective-permute-start.16 = (bf16[16,512]{1,0:T(8,128)(2,1)S(1)}, bf16[16,512]{1,0:T(8,128)(2,1)S(1)}, u32[]{:S(2)}, u32[]{:S(2)}) collective-permute-start(bf16[16,512]{1,0:T(8,128)(2,1)S(1)} %shard_map.111.refs_0_), channel_id=1, source_target_pairs={{0,8},{1,9},{2,10},{3,11},{4,12},{5,13},{6,14},{7,15},{8,0},{9,1},... | collective-permute-start | bytes 49160 | tf_op jit(solution)/shard_map/ppermute | solution.py:53
  51.4 5.5 %collective-permute-start.17 = (bf16[16,512]{1,0:T(8,128)(2,1)S(1)}, bf16[16,512]{1,0:T(8,128)(2,1)S(1)}, u32[]{:S(2)}, u32[]{:S(2)}) collective-permute-start(bf16[16,512]{1,0:T(8,128)(2,1)S(1)} %shard_map.111.refs_0_), channel_id=1, source_target_pairs={{0,12},{1,13},{2,14},{3,15},{4,8},{5,9},{6,10},{7,11},{8,4},{9,5},... | collective-permute-start | bytes 49160 | tf_op jit(solution)/shard_map/ppermute | solution.py:53
  56.9 4.3 %collective-permute-start.18 = (bf16[16,2048]{1,0:T(8,128)(2,1)S(1)}, bf16[16,2048]{1,0:T(8,128)(2,1)S(1)}, u32[]{:S(2)}, u32[]{:S(2)}) collective-permute-start(bf16[16,2048]{1,0:T(8,128)(2,1)S(1)} %shard_map.112.refs_0_), channel_id=1, source_target_pairs={{0,2},{1,3},{2,0},{3,1},{4,6},{5,7},{6,4},{7,5},{8,10},{9,11},{10,... | collective-permute-start | bytes 196616 | tf_op jit(solution)/shard_map/ppermute | solution.py:53
  67.8 1.5 %collective-permute-start.20 = (f32[16,4096]{1,0:T(8,128)S(1)}, f32[16,4096]{1,0:T(8,128)S(1)}, u32[]{:S(2)}, u32[]{:S(2)}) collective-permute-start(f32[16,4096]{1,0:T(8,128)S(1)} %get-tuple-element.42), channel_id=1, source_target_pairs={{0,1},{1,0},{2,3},{3,2},{4,5},{5,4},{6,7},{7,6},{8,9},{9,8},{10,11... | collective-permute-start | bytes 786440 | tf_op jit(solution)/shard_map/ppermute | solution.py:53
  69.4 4.3 %collective-permute-start.21 = (bf16[16,2048]{1,0:T(8,128)(2,1)S(1)}, bf16[16,2048]{1,0:T(8,128)(2,1)S(1)}, u32[]{:S(2)}, u32[]{:S(2)}) collective-permute-start(bf16[16,2048]{1,0:T(8,128)(2,1)S(1)} %get-tuple-element.44), channel_id=1, source_target_pairs={{0,2},{1,3},{2,0},{3,1},{4,6},{5,7},{6,4},{7,5},{8,10},{9,11},{10,... | collective-permute-start | bytes 196616 | tf_op jit(solution)/shard_map/ppermute | solution.py:53
  73.8 4.5 %collective-permute-start.22 = (f32[16,512]{1,0:T(8,128)S(1)}, f32[16,512]{1,0:T(8,128)S(1)}, u32[]{:S(2)}, u32[]{:S(2)}) collective-permute-start(f32[16,512]{1,0:T(8,128)S(1)} %get-tuple-element.46), channel_id=1, source_target_pairs={{0,4},{1,5},{2,6},{3,7},{4,0},{5,1},{6,2},{7,3},{8,12},{9,13},{10,... | collective-permute-start | bytes 98312 | tf_op jit(solution)/shard_map/ppermute | solution.py:53
  73.8 4.9 %collective-permute-start.23 = (f32[16,512]{1,0:T(8,128)S(1)}, f32[16,512]{1,0:T(8,128)S(1)}, u32[]{:S(2)}, u32[]{:S(2)}) collective-permute-start(f32[16,512]{1,0:T(8,128)S(1)} %get-tuple-element.47), channel_id=1, source_target_pairs={{0,8},{1,9},{2,10},{3,11},{4,12},{5,13},{6,14},{7,15},{8,0},{9,1},... | collective-permute-start | bytes 98312 | tf_op jit(solution)/shard_map/ppermute | solution.py:53
  75.9 5.7 %collective-permute-start.24 = (f32[16,512]{1,0:T(8,128)S(1)}, f32[16,512]{1,0:T(8,128)S(1)}, u32[]{:S(2)}, u32[]{:S(2)}) collective-permute-start(f32[16,512]{1,0:T(8,128)S(1)} %get-tuple-element.48), channel_id=1, source_target_pairs={{0,12},{1,13},{2,14},{3,15},{4,8},{5,9},{6,10},{7,11},{8,4},{9,5},... | collective-permute-start | bytes 98312 | tf_op jit(solution)/shard_map/ppermute | solution.py:53
  (22 other events, 386.8 us)

commit v3 on v2

--- a/solution.py
+++ b/solution.py
@@ -74,7 +74,7 @@
             out[2 * keys : 2 * keys + rows, at] = live_lanes(mask, head, rows)
 
 
-def route_kernel(outer, own_ref, other_ref, order_ref, *outs):
+def route_kernel(outer, own_ref, other_ref, *outs):
     z = lax.axis_index("seq") // QUAD
     size = own_ref.shape[0]
     for k in range(outer):
@@ -147,8 +147,7 @@
     scatter_dot(wide, left_ref[...], w_ref, out_ref, distances)
 
 
-def attend_kernel(wide, distances, spans, q_ref, *refs):
-    cache, w_ref, left_ref, send_ref = refs[:-3], *refs[-3:]
+def span_states(spans, q_ref, cache):
     rows = q_ref.shape[0]
     heads = q_ref.shape[1] // HEAD_DIM
     scale = 1.0 / HEAD_DIM**0.5
@@ -156,10 +155,10 @@
         [q_ref[:, h * HEAD_DIM : (h + 1) * HEAD_DIM] for h in range(heads)], axis=0
     )
     states = []
-    for ref, count in zip(cache, spans):
-        size = ref.shape[0] // count
+    for ref in cache:
+        size = ref.shape[0] // spans
         keys = (size - rows) // 2
-        for k in range(count):
+        for k in range(spans):
             at = k * size
             live = ref[at + 2 * keys : at + size, :].astype(f32)
             live = jnp.concatenate([live] * heads, axis=0) > 0.5
@@ -180,12 +179,33 @@
                 weight.astype(bf16), ref[at + keys : at + 2 * keys, :], preferred_element_type=f32
             )
             states.append((top, total, accum))
+    return states
+
+
+def combined(states):
     top = functools.reduce(jnp.maximum, [s[0] for s in states])
     total = accum = None
     for t, s, a in states:
         factor = jnp.exp(t - top)
         total = s * factor if total is None else total + s * factor
         accum = a * factor if accum is None else accum + a * factor
+    return top, total, accum
+
+
+def early_kernel(spans, q_ref, *refs):
+    cache, (top_ref, total_ref, accum_ref) = refs[:-3], refs[-3:]
+    top, total, accum_ref[...] = combined(span_states(spans, q_ref, cache))
+    top_ref[...] = jnp.broadcast_to(top, top_ref.shape)
+    total_ref[...] = jnp.broadcast_to(total, total_ref.shape)
+
+
+def attend_kernel(wide, distances, spans, q_ref, top_ref, total_ref, accum_ref, *refs):
+    cache, w_ref, left_ref, send_ref = refs[:-3], *refs[-3:]
+    rows = q_ref.shape[0]
+    heads = q_ref.shape[1] // HEAD_DIM
+    states = span_states(spans, q_ref, cache)
+    states.append((top_ref[:, 0:1], total_ref[:, 0:1], accum_ref[...]))
+    _, total, accum = combined(states)
     attended = (accum / total).astype(bf16)
     attended = jnp.concatenate([attended[h * rows : (h + 1) * rows] for h in range(heads)], axis=1)
     left_ref[...] = attended
@@ -224,13 +244,18 @@
     refs[-1][...] = (base_ref[...].astype(f32) + total).astype(bf16)
 
 
+def z_swapped(parts):
+    arrived = [swap(part, QUAD * k) for k, part in reversed(list(enumerate(parts))) if k > 0]
+    return [parts[0], *reversed(arrived)]
+
+
 def z_gathered(x, outer):
-    return stacked([x] + [swap(x, QUAD * k) for k in range(1, outer)], 1)
-
-
-def near_gathered(line):
+    return stacked(z_swapped([x] * outer), 1)
+
+
+def near_gathered(line, after=()):
     other = swap(line, 2)
-    return [line, other, swap(stacked([line, other], 1), 1)]
+    return [line, other, swap(stacked([line, other], 1, after), 1)]
 
 
 def scattered(base, send, left, weight, outer, wide, y_type, z_type, beside=()):
@@ -269,26 +294,29 @@
         beside,
     )
     other = swap(send, 2)
-    line = z_gathered(x_rows, outer)
+    x_line = z_swapped([x_rows] * outer)
+    line = stacked(x_line, 1)
     routed = call(
         functools.partial(route_kernel, outer),
         [like((2 * size, HEAD_DIM), bf16)] * outer,
-        [own, other, line],
-        beside,
-    )
+        [own, other],
+        [*[], *beside],
+    )
+    cache = z_swapped(routed)
     x_parts = near_gathered(line)
     queries = call(
         functools.partial(query_kernel, outer, wide),
         like((rows, columns), bf16),
         [*x_parts, attn_gain, q_weight],
     )
-    arrived = [swap(routed[k], QUAD * k) for k in range(1, outer)]
-    mine = stacked([routed[0], *arrived], 0, [queries])
-    cache = [mine, swap(mine, 1)]
+    first = stacked(cache, 0, [queries])
+    second = swap(first, 1)
+    tall = like((columns // HEAD_DIM * rows, HEAD_DIM), f32)
+    early = call(functools.partial(early_kernel, 2 * outer), [tall] * 3, [queries, first])
     left, send = call(
-        functools.partial(attend_kernel, wide, near, [2 * outer] * 2),
+        functools.partial(attend_kernel, wide, near, 2 * outer),
         [like((rows, columns), bf16), like((rows, 2 * outer * wide), f32)],
-        [queries, *cache, o_weight],
+        [queries, *early, second, o_weight],
     )
     stream = scattered(x_rows, send, left, o_weight, outer, wide, f32, f32, beside)
     parts = near_gathered(z_gathered(stream, outer))

time: 82.4 us -> 81 us (0.983)
  waiting for transfers between devices: 36.7 us -> 34.8 us
    ppermute x25, waiting for transfers between devices: 36.7 us -> 34.8 us  [swap(): return lax.ppermute(x, 'seq', [(i, i ^ distance) for i in range(size)])]
    pallas_call x18 -> x19, Pallas kernels: 13.7 us -> 13.9 us  [call(): pl.pallas_call(kernel, out_shape=outs, in_specs=[VMEM] * count + [pl.Bloc...]
  transfers between devices with their start and end apart: 25 -> 25, of which waited for: 17 -> 16; matrix products, arithmetic and copies ran while one was open for 0% -> 0% of each run, Pallas kernels for 4% -> 6%
where the time goes in v3:
time: 81 us; the launch traced here: 80.8 us
  waiting for transfers between devices  34.8 us (43%)
  starting transfers between devices  30.6 us (38%)
  Pallas kernels  13.9 us (17%)
  local copies, waits for them, and re-layouts  1.17 us (1%)
    ppermute x25, waiting for transfers between devices, swap(): return lax.ppermute(x, 'seq', [(i, i ^ distance) for i in range(size)])  34.8 us
    ppermute x25, starting transfers between devices, swap(): return lax.ppermute(x, 'seq', [(i, i ^ distance) for i in range(size)])  30.6 us
    pallas_call x19, Pallas kernels, call(): pl.pallas_call(kernel, out_shape=outs, in_specs=[VMEM] * count + [pl.Bloc...  13.9 us
  transfers between devices with their start and end apart: 25, of which 16 were waited for; matrix products, arithmetic and copies ran while one was open for 0% of the time, Pallas kernels for 6%

profile of v3, /device:TPU:0, one launch (start us, length us, event | category | flops | bytes accessed | tf_op | source)
XLA Modules:
  0.0 80.8 jit_solution(6350811716654605877)
XLA Ops:
  1.3 3.0 %collective-permute-start.5 = (bf16[272,512]{1,0:T(8,128)(2,1)S(1)}, bf16[272,512]{1,0:T(8,128)(2,1)S(1)}, u32[]{:S(2)}, u32[]{:S(2)}) collective-permute-start(bf16[272,512]{1,0:T(8,128)(2,1)S(1)} %get-tuple-element.31), channel_id=1, source_target_pairs={{0,2},{1,3},{2,0},{3,1},{4,6},{5,7},{6,4},{7,5},{8,10},{9,11},{10,... | collective-permute-start | bytes 835592 | tf_op jit(solution)/shard_map/ppermute | solution.py:53
  4.3 1.6 %collective-permute-start = (bf16[16,512]{1,0:T(8,128)(2,1)S(1)}, bf16[16,512]{1,0:T(8,128)(2,1)S(1)}, u32[]{:S(2)}, u32[]{:S(2)}) collective-permute-start(bf16[16,512]{1,0:T(8,128)(2,1)S(1)} %copy-done.1), channel_id=1, source_target_pairs={{0,4},{1,5},{2,6},{3,7},{4,0},{5,1},{6,2},{7,3},{8,12},{9,13},{10,... | collective-permute-start | bytes 49160 | tf_op jit(solution)/shard_map/ppermute | solution.py:53
  5.8 2.6 %collective-permute-start.1 = (bf16[16,512]{1,0:T(8,128)(2,1)S(1)}, bf16[16,512]{1,0:T(8,128)(2,1)S(1)}, u32[]{:S(2)}, u32[]{:S(2)}) collective-permute-start(bf16[16,512]{1,0:T(8,128)(2,1)S(1)} %copy-done.1), channel_id=1, source_target_pairs={{0,8},{1,9},{2,10},{3,11},{4,12},{5,13},{6,14},{7,15},{8,0},{9,1},... | collective-permute-start | bytes 49160 | tf_op jit(solution)/shard_map/ppermute | solution.py:53
  8.7 1.9 %collective-permute-done.1.refs_2_ = bf16[16,512]{1,0:T(8,128)(2,1)S(1)} collective-permute-done((bf16[16,512]{1,0:T(8,128)(2,1)S(1)}, bf16[16,512]{1,0:T(8,128)(2,1)S(1)}, u32[]{:S(2)}, u32[]{:S(2)}) %collective-permute-start.1) | collective-permute-done | bytes 16416 | tf_op jit(solution)/shard_map/ppermute | solution.py:53
  10.5 3.4 %collective-permute-done.2.refs_3_ = bf16[16,512]{1,0:T(8,128)(2,1)S(1)} collective-permute-done((bf16[16,512]{1,0:T(8,128)(2,1)S(1)}, bf16[16,512]{1,0:T(8,128)(2,1)S(1)}, u32[]{:S(2)}, u32[]{:S(2)}) %collective-permute-start.2) | collective-permute-done | bytes 16416 | tf_op jit(solution)/shard_map/ppermute | solution.py:53
  15.5 3.6 %collective-permute-start.8 = (bf16[544,128]{1,0:T(8,128)(2,1)S(1)}, bf16[544,128]{1,0:T(8,128)(2,1)S(1)}, u32[]{:S(2)}, u32[]{:S(2)}) collective-permute-start(bf16[544,128]{1,0:T(8,128)(2,1)S(1)} %get-tuple-element.35), channel_id=1, source_target_pairs={{0,12},{1,13},{2,14},{3,15},{4,8},{5,9},{6,10},{7,11},{8,4},{9,5},... | collective-permute-start | bytes 417800 | tf_op jit(solution)/shard_map/ppermute | solution.py:53
  21.8 4.7 %collective-permute-done.7.refs_2_ = bf16[544,128]{1,0:T(8,128)(2,1)S(1)} collective-permute-done((bf16[544,128]{1,0:T(8,128)(2,1)S(1)}, bf16[544,128]{1,0:T(8,128)(2,1)S(1)}, u32[]{:S(2)}, u32[]{:S(2)}) %collective-permute-start.7) | collective-permute-done | bytes 139296 | tf_op jit(solution)/shard_map/ppermute | solution.py:53
  26.7 2.0 %shard_map.107 = (f32[64,128]{1,0:T(8,128)S(1)}, f32[64,128]{1,0:T(8,128)S(1)}, f32[64,128]{1,0:T(8,128)S(1)}) custom-call(bf16[16,512]{1,0:T(8,128)(2,1)S(1)} %shard_map.102.refs_4_.refs_0_, bf16[2176,128]{1,0:T(8,128)(2,1)S(1)} %shard_map.106.refs_1_), custom_call_target="tpu_custom_call" | custom-call | tf_op jit(solution)/shard_map/pallas_call | solution.py:30
  28.7 2.7 %shard_map.108 = (bf16[16,512]{1,0:T(8,128)(2,1)S(1)}, f32[16,4096]{1,0:T(8,128)S(1)}) custom-call(bf16[16,512]{1,0:T(8,128)(2,1)S(1)} %shard_map.102.refs_4_.refs_0_, f32[64,128]{1,0:T(8,128)S(1)} %get-tuple-element.36.refs_1_, f32[64,128]{1,0:T(8,128)S(1)} %get-tuple-element.37.refs_2_, f32[64,128]{1,0:T(8,128)S(1)} %get-tuple-element.38.refs_3_, ...), custom_call_target="tpu_custom_call" | custom-call | tf_op jit(solution)/shard_map/pallas_call | solution.py:30
  33.2 1.4 %collective-permute-start.11 = (f32[16,2048]{1,0:T(8,128)S(1)}, f32[16,2048]{1,0:T(8,128)S(1)}, u32[]{:S(2)}, u32[]{:S(2)}) collective-permute-start(f32[16,2048]{1,0:T(8,128)S(1)} %get-tuple-element.42), channel_id=1, source_target_pairs={{0,2},{1,3},{2,0},{3,1},{4,6},{5,7},{6,4},{7,5},{8,10},{9,11},{10,... | collective-permute-start | bytes 393224 | tf_op jit(solution)/shard_map/ppermute | solution.py:53
  34.6 4.5 %collective-permute-done.11.refs_1_ = f32[16,2048]{1,0:T(8,128)S(1)} collective-permute-done((f32[16,2048]{1,0:T(8,128)S(1)}, f32[16,2048]{1,0:T(8,128)S(1)}, u32[]{:S(2)}, u32[]{:S(2)}) %collective-permute-start.11) | collective-permute-done | bytes 131104 | tf_op jit(solution)/shard_map/ppermute | solution.py:53
  39.1 2.1 %collective-permute-start.12 = (f32[16,512]{1,0:T(8,128)S(1)}, f32[16,512]{1,0:T(8,128)S(1)}, u32[]{:S(2)}, u32[]{:S(2)}) collective-permute-start(f32[16,512]{1,0:T(8,128)S(1)} %get-tuple-element.44), channel_id=1, source_target_pairs={{0,4},{1,5},{2,6},{3,7},{4,0},{5,1},{6,2},{7,3},{8,12},{9,13},{10,... | collective-permute-start | bytes 98312 | tf_op jit(solution)/shard_map/ppermute | solution.py:53
  41.3 2.3 %collective-permute-start.14 = (f32[16,512]{1,0:T(8,128)S(1)}, f32[16,512]{1,0:T(8,128)S(1)}, u32[]{:S(2)}, u32[]{:S(2)}) collective-permute-start(f32[16,512]{1,0:T(8,128)S(1)} %get-tuple-element.46), channel_id=1, source_target_pairs={{0,12},{1,13},{2,14},{3,15},{4,8},{5,9},{6,10},{7,11},{8,4},{9,5},... | collective-permute-start | bytes 98312 | tf_op jit(solution)/shard_map/ppermute | solution.py:53
  43.7 2.4 %collective-permute-done.13.refs_3_ = f32[16,512]{1,0:T(8,128)S(1)} collective-permute-done((f32[16,512]{1,0:T(8,128)S(1)}, f32[16,512]{1,0:T(8,128)S(1)}, u32[]{:S(2)}, u32[]{:S(2)}) %collective-permute-start.13) | collective-permute-done | bytes 32800 | tf_op jit(solution)/shard_map/ppermute | solution.py:53
  47.3 2.8 %collective-permute-start.16 = (bf16[16,512]{1,0:T(8,128)(2,1)S(1)}, bf16[16,512]{1,0:T(8,128)(2,1)S(1)}, u32[]{:S(2)}, u32[]{:S(2)}) collective-permute-start(bf16[16,512]{1,0:T(8,128)(2,1)S(1)} %shard_map.112.refs_0_), channel_id=1, source_target_pairs={{0,8},{1,9},{2,10},{3,11},{4,12},{5,13},{6,14},{7,15},{8,0},{9,1},... | collective-permute-start | bytes 49160 | tf_op jit(solution)/shard_map/ppermute | solution.py:53
  50.0 1.5 %collective-permute-start.17 = (bf16[16,512]{1,0:T(8,128)(2,1)S(1)}, bf16[16,512]{1,0:T(8,128)(2,1)S(1)}, u32[]{:S(2)}, u32[]{:S(2)}) collective-permute-start(bf16[16,512]{1,0:T(8,128)(2,1)S(1)} %shard_map.112.refs_0_), channel_id=1, source_target_pairs={{0,12},{1,13},{2,14},{3,15},{4,8},{5,9},{6,10},{7,11},{8,4},{9,5},... | collective-permute-start | bytes 49160 | tf_op jit(solution)/shard_map/ppermute | solution.py:53
  51.9 3.7 %collective-permute-done.17.refs_3_ = bf16[16,512]{1,0:T(8,128)(2,1)S(1)} collective-permute-done((bf16[16,512]{1,0:T(8,128)(2,1)S(1)}, bf16[16,512]{1,0:T(8,128)(2,1)S(1)}, u32[]{:S(2)}, u32[]{:S(2)}) %collective-permute-start.17) | collective-permute-done | bytes 16416 | tf_op jit(solution)/shard_map/ppermute | solution.py:53
  56.9 3.0 %collective-permute-done.18.refs_1_ = bf16[16,2048]{1,0:T(8,128)(2,1)S(1)} collective-permute-done((bf16[16,2048]{1,0:T(8,128)(2,1)S(1)}, bf16[16,2048]{1,0:T(8,128)(2,1)S(1)}, u32[]{:S(2)}, u32[]{:S(2)}) %collective-permute-start.18) | collective-permute-done | bytes 65568 | tf_op jit(solution)/shard_map/ppermute | solution.py:53
  61.4 5.1 %shard_map.115 = (bf16[16,896]{1,0:T(8,128)(2,1)S(1)}, f32[16,4096]{1,0:T(8,128)S(1)}) custom-call(bf16[16,2048]{1,0:T(8,128)(2,1)S(1)} %shard_map.113.refs_0_, bf16[16,2048]{1,0:T(8,128)(2,1)S(1)} %collective-permute-done.18.refs_1_, bf16[16,4096]{1,0:T(8,128)(2,1)S(1)} %collective-permute-done.19.refs_2_, bf16[1,8192]{1,0:T(2,128)(2,1)S(1)} %reshape.7.refs_3_, ...), custom_call_target="tpu_custom_call" | custom-call | tf_op jit(solution)/shard_map/pallas_call | solution.py:30
  68.1 1.3 %collective-permute-start.21 = (bf16[16,2048]{1,0:T(8,128)(2,1)S(1)}, bf16[16,2048]{1,0:T(8,128)(2,1)S(1)}, u32[]{:S(2)}, u32[]{:S(2)}) collective-permute-start(bf16[16,2048]{1,0:T(8,128)(2,1)S(1)} %get-tuple-element.50), channel_id=1, source_target_pairs={{0,2},{1,3},{2,0},{3,1},{4,6},{5,7},{6,4},{7,5},{8,10},{9,11},{10,... | collective-permute-start | bytes 196616 | tf_op jit(solution)/shard_map/ppermute | solution.py:53
  69.4 3.0 %collective-permute-done.21.refs_1_ = bf16[16,2048]{1,0:T(8,128)(2,1)S(1)} collective-permute-done((bf16[16,2048]{1,0:T(8,128)(2,1)S(1)}, bf16[16,2048]{1,0:T(8,128)(2,1)S(1)}, u32[]{:S(2)}, u32[]{:S(2)}) %collective-permute-start.21) | collective-permute-done | bytes 65568 | tf_op jit(solution)/shard_map/ppermute | solution.py:53
  72.5 2.0 %collective-permute-start.23 = (f32[16,512]{1,0:T(8,128)S(1)}, f32[16,512]{1,0:T(8,128)S(1)}, u32[]{:S(2)}, u32[]{:S(2)}) collective-permute-start(f32[16,512]{1,0:T(8,128)S(1)} %get-tuple-element.53), channel_id=1, source_target_pairs={{0,8},{1,9},{2,10},{3,11},{4,12},{5,13},{6,14},{7,15},{8,0},{9,1},... | collective-permute-start | bytes 98312 | tf_op jit(solution)/shard_map/ppermute | solution.py:53
  74.5 2.3 %collective-permute-start.24 = (f32[16,512]{1,0:T(8,128)S(1)}, f32[16,512]{1,0:T(8,128)S(1)}, u32[]{:S(2)}, u32[]{:S(2)}) collective-permute-start(f32[16,512]{1,0:T(8,128)S(1)} %get-tuple-element.54), channel_id=1, source_target_pairs={{0,12},{1,13},{2,14},{3,15},{4,8},{5,9},{6,10},{7,11},{8,4},{9,5},... | collective-permute-start | bytes 98312 | tf_op jit(solution)/shard_map/ppermute | solution.py:53
  77.4 2.8 %collective-permute-done.24.refs_4_ = f32[16,512]{1,0:T(8,128)S(1)} collective-permute-done((f32[16,512]{1,0:T(8,128)S(1)}, f32[16,512]{1,0:T(8,128)S(1)}, u32[]{:S(2)}, u32[]{:S(2)}) %collective-permute-start.24) | collective-permute-done | bytes 32800 | tf_op jit(solution)/shard_map/ppermute | solution.py:53
  (96 shorter events, 14.8 us)
Async XLA Ops:
  1.3 13.2 %collective-permute-start.5 = (bf16[272,512]{1,0:T(8,128)(2,1)S(1)}, bf16[272,512]{1,0:T(8,128)(2,1)S(1)}, u32[]{:S(2)}, u32[]{:S(2)}) collective-permute-start(bf16[272,512]{1,0:T(8,128)(2,1)S(1)} %get-tuple-element.31), channel_id=1, source_target_pairs={{0,2},{1,3},{2,0},{3,1},{4,6},{5,7},{6,4},{7,5},{8,10},{9,11},{10,... | collective-permute-start | bytes 835592 | tf_op jit(solution)/shard_map/ppermute | solution.py:53
  4.3 4.4 %collective-permute-start = (bf16[16,512]{1,0:T(8,128)(2,1)S(1)}, bf16[16,512]{1,0:T(8,128)(2,1)S(1)}, u32[]{:S(2)}, u32[]{:S(2)}) collective-permute-start(bf16[16,512]{1,0:T(8,128)(2,1)S(1)} %copy-done.1), channel_id=1, source_target_pairs={{0,4},{1,5},{2,6},{3,7},{4,0},{5,1},{6,2},{7,3},{8,12},{9,13},{10,... | collective-permute-start | bytes 49160 | tf_op jit(solution)/shard_map/ppermute | solution.py:53
  5.8 4.7 %collective-permute-start.1 = (bf16[16,512]{1,0:T(8,128)(2,1)S(1)}, bf16[16,512]{1,0:T(8,128)(2,1)S(1)}, u32[]{:S(2)}, u32[]{:S(2)}) collective-permute-start(bf16[16,512]{1,0:T(8,128)(2,1)S(1)} %copy-done.1), channel_id=1, source_target_pairs={{0,8},{1,9},{2,10},{3,11},{4,12},{5,13},{6,14},{7,15},{8,0},{9,1},... | collective-permute-start | bytes 49160 | tf_op jit(solution)/shard_map/ppermute | solution.py:53
  8.4 5.5 %collective-permute-start.2 = (bf16[16,512]{1,0:T(8,128)(2,1)S(1)}, bf16[16,512]{1,0:T(8,128)(2,1)S(1)}, u32[]{:S(2)}, u32[]{:S(2)}) collective-permute-start(bf16[16,512]{1,0:T(8,128)(2,1)S(1)} %copy-done.1), channel_id=1, source_target_pairs={{0,12},{1,13},{2,14},{3,15},{4,8},{5,9},{6,10},{7,11},{8,4},{9,5},... | collective-permute-start | bytes 49160 | tf_op jit(solution)/shard_map/ppermute | solution.py:53
  14.0 5.1 %collective-permute-start.3 = (bf16[16,2048]{1,0:T(8,128)(2,1)S(1)}, bf16[16,2048]{1,0:T(8,128)(2,1)S(1)}, u32[]{:S(2)}, u32[]{:S(2)}) collective-permute-start(bf16[16,2048]{1,0:T(8,128)(2,1)S(1)} %shard_map.100.refs_0_), channel_id=1, source_target_pairs={{0,2},{1,3},{2,0},{3,1},{4,6},{5,7},{6,4},{7,5},{8,10},{9,11},{10,... | collective-permute-start | bytes 196616 | tf_op jit(solution)/shard_map/ppermute | solution.py:53
  14.6 7.2 %collective-permute-start.6 = (bf16[544,128]{1,0:T(8,128)(2,1)S(1)}, bf16[544,128]{1,0:T(8,128)(2,1)S(1)}, u32[]{:S(2)}, u32[]{:S(2)}) collective-permute-start(bf16[544,128]{1,0:T(8,128)(2,1)S(1)} %get-tuple-element.33), channel_id=1, source_target_pairs={{0,4},{1,5},{2,6},{3,7},{4,0},{5,1},{6,2},{7,3},{8,12},{9,13},{10,... | collective-permute-start | bytes 417800 | tf_op jit(solution)/shard_map/ppermute | solution.py:53
  14.7 11.9 %collective-permute-start.7 = (bf16[544,128]{1,0:T(8,128)(2,1)S(1)}, bf16[544,128]{1,0:T(8,128)(2,1)S(1)}, u32[]{:S(2)}, u32[]{:S(2)}) collective-permute-start(bf16[544,128]{1,0:T(8,128)(2,1)S(1)} %get-tuple-element.34), channel_id=1, source_target_pairs={{0,8},{1,9},{2,10},{3,11},{4,12},{5,13},{6,14},{7,15},{8,0},{9,1},... | collective-permute-start | bytes 417800 | tf_op jit(solution)/shard_map/ppermute | solution.py:53
  15.5 11.1 %collective-permute-start.8 = (bf16[544,128]{1,0:T(8,128)(2,1)S(1)}, bf16[544,128]{1,0:T(8,128)(2,1)S(1)}, u32[]{:S(2)}, u32[]{:S(2)}) collective-permute-start(bf16[544,128]{1,0:T(8,128)(2,1)S(1)} %get-tuple-element.35), channel_id=1, source_target_pairs={{0,12},{1,13},{2,14},{3,15},{4,8},{5,9},{6,10},{7,11},{8,4},{9,5},... | collective-permute-start | bytes 417800 | tf_op jit(solution)/shard_map/ppermute | solution.py:53
  19.1 1.4 %collective-permute-start.4 = (bf16[16,4096]{1,0:T(8,128)(2,1)S(1)}, bf16[16,4096]{1,0:T(8,128)(2,1)S(1)}, u32[]{:S(2)}, u32[]{:S(2)}) collective-permute-start(bf16[16,4096]{1,0:T(8,128)(2,1)S(1)} %shard_map.101), channel_id=1, source_target_pairs={{0,1},{1,0},{2,3},{3,2},{4,5},{5,4},{6,7},{7,6},{8,9},{9,8},{10,11... | collective-permute-start | bytes 393224 | tf_op jit(solution)/shard_map/ppermute | solution.py:53
  26.6 2.1 %collective-permute-start.9 = (bf16[2176,128]{1,0:T(8,128)(2,1)S(1)}, bf16[2176,128]{1,0:T(8,128)(2,1)S(1)}, u32[]{:S(2)}, u32[]{:S(2)}) collective-permute-start(bf16[2176,128]{1,0:T(8,128)(2,1)S(1)} %shard_map.106.refs_1_), channel_id=1, source_target_pairs={{0,1},{1,0},{2,3},{3,2},{4,5},{5,4},{6,7},{7,6},{8,9},{9,8},{10,11... | collective-permute-start | bytes 1671176 | tf_op jit(solution)/shard_map/ppermute | solution.py:53
  31.5 1.7 %collective-permute-start.10 = (f32[16,4096]{1,0:T(8,128)S(1)}, f32[16,4096]{1,0:T(8,128)S(1)}, u32[]{:S(2)}, u32[]{:S(2)}) collective-permute-start(f32[16,4096]{1,0:T(8,128)S(1)} %get-tuple-element.40), channel_id=1, source_target_pairs={{0,1},{1,0},{2,3},{3,2},{4,5},{5,4},{6,7},{7,6},{8,9},{9,8},{10,11... | collective-permute-start | bytes 786440 | tf_op jit(solution)/shard_map/ppermute | solution.py:53
  33.2 5.8 %collective-permute-start.11 = (f32[16,2048]{1,0:T(8,128)S(1)}, f32[16,2048]{1,0:T(8,128)S(1)}, u32[]{:S(2)}, u32[]{:S(2)}) collective-permute-start(f32[16,2048]{1,0:T(8,128)S(1)} %get-tuple-element.42), channel_id=1, source_target_pairs={{0,2},{1,3},{2,0},{3,1},{4,6},{5,7},{6,4},{7,5},{8,10},{9,11},{10,... | collective-permute-start | bytes 393224 | tf_op jit(solution)/shard_map/ppermute | solution.py:53
  39.1 4.6 %collective-permute-start.12 = (f32[16,512]{1,0:T(8,128)S(1)}, f32[16,512]{1,0:T(8,128)S(1)}, u32[]{:S(2)}, u32[]{:S(2)}) collective-permute-start(f32[16,512]{1,0:T(8,128)S(1)} %get-tuple-element.44), channel_id=1, source_target_pairs={{0,4},{1,5},{2,6},{3,7},{4,0},{5,1},{6,2},{7,3},{8,12},{9,13},{10,... | collective-permute-start | bytes 98312 | tf_op jit(solution)/shard_map/ppermute | solution.py:53
  41.3 4.8 %collective-permute-start.13 = (f32[16,512]{1,0:T(8,128)S(1)}, f32[16,512]{1,0:T(8,128)S(1)}, u32[]{:S(2)}, u32[]{:S(2)}) collective-permute-start(f32[16,512]{1,0:T(8,128)S(1)} %get-tuple-element.45), channel_id=1, source_target_pairs={{0,8},{1,9},{2,10},{3,11},{4,12},{5,13},{6,14},{7,15},{8,0},{9,1},... | collective-permute-start | bytes 98312 | tf_op jit(solution)/shard_map/ppermute | solution.py:53
  41.3 5.7 %collective-permute-start.14 = (f32[16,512]{1,0:T(8,128)S(1)}, f32[16,512]{1,0:T(8,128)S(1)}, u32[]{:S(2)}, u32[]{:S(2)}) collective-permute-start(f32[16,512]{1,0:T(8,128)S(1)} %get-tuple-element.46), channel_id=1, source_target_pairs={{0,12},{1,13},{2,14},{3,15},{4,8},{5,9},{6,10},{7,11},{8,4},{9,5},... | collective-permute-start | bytes 98312 | tf_op jit(solution)/shard_map/ppermute | solution.py:53
  47.1 4.5 %collective-permute-start.15 = (bf16[16,512]{1,0:T(8,128)(2,1)S(1)}, bf16[16,512]{1,0:T(8,128)(2,1)S(1)}, u32[]{:S(2)}, u32[]{:S(2)}) collective-permute-start(bf16[16,512]{1,0:T(8,128)(2,1)S(1)} %shard_map.112.refs_0_), channel_id=1, source_target_pairs={{0,4},{1,5},{2,6},{3,7},{4,0},{5,1},{6,2},{7,3},{8,12},{9,13},{10,... | collective-permute-start | bytes 49160 | tf_op jit(solution)/shard_map/ppermute | solution.py:53
  47.3 4.6 %collective-permute-start.16 = (bf16[16,512]{1,0:T(8,128)(2,1)S(1)}, bf16[16,512]{1,0:T(8,128)(2,1)S(1)}, u32[]{:S(2)}, u32[]{:S(2)}) collective-permute-start(bf16[16,512]{1,0:T(8,128)(2,1)S(1)} %shard_map.112.refs_0_), channel_id=1, source_target_pairs={{0,8},{1,9},{2,10},{3,11},{4,12},{5,13},{6,14},{7,15},{8,0},{9,1},... | collective-permute-start | bytes 49160 | tf_op jit(solution)/shard_map/ppermute | solution.py:53
  50.0 5.5 %collective-permute-start.17 = (bf16[16,512]{1,0:T(8,128)(2,1)S(1)}, bf16[16,512]{1,0:T(8,128)(2,1)S(1)}, u32[]{:S(2)}, u32[]{:S(2)}) collective-permute-start(bf16[16,512]{1,0:T(8,128)(2,1)S(1)} %shard_map.112.refs_0_), channel_id=1, source_target_pairs={{0,12},{1,13},{2,14},{3,15},{4,8},{5,9},{6,10},{7,11},{8,4},{9,5},... | collective-permute-start | bytes 49160 | tf_op jit(solution)/shard_map/ppermute | solution.py:53
  55.6 4.3 %collective-permute-start.18 = (bf16[16,2048]{1,0:T(8,128)(2,1)S(1)}, bf16[16,2048]{1,0:T(8,128)(2,1)S(1)}, u32[]{:S(2)}, u32[]{:S(2)}) collective-permute-start(bf16[16,2048]{1,0:T(8,128)(2,1)S(1)} %shard_map.113.refs_0_), channel_id=1, source_target_pairs={{0,2},{1,3},{2,0},{3,1},{4,6},{5,7},{6,4},{7,5},{8,10},{9,11},{10,... | collective-permute-start | bytes 196616 | tf_op jit(solution)/shard_map/ppermute | solution.py:53
  66.5 1.5 %collective-permute-start.20 = (f32[16,4096]{1,0:T(8,128)S(1)}, f32[16,4096]{1,0:T(8,128)S(1)}, u32[]{:S(2)}, u32[]{:S(2)}) collective-permute-start(f32[16,4096]{1,0:T(8,128)S(1)} %get-tuple-element.48), channel_id=1, source_target_pairs={{0,1},{1,0},{2,3},{3,2},{4,5},{5,4},{6,7},{7,6},{8,9},{9,8},{10,11... | collective-permute-start | bytes 786440 | tf_op jit(solution)/shard_map/ppermute | solution.py:53
  68.1 4.3 %collective-permute-start.21 = (bf16[16,2048]{1,0:T(8,128)(2,1)S(1)}, bf16[16,2048]{1,0:T(8,128)(2,1)S(1)}, u32[]{:S(2)}, u32[]{:S(2)}) collective-permute-start(bf16[16,2048]{1,0:T(8,128)(2,1)S(1)} %get-tuple-element.50), channel_id=1, source_target_pairs={{0,2},{1,3},{2,0},{3,1},{4,6},{5,7},{6,4},{7,5},{8,10},{9,11},{10,... | collective-permute-start | bytes 196616 | tf_op jit(solution)/shard_map/ppermute | solution.py:53
  72.4 4.5 %collective-permute-start.22 = (f32[16,512]{1,0:T(8,128)S(1)}, f32[16,512]{1,0:T(8,128)S(1)}, u32[]{:S(2)}, u32[]{:S(2)}) collective-permute-start(f32[16,512]{1,0:T(8,128)S(1)} %get-tuple-element.52), channel_id=1, source_target_pairs={{0,4},{1,5},{2,6},{3,7},{4,0},{5,1},{6,2},{7,3},{8,12},{9,13},{10,... | collective-permute-start | bytes 98312 | tf_op jit(solution)/shard_map/ppermute | solution.py:53
  72.5 4.9 %collective-permute-start.23 = (f32[16,512]{1,0:T(8,128)S(1)}, f32[16,512]{1,0:T(8,128)S(1)}, u32[]{:S(2)}, u32[]{:S(2)}) collective-permute-start(f32[16,512]{1,0:T(8,128)S(1)} %get-tuple-element.53), channel_id=1, source_target_pairs={{0,8},{1,9},{2,10},{3,11},{4,12},{5,13},{6,14},{7,15},{8,0},{9,1},... | collective-permute-start | bytes 98312 | tf_op jit(solution)/shard_map/ppermute | solution.py:53
  74.5 5.7 %collective-permute-start.24 = (f32[16,512]{1,0:T(8,128)S(1)}, f32[16,512]{1,0:T(8,128)S(1)}, u32[]{:S(2)}, u32[]{:S(2)}) collective-permute-start(f32[16,512]{1,0:T(8,128)S(1)} %get-tuple-element.54), channel_id=1, source_target_pairs={{0,12},{1,13},{2,14},{3,15},{4,8},{5,9},{6,10},{7,11},{8,4},{9,5},... | collective-permute-start | bytes 98312 | tf_op jit(solution)/shard_map/ppermute | solution.py:53
  (22 other events, 388.5 us)

commit v4 on v3

--- a/solution.py
+++ b/solution.py
@@ -101,50 +101,68 @@
     return call(functools.partial(stack_kernel, axis), like(tuple(shape), parts[0].dtype), parts, beside)
 
 
-def normed_chunks(outer, wide, part_refs, gain_ref):
-    me = lax.axis_index("seq")
-    width = QUAD * outer * wide
+def normed_chunks(wide, chunks, gain_ref):
     squares = None
-    for ref, _ in part_refs:
-        v = ref[...].astype(f32)
+    for source, load in chunks:
+        v = load().astype(f32)
         s = jnp.sum(v * v, axis=1, keepdims=True)
         squares = s if squares is None else squares + s
-    inverse = lax.rsqrt(squares / width + eps)
-    for ref, distances in part_refs:
-        for i, distance in enumerate(distances):
-            source = jnp.bitwise_xor(me, distance)
-            at = pl.ds(pl.multiple_of(source * wide, wide), wide)
-            v = ref[:, i * wide : (i + 1) * wide].astype(f32)
-            yield at, (v * inverse * gain_ref[:, at].astype(f32)).astype(bf16)
+    inverse = lax.rsqrt(squares / (len(chunks) * wide) + eps)
+    for source, load in chunks:
+        at = pl.ds(pl.multiple_of(source * wide, wide), wide)
+        yield at, (load().astype(f32) * inverse * gain_ref[:, at].astype(f32)).astype(bf16)
+
+
+def to_members(parts):
+    size = lax.axis_size("seq")
+    groups = [list(range(core, size, 2)) for core in range(2)]
+    return lax.all_to_all(parts, "seq", 0, 0, axis_index_groups=groups, tiled=True)
+
+
+def member(i, other):
+    core = lax.axis_index("seq") % 2
+    return 2 * i + (1 - core if other else core)
 
 
 def line_of(outer, *nears):
     return [QUAD * k + j for j in nears for k in range(outer)]
 
 
-def part_list(outer, refs):
-    return list(zip(refs, (line_of(outer, 0), line_of(outer, 2), line_of(outer, 1, 3))))
+def line_chunks(outer, wide, refs):
+    me = lax.axis_index("seq")
+    lines = (line_of(outer, 0), line_of(outer, 2), line_of(outer, 1, 3))
+    return [
+        (jnp.bitwise_xor(me, distance), lambda r=ref, i=i: r[:, i * wide : (i + 1) * wide])
+        for ref, line in zip(refs, lines)
+        for i, distance in enumerate(line)
+    ]
+
+
+def member_chunks(refs):
+    return [
+        (member(i, other), lambda r=ref, i=i: r[i])
+        for other, ref in enumerate(refs)
+        for i in range(ref.shape[0])
+    ]
 
 
 def query_kernel(outer, wide, *refs):
     gain_ref, w_ref, out_ref = refs[3:]
     total = None
-    for at, chunk in normed_chunks(outer, wide, part_list(outer, refs[:3]), gain_ref):
+    for at, chunk in normed_chunks(wide, line_chunks(outer, wide, refs[:3]), gain_ref):
         term = jnp.dot(chunk, w_ref[at, :], preferred_element_type=f32)
         total = term if total is None else total + term
     out_ref[...] = total.astype(bf16)
 
 
-def scatter_dot(wide, left, w_ref, out_ref, distances):
-    me = lax.axis_index("seq")
-    for i, distance in enumerate(distances):
-        target = jnp.bitwise_xor(me, distance)
-        at = pl.ds(pl.multiple_of(target * wide, wide), wide)
-        out_ref[:, i * wide : (i + 1) * wide] = jnp.dot(left, w_ref[:, at], preferred_element_type=f32)
-
-
-def scatter_kernel(wide, distances, left_ref, w_ref, out_ref):
-    scatter_dot(wide, left_ref[...], w_ref, out_ref, distances)
+def scatter_dot(wide, other, left, w_ref, out_ref):
+    for i in range(out_ref.shape[0]):
+        at = pl.ds(pl.multiple_of(member(i, other) * wide, wide), wide)
+        out_ref[i] = jnp.dot(left, w_ref[:, at], preferred_element_type=f32)
+
+
+def keep_kernel(wide, left_ref, w_ref, out_ref):
+    scatter_dot(wide, False, left_ref[...], w_ref, out_ref)
 
 
 def span_states(spans, q_ref, cache):
@@ -199,7 +217,7 @@
     total_ref[...] = jnp.broadcast_to(total, total_ref.shape)
 
 
-def attend_kernel(wide, distances, spans, q_ref, top_ref, total_ref, accum_ref, *refs):
+def attend_kernel(wide, spans, q_ref, top_ref, total_ref, accum_ref, *refs):
     cache, w_ref, left_ref, send_ref = refs[:-3], *refs[-3:]
     rows = q_ref.shape[0]
     heads = q_ref.shape[1] // HEAD_DIM
@@ -209,39 +227,37 @@
     attended = (accum / total).astype(bf16)
     attended = jnp.concatenate([attended[h * rows : (h + 1) * rows] for h in range(heads)], axis=1)
     left_ref[...] = attended
-    scatter_dot(wide, attended, w_ref, send_ref, distances)
-
-
-def hidden_kernel(outer, wide, distances, *refs):
-    gain_ref, gate_ref, up_ref, down_ref, left_ref, send_ref = refs[3:]
+    scatter_dot(wide, True, attended, w_ref, send_ref)
+
+
+def hidden_kernel(wide, *refs):
+    gain_ref, gate_ref, up_ref, down_ref, left_ref, send_ref = refs[2:]
     gate = up = None
-    for at, chunk in normed_chunks(outer, wide, part_list(outer, refs[:3]), gain_ref):
+    for at, chunk in normed_chunks(wide, member_chunks(refs[:2]), gain_ref):
         g = jnp.dot(chunk, gate_ref[at, :], preferred_element_type=f32)
         u = jnp.dot(chunk, up_ref[at, :], preferred_element_type=f32)
         gate = g if gate is None else gate + g
         up = u if up is None else up + u
     hidden = (gate / (1.0 + jnp.exp(-gate)) * up).astype(bf16)
     left_ref[...] = hidden
-    scatter_dot(wide, hidden, down_ref, send_ref, distances)
-
-
-def half_kernel(own_ref, recv_ref, keep_ref, send_ref):
-    half = own_ref.shape[1] // 2
-    keep_ref[...] = own_ref[:, :half] + recv_ref[:, :half]
-    send_ref[...] = (own_ref[:, half:] + recv_ref[:, half:]).astype(send_ref.dtype)
-
-
-def fold_kernel(wide, own_ref, recv_ref, keep_ref, *sends):
-    for k, out in enumerate((keep_ref, *sends)):
-        at = slice(k * wide, (k + 1) * wide)
-        out[...] = (own_ref[:, at] + recv_ref[:, at].astype(f32)).astype(out.dtype)
-
-
-def final_kernel(base_ref, keep_ref, *refs):
-    total = keep_ref[...]
-    for r in refs[:-1]:
-        total = total + r[...].astype(f32)
-    refs[-1][...] = (base_ref[...].astype(f32) + total).astype(bf16)
+    scatter_dot(wide, True, hidden, down_ref, send_ref)
+
+
+def add_kernel(own_ref, recv_ref, out_ref):
+    out_ref[...] = (own_ref[...] + recv_ref[...]).astype(out_ref.dtype)
+
+
+def final_kernel(base_ref, parts_ref, *out_refs):
+    total = parts_ref[0].astype(f32)
+    for i in range(1, parts_ref.shape[0]):
+        total = total + parts_ref[i].astype(f32)
+    total = (base_ref[...].astype(f32) + total).astype(bf16)
+    for out in out_refs:
+        if len(out.shape) == 3:
+            for i in range(out.shape[0]):
+                out[i] = total
+        else:
+            out[...] = total
 
 
 def z_swapped(parts):
@@ -258,21 +274,11 @@
     return [line, other, swap(stacked([line, other], 1, after), 1)]
 
 
-def scattered(base, send, left, weight, outer, wide, y_type, z_type, beside=()):
-    rows = base.shape[0]
+def scattered(base, send, left, weight, wide, kind, outs, beside=()):
     far = swap(send, 1)
-    keep = call(
-        functools.partial(scatter_kernel, wide, line_of(outer, 0, 2)),
-        like((rows, 2 * outer * wide), f32),
-        [left, weight],
-    )
-    keep, send = call(
-        half_kernel, [like((rows, outer * wide), f32), like((rows, outer * wide), y_type)], [keep, far], beside
-    )
-    outs = [like((rows, wide), f32)] + [like((rows, wide), z_type)] * (outer - 1)
-    keep, *sends = call(functools.partial(fold_kernel, wide), outs, [keep, swap(send, 2)], beside)
-    arrived = [swap(s, QUAD * (k + 1)) for k, s in enumerate(sends)]
-    return call(final_kernel, like((rows, wide), bf16), [base, keep, *arrived])
+    own = call(functools.partial(keep_kernel, wide), like(send.shape, f32), [left, weight])
+    sums = call(add_kernel, like(send.shape, kind), [own, far], beside)
+    return call(final_kernel, outs, [base, to_members(sums)], beside)
 
 
 def local_pairs(
@@ -284,7 +290,9 @@
     beside = [room(18432)]
     attn_gain = attn_gain.reshape(1, -1)
     mlp_gain = mlp_gain.reshape(1, -1)
-    near = line_of(outer, 1, 3)
+    members = lax.axis_size("seq") // 2
+    partial_sums = like((members, rows, wide), f32)
+    own_columns = like((rows, wide), bf16)
 
     size = 2 * kv_cache.shape[1] + rows
     own, send = call(
@@ -314,18 +322,20 @@
     tall = like((columns // HEAD_DIM * rows, HEAD_DIM), f32)
     early = call(functools.partial(early_kernel, 2 * outer), [tall] * 3, [queries, first])
     left, send = call(
-        functools.partial(attend_kernel, wide, near, 2 * outer),
-        [like((rows, columns), bf16), like((rows, 2 * outer * wide), f32)],
+        functools.partial(attend_kernel, wide, 2 * outer),
+        [like((rows, columns), bf16), partial_sums],
         [queries, *early, second, o_weight],
     )
-    stream = scattered(x_rows, send, left, o_weight, outer, wide, f32, f32, beside)
-    parts = near_gathered(z_gathered(stream, outer))
+    stream, copies = scattered(
+        x_rows, send, left, o_weight, wide, f32, [own_columns, like(partial_sums.shape, bf16)], beside
+    )
+    parts = to_members(copies)
     left, send = call(
-        functools.partial(hidden_kernel, outer, wide, near),
-        [like((rows, gate_weight.shape[1]), bf16), like((rows, 2 * outer * wide), f32)],
-        [*parts, mlp_gain, gate_weight, up_weight, down_weight],
-    )
-    return scattered(stream, send, left, down_weight, outer, wide, bf16, f32)
+        functools.partial(hidden_kernel, wide),
+        [like((rows, gate_weight.shape[1]), bf16), partial_sums],
+        [parts, swap(parts, 1), mlp_gain, gate_weight, up_weight, down_weight],
+    )
+    return scattered(stream, send, left, down_weight, wide, bf16, [own_columns])[0]
 
 
 def rms_norm(values, gain):

time: 81 us -> 77.2 us (0.953)
  blocking collectives: 0 us -> 34.8 us
  waiting for transfers between devices: 34.8 us -> 13.6 us
  starting transfers between devices: 30.6 us -> 13.1 us
    all_to_all x0 -> x3, blocking collectives: none -> 34.8 us  [to_members(): lax.all_to_all(parts, 'seq', 0, 0, axis_index_groups=groups, tiled=True)]
    ppermute x25 -> x13, waiting for transfers between devices: 34.8 us -> 13.6 us  [swap(): return lax.ppermute(x, 'seq', [(i, i ^ distance) for i in range(size)])]
    ppermute x25 -> x13, starting transfers between devices: 30.6 us -> 13.1 us  [swap(): return lax.ppermute(x, 'seq', [(i, i ^ distance) for i in range(size)])]
    pallas_call x19 -> x15, Pallas kernels: 13.9 us -> 13.9 us  [call(): pl.pallas_call(kernel, out_shape=outs, in_specs=[VMEM] * count + [pl.Bloc...]
  transfers between devices with their start and end apart: 25 -> 13, of which waited for: 16 -> 7; matrix products, arithmetic and copies ran while one was open for 0% -> 0% of each run, Pallas kernels for 6% -> 7%
where the time goes in v4:
time: 77.2 us; the launch traced here: 76.9 us
  blocking collectives  34.8 us (45%)
  Pallas kernels  13.9 us (18%)
  waiting for transfers between devices  13.6 us (18%)
  starting transfers between devices  13.1 us (17%)
  local copies, waits for them, and re-layouts  1.18 us (2%)
    all_to_all x3, blocking collectives, to_members(): lax.all_to_all(parts, 'seq', 0, 0, axis_index_groups=groups, tiled=True)  34.8 us
    pallas_call x15, Pallas kernels, call(): pl.pallas_call(kernel, out_shape=outs, in_specs=[VMEM] * count + [pl.Bloc...  13.9 us
    ppermute x13, waiting for transfers between devices, swap(): return lax.ppermute(x, 'seq', [(i, i ^ distance) for i in range(size)])  13.6 us
    ppermute x13, starting transfers between devices, swap(): return lax.ppermute(x, 'seq', [(i, i ^ distance) for i in range(size)])  13.1 us
  transfers between devices with their start and end apart: 13, of which 7 were waited for; matrix products, arithmetic and copies ran while one was open for 0% of the time, Pallas kernels for 7%

profile of v4, /device:TPU:0, one launch (start us, length us, event | category | flops | bytes accessed | tf_op | source)
XLA Modules:
  0.0 76.9 jit_solution(5252292971590599049)
XLA Ops:
  0.0 0.7 copy-done.4
  1.3 3.0 %collective-permute-start.5 = (bf16[272,512]{1,0:T(8,128)(2,1)S(1)}, bf16[272,512]{1,0:T(8,128)(2,1)S(1)}, u32[]{:S(2)}, u32[]{:S(2)}) collective-permute-start(bf16[272,512]{1,0:T(8,128)(2,1)S(1)} %get-tuple-element.21), channel_id=1, source_target_pairs={{0,2},{1,3},{2,0},{3,1},{4,6},{5,7},{6,4},{7,5},{8,10},{9,11},{10,... | collective-permute-start | bytes 835592 | tf_op jit(solution)/shard_map/ppermute | solution.py:53
  4.3 1.6 %collective-permute-start = (bf16[16,512]{1,0:T(8,128)(2,1)S(1)}, bf16[16,512]{1,0:T(8,128)(2,1)S(1)}, u32[]{:S(2)}, u32[]{:S(2)}) collective-permute-start(bf16[16,512]{1,0:T(8,128)(2,1)S(1)} %copy-done.1), channel_id=1, source_target_pairs={{0,4},{1,5},{2,6},{3,7},{4,0},{5,1},{6,2},{7,3},{8,12},{9,13},{10,... | collective-permute-start | bytes 49160 | tf_op jit(solution)/shard_map/ppermute | solution.py:53
  5.8 2.6 %collective-permute-start.1 = (bf16[16,512]{1,0:T(8,128)(2,1)S(1)}, bf16[16,512]{1,0:T(8,128)(2,1)S(1)}, u32[]{:S(2)}, u32[]{:S(2)}) collective-permute-start(bf16[16,512]{1,0:T(8,128)(2,1)S(1)} %copy-done.1), channel_id=1, source_target_pairs={{0,8},{1,9},{2,10},{3,11},{4,12},{5,13},{6,14},{7,15},{8,0},{9,1},... | collective-permute-start | bytes 49160 | tf_op jit(solution)/shard_map/ppermute | solution.py:53
  8.7 1.9 %collective-permute-done.1.refs_2_ = bf16[16,512]{1,0:T(8,128)(2,1)S(1)} collective-permute-done((bf16[16,512]{1,0:T(8,128)(2,1)S(1)}, bf16[16,512]{1,0:T(8,128)(2,1)S(1)}, u32[]{:S(2)}, u32[]{:S(2)}) %collective-permute-start.1) | collective-permute-done | bytes 16416 | tf_op jit(solution)/shard_map/ppermute | solution.py:53
  10.5 3.4 %collective-permute-done.2.refs_3_ = bf16[16,512]{1,0:T(8,128)(2,1)S(1)} collective-permute-done((bf16[16,512]{1,0:T(8,128)(2,1)S(1)}, bf16[16,512]{1,0:T(8,128)(2,1)S(1)}, u32[]{:S(2)}, u32[]{:S(2)}) %collective-permute-start.2) | collective-permute-done | bytes 16416 | tf_op jit(solution)/shard_map/ppermute | solution.py:53
  14.0 0.5 collective-permute-start.3
  14.7 0.8 %collective-permute-start.7 = (bf16[544,128]{1,0:T(8,128)(2,1)S(1)}, bf16[544,128]{1,0:T(8,128)(2,1)S(1)}, u32[]{:S(2)}, u32[]{:S(2)}) collective-permute-start(bf16[544,128]{1,0:T(8,128)(2,1)S(1)} %get-tuple-element.24), channel_id=1, source_target_pairs={{0,8},{1,9},{2,10},{3,11},{4,12},{5,13},{6,14},{7,15},{8,0},{9,1},... | collective-permute-start | bytes 417800 | tf_op jit(solution)/shard_map/ppermute | solution.py:53
  15.5 3.6 %collective-permute-start.8 = (bf16[544,128]{1,0:T(8,128)(2,1)S(1)}, bf16[544,128]{1,0:T(8,128)(2,1)S(1)}, u32[]{:S(2)}, u32[]{:S(2)}) collective-permute-start(bf16[544,128]{1,0:T(8,128)(2,1)S(1)} %get-tuple-element.25), channel_id=1, source_target_pairs={{0,12},{1,13},{2,14},{3,15},{4,8},{5,9},{6,10},{7,11},{8,4},{9,5},... | collective-permute-start | bytes 417800 | tf_op jit(solution)/shard_map/ppermute | solution.py:53
  19.2 1.3 %collective-permute-done.4.refs_2_ = bf16[16,4096]{1,0:T(8,128)(2,1)S(1)} collective-permute-done((bf16[16,4096]{1,0:T(8,128)(2,1)S(1)}, bf16[16,4096]{1,0:T(8,128)(2,1)S(1)}, u32[]{:S(2)}, u32[]{:S(2)}) %collective-permute-start.4) | collective-permute-done | bytes 131104 | tf_op jit(solution)/shard_map/ppermute | solution.py:53
  20.5 1.3 %shard_map.102.refs_4_.refs_0_ = bf16[16,512]{1,0:T(8,128)(2,1)S(1)} custom-call(bf16[16,2048]{1,0:T(8,128)(2,1)S(1)} %shard_map.100.refs_0_, bf16[16,2048]{1,0:T(8,128)(2,1)S(1)} %collective-permute-done.3.refs_1_, bf16[16,4096]{1,0:T(8,128)(2,1)S(1)} %collective-permute-done.4.refs_2_, bf16[1,8192]{1,0:T(2,128)(2,1)S(1)} %reshape.6.refs_3_, ...), custom_call_target="tpu_custom_call" | custom-call | tf_op jit(solution)/shard_map/pallas_call | solution.py:30
  21.8 4.8 %collective-permute-done.7.refs_2_ = bf16[544,128]{1,0:T(8,128)(2,1)S(1)} collective-permute-done((bf16[544,128]{1,0:T(8,128)(2,1)S(1)}, bf16[544,128]{1,0:T(8,128)(2,1)S(1)}, u32[]{:S(2)}, u32[]{:S(2)}) %collective-permute-start.7) | collective-permute-done | bytes 139296 | tf_op jit(solution)/shard_map/ppermute | solution.py:53
  26.7 2.0 %shard_map.107 = (f32[64,128]{1,0:T(8,128)S(1)}, f32[64,128]{1,0:T(8,128)S(1)}, f32[64,128]{1,0:T(8,128)S(1)}) custom-call(bf16[16,512]{1,0:T(8,128)(2,1)S(1)} %shard_map.102.refs_4_.refs_0_, bf16[2176,128]{1,0:T(8,128)(2,1)S(1)} %shard_map.106.refs_1_), custom_call_target="tpu_custom_call" | custom-call | tf_op jit(solution)/shard_map/pallas_call | solution.py:30
  28.7 2.7 %shard_map.108 = (bf16[16,512]{1,0:T(8,128)(2,1)S(1)}, f32[8,16,512]{2,1,0:T(8,128)S(1)}) custom-call(bf16[16,512]{1,0:T(8,128)(2,1)S(1)} %shard_map.102.refs_4_.refs_0_, f32[64,128]{1,0:T(8,128)S(1)} %get-tuple-element.26.refs_1_, f32[64,128]{1,0:T(8,128)S(1)} %get-tuple-element.27.refs_2_, f32[64,128]{1,0:T(8,128)S(1)} %get-tuple-element.28.refs_3_, ...), custom_call_target="tpu_custom_call" | custom-call | tf_op jit(solution)/shard_map/pallas_call | solution.py:30
  31.5 0.5 collective-permute-start.10
  32.0 0.6 shard_map.109.refs_0_
  32.6 0.5 collective-permute-done.10.refs_1_
  33.3 13.8 %all_to_all.15.refs_1_ = f32[8,16,512]{2,1,0:T(8,128)S(1)} all-to-all(f32[8,16,512]{2,1,0:T(8,128)S(1)} %shard_map.110), channel_id=1, replica_groups={{0,2,4,6,8,10,12,14},{1,3,5,7,9,11,13,15},{16,18,20,22,24,26,28,30},{17..., dimensions={0} | all-to-all | bytes 524288 | tf_op jit(solution)/shard_map/all_to_all | solution.py:119
  47.1 11.0 %all_to_all.16.refs_0_ = bf16[8,16,512]{2,1,0:T(8,128)(2,1)S(1)} all-to-all(bf16[8,16,512]{2,1,0:T(8,128)(2,1)S(1)} %get-tuple-element.32), channel_id=1, replica_groups={{0,2,4,6,8,10,12,14},{1,3,5,7,9,11,13,15},{16,18,20,22,24,26,28,30},{17..., dimensions={0} | all-to-all | bytes 262144 | tf_op jit(solution)/shard_map/all_to_all | solution.py:119
  58.1 1.3 %collective-permute-done.11.refs_1_ = bf16[8,16,512]{2,1,0:T(8,128)(2,1)S(1)} collective-permute-done((bf16[8,16,512]{2,1,0:T(8,128)(2,1)S(1)}, bf16[8,16,512]{2,1,0:T(8,128)(2,1)S(1)}, u32[]{:S(2)}, u32[]{:S(2)}) %collective-permute-start.11) | collective-permute-done | bytes 131104 | tf_op jit(solution)/shard_map/ppermute | solution.py:53
  59.6 5.1 %shard_map.112 = (bf16[16,896]{1,0:T(8,128)(2,1)S(1)}, f32[8,16,512]{2,1,0:T(8,128)S(1)}) custom-call(bf16[8,16,512]{2,1,0:T(8,128)(2,1)S(1)} %all_to_all.16.refs_0_, bf16[8,16,512]{2,1,0:T(8,128)(2,1)S(1)} %collective-permute-done.11.refs_1_, bf16[1,8192]{1,0:T(2,128)(2,1)S(1)} %reshape.7.refs_2_, bf16[8192,896]{1,0:T(8,128)(2,1)S(1)} %bitcast.6, ...), custom_call_target="tpu_custom_call" | custom-call | tf_op jit(solution)/shard_map/pallas_call | solution.py:30
  64.9 1.1 %shard_map.113.refs_0_ = f32[8,16,512]{2,1,0:T(8,128)S(1)} custom-call(bf16[16,896]{1,0:T(8,128)(2,1)S(1)} %get-tuple-element.33.refs_0_, bf16[896,8192]{1,0:T(8,128)(2,1)S(1)} %bitcast.2), custom_call_target="tpu_custom_call" | custom-call | tf_op jit(solution)/shard_map/pallas_call | solution.py:30
  66.3 10.0 %all_to_all.17.refs_1_ = bf16[8,16,512]{2,1,0:T(8,128)(2,1)S(1)} all-to-all(bf16[8,16,512]{2,1,0:T(8,128)(2,1)S(1)} %shard_map.114), channel_id=1, replica_groups={{0,2,4,6,8,10,12,14},{1,3,5,7,9,11,13,15},{16,18,20,22,24,26,28,30},{17..., dimensions={0} | all-to-all | bytes 262144 | tf_op jit(solution)/shard_map/all_to_all | solution.py:119
  76.3 0.6 shard_map.115
  (71 shorter events, 1.9 us)
Async XLA Ops:
  1.1 19.5 %slice-start.14 = ((s8[8388608]{0:T(1024)(128)(4,1)}), s8[4194304]{0:T(1024)(128)(4,1)S(1)}, s32[]{:S(2)}) async-start(s8[8388608]{0:T(1024)(128)(4,1)} %bitcast.9), calls=%async_computation.17 | async-start | bytes 8388608
  1.3 13.2 %collective-permute-start.5 = (bf16[272,512]{1,0:T(8,128)(2,1)S(1)}, bf16[272,512]{1,0:T(8,128)(2,1)S(1)}, u32[]{:S(2)}, u32[]{:S(2)}) collective-permute-start(bf16[272,512]{1,0:T(8,128)(2,1)S(1)} %get-tuple-element.21), channel_id=1, source_target_pairs={{0,2},{1,3},{2,0},{3,1},{4,6},{5,7},{6,4},{7,5},{8,10},{9,11},{10,... | collective-permute-start | bytes 835592 | tf_op jit(solution)/shard_map/ppermute | solution.py:53
  4.3 4.4 %collective-permute-start = (bf16[16,512]{1,0:T(8,128)(2,1)S(1)}, bf16[16,512]{1,0:T(8,128)(2,1)S(1)}, u32[]{:S(2)}, u32[]{:S(2)}) collective-permute-start(bf16[16,512]{1,0:T(8,128)(2,1)S(1)} %copy-done.1), channel_id=1, source_target_pairs={{0,4},{1,5},{2,6},{3,7},{4,0},{5,1},{6,2},{7,3},{8,12},{9,13},{10,... | collective-permute-start | bytes 49160 | tf_op jit(solution)/shard_map/ppermute | solution.py:53
  5.8 4.7 %collective-permute-start.1 = (bf16[16,512]{1,0:T(8,128)(2,1)S(1)}, bf16[16,512]{1,0:T(8,128)(2,1)S(1)}, u32[]{:S(2)}, u32[]{:S(2)}) collective-permute-start(bf16[16,512]{1,0:T(8,128)(2,1)S(1)} %copy-done.1), channel_id=1, source_target_pairs={{0,8},{1,9},{2,10},{3,11},{4,12},{5,13},{6,14},{7,15},{8,0},{9,1},... | collective-permute-start | bytes 49160 | tf_op jit(solution)/shard_map/ppermute | solution.py:53
  8.4 5.5 %collective-permute-start.2 = (bf16[16,512]{1,0:T(8,128)(2,1)S(1)}, bf16[16,512]{1,0:T(8,128)(2,1)S(1)}, u32[]{:S(2)}, u32[]{:S(2)}) collective-permute-start(bf16[16,512]{1,0:T(8,128)(2,1)S(1)} %copy-done.1), channel_id=1, source_target_pairs={{0,12},{1,13},{2,14},{3,15},{4,8},{5,9},{6,10},{7,11},{8,4},{9,5},... | collective-permute-start | bytes 49160 | tf_op jit(solution)/shard_map/ppermute | solution.py:53
  14.0 5.1 %collective-permute-start.3 = (bf16[16,2048]{1,0:T(8,128)(2,1)S(1)}, bf16[16,2048]{1,0:T(8,128)(2,1)S(1)}, u32[]{:S(2)}, u32[]{:S(2)}) collective-permute-start(bf16[16,2048]{1,0:T(8,128)(2,1)S(1)} %shard_map.100.refs_0_), channel_id=1, source_target_pairs={{0,2},{1,3},{2,0},{3,1},{4,6},{5,7},{6,4},{7,5},{8,10},{9,11},{10,... | collective-permute-start | bytes 196616 | tf_op jit(solution)/shard_map/ppermute | solution.py:53
  14.5 14.2 %slice-start.4 = ((s8[8388608]{0:T(1024)(128)(4,1)}), s8[4194304]{0:T(1024)(128)(4,1)S(1)}, s32[]{:S(2)}) async-start(s8[8388608]{0:T(1024)(128)(4,1)} %bitcast.3), calls=%async_computation.7 | async-start | bytes 8388608
  14.6 7.2 %collective-permute-start.6 = (bf16[544,128]{1,0:T(8,128)(2,1)S(1)}, bf16[544,128]{1,0:T(8,128)(2,1)S(1)}, u32[]{:S(2)}, u32[]{:S(2)}) collective-permute-start(bf16[544,128]{1,0:T(8,128)(2,1)S(1)} %get-tuple-element.23), channel_id=1, source_target_pairs={{0,4},{1,5},{2,6},{3,7},{4,0},{5,1},{6,2},{7,3},{8,12},{9,13},{10,... | collective-permute-start | bytes 417800 | tf_op jit(solution)/shard_map/ppermute | solution.py:53
  14.7 11.9 %collective-permute-start.7 = (bf16[544,128]{1,0:T(8,128)(2,1)S(1)}, bf16[544,128]{1,0:T(8,128)(2,1)S(1)}, u32[]{:S(2)}, u32[]{:S(2)}) collective-permute-start(bf16[544,128]{1,0:T(8,128)(2,1)S(1)} %get-tuple-element.24), channel_id=1, source_target_pairs={{0,8},{1,9},{2,10},{3,11},{4,12},{5,13},{6,14},{7,15},{8,0},{9,1},... | collective-permute-start | bytes 417800 | tf_op jit(solution)/shard_map/ppermute | solution.py:53
  15.5 11.1 %collective-permute-start.8 = (bf16[544,128]{1,0:T(8,128)(2,1)S(1)}, bf16[544,128]{1,0:T(8,128)(2,1)S(1)}, u32[]{:S(2)}, u32[]{:S(2)}) collective-permute-start(bf16[544,128]{1,0:T(8,128)(2,1)S(1)} %get-tuple-element.25), channel_id=1, source_target_pairs={{0,12},{1,13},{2,14},{3,15},{4,8},{5,9},{6,10},{7,11},{8,4},{9,5},... | collective-permute-start | bytes 417800 | tf_op jit(solution)/shard_map/ppermute | solution.py:53
  19.1 1.4 %collective-permute-start.4 = (bf16[16,4096]{1,0:T(8,128)(2,1)S(1)}, bf16[16,4096]{1,0:T(8,128)(2,1)S(1)}, u32[]{:S(2)}, u32[]{:S(2)}) collective-permute-start(bf16[16,4096]{1,0:T(8,128)(2,1)S(1)} %shard_map.101), channel_id=1, source_target_pairs={{0,1},{1,0},{2,3},{3,2},{4,5},{5,4},{6,7},{7,6},{8,9},{9,8},{10,11... | collective-permute-start | bytes 393224 | tf_op jit(solution)/shard_map/ppermute | solution.py:53
  26.6 2.1 %collective-permute-start.9 = (bf16[2176,128]{1,0:T(8,128)(2,1)S(1)}, bf16[2176,128]{1,0:T(8,128)(2,1)S(1)}, u32[]{:S(2)}, u32[]{:S(2)}) collective-permute-start(bf16[2176,128]{1,0:T(8,128)(2,1)S(1)} %shard_map.106.refs_1_), channel_id=1, source_target_pairs={{0,1},{1,0},{2,3},{3,2},{4,5},{5,4},{6,7},{7,6},{8,9},{9,8},{10,11... | collective-permute-start | bytes 1671176 | tf_op jit(solution)/shard_map/ppermute | solution.py:53
  31.5 1.7 %collective-permute-start.10 = (f32[8,16,512]{2,1,0:T(8,128)S(1)}, f32[8,16,512]{2,1,0:T(8,128)S(1)}, u32[]{:S(2)}, u32[]{:S(2)}) collective-permute-start(f32[8,16,512]{2,1,0:T(8,128)S(1)} %get-tuple-element.30), channel_id=1, source_target_pairs={{0,1},{1,0},{2,3},{3,2},{4,5},{5,4},{6,7},{7,6},{8,9},{9,8},{10,11... | collective-permute-start | bytes 786440 | tf_op jit(solution)/shard_map/ppermute | solution.py:53
  33.1 26.3 %slice-start = ((s8[14680064]{0:T(1024)(128)(4,1)}), s8[4194304]{0:T(1024)(128)(4,1)S(1)}, s32[]{:S(2)}) async-start(s8[14680064]{0:T(1024)(128)(4,1)} %bitcast.1), calls=%async_computation.3 | async-start | bytes 8388608
  33.1 26.3 %slice-start.1 = ((s8[14680064]{0:T(1024)(128)(4,1)}), s8[4194304]{0:T(1024)(128)(4,1)S(1)}, s32[]{:S(2)}) async-start(s8[14680064]{0:T(1024)(128)(4,1)} %bitcast.1), calls=%async_computation.4 | async-start | bytes 8388608
  33.2 26.3 %slice-start.6 = ((s8[14680064]{0:T(1024)(128)(4,1)}), s8[4194304]{0:T(1024)(128)(4,1)S(1)}, s32[]{:S(2)}) async-start(s8[14680064]{0:T(1024)(128)(4,1)} %bitcast.5), calls=%async_computation.9 | async-start | bytes 8388608
  33.2 26.3 %slice-start.7 = ((s8[14680064]{0:T(1024)(128)(4,1)}), s8[4194304]{0:T(1024)(128)(4,1)S(1)}, s32[]{:S(2)}) async-start(s8[14680064]{0:T(1024)(128)(4,1)} %bitcast.5), calls=%async_computation.10 | async-start | bytes 8388608
  33.2 26.3 %slice-start.10 = ((s8[14680064]{0:T(1024)(128)(4,1)}), s8[4194304]{0:T(1024)(128)(4,1)S(1)}, s32[]{:S(2)}) async-start(s8[14680064]{0:T(1024)(128)(4,1)} %bitcast.7), calls=%async_computation.13 | async-start | bytes 8388608
  33.2 26.3 %slice-start.11 = ((s8[14680064]{0:T(1024)(128)(4,1)}), s8[4194304]{0:T(1024)(128)(4,1)S(1)}, s32[]{:S(2)}) async-start(s8[14680064]{0:T(1024)(128)(4,1)} %bitcast.7), calls=%async_computation.14 | async-start | bytes 8388608
  33.2 26.3 %slice-start.2 = ((s8[14680064]{0:T(1024)(128)(4,1)}), s8[4194304]{0:T(1024)(128)(4,1)S(1)}, s32[]{:S(2)}) async-start(s8[14680064]{0:T(1024)(128)(4,1)} %bitcast.1), calls=%async_computation.5 | async-start | bytes 8388608
  33.2 26.3 %slice-start.8 = ((s8[14680064]{0:T(1024)(128)(4,1)}), s8[4194304]{0:T(1024)(128)(4,1)S(1)}, s32[]{:S(2)}) async-start(s8[14680064]{0:T(1024)(128)(4,1)} %bitcast.5), calls=%async_computation.11 | async-start | bytes 8388608
  33.2 26.3 %slice-start.12 = ((s8[14680064]{0:T(1024)(128)(4,1)}), s8[4194304]{0:T(1024)(128)(4,1)S(1)}, s32[]{:S(2)}) async-start(s8[14680064]{0:T(1024)(128)(4,1)} %bitcast.7), calls=%async_computation.15 | async-start | bytes 8388608
  58.1 1.3 %collective-permute-start.11 = (bf16[8,16,512]{2,1,0:T(8,128)(2,1)S(1)}, bf16[8,16,512]{2,1,0:T(8,128)(2,1)S(1)}, u32[]{:S(2)}, u32[]{:S(2)}) collective-permute-start(bf16[8,16,512]{2,1,0:T(8,128)(2,1)S(1)} %all_to_all.16.refs_0_), channel_id=1, source_target_pairs={{0,1},{1,0},{2,3},{3,2},{4,5},{5,4},{6,7},{7,6},{8,9},{9,8},{10,11... | collective-permute-start | bytes 393224 | tf_op jit(solution)/shard_map/ppermute | solution.py:53
  64.7 1.5 %collective-permute-start.12 = (f32[8,16,512]{2,1,0:T(8,128)S(1)}, f32[8,16,512]{2,1,0:T(8,128)S(1)}, u32[]{:S(2)}, u32[]{:S(2)}) collective-permute-start(f32[8,16,512]{2,1,0:T(8,128)S(1)} %get-tuple-element.34), channel_id=1, source_target_pairs={{0,1},{1,0},{2,3},{3,2},{4,5},{5,4},{6,7},{7,6},{8,9},{9,8},{10,11... | collective-permute-start | bytes 786440 | tf_op jit(solution)/shard_map/ppermute | solution.py:53
  (10 other events, 78.3 us)

commit v5 on v4

--- a/solution.py
+++ b/solution.py
@@ -53,35 +53,46 @@
     return lax.ppermute(x, "seq", [(i, i ^ distance) for i in range(size)])
 
 
-def live_lanes(mask, head, rows):
-    lane = lax.broadcasted_iota(jnp.int32, mask.shape, 1)
-    live = jnp.where((lane == head) & (mask == 1), 1.0, 0.0).astype(f32)
-    return jnp.broadcast_to(jnp.sum(live, axis=1, keepdims=True), (rows, HEAD_DIM)).astype(bf16)
-
-
-def pack_kernel(outer, kv_ref, mask_ref, own_ref, send_ref):
-    y = (lax.axis_index("seq") // 2) % 2
+def pack_kernel(outer, kv_ref, mask_ref, x_ref, held_ref, send_ref):
+    me = lax.axis_index("seq")
+    z, y = me // QUAD, (me // 2) % 2
     keys = kv_ref.shape[1]
-    rows = mask_ref.shape[0]
-    mask = mask_ref[...]
-    for out, parity in ((send_ref, 1 - y), (own_ref, y)):
-        for z in range(outer):
-            head = 2 * z + parity
-            cols = pl.ds(pl.multiple_of(head * HEAD_DIM, HEAD_DIM), HEAD_DIM)
-            at = slice(z * HEAD_DIM, (z + 1) * HEAD_DIM)
-            out[0:keys, at] = kv_ref[0, :, cols]
-            out[keys : 2 * keys, at] = kv_ref[1, :, cols]
-            out[2 * keys : 2 * keys + rows, at] = live_lanes(mask, head, rows)
-
-
-def route_kernel(outer, own_ref, other_ref, *outs):
-    z = lax.axis_index("seq") // QUAD
-    size = own_ref.shape[0]
+    rows, wide = x_ref.shape
+    lane = lax.broadcasted_iota(jnp.int32, (rows, HEAD_DIM), 1)
+    mask = jnp.zeros((rows, HEAD_DIM), f32)
+    for head in range(mask_ref.shape[1]):
+        live = (mask_ref[:, head : head + 1] == 1).astype(f32)
+        mask = jnp.where(lane == head, jnp.broadcast_to(live, mask.shape), mask)
+    held_ref[:, 0:wide] = x_ref[...]
+    held_ref[:, wide:] = mask.astype(bf16)
     for k in range(outer):
-        peer = jnp.bitwise_xor(z, k)
-        cols = pl.ds(pl.multiple_of(peer * HEAD_DIM, HEAD_DIM), HEAD_DIM)
-        outs[k][0:size, :] = own_ref[:, cols]
-        outs[k][size : 2 * size, :] = other_ref[:, cols]
+        head = 2 * jnp.bitwise_xor(z, k) + 1 - y
+        cols = pl.ds(pl.multiple_of(head * HEAD_DIM, HEAD_DIM), HEAD_DIM)
+        at = slice(k * HEAD_DIM, (k + 1) * HEAD_DIM)
+        send_ref[0:keys, at] = kv_ref[0, :, cols]
+        send_ref[keys : 2 * keys, at] = kv_ref[1, :, cols]
+
+
+def z_slots(outer):
+    order = list(range(outer - 1, 0, -1))
+    return list(zip([0, *order[-1:], *order[:-1]], [0, *order]))
+
+
+def z_distance(slot, core):
+    return jnp.where(core == 0, slot[0], slot[1])
+
+
+def route_kernel(outer, kv_ref, other_ref, *outs):
+    me = lax.axis_index("seq")
+    z, y = me // QUAD, (me // 2) % 2
+    keys = kv_ref.shape[1]
+    for slot, out in zip(z_slots(outer), outs):
+        k = z_distance(slot, me % 2)
+        head = 2 * jnp.bitwise_xor(z, k) + y
+        cols = pl.ds(pl.multiple_of(head * HEAD_DIM, HEAD_DIM), HEAD_DIM)
+        out[0:keys, :] = kv_ref[0, :, cols]
+        out[keys : 2 * keys, :] = kv_ref[1, :, cols]
+        out[2 * keys :, :] = other_ref[:, pl.ds(pl.multiple_of(k * HEAD_DIM, HEAD_DIM), HEAD_DIM)]
 
 
 def stack_kernel(axis, *refs):
@@ -130,12 +141,21 @@
 
 def line_chunks(outer, wide, refs):
     me = lax.axis_index("seq")
-    lines = (line_of(outer, 0), line_of(outer, 2), line_of(outer, 1, 3))
+    lines = [line_of(outer, near) for near in range(QUAD)]
+    step = wide + HEAD_DIM
     return [
-        (jnp.bitwise_xor(me, distance), lambda r=ref, i=i: r[:, i * wide : (i + 1) * wide])
+        (jnp.bitwise_xor(me, distance), lambda r=ref, i=i: r[:, i * step : i * step + wide])
         for ref, line in zip(refs, lines)
         for i, distance in enumerate(line)
     ]
+
+
+def line_mask(wide, ref, i):
+    at = pl.multiple_of(i * (wide + HEAD_DIM) + wide, HEAD_DIM)
+    tile = ref[:, pl.ds(at, HEAD_DIM)].astype(f32)
+    lane = lax.broadcasted_iota(jnp.int32, tile.shape, 1)
+    mine = jnp.where(lane == lax.axis_index("seq") // 2, tile, 0.0)
+    return jnp.broadcast_to(jnp.sum(mine, axis=1, keepdims=True), tile.shape)
 
 
 def member_chunks(refs):
@@ -147,9 +167,9 @@
 
 
 def query_kernel(outer, wide, *refs):
-    gain_ref, w_ref, out_ref = refs[3:]
+    gain_ref, w_ref, out_ref = refs[QUAD:]
     total = None
-    for at, chunk in normed_chunks(wide, line_chunks(outer, wide, refs[:3]), gain_ref):
+    for at, chunk in normed_chunks(wide, line_chunks(outer, wide, refs[:QUAD]), gain_ref):
         term = jnp.dot(chunk, w_ref[at, :], preferred_element_type=f32)
         total = term if total is None else total + term
     out_ref[...] = total.astype(bf16)
@@ -165,39 +185,39 @@
     scatter_dot(wide, False, left_ref[...], w_ref, out_ref)
 
 
-def span_states(spans, q_ref, cache):
-    rows = q_ref.shape[0]
+def span_states(q_ref, cache_ref, masks):
     heads = q_ref.shape[1] // HEAD_DIM
     scale = 1.0 / HEAD_DIM**0.5
+    keys = cache_ref.shape[0] // (2 * len(masks))
     queries = jnp.concatenate(
         [q_ref[:, h * HEAD_DIM : (h + 1) * HEAD_DIM] for h in range(heads)], axis=0
     )
-    states = []
-    for ref in cache:
-        size = ref.shape[0] // spans
-        keys = (size - rows) // 2
-        for k in range(spans):
-            at = k * size
-            live = ref[at + 2 * keys : at + size, :].astype(f32)
-            live = jnp.concatenate([live] * heads, axis=0) > 0.5
-            score = (
-                lax.dot_general(
-                    queries,
-                    ref[at : at + keys, :],
-                    (((1,), (1,)), ((), ())),
-                    preferred_element_type=f32,
-                )
-                * scale
-            )
-            masked = jnp.where(live, score, floor_score)
-            top = jnp.max(masked, axis=1, keepdims=True)
-            weight = jnp.where(live, jnp.exp(masked - top), 0.0)
-            total = jnp.sum(weight, axis=1, keepdims=True)
-            accum = jnp.dot(
-                weight.astype(bf16), ref[at + keys : at + 2 * keys, :], preferred_element_type=f32
-            )
-            states.append((top, total, accum))
-    return states
+    scores = [
+        lax.dot_general(
+            queries,
+            cache_ref[2 * i * keys : (2 * i + 1) * keys, :],
+            (((1,), (1,)), ((), ())),
+            preferred_element_type=f32,
+        )
+        * scale
+        for i in range(len(masks))
+    ]
+    lives = [jnp.concatenate([mask] * heads, axis=0) > 0.5 for mask in masks]
+    scores = [jnp.where(live, score, floor_score) for live, score in zip(lives, scores)]
+    tops = [jnp.max(score, axis=1, keepdims=True) for score in scores]
+    weights = [
+        jnp.where(live, jnp.exp(score - top), 0.0) for live, score, top in zip(lives, scores, tops)
+    ]
+    totals = [jnp.sum(weight, axis=1, keepdims=True) for weight in weights]
+    accums = [
+        jnp.dot(
+            weight.astype(bf16),
+            cache_ref[(2 * i + 1) * keys : (2 * i + 2) * keys, :],
+            preferred_element_type=f32,
+        )
+        for i, weight in enumerate(weights)
+    ]
+    return list(zip(tops, totals, accums))
 
 
 def combined(states):
@@ -210,18 +230,30 @@
     return top, total, accum
 
 
-def early_kernel(spans, q_ref, *refs):
-    cache, (top_ref, total_ref, accum_ref) = refs[:-3], refs[-3:]
-    top, total, accum_ref[...] = combined(span_states(spans, q_ref, cache))
+def early_kernel(outer, wide, q_ref, cache_ref, line_ref, other_ref, top_ref, total_ref, accum_ref):
+    core = lax.axis_index("seq") % 2
+    masks = [
+        line_mask(wide, ref, z_distance(slot, core))
+        for slot in z_slots(outer)
+        for ref in (line_ref, other_ref)
+    ]
+    top, total, accum_ref[...] = combined(span_states(q_ref, cache_ref, masks))
     top_ref[...] = jnp.broadcast_to(top, top_ref.shape)
     total_ref[...] = jnp.broadcast_to(total, total_ref.shape)
 
 
-def attend_kernel(wide, spans, q_ref, top_ref, total_ref, accum_ref, *refs):
-    cache, w_ref, left_ref, send_ref = refs[:-3], *refs[-3:]
+def attend_kernel(
+    outer, wide, q_ref, top_ref, total_ref, accum_ref, cache_ref, core_ref, far_ref, w_ref, left_ref, send_ref
+):
     rows = q_ref.shape[0]
     heads = q_ref.shape[1] // HEAD_DIM
-    states = span_states(spans, q_ref, cache)
+    core = 1 - lax.axis_index("seq") % 2
+    masks = [
+        line_mask(wide, ref, z_distance(slot, core))
+        for slot in z_slots(outer)
+        for ref in (core_ref, far_ref)
+    ]
+    states = span_states(q_ref, cache_ref, masks)
     states.append((top_ref[:, 0:1], total_ref[:, 0:1], accum_ref[...]))
     _, total, accum = combined(states)
     attended = (accum / total).astype(bf16)
@@ -265,13 +297,17 @@
     return [parts[0], *reversed(arrived)]
 
 
-def z_gathered(x, outer):
-    return stacked(z_swapped([x] * outer), 1)
-
-
-def near_gathered(line, after=()):
-    other = swap(line, 2)
-    return [line, other, swap(stacked([line, other], 1, after), 1)]
+def z_routed(parts):
+    size = lax.axis_size("seq")
+    return [parts[0]] + [
+        lax.ppermute(part, "seq", [(i, i ^ QUAD * slot[i % 2]) for i in range(size)])
+        for slot, part in list(zip(z_slots(len(parts)), parts))[1:]
+    ]
+
+
+def near_gathered(line):
+    far, y, core = swap(line, 3), swap(line, 2), swap(line, 1)
+    return [line, core, y, far]
 
 
 def scattered(base, send, left, weight, wide, kind, outs, beside=()):
@@ -294,37 +330,38 @@
     partial_sums = like((members, rows, wide), f32)
     own_columns = like((rows, wide), bf16)
 
-    size = 2 * kv_cache.shape[1] + rows
-    own, send = call(
+    keys = kv_cache.shape[1]
+    held, send = call(
         functools.partial(pack_kernel, outer),
-        [like((size, outer * HEAD_DIM), bf16)] * 2,
-        [kv_cache, block_mask[:, :, 0]],
+        [like((rows, wide + HEAD_DIM), bf16), like((2 * keys, outer * HEAD_DIM), bf16)],
+        [kv_cache, block_mask[:, :, 0], x_rows],
         beside,
     )
     other = swap(send, 2)
-    x_line = z_swapped([x_rows] * outer)
-    line = stacked(x_line, 1)
+    line = stacked(z_swapped([held] * outer), 1)
     routed = call(
         functools.partial(route_kernel, outer),
-        [like((2 * size, HEAD_DIM), bf16)] * outer,
-        [own, other],
-        [*[], *beside],
-    )
-    cache = z_swapped(routed)
+        [like((4 * keys, HEAD_DIM), bf16)] * outer,
+        [kv_cache, other],
+        [line, *beside],
+    )
+    routed = z_routed(routed)
     x_parts = near_gathered(line)
     queries = call(
         functools.partial(query_kernel, outer, wide),
         like((rows, columns), bf16),
         [*x_parts, attn_gain, q_weight],
     )
-    first = stacked(cache, 0, [queries])
-    second = swap(first, 1)
+    cache = stacked(routed, 0, [queries])
+    far_cache = swap(cache, 1)
     tall = like((columns // HEAD_DIM * rows, HEAD_DIM), f32)
-    early = call(functools.partial(early_kernel, 2 * outer), [tall] * 3, [queries, first])
+    early = call(
+        functools.partial(early_kernel, outer, wide), [tall] * 3, [queries, cache, *x_parts[0::2]]
+    )
     left, send = call(
-        functools.partial(attend_kernel, wide, 2 * outer),
+        functools.partial(attend_kernel, outer, wide),
         [like((rows, columns), bf16), partial_sums],
-        [queries, *early, second, o_weight],
+        [queries, *early, far_cache, *x_parts[1::2], o_weight],
     )
     stream, copies = scattered(
         x_rows, send, left, o_weight, wide, f32, [own_columns, like(partial_sums.shape, bf16)], beside

time: 77.2 us -> 75.7 us (0.981)
  Pallas kernels: 13.9 us -> 10.9 us
  waiting for transfers between devices: 13.6 us -> 16.3 us
  blocking collectives: 34.8 us -> 33.4 us
    ppermute x0 -> x3, starting transfers between devices: none -> 3.55 us  [z_routed(): lax.ppermute(part, 'seq', [(i, i ^ QUAD * slot[i % 2]) for i in range(siz...]
    ppermute x13 -> x11, starting transfers between devices: 13.1 us -> 9.77 us  [swap(): return lax.ppermute(x, 'seq', [(i, i ^ distance) for i in range(size)])]
    pallas_call x15 -> x14, Pallas kernels: 13.9 us -> 10.9 us  [call(): pl.pallas_call(kernel, out_shape=outs, in_specs=[VMEM] * count + [pl.Bloc...]
    ppermute x0 -> x3, waiting for transfers between devices: none -> 2.77 us  [z_routed(): lax.ppermute(part, 'seq', [(i, i ^ QUAD * slot[i % 2]) for i in range(siz...]
    all_to_all x3, blocking collectives: 34.8 us -> 33.4 us  [to_members(): lax.all_to_all(parts, 'seq', 0, 0, axis_index_groups=groups, tiled=True)]
    ppermute x13 -> x11, waiting for transfers between devices: 13.6 us -> 13.5 us  [swap(): return lax.ppermute(x, 'seq', [(i, i ^ distance) for i in range(size)])]
  transfers between devices with their start and end apart: 13 -> 14, of which waited for: 7 -> 9; matrix products, arithmetic and copies ran while one was open for 0% -> 0% of each run, Pallas kernels for 7% -> 5%
where the time goes in v5:
time: 75.7 us; the launch traced here: 75.4 us
  blocking collectives  33.4 us (44%)
  waiting for transfers between devices  16.3 us (22%)
  starting transfers between devices  13.3 us (18%)
  Pallas kernels  10.9 us (14%)
  local copies, waits for them, and re-layouts  1.2 us (2%)
    all_to_all x3, blocking collectives, to_members(): lax.all_to_all(parts, 'seq', 0, 0, axis_index_groups=groups, tiled=True)  33.4 us
    ppermute x11, waiting for transfers between devices, swap(): return lax.ppermute(x, 'seq', [(i, i ^ distance) for i in range(size)])  13.5 us
    pallas_call x14, Pallas kernels, call(): pl.pallas_call(kernel, out_shape=outs, in_specs=[VMEM] * count + [pl.Bloc...  10.9 us
    ppermute x11, starting transfers between devices, swap(): return lax.ppermute(x, 'seq', [(i, i ^ distance) for i in range(size)])  9.77 us
    ppermute x3, starting transfers between devices, z_routed(): lax.ppermute(part, 'seq', [(i, i ^ QUAD * slot[i % 2]) for i in range(siz...  3.55 us
    ppermute x3, waiting for transfers between devices, z_routed(): lax.ppermute(part, 'seq', [(i, i ^ QUAD * slot[i % 2]) for i in range(siz...  2.77 us
  transfers between devices with their start and end apart: 14, of which 9 were waited for; matrix products, arithmetic and copies ran while one was open for 0% of the time, Pallas kernels for 5%

profile of v5, /device:TPU:0, one launch (start us, length us, event | category | flops | bytes accessed | tf_op | source)
XLA Modules:
  0.0 75.4 jit_solution(5632637685965217458)
XLA Ops:
  0.0 0.7 copy-done.4
  1.2 3.0 %collective-permute-start.6 = (bf16[256,512]{1,0:T(8,128)(2,1)S(1)}, bf16[256,512]{1,0:T(8,128)(2,1)S(1)}, u32[]{:S(2)}, u32[]{:S(2)}) collective-permute-start(bf16[256,512]{1,0:T(8,128)(2,1)S(1)} %get-tuple-element.21), channel_id=1, source_target_pairs={{0,2},{1,3},{2,0},{3,1},{4,6},{5,7},{6,4},{7,5},{8,10},{9,11},{10,... | collective-permute-start | bytes 786440 | tf_op jit(solution)/shard_map/ppermute | solution.py:53
  4.2 1.6 %collective-permute-start = (bf16[16,640]{1,0:T(8,128)(2,1)S(1)}, bf16[16,640]{1,0:T(8,128)(2,1)S(1)}, u32[]{:S(2)}, u32[]{:S(2)}) collective-permute-start(bf16[16,640]{1,0:T(8,128)(2,1)S(1)} %get-tuple-element.20.refs_0_), channel_id=1, source_target_pairs={{0,4},{1,5},{2,6},{3,7},{4,0},{5,1},{6,2},{7,3},{8,12},{9,13},{10,... | collective-permute-start | bytes 61448 | tf_op jit(solution)/shard_map/ppermute | solution.py:53
  5.8 2.6 %collective-permute-start.1 = (bf16[16,640]{1,0:T(8,128)(2,1)S(1)}, bf16[16,640]{1,0:T(8,128)(2,1)S(1)}, u32[]{:S(2)}, u32[]{:S(2)}) collective-permute-start(bf16[16,640]{1,0:T(8,128)(2,1)S(1)} %get-tuple-element.20.refs_0_), channel_id=1, source_target_pairs={{0,8},{1,9},{2,10},{3,11},{4,12},{5,13},{6,14},{7,15},{8,0},{9,1},... | collective-permute-start | bytes 61448 | tf_op jit(solution)/shard_map/ppermute | solution.py:53
  8.6 2.0 %collective-permute-done.1.refs_2_ = bf16[16,640]{1,0:T(8,128)(2,1)S(1)} collective-permute-done((bf16[16,640]{1,0:T(8,128)(2,1)S(1)}, bf16[16,640]{1,0:T(8,128)(2,1)S(1)}, u32[]{:S(2)}, u32[]{:S(2)}) %collective-permute-start.1) | collective-permute-done | bytes 20512 | tf_op jit(solution)/shard_map/ppermute | solution.py:53
  10.6 3.4 %collective-permute-done.2.refs_3_ = bf16[16,640]{1,0:T(8,128)(2,1)S(1)} collective-permute-done((bf16[16,640]{1,0:T(8,128)(2,1)S(1)}, bf16[16,640]{1,0:T(8,128)(2,1)S(1)}, u32[]{:S(2)}, u32[]{:S(2)}) %collective-permute-start.2) | collective-permute-done | bytes 20512 | tf_op jit(solution)/shard_map/ppermute | solution.py:53
  14.3 0.7 collective-permute-start.8
  15.0 2.8 %collective-permute-start.9 = (bf16[512,128]{1,0:T(8,128)(2,1)S(1)}, bf16[512,128]{1,0:T(8,128)(2,1)S(1)}, u32[]{:S(2)}, u32[]{:S(2)}) collective-permute-start(bf16[512,128]{1,0:T(8,128)(2,1)S(1)} %get-tuple-element.25), channel_id=1, source_target_pairs={{0,8},{1,5},{2,10},{3,7},{4,12},{5,1},{6,14},{7,3},{8,0},{9,13},{1... | collective-permute-start | bytes 393224 | tf_op jit(solution)/shard_map/ppermute | solution.py:303
  18.3 1.4 %collective-permute-start.5 = (bf16[16,2560]{1,0:T(8,128)(2,1)S(1)}, bf16[16,2560]{1,0:T(8,128)(2,1)S(1)}, u32[]{:S(2)}, u32[]{:S(2)}) collective-permute-start(bf16[16,2560]{1,0:T(8,128)(2,1)S(1)} %shard_map.102.refs_0_.refs_2_), channel_id=1, source_target_pairs={{0,3},{1,2},{2,1},{3,0},{4,7},{5,6},{6,5},{7,4},{8,11},{9,10},{10,... | collective-permute-start | bytes 245768 | tf_op jit(solution)/shard_map/ppermute | solution.py:53
  19.7 3.3 %collective-permute-done.4.refs_2_.refs_3_ = bf16[16,2560]{1,0:T(8,128)(2,1)S(1)} collective-permute-done((bf16[16,2560]{1,0:T(8,128)(2,1)S(1)}, bf16[16,2560]{1,0:T(8,128)(2,1)S(1)}, u32[]{:S(2)}, u32[]{:S(2)}) %collective-permute-start.4) | collective-permute-done | bytes 81952 | tf_op jit(solution)/shard_map/ppermute | solution.py:53
  23.0 1.1 %collective-permute-done.5.refs_3_.refs_6_ = bf16[16,2560]{1,0:T(8,128)(2,1)S(1)} collective-permute-done((bf16[16,2560]{1,0:T(8,128)(2,1)S(1)}, bf16[16,2560]{1,0:T(8,128)(2,1)S(1)}, u32[]{:S(2)}, u32[]{:S(2)}) %collective-permute-start.5) | collective-permute-done | bytes 81952 | tf_op jit(solution)/shard_map/ppermute | solution.py:53
  24.1 1.3 %shard_map.103.refs_4_.refs_0_ = bf16[16,512]{1,0:T(8,128)(2,1)S(1)} custom-call(bf16[16,2560]{1,0:T(8,128)(2,1)S(1)} %shard_map.102.refs_0_.refs_2_, bf16[16,2560]{1,0:T(8,128)(2,1)S(1)} %collective-permute-done.3.refs_1_.refs_5_, bf16[16,2560]{1,0:T(8,128)(2,1)S(1)} %collective-permute-done.4.refs_2_.refs_3_, ...), custom_call_target="tpu_custom_call" | custom-call | tf_op jit(solution)/shard_map/pallas_call | solution.py:30
  25.4 2.8 %collective-permute-done.9.refs_3_ = bf16[512,128]{1,0:T(8,128)(2,1)S(1)} collective-permute-done((bf16[512,128]{1,0:T(8,128)(2,1)S(1)}, bf16[512,128]{1,0:T(8,128)(2,1)S(1)}, u32[]{:S(2)}, u32[]{:S(2)}) %collective-permute-start.9) | collective-permute-done | bytes 131104 | tf_op jit(solution)/shard_map/ppermute | solution.py:303
  28.9 1.4 %collective-permute-done.10.refs_4_ = bf16[2048,128]{1,0:T(8,128)(2,1)S(1)} collective-permute-done((bf16[2048,128]{1,0:T(8,128)(2,1)S(1)}, bf16[2048,128]{1,0:T(8,128)(2,1)S(1)}, u32[]{:S(2)}, u32[]{:S(2)}) %collective-permute-start.10) | collective-permute-done | bytes 524320 | tf_op jit(solution)/shard_map/ppermute | solution.py:53
  30.2 1.2 %shard_map.107 = (bf16[16,512]{1,0:T(8,128)(2,1)S(1)}, f32[8,16,512]{2,1,0:T(8,128)S(1)}) custom-call(bf16[16,512]{1,0:T(8,128)(2,1)S(1)} %shard_map.103.refs_4_.refs_0_, f32[64,128]{1,0:T(8,128)S(1)} %get-tuple-element.26.refs_1_, f32[64,128]{1,0:T(8,128)S(1)} %get-tuple-element.27.refs_2_, f32[64,128]{1,0:T(8,128)S(1)} %get-tuple-element.28.refs_3_, ...), custom_call_target="tpu_custom_call" | custom-call | tf_op jit(solution)/shard_map/pallas_call | solution.py:30
  31.6 0.6 shard_map.108.refs_0_
  32.3 0.8 collective-permute-done.11.refs_1_
  33.1 12.4 %all_to_all.15.refs_1_ = f32[8,16,512]{2,1,0:T(8,128)S(1)} all-to-all(f32[8,16,512]{2,1,0:T(8,128)S(1)} %shard_map.109), channel_id=1, replica_groups={{0,2,4,6,8,10,12,14},{1,3,5,7,9,11,13,15},{16,18,20,22,24,26,28,30},{17..., dimensions={0} | all-to-all | bytes 524288 | tf_op jit(solution)/shard_map/all_to_all | solution.py:130
  45.6 11.0 %all_to_all.16.refs_0_ = bf16[8,16,512]{2,1,0:T(8,128)(2,1)S(1)} all-to-all(bf16[8,16,512]{2,1,0:T(8,128)(2,1)S(1)} %get-tuple-element.32), channel_id=1, replica_groups={{0,2,4,6,8,10,12,14},{1,3,5,7,9,11,13,15},{16,18,20,22,24,26,28,30},{17..., dimensions={0} | all-to-all | bytes 262144 | tf_op jit(solution)/shard_map/all_to_all | solution.py:130
  56.6 1.3 %collective-permute-done.12.refs_1_ = bf16[8,16,512]{2,1,0:T(8,128)(2,1)S(1)} collective-permute-done((bf16[8,16,512]{2,1,0:T(8,128)(2,1)S(1)}, bf16[8,16,512]{2,1,0:T(8,128)(2,1)S(1)}, u32[]{:S(2)}, u32[]{:S(2)}) %collective-permute-start.12) | collective-permute-done | bytes 131104 | tf_op jit(solution)/shard_map/ppermute | solution.py:53
  58.1 5.1 %shard_map.111 = (bf16[16,896]{1,0:T(8,128)(2,1)S(1)}, f32[8,16,512]{2,1,0:T(8,128)S(1)}) custom-call(bf16[8,16,512]{2,1,0:T(8,128)(2,1)S(1)} %all_to_all.16.refs_0_, bf16[8,16,512]{2,1,0:T(8,128)(2,1)S(1)} %collective-permute-done.12.refs_1_, bf16[1,8192]{1,0:T(2,128)(2,1)S(1)} %reshape.7.refs_2_, bf16[8192,896]{1,0:T(8,128)(2,1)S(1)} %bitcast.6, ...), custom_call_target="tpu_custom_call" | custom-call | tf_op jit(solution)/shard_map/pallas_call | solution.py:30
  63.4 1.1 %shard_map.112.refs_0_ = f32[8,16,512]{2,1,0:T(8,128)S(1)} custom-call(bf16[16,896]{1,0:T(8,128)(2,1)S(1)} %get-tuple-element.33.refs_0_, bf16[896,8192]{1,0:T(8,128)(2,1)S(1)} %bitcast.2), custom_call_target="tpu_custom_call" | custom-call | tf_op jit(solution)/shard_map/pallas_call | solution.py:30
  64.8 10.0 %all_to_all.17.refs_1_ = bf16[8,16,512]{2,1,0:T(8,128)(2,1)S(1)} all-to-all(bf16[8,16,512]{2,1,0:T(8,128)(2,1)S(1)} %shard_map.113), channel_id=1, replica_groups={{0,2,4,6,8,10,12,14},{1,3,5,7,9,11,13,15},{16,18,20,22,24,26,28,30},{17..., dimensions={0} | all-to-all | bytes 262144 | tf_op jit(solution)/shard_map/all_to_all | solution.py:130
  74.7 0.6 shard_map.114
  (72 shorter events, 3.0 us)
Async XLA Ops:
  1.2 12.9 %collective-permute-start.6 = (bf16[256,512]{1,0:T(8,128)(2,1)S(1)}, bf16[256,512]{1,0:T(8,128)(2,1)S(1)}, u32[]{:S(2)}, u32[]{:S(2)}) collective-permute-start(bf16[256,512]{1,0:T(8,128)(2,1)S(1)} %get-tuple-element.21), channel_id=1, source_target_pairs={{0,2},{1,3},{2,0},{3,1},{4,6},{5,7},{6,4},{7,5},{8,10},{9,11},{10,... | collective-permute-start | bytes 786440 | tf_op jit(solution)/shard_map/ppermute | solution.py:53
  4.2 4.4 %collective-permute-start = (bf16[16,640]{1,0:T(8,128)(2,1)S(1)}, bf16[16,640]{1,0:T(8,128)(2,1)S(1)}, u32[]{:S(2)}, u32[]{:S(2)}) collective-permute-start(bf16[16,640]{1,0:T(8,128)(2,1)S(1)} %get-tuple-element.20.refs_0_), channel_id=1, source_target_pairs={{0,4},{1,5},{2,6},{3,7},{4,0},{5,1},{6,2},{7,3},{8,12},{9,13},{10,... | collective-permute-start | bytes 61448 | tf_op jit(solution)/shard_map/ppermute | solution.py:53
  5.8 4.8 %collective-permute-start.1 = (bf16[16,640]{1,0:T(8,128)(2,1)S(1)}, bf16[16,640]{1,0:T(8,128)(2,1)S(1)}, u32[]{:S(2)}, u32[]{:S(2)}) collective-permute-start(bf16[16,640]{1,0:T(8,128)(2,1)S(1)} %get-tuple-element.20.refs_0_), channel_id=1, source_target_pairs={{0,8},{1,9},{2,10},{3,11},{4,12},{5,13},{6,14},{7,15},{8,0},{9,1},... | collective-permute-start | bytes 61448 | tf_op jit(solution)/shard_map/ppermute | solution.py:53
  8.4 5.6 %collective-permute-start.2 = (bf16[16,640]{1,0:T(8,128)(2,1)S(1)}, bf16[16,640]{1,0:T(8,128)(2,1)S(1)}, u32[]{:S(2)}, u32[]{:S(2)}) collective-permute-start(bf16[16,640]{1,0:T(8,128)(2,1)S(1)} %get-tuple-element.20.refs_0_), channel_id=1, source_target_pairs={{0,12},{1,13},{2,14},{3,15},{4,8},{5,9},{6,10},{7,11},{8,4},{9,5},... | collective-permute-start | bytes 61448 | tf_op jit(solution)/shard_map/ppermute | solution.py:53
  14.0 16.3 %slice-start.4 = ((s8[8388608]{0:T(1024)(128)(4,1)}), s8[4194304]{0:T(1024)(128)(4,1)S(1)}, s32[]{:S(2)}) async-start(s8[8388608]{0:T(1024)(128)(4,1)} %bitcast.3), calls=%async_computation.7 | async-start | bytes 8388608
  14.0 4.3 %collective-permute-start.3 = (bf16[16,2560]{1,0:T(8,128)(2,1)S(1)}, bf16[16,2560]{1,0:T(8,128)(2,1)S(1)}, u32[]{:S(2)}, u32[]{:S(2)}) collective-permute-start(bf16[16,2560]{1,0:T(8,128)(2,1)S(1)} %shard_map.102.refs_0_.refs_2_), channel_id=1, source_target_pairs={{0,1},{1,0},{2,3},{3,2},{4,5},{5,4},{6,7},{7,6},{8,9},{9,8},{10,11... | collective-permute-start | bytes 245768 | tf_op jit(solution)/shard_map/ppermute | solution.py:53
  14.2 11.2 %collective-permute-start.7 = (bf16[512,128]{1,0:T(8,128)(2,1)S(1)}, bf16[512,128]{1,0:T(8,128)(2,1)S(1)}, u32[]{:S(2)}, u32[]{:S(2)}) collective-permute-start(bf16[512,128]{1,0:T(8,128)(2,1)S(1)} %get-tuple-element.23), channel_id=1, source_target_pairs={{0,4},{1,13},{2,6},{3,15},{4,0},{5,9},{6,2},{7,11},{8,12},{9,5},{1... | collective-permute-start | bytes 393224 | tf_op jit(solution)/shard_map/ppermute | solution.py:303
  14.3 11.1 %collective-permute-start.8 = (bf16[512,128]{1,0:T(8,128)(2,1)S(1)}, bf16[512,128]{1,0:T(8,128)(2,1)S(1)}, u32[]{:S(2)}, u32[]{:S(2)}) collective-permute-start(bf16[512,128]{1,0:T(8,128)(2,1)S(1)} %get-tuple-element.24), channel_id=1, source_target_pairs={{0,12},{1,9},{2,14},{3,11},{4,8},{5,13},{6,10},{7,15},{8,4},{9,1},... | collective-permute-start | bytes 393224 | tf_op jit(solution)/shard_map/ppermute | solution.py:303
  15.0 13.2 %collective-permute-start.9 = (bf16[512,128]{1,0:T(8,128)(2,1)S(1)}, bf16[512,128]{1,0:T(8,128)(2,1)S(1)}, u32[]{:S(2)}, u32[]{:S(2)}) collective-permute-start(bf16[512,128]{1,0:T(8,128)(2,1)S(1)} %get-tuple-element.25), channel_id=1, source_target_pairs={{0,8},{1,5},{2,10},{3,7},{4,12},{5,1},{6,14},{7,3},{8,0},{9,13},{1... | collective-permute-start | bytes 393224 | tf_op jit(solution)/shard_map/ppermute | solution.py:303
  17.8 5.2 %collective-permute-start.4 = (bf16[16,2560]{1,0:T(8,128)(2,1)S(1)}, bf16[16,2560]{1,0:T(8,128)(2,1)S(1)}, u32[]{:S(2)}, u32[]{:S(2)}) collective-permute-start(bf16[16,2560]{1,0:T(8,128)(2,1)S(1)} %shard_map.102.refs_0_.refs_2_), channel_id=1, source_target_pairs={{0,2},{1,3},{2,0},{3,1},{4,6},{5,7},{6,4},{7,5},{8,10},{9,11},{10,... | collective-permute-start | bytes 245768 | tf_op jit(solution)/shard_map/ppermute | solution.py:53
  18.3 5.8 %collective-permute-start.5 = (bf16[16,2560]{1,0:T(8,128)(2,1)S(1)}, bf16[16,2560]{1,0:T(8,128)(2,1)S(1)}, u32[]{:S(2)}, u32[]{:S(2)}) collective-permute-start(bf16[16,2560]{1,0:T(8,128)(2,1)S(1)} %shard_map.102.refs_0_.refs_2_), channel_id=1, source_target_pairs={{0,3},{1,2},{2,1},{3,0},{4,7},{5,6},{6,5},{7,4},{8,11},{9,10},{10,... | collective-permute-start | bytes 245768 | tf_op jit(solution)/shard_map/ppermute | solution.py:53
  28.2 2.0 %collective-permute-start.10 = (bf16[2048,128]{1,0:T(8,128)(2,1)S(1)}, bf16[2048,128]{1,0:T(8,128)(2,1)S(1)}, u32[]{:S(2)}, u32[]{:S(2)}) collective-permute-start(bf16[2048,128]{1,0:T(8,128)(2,1)S(1)} %shard_map.105.refs_1_), channel_id=1, source_target_pairs={{0,1},{1,0},{2,3},{3,2},{4,5},{5,4},{6,7},{7,6},{8,9},{9,8},{10,11... | collective-permute-start | bytes 1572872 | tf_op jit(solution)/shard_map/ppermute | solution.py:53
  31.5 1.5 %collective-permute-start.11 = (f32[8,16,512]{2,1,0:T(8,128)S(1)}, f32[8,16,512]{2,1,0:T(8,128)S(1)}, u32[]{:S(2)}, u32[]{:S(2)}) collective-permute-start(f32[8,16,512]{2,1,0:T(8,128)S(1)} %get-tuple-element.30), channel_id=1, source_target_pairs={{0,1},{1,0},{2,3},{3,2},{4,5},{5,4},{6,7},{7,6},{8,9},{9,8},{10,11... | collective-permute-start | bytes 786440 | tf_op jit(solution)/shard_map/ppermute | solution.py:53
  33.0 24.9 %slice-start = ((s8[14680064]{0:T(1024)(128)(4,1)}), s8[4194304]{0:T(1024)(128)(4,1)S(1)}, s32[]{:S(2)}) async-start(s8[14680064]{0:T(1024)(128)(4,1)} %bitcast.1), calls=%async_computation.3 | async-start | bytes 8388608
  33.0 24.9 %slice-start.1 = ((s8[14680064]{0:T(1024)(128)(4,1)}), s8[4194304]{0:T(1024)(128)(4,1)S(1)}, s32[]{:S(2)}) async-start(s8[14680064]{0:T(1024)(128)(4,1)} %bitcast.1), calls=%async_computation.4 | async-start | bytes 8388608
  33.0 24.9 %slice-start.6 = ((s8[14680064]{0:T(1024)(128)(4,1)}), s8[4194304]{0:T(1024)(128)(4,1)S(1)}, s32[]{:S(2)}) async-start(s8[14680064]{0:T(1024)(128)(4,1)} %bitcast.5), calls=%async_computation.9 | async-start | bytes 8388608
  33.0 24.9 %slice-start.7 = ((s8[14680064]{0:T(1024)(128)(4,1)}), s8[4194304]{0:T(1024)(128)(4,1)S(1)}, s32[]{:S(2)}) async-start(s8[14680064]{0:T(1024)(128)(4,1)} %bitcast.5), calls=%async_computation.10 | async-start | bytes 8388608
  33.0 24.9 %slice-start.10 = ((s8[14680064]{0:T(1024)(128)(4,1)}), s8[4194304]{0:T(1024)(128)(4,1)S(1)}, s32[]{:S(2)}) async-start(s8[14680064]{0:T(1024)(128)(4,1)} %bitcast.7), calls=%async_computation.13 | async-start | bytes 8388608
  33.0 24.9 %slice-start.11 = ((s8[14680064]{0:T(1024)(128)(4,1)}), s8[4194304]{0:T(1024)(128)(4,1)S(1)}, s32[]{:S(2)}) async-start(s8[14680064]{0:T(1024)(128)(4,1)} %bitcast.7), calls=%async_computation.14 | async-start | bytes 8388608
  33.1 24.9 %slice-start.2 = ((s8[14680064]{0:T(1024)(128)(4,1)}), s8[4194304]{0:T(1024)(128)(4,1)S(1)}, s32[]{:S(2)}) async-start(s8[14680064]{0:T(1024)(128)(4,1)} %bitcast.1), calls=%async_computation.5 | async-start | bytes 8388608
  33.1 24.9 %slice-start.8 = ((s8[14680064]{0:T(1024)(128)(4,1)}), s8[4194304]{0:T(1024)(128)(4,1)S(1)}, s32[]{:S(2)}) async-start(s8[14680064]{0:T(1024)(128)(4,1)} %bitcast.5), calls=%async_computation.11 | async-start | bytes 8388608
  33.1 24.9 %slice-start.12 = ((s8[14680064]{0:T(1024)(128)(4,1)}), s8[4194304]{0:T(1024)(128)(4,1)S(1)}, s32[]{:S(2)}) async-start(s8[14680064]{0:T(1024)(128)(4,1)} %bitcast.7), calls=%async_computation.15 | async-start | bytes 8388608
  56.6 1.3 %collective-permute-start.12 = (bf16[8,16,512]{2,1,0:T(8,128)(2,1)S(1)}, bf16[8,16,512]{2,1,0:T(8,128)(2,1)S(1)}, u32[]{:S(2)}, u32[]{:S(2)}) collective-permute-start(bf16[8,16,512]{2,1,0:T(8,128)(2,1)S(1)} %all_to_all.16.refs_0_), channel_id=1, source_target_pairs={{0,1},{1,0},{2,3},{3,2},{4,5},{5,4},{6,7},{7,6},{8,9},{9,8},{10,11... | collective-permute-start | bytes 393224 | tf_op jit(solution)/shard_map/ppermute | solution.py:53
  63.2 1.5 %collective-permute-start.13 = (f32[8,16,512]{2,1,0:T(8,128)S(1)}, f32[8,16,512]{2,1,0:T(8,128)S(1)}, u32[]{:S(2)}, u32[]{:S(2)}) collective-permute-start(f32[8,16,512]{2,1,0:T(8,128)S(1)} %get-tuple-element.34), channel_id=1, source_target_pairs={{0,1},{1,0},{2,3},{3,2},{4,5},{5,4},{6,7},{7,6},{8,9},{9,8},{10,11... | collective-permute-start | bytes 786440 | tf_op jit(solution)/shard_map/ppermute | solution.py:53
  (11 other events, 93.2 us)

commit v6 on v5

--- a/solution.py
+++ b/solution.py
@@ -53,24 +53,38 @@
     return lax.ppermute(x, "seq", [(i, i ^ distance) for i in range(size)])
 
 
-def pack_kernel(outer, kv_ref, mask_ref, x_ref, held_ref, send_ref):
+def pack_kernel(outer, kv_ref, mask_ref, x_ref, send_ref, *outs):
     me = lax.axis_index("seq")
     z, y = me // QUAD, (me // 2) % 2
     keys = kv_ref.shape[1]
-    rows, wide = x_ref.shape
+    rows = mask_ref.shape[0]
+    pieces = [x_ref[:, at : at + HEAD_DIM] for at in range(0, x_ref.shape[1], HEAD_DIM)]
     lane = lax.broadcasted_iota(jnp.int32, (rows, HEAD_DIM), 1)
     mask = jnp.zeros((rows, HEAD_DIM), f32)
     for head in range(mask_ref.shape[1]):
         live = (mask_ref[:, head : head + 1] == 1).astype(f32)
         mask = jnp.where(lane == head, jnp.broadcast_to(live, mask.shape), mask)
-    held_ref[:, 0:wide] = x_ref[...]
-    held_ref[:, wide:] = mask.astype(bf16)
+    pieces.append(mask.astype(bf16))
     for k in range(outer):
-        head = 2 * jnp.bitwise_xor(z, k) + 1 - y
-        cols = pl.ds(pl.multiple_of(head * HEAD_DIM, HEAD_DIM), HEAD_DIM)
+        peer = jnp.bitwise_xor(z, k)
+        cols = pl.ds(pl.multiple_of((2 * peer + y) * HEAD_DIM, HEAD_DIM), HEAD_DIM)
+        outs[k][0:keys, :] = kv_ref[0, :, cols]
+        for i, piece in enumerate(pieces):
+            outs[k][keys + i * rows : keys + (i + 1) * rows, :] = piece
+        cols = pl.ds(pl.multiple_of((2 * peer + 1 - y) * HEAD_DIM, HEAD_DIM), HEAD_DIM)
         at = slice(k * HEAD_DIM, (k + 1) * HEAD_DIM)
         send_ref[0:keys, at] = kv_ref[0, :, cols]
         send_ref[keys : 2 * keys, at] = kv_ref[1, :, cols]
+
+
+def unpack_kernel(keys, *refs):
+    line_ref = refs[-1]
+    rows = line_ref.shape[0]
+    at = 0
+    for ref in refs[:-1]:
+        for i in range((ref.shape[0] - keys) // rows):
+            line_ref[:, at : at + HEAD_DIM] = ref[keys + i * rows : keys + (i + 1) * rows, :]
+            at += HEAD_DIM
 
 
 def z_slots(outer):
@@ -90,9 +104,22 @@
         k = z_distance(slot, me % 2)
         head = 2 * jnp.bitwise_xor(z, k) + y
         cols = pl.ds(pl.multiple_of(head * HEAD_DIM, HEAD_DIM), HEAD_DIM)
-        out[0:keys, :] = kv_ref[0, :, cols]
-        out[keys : 2 * keys, :] = kv_ref[1, :, cols]
-        out[2 * keys :, :] = other_ref[:, pl.ds(pl.multiple_of(k * HEAD_DIM, HEAD_DIM), HEAD_DIM)]
+        out[0:keys, :] = kv_ref[1, :, cols]
+        out[keys:, :] = other_ref[:, pl.ds(pl.multiple_of(k * HEAD_DIM, HEAD_DIM), HEAD_DIM)]
+
+
+def cache_kernel(outer, keys, *refs):
+    firsts, rests, out_ref = refs[:outer], refs[outer : 2 * outer], refs[2 * outer]
+    core = lax.axis_index("seq") % 2
+    for i, slot in enumerate(z_slots(outer)):
+        at = 4 * i * keys
+        for at_core in range(2):
+
+            @pl.when(core == at_core)
+            def _():
+                out_ref[at : at + keys, :] = firsts[slot[at_core]][0:keys, :]
+
+        out_ref[at + keys : at + 4 * keys, :] = rests[i][...]
 
 
 def stack_kernel(axis, *refs):
@@ -331,17 +358,20 @@
     own_columns = like((rows, wide), bf16)
 
     keys = kv_cache.shape[1]
-    held, send = call(
+    step = wide + HEAD_DIM
+    send, *firsts = call(
         functools.partial(pack_kernel, outer),
-        [like((rows, wide + HEAD_DIM), bf16), like((2 * keys, outer * HEAD_DIM), bf16)],
+        [like((2 * keys, outer * HEAD_DIM), bf16)]
+        + [like((keys + step // HEAD_DIM * rows, HEAD_DIM), bf16)] * outer,
         [kv_cache, block_mask[:, :, 0], x_rows],
         beside,
     )
     other = swap(send, 2)
-    line = stacked(z_swapped([held] * outer), 1)
+    firsts = z_swapped(firsts)
+    line = call(functools.partial(unpack_kernel, keys), like((rows, outer * step), bf16), firsts)
     routed = call(
         functools.partial(route_kernel, outer),
-        [like((4 * keys, HEAD_DIM), bf16)] * outer,
+        [like((3 * keys, HEAD_DIM), bf16)] * outer,
         [kv_cache, other],
         [line, *beside],
     )
@@ -352,7 +382,12 @@
         like((rows, columns), bf16),
         [*x_parts, attn_gain, q_weight],
     )
-    cache = stacked(routed, 0, [queries])
+    cache = call(
+        functools.partial(cache_kernel, outer, keys),
+        like((4 * outer * keys, HEAD_DIM), bf16),
+        [*firsts, *routed],
+        [queries],
+    )
     far_cache = swap(cache, 1)
     tall = like((columns // HEAD_DIM * rows, HEAD_DIM), f32)
     early = call(

time: 75.7 us -> 73.9 us (0.976)
  waiting for transfers between devices: 16.3 us -> 14.5 us
    ppermute x3, waiting for transfers between devices: 2.77 us -> 0.64 us  [z_routed(): lax.ppermute(part, 'seq', [(i, i ^ QUAD * slot[i % 2]) for i in range(siz...]
where the time goes in v6:
time: 73.9 us; the launch traced here: 73.6 us
  blocking collectives  33.4 us (45%)
  waiting for transfers between devices  14.5 us (20%)
  starting transfers between devices  13.3 us (18%)
  Pallas kernels  10.9 us (15%)
  local copies, waits for them, and re-layouts  1.2 us (2%)
    all_to_all x3, blocking collectives, to_members(): lax.all_to_all(parts, 'seq', 0, 0, axis_index_groups=groups, tiled=True)  33.4 us
    ppermute x11, waiting for transfers between devices, swap(): return lax.ppermute(x, 'seq', [(i, i ^ distance) for i in range(size)])  13.9 us
    pallas_call x14, Pallas kernels, call(): pl.pallas_call(kernel, out_shape=outs, in_specs=[VMEM] * count + [pl.Bloc...  10.9 us
    ppermute x11, starting transfers between devices, swap(): return lax.ppermute(x, 'seq', [(i, i ^ distance) for i in range(size)])  9.77 us
    ppermute x3, starting transfers between devices, z_routed(): lax.ppermute(part, 'seq', [(i, i ^ QUAD * slot[i % 2]) for i in range(siz...  3.55 us
  transfers between devices with their start and end apart: 14, of which 9 were waited for; matrix products, arithmetic and copies ran while one was open for 0% of the time, Pallas kernels for 5%

profile of v6, /device:TPU:0, one launch (start us, length us, event | category | flops | bytes accessed | tf_op | source)
XLA Modules:
  0.0 73.6 jit_solution(13731162508739602021)
XLA Ops:
  0.0 0.7 copy-done.4
  1.2 3.0 %collective-permute-start.6 = (bf16[256,512]{1,0:T(8,128)(2,1)S(1)}, bf16[256,512]{1,0:T(8,128)(2,1)S(1)}, u32[]{:S(2)}, u32[]{:S(2)}) collective-permute-start(bf16[256,512]{1,0:T(8,128)(2,1)S(1)} %get-tuple-element.27), channel_id=1, source_target_pairs={{0,2},{1,3},{2,0},{3,1},{4,6},{5,7},{6,4},{7,5},{8,10},{9,11},{10,... | collective-permute-start | bytes 786440 | tf_op jit(solution)/shard_map/ppermute | solution.py:53
  4.2 1.6 %collective-permute-start = (bf16[208,128]{1,0:T(8,128)(2,1)S(1)}, bf16[208,128]{1,0:T(8,128)(2,1)S(1)}, u32[]{:S(2)}, u32[]{:S(2)}) collective-permute-start(bf16[208,128]{1,0:T(8,128)(2,1)S(1)} %get-tuple-element.24), channel_id=1, source_target_pairs={{0,4},{1,5},{2,6},{3,7},{4,0},{5,1},{6,2},{7,3},{8,12},{9,13},{10,... | collective-permute-start | bytes 159752 | tf_op jit(solution)/shard_map/ppermute | solution.py:53
  5.8 2.6 %collective-permute-start.1 = (bf16[208,128]{1,0:T(8,128)(2,1)S(1)}, bf16[208,128]{1,0:T(8,128)(2,1)S(1)}, u32[]{:S(2)}, u32[]{:S(2)}) collective-permute-start(bf16[208,128]{1,0:T(8,128)(2,1)S(1)} %get-tuple-element.25), channel_id=1, source_target_pairs={{0,8},{1,9},{2,10},{3,11},{4,12},{5,13},{6,14},{7,15},{8,0},{9,1},... | collective-permute-start | bytes 159752 | tf_op jit(solution)/shard_map/ppermute | solution.py:53
  8.6 3.0 %collective-permute-done.1.refs_2_ = bf16[208,128]{1,0:T(8,128)(2,1)S(1)} collective-permute-done((bf16[208,128]{1,0:T(8,128)(2,1)S(1)}, bf16[208,128]{1,0:T(8,128)(2,1)S(1)}, u32[]{:S(2)}, u32[]{:S(2)}) %collective-permute-start.1) | collective-permute-done | bytes 53280 | tf_op jit(solution)/shard_map/ppermute | solution.py:53
  11.6 2.7 %collective-permute-done.2.refs_3_ = bf16[208,128]{1,0:T(8,128)(2,1)S(1)} collective-permute-done((bf16[208,128]{1,0:T(8,128)(2,1)S(1)}, bf16[208,128]{1,0:T(8,128)(2,1)S(1)}, u32[]{:S(2)}, u32[]{:S(2)}) %collective-permute-start.2) | collective-permute-done | bytes 53280 | tf_op jit(solution)/shard_map/ppermute | solution.py:53
  14.7 1.8 %collective-permute-start.8 = (bf16[384,128]{1,0:T(8,128)(2,1)S(1)}, bf16[384,128]{1,0:T(8,128)(2,1)S(1)}, u32[]{:S(2)}, u32[]{:S(2)}) collective-permute-start(bf16[384,128]{1,0:T(8,128)(2,1)S(1)} %get-tuple-element.30), channel_id=1, source_target_pairs={{0,12},{1,9},{2,14},{3,11},{4,8},{5,13},{6,10},{7,15},{8,4},{9,1},... | collective-permute-start | bytes 294920 | tf_op jit(solution)/shard_map/ppermute | solution.py:330
  16.5 1.6 %collective-permute-start.9 = (bf16[384,128]{1,0:T(8,128)(2,1)S(1)}, bf16[384,128]{1,0:T(8,128)(2,1)S(1)}, u32[]{:S(2)}, u32[]{:S(2)}) collective-permute-start(bf16[384,128]{1,0:T(8,128)(2,1)S(1)} %get-tuple-element.31), channel_id=1, source_target_pairs={{0,8},{1,5},{2,10},{3,7},{4,12},{5,1},{6,14},{7,3},{8,0},{9,13},{1... | collective-permute-start | bytes 294920 | tf_op jit(solution)/shard_map/ppermute | solution.py:330
  18.7 1.4 %collective-permute-start.5 = (bf16[16,2560]{1,0:T(8,128)(2,1)S(1)}, bf16[16,2560]{1,0:T(8,128)(2,1)S(1)}, u32[]{:S(2)}, u32[]{:S(2)}) collective-permute-start(bf16[16,2560]{1,0:T(8,128)(2,1)S(1)} %shard_map.102.refs_0_.refs_2_), channel_id=1, source_target_pairs={{0,3},{1,2},{2,1},{3,0},{4,7},{5,6},{6,5},{7,4},{8,11},{9,10},{10,... | collective-permute-start | bytes 245768 | tf_op jit(solution)/shard_map/ppermute | solution.py:53
  20.1 3.3 %collective-permute-done.4.refs_2_.refs_3_ = bf16[16,2560]{1,0:T(8,128)(2,1)S(1)} collective-permute-done((bf16[16,2560]{1,0:T(8,128)(2,1)S(1)}, bf16[16,2560]{1,0:T(8,128)(2,1)S(1)}, u32[]{:S(2)}, u32[]{:S(2)}) %collective-permute-start.4) | collective-permute-done | bytes 81952 | tf_op jit(solution)/shard_map/ppermute | solution.py:53
  23.4 1.1 %collective-permute-done.5.refs_3_.refs_6_ = bf16[16,2560]{1,0:T(8,128)(2,1)S(1)} collective-permute-done((bf16[16,2560]{1,0:T(8,128)(2,1)S(1)}, bf16[16,2560]{1,0:T(8,128)(2,1)S(1)}, u32[]{:S(2)}, u32[]{:S(2)}) %collective-permute-start.5) | collective-permute-done | bytes 81952 | tf_op jit(solution)/shard_map/ppermute | solution.py:53
  24.5 1.3 %shard_map.103.refs_8_.refs_0_ = bf16[16,512]{1,0:T(8,128)(2,1)S(1)} custom-call(bf16[16,2560]{1,0:T(8,128)(2,1)S(1)} %shard_map.102.refs_0_.refs_2_, bf16[16,2560]{1,0:T(8,128)(2,1)S(1)} %collective-permute-done.3.refs_1_.refs_5_, bf16[16,2560]{1,0:T(8,128)(2,1)S(1)} %collective-permute-done.4.refs_2_.refs_3_, ...), custom_call_target="tpu_custom_call" | custom-call | tf_op jit(solution)/shard_map/pallas_call | solution.py:30
  25.8 0.6 collective-permute-done.9.refs_7_
  27.1 1.4 %collective-permute-done.10.refs_4_ = bf16[2048,128]{1,0:T(8,128)(2,1)S(1)} collective-permute-done((bf16[2048,128]{1,0:T(8,128)(2,1)S(1)}, bf16[2048,128]{1,0:T(8,128)(2,1)S(1)}, u32[]{:S(2)}, u32[]{:S(2)}) %collective-permute-start.10) | collective-permute-done | bytes 524320 | tf_op jit(solution)/shard_map/ppermute | solution.py:53
  28.5 1.2 %shard_map.107 = (bf16[16,512]{1,0:T(8,128)(2,1)S(1)}, f32[8,16,512]{2,1,0:T(8,128)S(1)}) custom-call(bf16[16,512]{1,0:T(8,128)(2,1)S(1)} %shard_map.103.refs_8_.refs_0_, f32[64,128]{1,0:T(8,128)S(1)} %get-tuple-element.32.refs_1_, f32[64,128]{1,0:T(8,128)S(1)} %get-tuple-element.33.refs_2_, f32[64,128]{1,0:T(8,128)S(1)} %get-tuple-element.34.refs_3_, ...), custom_call_target="tpu_custom_call" | custom-call | tf_op jit(solution)/shard_map/pallas_call | solution.py:30
  29.9 0.6 shard_map.108.refs_0_
  30.5 0.8 %collective-permute-done.11.refs_1_ = f32[8,16,512]{2,1,0:T(8,128)S(1)} collective-permute-done((f32[8,16,512]{2,1,0:T(8,128)S(1)}, f32[8,16,512]{2,1,0:T(8,128)S(1)}, u32[]{:S(2)}, u32[]{:S(2)}) %collective-permute-start.11) | collective-permute-done | bytes 262176 | tf_op jit(solution)/shard_map/ppermute | solution.py:53
  31.4 12.4 %all_to_all.15.refs_1_ = f32[8,16,512]{2,1,0:T(8,128)S(1)} all-to-all(f32[8,16,512]{2,1,0:T(8,128)S(1)} %shard_map.109), channel_id=1, replica_groups={{0,2,4,6,8,10,12,14},{1,3,5,7,9,11,13,15},{16,18,20,22,24,26,28,30},{17..., dimensions={0} | all-to-all | bytes 524288 | tf_op jit(solution)/shard_map/all_to_all | solution.py:157
  43.9 11.0 %all_to_all.16.refs_0_ = bf16[8,16,512]{2,1,0:T(8,128)(2,1)S(1)} all-to-all(bf16[8,16,512]{2,1,0:T(8,128)(2,1)S(1)} %get-tuple-element.38), channel_id=1, replica_groups={{0,2,4,6,8,10,12,14},{1,3,5,7,9,11,13,15},{16,18,20,22,24,26,28,30},{17..., dimensions={0} | all-to-all | bytes 262144 | tf_op jit(solution)/shard_map/all_to_all | solution.py:157
  54.9 1.3 %collective-permute-done.12.refs_1_ = bf16[8,16,512]{2,1,0:T(8,128)(2,1)S(1)} collective-permute-done((bf16[8,16,512]{2,1,0:T(8,128)(2,1)S(1)}, bf16[8,16,512]{2,1,0:T(8,128)(2,1)S(1)}, u32[]{:S(2)}, u32[]{:S(2)}) %collective-permute-start.12) | collective-permute-done | bytes 131104 | tf_op jit(solution)/shard_map/ppermute | solution.py:53
  56.3 5.1 %shard_map.111 = (bf16[16,896]{1,0:T(8,128)(2,1)S(1)}, f32[8,16,512]{2,1,0:T(8,128)S(1)}) custom-call(bf16[8,16,512]{2,1,0:T(8,128)(2,1)S(1)} %all_to_all.16.refs_0_, bf16[8,16,512]{2,1,0:T(8,128)(2,1)S(1)} %collective-permute-done.12.refs_1_, bf16[1,8192]{1,0:T(2,128)(2,1)S(1)} %reshape.7.refs_2_, bf16[8192,896]{1,0:T(8,128)(2,1)S(1)} %bitcast.6, ...), custom_call_target="tpu_custom_call" | custom-call | tf_op jit(solution)/shard_map/pallas_call | solution.py:30
  61.6 1.1 %shard_map.112.refs_0_ = f32[8,16,512]{2,1,0:T(8,128)S(1)} custom-call(bf16[16,896]{1,0:T(8,128)(2,1)S(1)} %get-tuple-element.39.refs_0_, bf16[896,8192]{1,0:T(8,128)(2,1)S(1)} %bitcast.2), custom_call_target="tpu_custom_call" | custom-call | tf_op jit(solution)/shard_map/pallas_call | solution.py:30
  63.0 10.0 %all_to_all.17.refs_1_ = bf16[8,16,512]{2,1,0:T(8,128)(2,1)S(1)} all-to-all(bf16[8,16,512]{2,1,0:T(8,128)(2,1)S(1)} %shard_map.113), channel_id=1, replica_groups={{0,2,4,6,8,10,12,14},{1,3,5,7,9,11,13,15},{16,18,20,22,24,26,28,30},{17..., dimensions={0} | all-to-all | bytes 262144 | tf_op jit(solution)/shard_map/all_to_all | solution.py:157
  73.0 0.6 shard_map.114
  (72 shorter events, 3.0 us)
Async XLA Ops:
  1.2 13.3 %collective-permute-start.6 = (bf16[256,512]{1,0:T(8,128)(2,1)S(1)}, bf16[256,512]{1,0:T(8,128)(2,1)S(1)}, u32[]{:S(2)}, u32[]{:S(2)}) collective-permute-start(bf16[256,512]{1,0:T(8,128)(2,1)S(1)} %get-tuple-element.27), channel_id=1, source_target_pairs={{0,2},{1,3},{2,0},{3,1},{4,6},{5,7},{6,4},{7,5},{8,10},{9,11},{10,... | collective-permute-start | bytes 786440 | tf_op jit(solution)/shard_map/ppermute | solution.py:53
  4.2 4.4 %collective-permute-start = (bf16[208,128]{1,0:T(8,128)(2,1)S(1)}, bf16[208,128]{1,0:T(8,128)(2,1)S(1)}, u32[]{:S(2)}, u32[]{:S(2)}) collective-permute-start(bf16[208,128]{1,0:T(8,128)(2,1)S(1)} %get-tuple-element.24), channel_id=1, source_target_pairs={{0,4},{1,5},{2,6},{3,7},{4,0},{5,1},{6,2},{7,3},{8,12},{9,13},{10,... | collective-permute-start | bytes 159752 | tf_op jit(solution)/shard_map/ppermute | solution.py:53
  5.8 5.8 %collective-permute-start.1 = (bf16[208,128]{1,0:T(8,128)(2,1)S(1)}, bf16[208,128]{1,0:T(8,128)(2,1)S(1)}, u32[]{:S(2)}, u32[]{:S(2)}) collective-permute-start(bf16[208,128]{1,0:T(8,128)(2,1)S(1)} %get-tuple-element.25), channel_id=1, source_target_pairs={{0,8},{1,9},{2,10},{3,11},{4,12},{5,13},{6,14},{7,15},{8,0},{9,1},... | collective-permute-start | bytes 159752 | tf_op jit(solution)/shard_map/ppermute | solution.py:53
  8.4 5.9 %collective-permute-start.2 = (bf16[208,128]{1,0:T(8,128)(2,1)S(1)}, bf16[208,128]{1,0:T(8,128)(2,1)S(1)}, u32[]{:S(2)}, u32[]{:S(2)}) collective-permute-start(bf16[208,128]{1,0:T(8,128)(2,1)S(1)} %get-tuple-element.26), channel_id=1, source_target_pairs={{0,12},{1,13},{2,14},{3,15},{4,8},{5,9},{6,10},{7,11},{8,4},{9,5},... | collective-permute-start | bytes 159752 | tf_op jit(solution)/shard_map/ppermute | solution.py:53
  14.3 14.1 %slice-start.4 = ((s8[8388608]{0:T(1024)(128)(4,1)}), s8[4194304]{0:T(1024)(128)(4,1)S(1)}, s32[]{:S(2)}) async-start(s8[8388608]{0:T(1024)(128)(4,1)} %bitcast.3), calls=%async_computation.7 | async-start | bytes 8388608
  14.4 4.3 %collective-permute-start.3 = (bf16[16,2560]{1,0:T(8,128)(2,1)S(1)}, bf16[16,2560]{1,0:T(8,128)(2,1)S(1)}, u32[]{:S(2)}, u32[]{:S(2)}) collective-permute-start(bf16[16,2560]{1,0:T(8,128)(2,1)S(1)} %shard_map.102.refs_0_.refs_2_), channel_id=1, source_target_pairs={{0,1},{1,0},{2,3},{3,2},{4,5},{5,4},{6,7},{7,6},{8,9},{9,8},{10,11... | collective-permute-start | bytes 245768 | tf_op jit(solution)/shard_map/ppermute | solution.py:53
  14.6 11.2 %collective-permute-start.7 = (bf16[384,128]{1,0:T(8,128)(2,1)S(1)}, bf16[384,128]{1,0:T(8,128)(2,1)S(1)}, u32[]{:S(2)}, u32[]{:S(2)}) collective-permute-start(bf16[384,128]{1,0:T(8,128)(2,1)S(1)} %get-tuple-element.29), channel_id=1, source_target_pairs={{0,4},{1,13},{2,6},{3,15},{4,0},{5,9},{6,2},{7,11},{8,12},{9,5},{1... | collective-permute-start | bytes 294920 | tf_op jit(solution)/shard_map/ppermute | solution.py:330
  14.7 11.1 %collective-permute-start.8 = (bf16[384,128]{1,0:T(8,128)(2,1)S(1)}, bf16[384,128]{1,0:T(8,128)(2,1)S(1)}, u32[]{:S(2)}, u32[]{:S(2)}) collective-permute-start(bf16[384,128]{1,0:T(8,128)(2,1)S(1)} %get-tuple-element.30), channel_id=1, source_target_pairs={{0,12},{1,9},{2,14},{3,11},{4,8},{5,13},{6,10},{7,15},{8,4},{9,1},... | collective-permute-start | bytes 294920 | tf_op jit(solution)/shard_map/ppermute | solution.py:330
  16.5 9.9 %collective-permute-start.9 = (bf16[384,128]{1,0:T(8,128)(2,1)S(1)}, bf16[384,128]{1,0:T(8,128)(2,1)S(1)}, u32[]{:S(2)}, u32[]{:S(2)}) collective-permute-start(bf16[384,128]{1,0:T(8,128)(2,1)S(1)} %get-tuple-element.31), channel_id=1, source_target_pairs={{0,8},{1,5},{2,10},{3,7},{4,12},{5,1},{6,14},{7,3},{8,0},{9,13},{1... | collective-permute-start | bytes 294920 | tf_op jit(solution)/shard_map/ppermute | solution.py:330
  18.1 5.2 %collective-permute-start.4 = (bf16[16,2560]{1,0:T(8,128)(2,1)S(1)}, bf16[16,2560]{1,0:T(8,128)(2,1)S(1)}, u32[]{:S(2)}, u32[]{:S(2)}) collective-permute-start(bf16[16,2560]{1,0:T(8,128)(2,1)S(1)} %shard_map.102.refs_0_.refs_2_), channel_id=1, source_target_pairs={{0,2},{1,3},{2,0},{3,1},{4,6},{5,7},{6,4},{7,5},{8,10},{9,11},{10,... | collective-permute-start | bytes 245768 | tf_op jit(solution)/shard_map/ppermute | solution.py:53
  18.7 5.8 %collective-permute-start.5 = (bf16[16,2560]{1,0:T(8,128)(2,1)S(1)}, bf16[16,2560]{1,0:T(8,128)(2,1)S(1)}, u32[]{:S(2)}, u32[]{:S(2)}) collective-permute-start(bf16[16,2560]{1,0:T(8,128)(2,1)S(1)} %shard_map.102.refs_0_.refs_2_), channel_id=1, source_target_pairs={{0,3},{1,2},{2,1},{3,0},{4,7},{5,6},{6,5},{7,4},{8,11},{9,10},{10,... | collective-permute-start | bytes 245768 | tf_op jit(solution)/shard_map/ppermute | solution.py:53
  26.5 2.0 %collective-permute-start.10 = (bf16[2048,128]{1,0:T(8,128)(2,1)S(1)}, bf16[2048,128]{1,0:T(8,128)(2,1)S(1)}, u32[]{:S(2)}, u32[]{:S(2)}) collective-permute-start(bf16[2048,128]{1,0:T(8,128)(2,1)S(1)} %shard_map.105.refs_1_), channel_id=1, source_target_pairs={{0,1},{1,0},{2,3},{3,2},{4,5},{5,4},{6,7},{7,6},{8,9},{9,8},{10,11... | collective-permute-start | bytes 1572872 | tf_op jit(solution)/shard_map/ppermute | solution.py:53
  29.7 1.5 %collective-permute-start.11 = (f32[8,16,512]{2,1,0:T(8,128)S(1)}, f32[8,16,512]{2,1,0:T(8,128)S(1)}, u32[]{:S(2)}, u32[]{:S(2)}) collective-permute-start(f32[8,16,512]{2,1,0:T(8,128)S(1)} %get-tuple-element.36), channel_id=1, source_target_pairs={{0,1},{1,0},{2,3},{3,2},{4,5},{5,4},{6,7},{7,6},{8,9},{9,8},{10,11... | collective-permute-start | bytes 786440 | tf_op jit(solution)/shard_map/ppermute | solution.py:53
  31.3 24.9 %slice-start = ((s8[14680064]{0:T(1024)(128)(4,1)}), s8[4194304]{0:T(1024)(128)(4,1)S(1)}, s32[]{:S(2)}) async-start(s8[14680064]{0:T(1024)(128)(4,1)} %bitcast.1), calls=%async_computation.3 | async-start | bytes 8388608
  31.3 24.9 %slice-start.1 = ((s8[14680064]{0:T(1024)(128)(4,1)}), s8[4194304]{0:T(1024)(128)(4,1)S(1)}, s32[]{:S(2)}) async-start(s8[14680064]{0:T(1024)(128)(4,1)} %bitcast.1), calls=%async_computation.4 | async-start | bytes 8388608
  31.3 24.9 %slice-start.6 = ((s8[14680064]{0:T(1024)(128)(4,1)}), s8[4194304]{0:T(1024)(128)(4,1)S(1)}, s32[]{:S(2)}) async-start(s8[14680064]{0:T(1024)(128)(4,1)} %bitcast.5), calls=%async_computation.9 | async-start | bytes 8388608
  31.3 24.9 %slice-start.7 = ((s8[14680064]{0:T(1024)(128)(4,1)}), s8[4194304]{0:T(1024)(128)(4,1)S(1)}, s32[]{:S(2)}) async-start(s8[14680064]{0:T(1024)(128)(4,1)} %bitcast.5), calls=%async_computation.10 | async-start | bytes 8388608
  31.3 24.9 %slice-start.10 = ((s8[14680064]{0:T(1024)(128)(4,1)}), s8[4194304]{0:T(1024)(128)(4,1)S(1)}, s32[]{:S(2)}) async-start(s8[14680064]{0:T(1024)(128)(4,1)} %bitcast.7), calls=%async_computation.13 | async-start | bytes 8388608
  31.3 24.9 %slice-start.11 = ((s8[14680064]{0:T(1024)(128)(4,1)}), s8[4194304]{0:T(1024)(128)(4,1)S(1)}, s32[]{:S(2)}) async-start(s8[14680064]{0:T(1024)(128)(4,1)} %bitcast.7), calls=%async_computation.14 | async-start | bytes 8388608
  31.3 24.9 %slice-start.2 = ((s8[14680064]{0:T(1024)(128)(4,1)}), s8[4194304]{0:T(1024)(128)(4,1)S(1)}, s32[]{:S(2)}) async-start(s8[14680064]{0:T(1024)(128)(4,1)} %bitcast.1), calls=%async_computation.5 | async-start | bytes 8388608
  31.4 24.9 %slice-start.8 = ((s8[14680064]{0:T(1024)(128)(4,1)}), s8[4194304]{0:T(1024)(128)(4,1)S(1)}, s32[]{:S(2)}) async-start(s8[14680064]{0:T(1024)(128)(4,1)} %bitcast.5), calls=%async_computation.11 | async-start | bytes 8388608
  31.4 24.9 %slice-start.12 = ((s8[14680064]{0:T(1024)(128)(4,1)}), s8[4194304]{0:T(1024)(128)(4,1)S(1)}, s32[]{:S(2)}) async-start(s8[14680064]{0:T(1024)(128)(4,1)} %bitcast.7), calls=%async_computation.15 | async-start | bytes 8388608
  54.8 1.3 %collective-permute-start.12 = (bf16[8,16,512]{2,1,0:T(8,128)(2,1)S(1)}, bf16[8,16,512]{2,1,0:T(8,128)(2,1)S(1)}, u32[]{:S(2)}, u32[]{:S(2)}) collective-permute-start(bf16[8,16,512]{2,1,0:T(8,128)(2,1)S(1)} %all_to_all.16.refs_0_), channel_id=1, source_target_pairs={{0,1},{1,0},{2,3},{3,2},{4,5},{5,4},{6,7},{7,6},{8,9},{9,8},{10,11... | collective-permute-start | bytes 393224 | tf_op jit(solution)/shard_map/ppermute | solution.py:53
  61.4 1.5 %collective-permute-start.13 = (f32[8,16,512]{2,1,0:T(8,128)S(1)}, f32[8,16,512]{2,1,0:T(8,128)S(1)}, u32[]{:S(2)}, u32[]{:S(2)}) collective-permute-start(f32[8,16,512]{2,1,0:T(8,128)S(1)} %get-tuple-element.40), channel_id=1, source_target_pairs={{0,1},{1,0},{2,3},{3,2},{4,5},{5,4},{6,7},{7,6},{8,9},{9,8},{10,11... | collective-permute-start | bytes 786440 | tf_op jit(solution)/shard_map/ppermute | solution.py:53
  (11 other events, 91.0 us)

commit v7 on v6

--- a/solution.py
+++ b/solution.py
@@ -12,6 +12,8 @@
 HEAD_DIM = 128
 BLOCK = 128
 QUAD = 4
+RANGE = 32000.0
+STEPS = 256.0
 
 eps = 1e-05
 floor_score = -1e30
@@ -306,10 +308,32 @@
     out_ref[...] = (own_ref[...] + recv_ref[...]).astype(out_ref.dtype)
 
 
+def code_kernel(own_ref, recv_ref, out_ref):
+    members, rows, wide = own_ref.shape
+    sums = [own_ref[i] + recv_ref[i] for i in range(members)]
+    largest = functools.reduce(jnp.maximum, [jnp.max(jnp.abs(s), axis=1, keepdims=True) for s in sums])
+    level = jnp.ceil(jnp.log(jnp.maximum(largest, 1e-30)) * STEPS)
+    scale = jnp.exp(level * (-1.0 / STEPS)) * RANGE
+    level = jnp.broadcast_to(level, (rows, HEAD_DIM)).astype(jnp.int32).astype(jnp.int16)
+    for i, s in enumerate(sums):
+        out_ref[i, :, 0:wide] = jnp.round(s * scale).astype(jnp.int32).astype(jnp.int16)
+        out_ref[i, :, wide:] = level
+
+
+def decoded(ref, i, wide):
+    level = ref[i, :, wide:].astype(jnp.int32).astype(f32)[:, 0:1]
+    scale = jnp.exp(level * (1.0 / STEPS)) * (1.0 / RANGE)
+    return ref[i, :, 0:wide].astype(jnp.int32).astype(f32) * scale
+
+
 def final_kernel(base_ref, parts_ref, *out_refs):
-    total = parts_ref[0].astype(f32)
+    wide = base_ref.shape[1]
+    load = lambda i: parts_ref[i].astype(f32)
+    if parts_ref.dtype == jnp.int16:
+        load = lambda i: decoded(parts_ref, i, wide)
+    total = load(0)
     for i in range(1, parts_ref.shape[0]):
-        total = total + parts_ref[i].astype(f32)
+        total = total + load(i)
     total = (base_ref[...].astype(f32) + total).astype(bf16)
     for out in out_refs:
         if len(out.shape) == 3:
@@ -340,7 +364,11 @@
 def scattered(base, send, left, weight, wide, kind, outs, beside=()):
     far = swap(send, 1)
     own = call(functools.partial(keep_kernel, wide), like(send.shape, f32), [left, weight])
-    sums = call(add_kernel, like(send.shape, kind), [own, far], beside)
+    if kind == jnp.int16:
+        members, rows, _ = send.shape
+        sums = call(code_kernel, like((members, rows, wide + HEAD_DIM), kind), [own, far], beside)
+    else:
+        sums = call(add_kernel, like(send.shape, kind), [own, far], beside)
     return call(final_kernel, outs, [base, to_members(sums)], beside)
 
 
@@ -399,7 +427,7 @@
         [queries, *early, far_cache, *x_parts[1::2], o_weight],
     )
     stream, copies = scattered(
-        x_rows, send, left, o_weight, wide, f32, [own_columns, like(partial_sums.shape, bf16)], beside
+        x_rows, send, left, o_weight, wide, jnp.int16, [own_columns, like(partial_sums.shape, bf16)], beside
     )
     parts = to_members(copies)
     left, send = call(

time: 73.9 us -> 72 us (0.974)
  blocking collectives: 33.4 us -> 31.3 us
    all_to_all x3, blocking collectives: 33.4 us -> 31.3 us  [to_members(): lax.all_to_all(parts, 'seq', 0, 0, axis_index_groups=groups, tiled=True)]
where the time goes in v7:
time: 72 us; the launch traced here: 71.7 us
  blocking collectives  31.3 us (43%)
  waiting for transfers between devices  14.5 us (20%)
  starting transfers between devices  13.3 us (18%)
  Pallas kernels  11.1 us (15%)
  local copies, waits for them, and re-layouts  1.2 us (2%)
    all_to_all x3, blocking collectives, to_members(): lax.all_to_all(parts, 'seq', 0, 0, axis_index_groups=groups, tiled=True)  31.3 us
    ppermute x11, waiting for transfers between devices, swap(): return lax.ppermute(x, 'seq', [(i, i ^ distance) for i in range(size)])  13.9 us
    pallas_call x14, Pallas kernels, call(): pl.pallas_call(kernel, out_shape=outs, in_specs=[VMEM] * count + [pl.Bloc...  11.1 us
    ppermute x11, starting transfers between devices, swap(): return lax.ppermute(x, 'seq', [(i, i ^ distance) for i in range(size)])  9.77 us
    ppermute x3, starting transfers between devices, z_routed(): lax.ppermute(part, 'seq', [(i, i ^ QUAD * slot[i % 2]) for i in range(siz...  3.55 us
  transfers between devices with their start and end apart: 14, of which 9 were waited for; matrix products, arithmetic and copies ran while one was open for 0% of the time, Pallas kernels for 5%

profile of v7, /device:TPU:0, one launch (start us, length us, event | category | flops | bytes accessed | tf_op | source)
XLA Modules:
  0.0 71.7 jit_solution(6954250930659832)
XLA Ops:
  0.0 0.7 copy-done.4
  1.2 3.0 %collective-permute-start.6 = (bf16[256,512]{1,0:T(8,128)(2,1)S(1)}, bf16[256,512]{1,0:T(8,128)(2,1)S(1)}, u32[]{:S(2)}, u32[]{:S(2)}) collective-permute-start(bf16[256,512]{1,0:T(8,128)(2,1)S(1)} %get-tuple-element.27), channel_id=1, source_target_pairs={{0,2},{1,3},{2,0},{3,1},{4,6},{5,7},{6,4},{7,5},{8,10},{9,11},{10,... | collective-permute-start | bytes 786440 | tf_op jit(solution)/shard_map/ppermute | solution.py:55
  4.2 1.6 %collective-permute-start = (bf16[208,128]{1,0:T(8,128)(2,1)S(1)}, bf16[208,128]{1,0:T(8,128)(2,1)S(1)}, u32[]{:S(2)}, u32[]{:S(2)}) collective-permute-start(bf16[208,128]{1,0:T(8,128)(2,1)S(1)} %get-tuple-element.24), channel_id=1, source_target_pairs={{0,4},{1,5},{2,6},{3,7},{4,0},{5,1},{6,2},{7,3},{8,12},{9,13},{10,... | collective-permute-start | bytes 159752 | tf_op jit(solution)/shard_map/ppermute | solution.py:55
  5.8 2.6 %collective-permute-start.1 = (bf16[208,128]{1,0:T(8,128)(2,1)S(1)}, bf16[208,128]{1,0:T(8,128)(2,1)S(1)}, u32[]{:S(2)}, u32[]{:S(2)}) collective-permute-start(bf16[208,128]{1,0:T(8,128)(2,1)S(1)} %get-tuple-element.25), channel_id=1, source_target_pairs={{0,8},{1,9},{2,10},{3,11},{4,12},{5,13},{6,14},{7,15},{8,0},{9,1},... | collective-permute-start | bytes 159752 | tf_op jit(solution)/shard_map/ppermute | solution.py:55
  8.6 3.0 %collective-permute-done.1.refs_2_ = bf16[208,128]{1,0:T(8,128)(2,1)S(1)} collective-permute-done((bf16[208,128]{1,0:T(8,128)(2,1)S(1)}, bf16[208,128]{1,0:T(8,128)(2,1)S(1)}, u32[]{:S(2)}, u32[]{:S(2)}) %collective-permute-start.1) | collective-permute-done | bytes 53280 | tf_op jit(solution)/shard_map/ppermute | solution.py:55
  11.6 2.7 %collective-permute-done.2.refs_3_ = bf16[208,128]{1,0:T(8,128)(2,1)S(1)} collective-permute-done((bf16[208,128]{1,0:T(8,128)(2,1)S(1)}, bf16[208,128]{1,0:T(8,128)(2,1)S(1)}, u32[]{:S(2)}, u32[]{:S(2)}) %collective-permute-start.2) | collective-permute-done | bytes 53280 | tf_op jit(solution)/shard_map/ppermute | solution.py:55
  14.7 1.8 %collective-permute-start.8 = (bf16[384,128]{1,0:T(8,128)(2,1)S(1)}, bf16[384,128]{1,0:T(8,128)(2,1)S(1)}, u32[]{:S(2)}, u32[]{:S(2)}) collective-permute-start(bf16[384,128]{1,0:T(8,128)(2,1)S(1)} %get-tuple-element.30), channel_id=1, source_target_pairs={{0,12},{1,9},{2,14},{3,11},{4,8},{5,13},{6,10},{7,15},{8,4},{9,1},... | collective-permute-start | bytes 294920 | tf_op jit(solution)/shard_map/ppermute | solution.py:354
  16.5 1.6 %collective-permute-start.9 = (bf16[384,128]{1,0:T(8,128)(2,1)S(1)}, bf16[384,128]{1,0:T(8,128)(2,1)S(1)}, u32[]{:S(2)}, u32[]{:S(2)}) collective-permute-start(bf16[384,128]{1,0:T(8,128)(2,1)S(1)} %get-tuple-element.31), channel_id=1, source_target_pairs={{0,8},{1,5},{2,10},{3,7},{4,12},{5,1},{6,14},{7,3},{8,0},{9,13},{1... | collective-permute-start | bytes 294920 | tf_op jit(solution)/shard_map/ppermute | solution.py:354
  18.7 1.4 %collective-permute-start.5 = (bf16[16,2560]{1,0:T(8,128)(2,1)S(1)}, bf16[16,2560]{1,0:T(8,128)(2,1)S(1)}, u32[]{:S(2)}, u32[]{:S(2)}) collective-permute-start(bf16[16,2560]{1,0:T(8,128)(2,1)S(1)} %shard_map.102.refs_0_.refs_2_), channel_id=1, source_target_pairs={{0,3},{1,2},{2,1},{3,0},{4,7},{5,6},{6,5},{7,4},{8,11},{9,10},{10,... | collective-permute-start | bytes 245768 | tf_op jit(solution)/shard_map/ppermute | solution.py:55
  20.1 3.3 %collective-permute-done.4.refs_2_.refs_3_ = bf16[16,2560]{1,0:T(8,128)(2,1)S(1)} collective-permute-done((bf16[16,2560]{1,0:T(8,128)(2,1)S(1)}, bf16[16,2560]{1,0:T(8,128)(2,1)S(1)}, u32[]{:S(2)}, u32[]{:S(2)}) %collective-permute-start.4) | collective-permute-done | bytes 81952 | tf_op jit(solution)/shard_map/ppermute | solution.py:55
  23.4 1.1 %collective-permute-done.5.refs_3_.refs_6_ = bf16[16,2560]{1,0:T(8,128)(2,1)S(1)} collective-permute-done((bf16[16,2560]{1,0:T(8,128)(2,1)S(1)}, bf16[16,2560]{1,0:T(8,128)(2,1)S(1)}, u32[]{:S(2)}, u32[]{:S(2)}) %collective-permute-start.5) | collective-permute-done | bytes 81952 | tf_op jit(solution)/shard_map/ppermute | solution.py:55
  24.5 1.3 %shard_map.103.refs_8_.refs_0_ = bf16[16,512]{1,0:T(8,128)(2,1)S(1)} custom-call(bf16[16,2560]{1,0:T(8,128)(2,1)S(1)} %shard_map.102.refs_0_.refs_2_, bf16[16,2560]{1,0:T(8,128)(2,1)S(1)} %collective-permute-done.3.refs_1_.refs_5_, bf16[16,2560]{1,0:T(8,128)(2,1)S(1)} %collective-permute-done.4.refs_2_.refs_3_, ...), custom_call_target="tpu_custom_call" | custom-call | tf_op jit(solution)/shard_map/pallas_call | solution.py:32
  25.8 0.6 collective-permute-done.9.refs_7_
  27.1 1.4 %collective-permute-done.10.refs_4_ = bf16[2048,128]{1,0:T(8,128)(2,1)S(1)} collective-permute-done((bf16[2048,128]{1,0:T(8,128)(2,1)S(1)}, bf16[2048,128]{1,0:T(8,128)(2,1)S(1)}, u32[]{:S(2)}, u32[]{:S(2)}) %collective-permute-start.10) | collective-permute-done | bytes 524320 | tf_op jit(solution)/shard_map/ppermute | solution.py:55
  28.5 1.2 %shard_map.107 = (bf16[16,512]{1,0:T(8,128)(2,1)S(1)}, f32[8,16,512]{2,1,0:T(8,128)S(1)}) custom-call(bf16[16,512]{1,0:T(8,128)(2,1)S(1)} %shard_map.103.refs_8_.refs_0_, f32[64,128]{1,0:T(8,128)S(1)} %get-tuple-element.32.refs_1_, f32[64,128]{1,0:T(8,128)S(1)} %get-tuple-element.33.refs_2_, f32[64,128]{1,0:T(8,128)S(1)} %get-tuple-element.34.refs_3_, ...), custom_call_target="tpu_custom_call" | custom-call | tf_op jit(solution)/shard_map/pallas_call | solution.py:32
  29.9 0.6 shard_map.108.refs_0_
  30.5 0.8 %collective-permute-done.11.refs_1_ = f32[8,16,512]{2,1,0:T(8,128)S(1)} collective-permute-done((f32[8,16,512]{2,1,0:T(8,128)S(1)}, f32[8,16,512]{2,1,0:T(8,128)S(1)}, u32[]{:S(2)}, u32[]{:S(2)}) %collective-permute-start.11) | collective-permute-done | bytes 262176 | tf_op jit(solution)/shard_map/ppermute | solution.py:55
  31.5 11.0 %all_to_all.15.refs_1_ = s16[8,16,640]{2,1,0:T(8,128)(2,1)S(1)} all-to-all(s16[8,16,640]{2,1,0:T(8,128)(2,1)S(1)} %shard_map.109), channel_id=1, replica_groups={{0,2,4,6,8,10,12,14},{1,3,5,7,9,11,13,15},{16,18,20,22,24,26,28,30},{17..., dimensions={0} | all-to-all | bytes 327680 | tf_op jit(solution)/shard_map/all_to_all | solution.py:159
  42.6 10.3 %all_to_all.16.refs_0_ = bf16[8,16,512]{2,1,0:T(8,128)(2,1)S(1)} all-to-all(bf16[8,16,512]{2,1,0:T(8,128)(2,1)S(1)} %get-tuple-element.38), channel_id=1, replica_groups={{0,2,4,6,8,10,12,14},{1,3,5,7,9,11,13,15},{16,18,20,22,24,26,28,30},{17..., dimensions={0} | all-to-all | bytes 262144 | tf_op jit(solution)/shard_map/all_to_all | solution.py:159
  52.9 1.3 %collective-permute-done.12.refs_1_ = bf16[8,16,512]{2,1,0:T(8,128)(2,1)S(1)} collective-permute-done((bf16[8,16,512]{2,1,0:T(8,128)(2,1)S(1)}, bf16[8,16,512]{2,1,0:T(8,128)(2,1)S(1)}, u32[]{:S(2)}, u32[]{:S(2)}) %collective-permute-start.12) | collective-permute-done | bytes 131104 | tf_op jit(solution)/shard_map/ppermute | solution.py:55
  54.4 5.1 %shard_map.111 = (bf16[16,896]{1,0:T(8,128)(2,1)S(1)}, f32[8,16,512]{2,1,0:T(8,128)S(1)}) custom-call(bf16[8,16,512]{2,1,0:T(8,128)(2,1)S(1)} %all_to_all.16.refs_0_, bf16[8,16,512]{2,1,0:T(8,128)(2,1)S(1)} %collective-permute-done.12.refs_1_, bf16[1,8192]{1,0:T(2,128)(2,1)S(1)} %reshape.7.refs_2_, bf16[8192,896]{1,0:T(8,128)(2,1)S(1)} %bitcast.6, ...), custom_call_target="tpu_custom_call" | custom-call | tf_op jit(solution)/shard_map/pallas_call | solution.py:32
  59.7 1.1 %shard_map.112.refs_0_ = f32[8,16,512]{2,1,0:T(8,128)S(1)} custom-call(bf16[16,896]{1,0:T(8,128)(2,1)S(1)} %get-tuple-element.39.refs_0_, bf16[896,8192]{1,0:T(8,128)(2,1)S(1)} %bitcast.2), custom_call_target="tpu_custom_call" | custom-call | tf_op jit(solution)/shard_map/pallas_call | solution.py:32
  61.1 10.0 %all_to_all.17.refs_1_ = bf16[8,16,512]{2,1,0:T(8,128)(2,1)S(1)} all-to-all(bf16[8,16,512]{2,1,0:T(8,128)(2,1)S(1)} %shard_map.113), channel_id=1, replica_groups={{0,2,4,6,8,10,12,14},{1,3,5,7,9,11,13,15},{16,18,20,22,24,26,28,30},{17..., dimensions={0} | all-to-all | bytes 262144 | tf_op jit(solution)/shard_map/all_to_all | solution.py:159
  71.1 0.6 shard_map.114
  (72 shorter events, 3.2 us)
Async XLA Ops:
  1.2 13.3 %collective-permute-start.6 = (bf16[256,512]{1,0:T(8,128)(2,1)S(1)}, bf16[256,512]{1,0:T(8,128)(2,1)S(1)}, u32[]{:S(2)}, u32[]{:S(2)}) collective-permute-start(bf16[256,512]{1,0:T(8,128)(2,1)S(1)} %get-tuple-element.27), channel_id=1, source_target_pairs={{0,2},{1,3},{2,0},{3,1},{4,6},{5,7},{6,4},{7,5},{8,10},{9,11},{10,... | collective-permute-start | bytes 786440 | tf_op jit(solution)/shard_map/ppermute | solution.py:55
  4.2 4.4 %collective-permute-start = (bf16[208,128]{1,0:T(8,128)(2,1)S(1)}, bf16[208,128]{1,0:T(8,128)(2,1)S(1)}, u32[]{:S(2)}, u32[]{:S(2)}) collective-permute-start(bf16[208,128]{1,0:T(8,128)(2,1)S(1)} %get-tuple-element.24), channel_id=1, source_target_pairs={{0,4},{1,5},{2,6},{3,7},{4,0},{5,1},{6,2},{7,3},{8,12},{9,13},{10,... | collective-permute-start | bytes 159752 | tf_op jit(solution)/shard_map/ppermute | solution.py:55
  5.8 5.8 %collective-permute-start.1 = (bf16[208,128]{1,0:T(8,128)(2,1)S(1)}, bf16[208,128]{1,0:T(8,128)(2,1)S(1)}, u32[]{:S(2)}, u32[]{:S(2)}) collective-permute-start(bf16[208,128]{1,0:T(8,128)(2,1)S(1)} %get-tuple-element.25), channel_id=1, source_target_pairs={{0,8},{1,9},{2,10},{3,11},{4,12},{5,13},{6,14},{7,15},{8,0},{9,1},... | collective-permute-start | bytes 159752 | tf_op jit(solution)/shard_map/ppermute | solution.py:55
  8.4 5.9 %collective-permute-start.2 = (bf16[208,128]{1,0:T(8,128)(2,1)S(1)}, bf16[208,128]{1,0:T(8,128)(2,1)S(1)}, u32[]{:S(2)}, u32[]{:S(2)}) collective-permute-start(bf16[208,128]{1,0:T(8,128)(2,1)S(1)} %get-tuple-element.26), channel_id=1, source_target_pairs={{0,12},{1,13},{2,14},{3,15},{4,8},{5,9},{6,10},{7,11},{8,4},{9,5},... | collective-permute-start | bytes 159752 | tf_op jit(solution)/shard_map/ppermute | solution.py:55
  14.3 14.1 %slice-start.4 = ((s8[8388608]{0:T(1024)(128)(4,1)}), s8[4194304]{0:T(1024)(128)(4,1)S(1)}, s32[]{:S(2)}) async-start(s8[8388608]{0:T(1024)(128)(4,1)} %bitcast.3), calls=%async_computation.7 | async-start | bytes 8388608
  14.4 4.3 %collective-permute-start.3 = (bf16[16,2560]{1,0:T(8,128)(2,1)S(1)}, bf16[16,2560]{1,0:T(8,128)(2,1)S(1)}, u32[]{:S(2)}, u32[]{:S(2)}) collective-permute-start(bf16[16,2560]{1,0:T(8,128)(2,1)S(1)} %shard_map.102.refs_0_.refs_2_), channel_id=1, source_target_pairs={{0,1},{1,0},{2,3},{3,2},{4,5},{5,4},{6,7},{7,6},{8,9},{9,8},{10,11... | collective-permute-start | bytes 245768 | tf_op jit(solution)/shard_map/ppermute | solution.py:55
  14.6 11.2 %collective-permute-start.7 = (bf16[384,128]{1,0:T(8,128)(2,1)S(1)}, bf16[384,128]{1,0:T(8,128)(2,1)S(1)}, u32[]{:S(2)}, u32[]{:S(2)}) collective-permute-start(bf16[384,128]{1,0:T(8,128)(2,1)S(1)} %get-tuple-element.29), channel_id=1, source_target_pairs={{0,4},{1,13},{2,6},{3,15},{4,0},{5,9},{6,2},{7,11},{8,12},{9,5},{1... | collective-permute-start | bytes 294920 | tf_op jit(solution)/shard_map/ppermute | solution.py:354
  14.7 11.1 %collective-permute-start.8 = (bf16[384,128]{1,0:T(8,128)(2,1)S(1)}, bf16[384,128]{1,0:T(8,128)(2,1)S(1)}, u32[]{:S(2)}, u32[]{:S(2)}) collective-permute-start(bf16[384,128]{1,0:T(8,128)(2,1)S(1)} %get-tuple-element.30), channel_id=1, source_target_pairs={{0,12},{1,9},{2,14},{3,11},{4,8},{5,13},{6,10},{7,15},{8,4},{9,1},... | collective-permute-start | bytes 294920 | tf_op jit(solution)/shard_map/ppermute | solution.py:354
  16.5 9.9 %collective-permute-start.9 = (bf16[384,128]{1,0:T(8,128)(2,1)S(1)}, bf16[384,128]{1,0:T(8,128)(2,1)S(1)}, u32[]{:S(2)}, u32[]{:S(2)}) collective-permute-start(bf16[384,128]{1,0:T(8,128)(2,1)S(1)} %get-tuple-element.31), channel_id=1, source_target_pairs={{0,8},{1,5},{2,10},{3,7},{4,12},{5,1},{6,14},{7,3},{8,0},{9,13},{1... | collective-permute-start | bytes 294920 | tf_op jit(solution)/shard_map/ppermute | solution.py:354
  18.1 5.2 %collective-permute-start.4 = (bf16[16,2560]{1,0:T(8,128)(2,1)S(1)}, bf16[16,2560]{1,0:T(8,128)(2,1)S(1)}, u32[]{:S(2)}, u32[]{:S(2)}) collective-permute-start(bf16[16,2560]{1,0:T(8,128)(2,1)S(1)} %shard_map.102.refs_0_.refs_2_), channel_id=1, source_target_pairs={{0,2},{1,3},{2,0},{3,1},{4,6},{5,7},{6,4},{7,5},{8,10},{9,11},{10,... | collective-permute-start | bytes 245768 | tf_op jit(solution)/shard_map/ppermute | solution.py:55
  18.7 5.8 %collective-permute-start.5 = (bf16[16,2560]{1,0:T(8,128)(2,1)S(1)}, bf16[16,2560]{1,0:T(8,128)(2,1)S(1)}, u32[]{:S(2)}, u32[]{:S(2)}) collective-permute-start(bf16[16,2560]{1,0:T(8,128)(2,1)S(1)} %shard_map.102.refs_0_.refs_2_), channel_id=1, source_target_pairs={{0,3},{1,2},{2,1},{3,0},{4,7},{5,6},{6,5},{7,4},{8,11},{9,10},{10,... | collective-permute-start | bytes 245768 | tf_op jit(solution)/shard_map/ppermute | solution.py:55
  26.5 2.0 %collective-permute-start.10 = (bf16[2048,128]{1,0:T(8,128)(2,1)S(1)}, bf16[2048,128]{1,0:T(8,128)(2,1)S(1)}, u32[]{:S(2)}, u32[]{:S(2)}) collective-permute-start(bf16[2048,128]{1,0:T(8,128)(2,1)S(1)} %shard_map.105.refs_1_), channel_id=1, source_target_pairs={{0,1},{1,0},{2,3},{3,2},{4,5},{5,4},{6,7},{7,6},{8,9},{9,8},{10,11... | collective-permute-start | bytes 1572872 | tf_op jit(solution)/shard_map/ppermute | solution.py:55
  29.7 1.5 %collective-permute-start.11 = (f32[8,16,512]{2,1,0:T(8,128)S(1)}, f32[8,16,512]{2,1,0:T(8,128)S(1)}, u32[]{:S(2)}, u32[]{:S(2)}) collective-permute-start(f32[8,16,512]{2,1,0:T(8,128)S(1)} %get-tuple-element.36), channel_id=1, source_target_pairs={{0,1},{1,0},{2,3},{3,2},{4,5},{5,4},{6,7},{7,6},{8,9},{9,8},{10,11... | collective-permute-start | bytes 786440 | tf_op jit(solution)/shard_map/ppermute | solution.py:55
  31.3 23.0 %slice-start = ((s8[14680064]{0:T(1024)(128)(4,1)}), s8[4194304]{0:T(1024)(128)(4,1)S(1)}, s32[]{:S(2)}) async-start(s8[14680064]{0:T(1024)(128)(4,1)} %bitcast.1), calls=%async_computation.3 | async-start | bytes 8388608
  31.3 23.0 %slice-start.1 = ((s8[14680064]{0:T(1024)(128)(4,1)}), s8[4194304]{0:T(1024)(128)(4,1)S(1)}, s32[]{:S(2)}) async-start(s8[14680064]{0:T(1024)(128)(4,1)} %bitcast.1), calls=%async_computation.4 | async-start | bytes 8388608
  31.3 23.0 %slice-start.6 = ((s8[14680064]{0:T(1024)(128)(4,1)}), s8[4194304]{0:T(1024)(128)(4,1)S(1)}, s32[]{:S(2)}) async-start(s8[14680064]{0:T(1024)(128)(4,1)} %bitcast.5), calls=%async_computation.9 | async-start | bytes 8388608
  31.3 23.0 %slice-start.7 = ((s8[14680064]{0:T(1024)(128)(4,1)}), s8[4194304]{0:T(1024)(128)(4,1)S(1)}, s32[]{:S(2)}) async-start(s8[14680064]{0:T(1024)(128)(4,1)} %bitcast.5), calls=%async_computation.10 | async-start | bytes 8388608
  31.3 23.0 %slice-start.10 = ((s8[14680064]{0:T(1024)(128)(4,1)}), s8[4194304]{0:T(1024)(128)(4,1)S(1)}, s32[]{:S(2)}) async-start(s8[14680064]{0:T(1024)(128)(4,1)} %bitcast.7), calls=%async_computation.13 | async-start | bytes 8388608
  31.3 23.0 %slice-start.11 = ((s8[14680064]{0:T(1024)(128)(4,1)}), s8[4194304]{0:T(1024)(128)(4,1)S(1)}, s32[]{:S(2)}) async-start(s8[14680064]{0:T(1024)(128)(4,1)} %bitcast.7), calls=%async_computation.14 | async-start | bytes 8388608
  31.5 22.9 %slice-start.2 = ((s8[14680064]{0:T(1024)(128)(4,1)}), s8[4194304]{0:T(1024)(128)(4,1)S(1)}, s32[]{:S(2)}) async-start(s8[14680064]{0:T(1024)(128)(4,1)} %bitcast.1), calls=%async_computation.5 | async-start | bytes 8388608
  31.5 22.8 %slice-start.8 = ((s8[14680064]{0:T(1024)(128)(4,1)}), s8[4194304]{0:T(1024)(128)(4,1)S(1)}, s32[]{:S(2)}) async-start(s8[14680064]{0:T(1024)(128)(4,1)} %bitcast.5), calls=%async_computation.11 | async-start | bytes 8388608
  31.5 22.8 %slice-start.12 = ((s8[14680064]{0:T(1024)(128)(4,1)}), s8[4194304]{0:T(1024)(128)(4,1)S(1)}, s32[]{:S(2)}) async-start(s8[14680064]{0:T(1024)(128)(4,1)} %bitcast.7), calls=%async_computation.15 | async-start | bytes 8388608
  52.9 1.3 %collective-permute-start.12 = (bf16[8,16,512]{2,1,0:T(8,128)(2,1)S(1)}, bf16[8,16,512]{2,1,0:T(8,128)(2,1)S(1)}, u32[]{:S(2)}, u32[]{:S(2)}) collective-permute-start(bf16[8,16,512]{2,1,0:T(8,128)(2,1)S(1)} %all_to_all.16.refs_0_), channel_id=1, source_target_pairs={{0,1},{1,0},{2,3},{3,2},{4,5},{5,4},{6,7},{7,6},{8,9},{9,8},{10,11... | collective-permute-start | bytes 393224 | tf_op jit(solution)/shard_map/ppermute | solution.py:55
  59.5 1.5 %collective-permute-start.13 = (f32[8,16,512]{2,1,0:T(8,128)S(1)}, f32[8,16,512]{2,1,0:T(8,128)S(1)}, u32[]{:S(2)}, u32[]{:S(2)}) collective-permute-start(f32[8,16,512]{2,1,0:T(8,128)S(1)} %get-tuple-element.40), channel_id=1, source_target_pairs={{0,1},{1,0},{2,3},{3,2},{4,5},{5,4},{6,7},{7,6},{8,9},{9,8},{10,11... | collective-permute-start | bytes 786440 | tf_op jit(solution)/shard_map/ppermute | solution.py:55
  (11 other events, 88.7 us)

commit v8 on v7

--- a/solution.py
+++ b/solution.py
@@ -357,7 +357,8 @@
 
 
 def near_gathered(line):
-    far, y, core = swap(line, 3), swap(line, 2), swap(line, 1)
+    y = swap(line, 2)
+    core, far = swap(line, 1), swap(y, 1)
     return [line, core, y, far]
 
 

time: 72 us -> 70.4 us (0.978)
  starting transfers between devices: 13.3 us -> 12.1 us
  waiting for transfers between devices: 14.5 us -> 13.7 us
    ppermute x11, waiting for transfers between devices: 13.9 us -> 10.8 us  [swap(): return lax.ppermute(x, 'seq', [(i, i ^ distance) for i in range(size)])]
    ppermute x3, waiting for transfers between devices: 0.64 us -> 2.89 us  [z_routed(): lax.ppermute(part, 'seq', [(i, i ^ QUAD * slot[i % 2]) for i in range(siz...]
    ppermute x11, starting transfers between devices: 9.77 us -> 8.59 us  [swap(): return lax.ppermute(x, 'seq', [(i, i ^ distance) for i in range(size)])]
  transfers between devices with their start and end apart: 14 -> 14, of which waited for: 9 -> 11; matrix products, arithmetic and copies ran while one was open for 0% -> 0% of each run, Pallas kernels for 5% -> 5%
where the time goes in v8:
time: 70.4 us; the launch traced here: 70.1 us
  blocking collectives  31.8 us (45%)
  waiting for transfers between devices  13.7 us (19%)
  starting transfers between devices  12.1 us (17%)
  Pallas kernels  11.1 us (16%)
  local copies, waits for them, and re-layouts  1.2 us (2%)
    all_to_all x3, blocking collectives, to_members(): lax.all_to_all(parts, 'seq', 0, 0, axis_index_groups=groups, tiled=True)  31.8 us
    pallas_call x14, Pallas kernels, call(): pl.pallas_call(kernel, out_shape=outs, in_specs=[VMEM] * count + [pl.Bloc...  11.1 us
    ppermute x11, waiting for transfers between devices, swap(): return lax.ppermute(x, 'seq', [(i, i ^ distance) for i in range(size)])  10.8 us
    ppermute x11, starting transfers between devices, swap(): return lax.ppermute(x, 'seq', [(i, i ^ distance) for i in range(size)])  8.59 us
    ppermute x3, starting transfers between devices, z_routed(): lax.ppermute(part, 'seq', [(i, i ^ QUAD * slot[i % 2]) for i in range(siz...  3.55 us
    ppermute x3, waiting for transfers between devices, z_routed(): lax.ppermute(part, 'seq', [(i, i ^ QUAD * slot[i % 2]) for i in range(siz...  2.89 us
  transfers between devices with their start and end apart: 14, of which 11 were waited for; matrix products, arithmetic and copies ran while one was open for 0% of the time, Pallas kernels for 5%

profile of v8, /device:TPU:0, one launch (start us, length us, event | category | flops | bytes accessed | tf_op | source)
XLA Modules:
  0.0 70.1 jit_solution(1141442610227754111)
XLA Ops:
  0.0 0.7 copy-done.4
  1.2 3.0 %collective-permute-start.6 = (bf16[256,512]{1,0:T(8,128)(2,1)S(1)}, bf16[256,512]{1,0:T(8,128)(2,1)S(1)}, u32[]{:S(2)}, u32[]{:S(2)}) collective-permute-start(bf16[256,512]{1,0:T(8,128)(2,1)S(1)} %get-tuple-element.27), channel_id=1, source_target_pairs={{0,2},{1,3},{2,0},{3,1},{4,6},{5,7},{6,4},{7,5},{8,10},{9,11},{10,... | collective-permute-start | bytes 786440 | tf_op jit(solution)/shard_map/ppermute | solution.py:55
  4.2 1.6 %collective-permute-start = (bf16[208,128]{1,0:T(8,128)(2,1)S(1)}, bf16[208,128]{1,0:T(8,128)(2,1)S(1)}, u32[]{:S(2)}, u32[]{:S(2)}) collective-permute-start(bf16[208,128]{1,0:T(8,128)(2,1)S(1)} %get-tuple-element.24), channel_id=1, source_target_pairs={{0,4},{1,5},{2,6},{3,7},{4,0},{5,1},{6,2},{7,3},{8,12},{9,13},{10,... | collective-permute-start | bytes 159752 | tf_op jit(solution)/shard_map/ppermute | solution.py:55
  5.8 2.6 %collective-permute-start.1 = (bf16[208,128]{1,0:T(8,128)(2,1)S(1)}, bf16[208,128]{1,0:T(8,128)(2,1)S(1)}, u32[]{:S(2)}, u32[]{:S(2)}) collective-permute-start(bf16[208,128]{1,0:T(8,128)(2,1)S(1)} %get-tuple-element.25), channel_id=1, source_target_pairs={{0,8},{1,9},{2,10},{3,11},{4,12},{5,13},{6,14},{7,15},{8,0},{9,1},... | collective-permute-start | bytes 159752 | tf_op jit(solution)/shard_map/ppermute | solution.py:55
  8.6 3.0 %collective-permute-done.1.refs_2_ = bf16[208,128]{1,0:T(8,128)(2,1)S(1)} collective-permute-done((bf16[208,128]{1,0:T(8,128)(2,1)S(1)}, bf16[208,128]{1,0:T(8,128)(2,1)S(1)}, u32[]{:S(2)}, u32[]{:S(2)}) %collective-permute-start.1) | collective-permute-done | bytes 53280 | tf_op jit(solution)/shard_map/ppermute | solution.py:55
  11.6 2.7 %collective-permute-done.2.refs_3_ = bf16[208,128]{1,0:T(8,128)(2,1)S(1)} collective-permute-done((bf16[208,128]{1,0:T(8,128)(2,1)S(1)}, bf16[208,128]{1,0:T(8,128)(2,1)S(1)}, u32[]{:S(2)}, u32[]{:S(2)}) %collective-permute-start.2) | collective-permute-done | bytes 53280 | tf_op jit(solution)/shard_map/ppermute | solution.py:55
  14.4 0.6 collective-permute-start.4
  15.1 1.8 %collective-permute-start.8 = (bf16[384,128]{1,0:T(8,128)(2,1)S(1)}, bf16[384,128]{1,0:T(8,128)(2,1)S(1)}, u32[]{:S(2)}, u32[]{:S(2)}) collective-permute-start(bf16[384,128]{1,0:T(8,128)(2,1)S(1)} %get-tuple-element.30), channel_id=1, source_target_pairs={{0,12},{1,9},{2,14},{3,11},{4,8},{5,13},{6,10},{7,15},{8,4},{9,1},... | collective-permute-start | bytes 294920 | tf_op jit(solution)/shard_map/ppermute | solution.py:354
  17.0 1.6 %collective-permute-start.9 = (bf16[384,128]{1,0:T(8,128)(2,1)S(1)}, bf16[384,128]{1,0:T(8,128)(2,1)S(1)}, u32[]{:S(2)}, u32[]{:S(2)}) collective-permute-start(bf16[384,128]{1,0:T(8,128)(2,1)S(1)} %get-tuple-element.31), channel_id=1, source_target_pairs={{0,8},{1,5},{2,10},{3,7},{4,12},{5,1},{6,14},{7,3},{8,0},{9,13},{1... | collective-permute-start | bytes 294920 | tf_op jit(solution)/shard_map/ppermute | solution.py:354
  19.2 0.7 %collective-permute-done.3.refs_1_.refs_5_ = bf16[16,2560]{1,0:T(8,128)(2,1)S(1)} collective-permute-done((bf16[16,2560]{1,0:T(8,128)(2,1)S(1)}, bf16[16,2560]{1,0:T(8,128)(2,1)S(1)}, u32[]{:S(2)}, u32[]{:S(2)}) %collective-permute-start.3) | collective-permute-done | bytes 81952 | tf_op jit(solution)/shard_map/ppermute | solution.py:55
  20.2 1.3 %shard_map.103.refs_8_.refs_0_ = bf16[16,512]{1,0:T(8,128)(2,1)S(1)} custom-call(bf16[16,2560]{1,0:T(8,128)(2,1)S(1)} %shard_map.102.refs_0_.refs_2_, bf16[16,2560]{1,0:T(8,128)(2,1)S(1)} %collective-permute-done.3.refs_1_.refs_5_, bf16[16,2560]{1,0:T(8,128)(2,1)S(1)} %collective-permute-done.4.refs_2_.refs_3_, ...), custom_call_target="tpu_custom_call" | custom-call | tf_op jit(solution)/shard_map/pallas_call | solution.py:32
  21.5 1.1 %collective-permute-done.8.refs_6_ = bf16[384,128]{1,0:T(8,128)(2,1)S(1)} collective-permute-done((bf16[384,128]{1,0:T(8,128)(2,1)S(1)}, bf16[384,128]{1,0:T(8,128)(2,1)S(1)}, u32[]{:S(2)}, u32[]{:S(2)}) %collective-permute-start.8) | collective-permute-done | bytes 98336 | tf_op jit(solution)/shard_map/ppermute | solution.py:354
  22.6 1.8 %collective-permute-done.9.refs_7_ = bf16[384,128]{1,0:T(8,128)(2,1)S(1)} collective-permute-done((bf16[384,128]{1,0:T(8,128)(2,1)S(1)}, bf16[384,128]{1,0:T(8,128)(2,1)S(1)}, u32[]{:S(2)}, u32[]{:S(2)}) %collective-permute-start.9) | collective-permute-done | bytes 98336 | tf_op jit(solution)/shard_map/ppermute | solution.py:354
  25.0 1.4 %collective-permute-done.10.refs_4_ = bf16[2048,128]{1,0:T(8,128)(2,1)S(1)} collective-permute-done((bf16[2048,128]{1,0:T(8,128)(2,1)S(1)}, bf16[2048,128]{1,0:T(8,128)(2,1)S(1)}, u32[]{:S(2)}, u32[]{:S(2)}) %collective-permute-start.10) | collective-permute-done | bytes 524320 | tf_op jit(solution)/shard_map/ppermute | solution.py:55
  26.4 1.2 %shard_map.107 = (bf16[16,512]{1,0:T(8,128)(2,1)S(1)}, f32[8,16,512]{2,1,0:T(8,128)S(1)}) custom-call(bf16[16,512]{1,0:T(8,128)(2,1)S(1)} %shard_map.103.refs_8_.refs_0_, f32[64,128]{1,0:T(8,128)S(1)} %get-tuple-element.32.refs_1_, f32[64,128]{1,0:T(8,128)S(1)} %get-tuple-element.33.refs_2_, f32[64,128]{1,0:T(8,128)S(1)} %get-tuple-element.34.refs_3_, ...), custom_call_target="tpu_custom_call" | custom-call | tf_op jit(solution)/shard_map/pallas_call | solution.py:32
  27.8 0.6 shard_map.108.refs_0_
  28.4 0.8 %collective-permute-done.11.refs_1_ = f32[8,16,512]{2,1,0:T(8,128)S(1)} collective-permute-done((f32[8,16,512]{2,1,0:T(8,128)S(1)}, f32[8,16,512]{2,1,0:T(8,128)S(1)}, u32[]{:S(2)}, u32[]{:S(2)}) %collective-permute-start.11) | collective-permute-done | bytes 262176 | tf_op jit(solution)/shard_map/ppermute | solution.py:55
  29.4 11.5 %all_to_all.15.refs_1_ = s16[8,16,640]{2,1,0:T(8,128)(2,1)S(1)} all-to-all(s16[8,16,640]{2,1,0:T(8,128)(2,1)S(1)} %shard_map.109), channel_id=1, replica_groups={{0,2,4,6,8,10,12,14},{1,3,5,7,9,11,13,15},{16,18,20,22,24,26,28,30},{17..., dimensions={0} | all-to-all | bytes 327680 | tf_op jit(solution)/shard_map/all_to_all | solution.py:159
  41.0 10.3 %all_to_all.16.refs_0_ = bf16[8,16,512]{2,1,0:T(8,128)(2,1)S(1)} all-to-all(bf16[8,16,512]{2,1,0:T(8,128)(2,1)S(1)} %get-tuple-element.38), channel_id=1, replica_groups={{0,2,4,6,8,10,12,14},{1,3,5,7,9,11,13,15},{16,18,20,22,24,26,28,30},{17..., dimensions={0} | all-to-all | bytes 262144 | tf_op jit(solution)/shard_map/all_to_all | solution.py:159
  51.4 1.3 %collective-permute-done.12.refs_1_ = bf16[8,16,512]{2,1,0:T(8,128)(2,1)S(1)} collective-permute-done((bf16[8,16,512]{2,1,0:T(8,128)(2,1)S(1)}, bf16[8,16,512]{2,1,0:T(8,128)(2,1)S(1)}, u32[]{:S(2)}, u32[]{:S(2)}) %collective-permute-start.12) | collective-permute-done | bytes 131104 | tf_op jit(solution)/shard_map/ppermute | solution.py:55
  52.8 5.1 %shard_map.111 = (bf16[16,896]{1,0:T(8,128)(2,1)S(1)}, f32[8,16,512]{2,1,0:T(8,128)S(1)}) custom-call(bf16[8,16,512]{2,1,0:T(8,128)(2,1)S(1)} %all_to_all.16.refs_0_, bf16[8,16,512]{2,1,0:T(8,128)(2,1)S(1)} %collective-permute-done.12.refs_1_, bf16[1,8192]{1,0:T(2,128)(2,1)S(1)} %reshape.7.refs_2_, bf16[8192,896]{1,0:T(8,128)(2,1)S(1)} %bitcast.6, ...), custom_call_target="tpu_custom_call" | custom-call | tf_op jit(solution)/shard_map/pallas_call | solution.py:32
  58.1 1.1 %shard_map.112.refs_0_ = f32[8,16,512]{2,1,0:T(8,128)S(1)} custom-call(bf16[16,896]{1,0:T(8,128)(2,1)S(1)} %get-tuple-element.39.refs_0_, bf16[896,8192]{1,0:T(8,128)(2,1)S(1)} %bitcast.2), custom_call_target="tpu_custom_call" | custom-call | tf_op jit(solution)/shard_map/pallas_call | solution.py:32
  59.5 10.0 %all_to_all.17.refs_1_ = bf16[8,16,512]{2,1,0:T(8,128)(2,1)S(1)} all-to-all(bf16[8,16,512]{2,1,0:T(8,128)(2,1)S(1)} %shard_map.113), channel_id=1, replica_groups={{0,2,4,6,8,10,12,14},{1,3,5,7,9,11,13,15},{16,18,20,22,24,26,28,30},{17..., dimensions={0} | all-to-all | bytes 262144 | tf_op jit(solution)/shard_map/all_to_all | solution.py:159
  69.5 0.6 shard_map.114
  (72 shorter events, 3.4 us)
Async XLA Ops:
  1.2 13.8 %collective-permute-start.6 = (bf16[256,512]{1,0:T(8,128)(2,1)S(1)}, bf16[256,512]{1,0:T(8,128)(2,1)S(1)}, u32[]{:S(2)}, u32[]{:S(2)}) collective-permute-start(bf16[256,512]{1,0:T(8,128)(2,1)S(1)} %get-tuple-element.27), channel_id=1, source_target_pairs={{0,2},{1,3},{2,0},{3,1},{4,6},{5,7},{6,4},{7,5},{8,10},{9,11},{10,... | collective-permute-start | bytes 786440 | tf_op jit(solution)/shard_map/ppermute | solution.py:55
  4.2 4.4 %collective-permute-start = (bf16[208,128]{1,0:T(8,128)(2,1)S(1)}, bf16[208,128]{1,0:T(8,128)(2,1)S(1)}, u32[]{:S(2)}, u32[]{:S(2)}) collective-permute-start(bf16[208,128]{1,0:T(8,128)(2,1)S(1)} %get-tuple-element.24), channel_id=1, source_target_pairs={{0,4},{1,5},{2,6},{3,7},{4,0},{5,1},{6,2},{7,3},{8,12},{9,13},{10,... | collective-permute-start | bytes 159752 | tf_op jit(solution)/shard_map/ppermute | solution.py:55
  5.8 5.8 %collective-permute-start.1 = (bf16[208,128]{1,0:T(8,128)(2,1)S(1)}, bf16[208,128]{1,0:T(8,128)(2,1)S(1)}, u32[]{:S(2)}, u32[]{:S(2)}) collective-permute-start(bf16[208,128]{1,0:T(8,128)(2,1)S(1)} %get-tuple-element.25), channel_id=1, source_target_pairs={{0,8},{1,9},{2,10},{3,11},{4,12},{5,13},{6,14},{7,15},{8,0},{9,1},... | collective-permute-start | bytes 159752 | tf_op jit(solution)/shard_map/ppermute | solution.py:55
  8.4 5.9 %collective-permute-start.2 = (bf16[208,128]{1,0:T(8,128)(2,1)S(1)}, bf16[208,128]{1,0:T(8,128)(2,1)S(1)}, u32[]{:S(2)}, u32[]{:S(2)}) collective-permute-start(bf16[208,128]{1,0:T(8,128)(2,1)S(1)} %get-tuple-element.26), channel_id=1, source_target_pairs={{0,12},{1,13},{2,14},{3,15},{4,8},{5,9},{6,10},{7,11},{8,4},{9,5},... | collective-permute-start | bytes 159752 | tf_op jit(solution)/shard_map/ppermute | solution.py:55
  14.3 12.1 %slice-start.4 = ((s8[8388608]{0:T(1024)(128)(4,1)}), s8[4194304]{0:T(1024)(128)(4,1)S(1)}, s32[]{:S(2)}) async-start(s8[8388608]{0:T(1024)(128)(4,1)} %bitcast.3), calls=%async_computation.7 | async-start | bytes 8388608
  14.4 4.5 %collective-permute-start.4 = (bf16[16,2560]{1,0:T(8,128)(2,1)S(1)}, bf16[16,2560]{1,0:T(8,128)(2,1)S(1)}, u32[]{:S(2)}, u32[]{:S(2)}) collective-permute-start(bf16[16,2560]{1,0:T(8,128)(2,1)S(1)} %shard_map.102.refs_0_.refs_2_), channel_id=1, source_target_pairs={{0,2},{1,3},{2,0},{3,1},{4,6},{5,7},{6,4},{7,5},{8,10},{9,11},{10,... | collective-permute-start | bytes 245768 | tf_op jit(solution)/shard_map/ppermute | solution.py:55
  15.1 6.4 %collective-permute-start.7 = (bf16[384,128]{1,0:T(8,128)(2,1)S(1)}, bf16[384,128]{1,0:T(8,128)(2,1)S(1)}, u32[]{:S(2)}, u32[]{:S(2)}) collective-permute-start(bf16[384,128]{1,0:T(8,128)(2,1)S(1)} %get-tuple-element.29), channel_id=1, source_target_pairs={{0,4},{1,13},{2,6},{3,15},{4,0},{5,9},{6,2},{7,11},{8,12},{9,5},{1... | collective-permute-start | bytes 294920 | tf_op jit(solution)/shard_map/ppermute | solution.py:354
  15.1 7.4 %collective-permute-start.8 = (bf16[384,128]{1,0:T(8,128)(2,1)S(1)}, bf16[384,128]{1,0:T(8,128)(2,1)S(1)}, u32[]{:S(2)}, u32[]{:S(2)}) collective-permute-start(bf16[384,128]{1,0:T(8,128)(2,1)S(1)} %get-tuple-element.30), channel_id=1, source_target_pairs={{0,12},{1,9},{2,14},{3,11},{4,8},{5,13},{6,10},{7,15},{8,4},{9,1},... | collective-permute-start | bytes 294920 | tf_op jit(solution)/shard_map/ppermute | solution.py:354
  17.0 7.4 %collective-permute-start.9 = (bf16[384,128]{1,0:T(8,128)(2,1)S(1)}, bf16[384,128]{1,0:T(8,128)(2,1)S(1)}, u32[]{:S(2)}, u32[]{:S(2)}) collective-permute-start(bf16[384,128]{1,0:T(8,128)(2,1)S(1)} %get-tuple-element.31), channel_id=1, source_target_pairs={{0,8},{1,5},{2,10},{3,7},{4,12},{5,1},{6,14},{7,3},{8,0},{9,13},{1... | collective-permute-start | bytes 294920 | tf_op jit(solution)/shard_map/ppermute | solution.py:354
  18.6 1.3 %collective-permute-start.3 = (bf16[16,2560]{1,0:T(8,128)(2,1)S(1)}, bf16[16,2560]{1,0:T(8,128)(2,1)S(1)}, u32[]{:S(2)}, u32[]{:S(2)}) collective-permute-start(bf16[16,2560]{1,0:T(8,128)(2,1)S(1)} %shard_map.102.refs_0_.refs_2_), channel_id=1, source_target_pairs={{0,1},{1,0},{2,3},{3,2},{4,5},{5,4},{6,7},{7,6},{8,9},{9,8},{10,11... | collective-permute-start | bytes 245768 | tf_op jit(solution)/shard_map/ppermute | solution.py:55
  18.9 1.3 %collective-permute-start.5 = (bf16[16,2560]{1,0:T(8,128)(2,1)S(1)}, bf16[16,2560]{1,0:T(8,128)(2,1)S(1)}, u32[]{:S(2)}, u32[]{:S(2)}) collective-permute-start(bf16[16,2560]{1,0:T(8,128)(2,1)S(1)} %collective-permute-done.4.refs_2_.refs_3_), channel_id=1, source_target_pairs={{0,1},{1,0},{2,3},{3,2},{4,5},{5,4},{6,7},{7,6},{8,9},{9,8},{10,11... | collective-permute-start | bytes 245768 | tf_op jit(solution)/shard_map/ppermute | solution.py:55
  24.4 2.0 %collective-permute-start.10 = (bf16[2048,128]{1,0:T(8,128)(2,1)S(1)}, bf16[2048,128]{1,0:T(8,128)(2,1)S(1)}, u32[]{:S(2)}, u32[]{:S(2)}) collective-permute-start(bf16[2048,128]{1,0:T(8,128)(2,1)S(1)} %shard_map.105.refs_1_), channel_id=1, source_target_pairs={{0,1},{1,0},{2,3},{3,2},{4,5},{5,4},{6,7},{7,6},{8,9},{9,8},{10,11... | collective-permute-start | bytes 1572872 | tf_op jit(solution)/shard_map/ppermute | solution.py:55
  27.7 1.5 %collective-permute-start.11 = (f32[8,16,512]{2,1,0:T(8,128)S(1)}, f32[8,16,512]{2,1,0:T(8,128)S(1)}, u32[]{:S(2)}, u32[]{:S(2)}) collective-permute-start(f32[8,16,512]{2,1,0:T(8,128)S(1)} %get-tuple-element.36), channel_id=1, source_target_pairs={{0,1},{1,0},{2,3},{3,2},{4,5},{5,4},{6,7},{7,6},{8,9},{9,8},{10,11... | collective-permute-start | bytes 786440 | tf_op jit(solution)/shard_map/ppermute | solution.py:55
  29.2 23.5 %slice-start = ((s8[14680064]{0:T(1024)(128)(4,1)}), s8[4194304]{0:T(1024)(128)(4,1)S(1)}, s32[]{:S(2)}) async-start(s8[14680064]{0:T(1024)(128)(4,1)} %bitcast.1), calls=%async_computation.3 | async-start | bytes 8388608
  29.2 23.5 %slice-start.1 = ((s8[14680064]{0:T(1024)(128)(4,1)}), s8[4194304]{0:T(1024)(128)(4,1)S(1)}, s32[]{:S(2)}) async-start(s8[14680064]{0:T(1024)(128)(4,1)} %bitcast.1), calls=%async_computation.4 | async-start | bytes 8388608
  29.2 23.5 %slice-start.6 = ((s8[14680064]{0:T(1024)(128)(4,1)}), s8[4194304]{0:T(1024)(128)(4,1)S(1)}, s32[]{:S(2)}) async-start(s8[14680064]{0:T(1024)(128)(4,1)} %bitcast.5), calls=%async_computation.9 | async-start | bytes 8388608
  29.2 23.5 %slice-start.7 = ((s8[14680064]{0:T(1024)(128)(4,1)}), s8[4194304]{0:T(1024)(128)(4,1)S(1)}, s32[]{:S(2)}) async-start(s8[14680064]{0:T(1024)(128)(4,1)} %bitcast.5), calls=%async_computation.10 | async-start | bytes 8388608
  29.2 23.5 %slice-start.10 = ((s8[14680064]{0:T(1024)(128)(4,1)}), s8[4194304]{0:T(1024)(128)(4,1)S(1)}, s32[]{:S(2)}) async-start(s8[14680064]{0:T(1024)(128)(4,1)} %bitcast.7), calls=%async_computation.13 | async-start | bytes 8388608
  29.2 23.5 %slice-start.11 = ((s8[14680064]{0:T(1024)(128)(4,1)}), s8[4194304]{0:T(1024)(128)(4,1)S(1)}, s32[]{:S(2)}) async-start(s8[14680064]{0:T(1024)(128)(4,1)} %bitcast.7), calls=%async_computation.14 | async-start | bytes 8388608
  29.4 23.3 %slice-start.2 = ((s8[14680064]{0:T(1024)(128)(4,1)}), s8[4194304]{0:T(1024)(128)(4,1)S(1)}, s32[]{:S(2)}) async-start(s8[14680064]{0:T(1024)(128)(4,1)} %bitcast.1), calls=%async_computation.5 | async-start | bytes 8388608
  29.4 23.3 %slice-start.8 = ((s8[14680064]{0:T(1024)(128)(4,1)}), s8[4194304]{0:T(1024)(128)(4,1)S(1)}, s32[]{:S(2)}) async-start(s8[14680064]{0:T(1024)(128)(4,1)} %bitcast.5), calls=%async_computation.11 | async-start | bytes 8388608
  29.4 23.3 %slice-start.12 = ((s8[14680064]{0:T(1024)(128)(4,1)}), s8[4194304]{0:T(1024)(128)(4,1)S(1)}, s32[]{:S(2)}) async-start(s8[14680064]{0:T(1024)(128)(4,1)} %bitcast.7), calls=%async_computation.15 | async-start | bytes 8388608
  51.3 1.3 %collective-permute-start.12 = (bf16[8,16,512]{2,1,0:T(8,128)(2,1)S(1)}, bf16[8,16,512]{2,1,0:T(8,128)(2,1)S(1)}, u32[]{:S(2)}, u32[]{:S(2)}) collective-permute-start(bf16[8,16,512]{2,1,0:T(8,128)(2,1)S(1)} %all_to_all.16.refs_0_), channel_id=1, source_target_pairs={{0,1},{1,0},{2,3},{3,2},{4,5},{5,4},{6,7},{7,6},{8,9},{9,8},{10,11... | collective-permute-start | bytes 393224 | tf_op jit(solution)/shard_map/ppermute | solution.py:55
  57.9 1.5 %collective-permute-start.13 = (f32[8,16,512]{2,1,0:T(8,128)S(1)}, f32[8,16,512]{2,1,0:T(8,128)S(1)}, u32[]{:S(2)}, u32[]{:S(2)}) collective-permute-start(f32[8,16,512]{2,1,0:T(8,128)S(1)} %get-tuple-element.40), channel_id=1, source_target_pairs={{0,1},{1,0},{2,3},{3,2},{4,5},{5,4},{6,7},{7,6},{8,9},{9,8},{10,11... | collective-permute-start | bytes 786440 | tf_op jit(solution)/shard_map/ppermute | solution.py:55
  (11 other events, 77.1 us)

commit v9 on v6

--- a/solution.py
+++ b/solution.py
@@ -12,6 +12,8 @@
 HEAD_DIM = 128
 BLOCK = 128
 QUAD = 4
+RANGE = 32000.0
+STEPS = 256.0
 
 eps = 1e-05
 floor_score = -1e30
@@ -185,11 +187,15 @@
     return jnp.broadcast_to(jnp.sum(mine, axis=1, keepdims=True), tile.shape)
 
 
-def member_chunks(refs):
+def in_line(near, z):
+    return QUAD * z + jnp.bitwise_xor(lax.axis_index("seq") % QUAD, near)
+
+
+def z_line_chunks(wide, refs):
     return [
-        (member(i, other), lambda r=ref, i=i: r[i])
-        for other, ref in enumerate(refs)
-        for i in range(ref.shape[0])
+        (in_line(near, z), lambda r=ref, z=z: r[:, z * wide : (z + 1) * wide])
+        for near, ref in enumerate(refs)
+        for z in range(ref.shape[1] // wide)
     ]
 
 
@@ -208,8 +214,21 @@
         out_ref[i] = jnp.dot(left, w_ref[:, at], preferred_element_type=f32)
 
 
+def line_dot(wide, nears, left, w_ref, out_ref):
+    outer = out_ref.shape[1] // (len(nears) * wide)
+    for i, near in enumerate(nears):
+        for z in range(outer):
+            at = pl.ds(pl.multiple_of(in_line(near, z) * wide, wide), wide)
+            to = (i * outer + z) * wide
+            out_ref[:, to : to + wide] = jnp.dot(left, w_ref[:, at], preferred_element_type=f32)
+
+
 def keep_kernel(wide, left_ref, w_ref, out_ref):
     scatter_dot(wide, False, left_ref[...], w_ref, out_ref)
+
+
+def keep_line_kernel(wide, left_ref, w_ref, out_ref):
+    line_dot(wide, (0, 2), left_ref[...], w_ref, out_ref)
 
 
 def span_states(q_ref, cache_ref, masks):
@@ -286,13 +305,13 @@
     attended = (accum / total).astype(bf16)
     attended = jnp.concatenate([attended[h * rows : (h + 1) * rows] for h in range(heads)], axis=1)
     left_ref[...] = attended
-    scatter_dot(wide, True, attended, w_ref, send_ref)
+    line_dot(wide, (1, 3), attended, w_ref, send_ref)
 
 
 def hidden_kernel(wide, *refs):
-    gain_ref, gate_ref, up_ref, down_ref, left_ref, send_ref = refs[2:]
+    gain_ref, gate_ref, up_ref, down_ref, left_ref, send_ref = refs[QUAD:]
     gate = up = None
-    for at, chunk in normed_chunks(wide, member_chunks(refs[:2]), gain_ref):
+    for at, chunk in normed_chunks(wide, z_line_chunks(wide, refs[:QUAD]), gain_ref):
         g = jnp.dot(chunk, gate_ref[at, :], preferred_element_type=f32)
         u = jnp.dot(chunk, up_ref[at, :], preferred_element_type=f32)
         gate = g if gate is None else gate + g
@@ -306,17 +325,51 @@
     out_ref[...] = (own_ref[...] + recv_ref[...]).astype(out_ref.dtype)
 
 
-def final_kernel(base_ref, parts_ref, *out_refs):
+def coded(out_ref, sums):
+    rows, wide = sums.shape
+    largest = jnp.max(jnp.abs(sums), axis=1, keepdims=True)
+    level = jnp.ceil(jnp.log(jnp.maximum(largest, 1e-30)) * STEPS)
+    scale = jnp.exp(level * (-1.0 / STEPS)) * RANGE
+    out_ref[:, 0:wide] = jnp.round(sums * scale).astype(jnp.int32).astype(jnp.int16)
+    level = jnp.broadcast_to(level, (rows, HEAD_DIM)).astype(jnp.int32)
+    out_ref[:, wide:] = level.astype(jnp.int16)
+
+
+def decoded(ref):
+    wide = ref.shape[1] - HEAD_DIM
+    level = ref[:, wide:].astype(jnp.int32).astype(f32)[:, 0:1]
+    scale = jnp.exp(level * (1.0 / STEPS)) * (1.0 / RANGE)
+    return ref[:, 0:wide].astype(jnp.int32).astype(f32) * scale
+
+
+def chip_kernel(own_ref, recv_ref, keep_ref, send_ref):
+    half = own_ref.shape[1] // 2
+    keep_ref[...] = own_ref[:, :half] + recv_ref[:, :half]
+    coded(send_ref, own_ref[:, half:] + recv_ref[:, half:])
+
+
+def pair_kernel(keep_ref, recv_ref, out_ref):
+    coded(out_ref, keep_ref[...] + decoded(recv_ref))
+
+
+def stream_kernel(wide, x_ref, *refs):
+    parts, (line_ref, own_ref) = refs[:-2], refs[-2:]
+    z = lax.axis_index("seq") // QUAD
+    sums = [decoded(part) for part in parts]
+    while len(sums) > 1:
+        sums = [first + second for first, second in zip(sums[0::2], sums[1::2])]
+    for to in range(len(parts)):
+        at = pl.multiple_of(jnp.bitwise_xor(z, to) * (wide + HEAD_DIM), HEAD_DIM)
+        cols = slice(to * wide, (to + 1) * wide)
+        line_ref[:, cols] = (x_ref[:, pl.ds(at, wide)].astype(f32) + sums[0][:, cols]).astype(bf16)
+    own_ref[...] = line_ref[:, pl.ds(pl.multiple_of(z * wide, wide), wide)]
+
+
+def final_kernel(base_ref, parts_ref, out_ref):
     total = parts_ref[0].astype(f32)
     for i in range(1, parts_ref.shape[0]):
         total = total + parts_ref[i].astype(f32)
-    total = (base_ref[...].astype(f32) + total).astype(bf16)
-    for out in out_refs:
-        if len(out.shape) == 3:
-            for i in range(out.shape[0]):
-                out[i] = total
-        else:
-            out[...] = total
+    out_ref[...] = (base_ref[...].astype(f32) + total).astype(bf16)
 
 
 def z_swapped(parts):
@@ -333,15 +386,31 @@
 
 
 def near_gathered(line):
-    far, y, core = swap(line, 3), swap(line, 2), swap(line, 1)
+    y = swap(line, 2)
+    core, far = swap(line, 1), swap(y, 1)
     return [line, core, y, far]
 
 
-def scattered(base, send, left, weight, wide, kind, outs, beside=()):
+def updated(x_line, send, left, weight, wide, beside):
+    rows, columns = send.shape
+    half = columns // 2
+    code = like((rows, half + HEAD_DIM), jnp.int16)
+    far = swap(send, 1)
+    own = call(functools.partial(keep_line_kernel, wide), like(send.shape, f32), [left, weight])
+    keep, send = call(chip_kernel, [like((rows, half), f32), code], [own, far], beside)
+    sums = call(pair_kernel, code, [keep, swap(send, 2)], beside)
+    return call(
+        functools.partial(stream_kernel, wide),
+        [like((rows, half), bf16), like((rows, wide), bf16)],
+        [x_line, *z_routed([sums] * (half // wide))],
+    )
+
+
+def scattered(base, send, left, weight, wide):
     far = swap(send, 1)
     own = call(functools.partial(keep_kernel, wide), like(send.shape, f32), [left, weight])
-    sums = call(add_kernel, like(send.shape, kind), [own, far], beside)
-    return call(final_kernel, outs, [base, to_members(sums)], beside)
+    sums = call(add_kernel, like(send.shape, bf16), [own, far])
+    return call(final_kernel, like(base.shape, bf16), [base, to_members(sums)])
 
 
 def local_pairs(
@@ -355,7 +424,6 @@
     mlp_gain = mlp_gain.reshape(1, -1)
     members = lax.axis_size("seq") // 2
     partial_sums = like((members, rows, wide), f32)
-    own_columns = like((rows, wide), bf16)
 
     keys = kv_cache.shape[1]
     step = wide + HEAD_DIM
@@ -395,19 +463,16 @@
     )
     left, send = call(
         functools.partial(attend_kernel, outer, wide),
-        [like((rows, columns), bf16), partial_sums],
+        [like((rows, columns), bf16), like((rows, 2 * outer * wide), f32)],
         [queries, *early, far_cache, *x_parts[1::2], o_weight],
     )
-    stream, copies = scattered(
-        x_rows, send, left, o_weight, wide, f32, [own_columns, like(partial_sums.shape, bf16)], beside
-    )
-    parts = to_members(copies)
+    line, stream = updated(x_parts[0], send, left, o_weight, wide, beside)
     left, send = call(
         functools.partial(hidden_kernel, wide),
         [like((rows, gate_weight.shape[1]), bf16), partial_sums],
-        [parts, swap(parts, 1), mlp_gain, gate_weight, up_weight, down_weight],
-    )
-    return scattered(stream, send, left, down_weight, wide, bf16, [own_columns])[0]
+        [*near_gathered(line), mlp_gain, gate_weight, up_weight, down_weight],
+    )
+    return scattered(stream, send, left, down_weight, wide)
 
 
 def rms_norm(values, gain):

time: 73.9 us -> 67.2 us (0.909)
  blocking collectives: 33.4 us -> 11.1 us
  waiting for transfers between devices: 14.5 us -> 24.3 us
  starting transfers between devices: 13.3 us -> 18.9 us
    all_to_all x3 -> x1, blocking collectives: 33.4 us -> 11.1 us  [to_members(): lax.all_to_all(parts, 'seq', 0, 0, axis_index_groups=groups, tiled=True)]
    ppermute x3 -> x6, waiting for transfers between devices: 0.64 us -> 8.07 us  [z_routed(): lax.ppermute(part, 'seq', [(i, i ^ QUAD * slot[i % 2]) for i in range(siz...]
    ppermute x3 -> x6, starting transfers between devices: 3.55 us -> 7.09 us  [z_routed(): lax.ppermute(part, 'seq', [(i, i ^ QUAD * slot[i % 2]) for i in range(siz...]
    ppermute x11 -> x14, waiting for transfers between devices: 13.9 us -> 16.2 us  [swap(): return lax.ppermute(x, 'seq', [(i, i ^ distance) for i in range(size)])]
    ppermute x11 -> x14, starting transfers between devices: 9.77 us -> 11.8 us  [swap(): return lax.ppermute(x, 'seq', [(i, i ^ distance) for i in range(size)])]
    pallas_call x14 -> x15, Pallas kernels: 10.9 us -> 11.3 us  [call(): pl.pallas_call(kernel, out_shape=outs, in_specs=[VMEM] * count + [pl.Bloc...]
  transfers between devices with their start and end apart: 14 -> 20, of which waited for: 9 -> 15; matrix products, arithmetic and copies ran while one was open for 0% -> 0% of each run, Pallas kernels for 5% -> 5%
where the time goes in v9:
time: 67.2 us; the launch traced here: 67 us
  waiting for transfers between devices  24.3 us (36%)
  starting transfers between devices  18.9 us (28%)
  Pallas kernels  11.3 us (17%)
  blocking collectives  11.1 us (17%)
  local copies, waits for them, and re-layouts  1.18 us (2%)
    ppermute x14, waiting for transfers between devices, swap(): return lax.ppermute(x, 'seq', [(i, i ^ distance) for i in range(size)])  16.2 us
    ppermute x14, starting transfers between devices, swap(): return lax.ppermute(x, 'seq', [(i, i ^ distance) for i in range(size)])  11.8 us
    pallas_call x15, Pallas kernels, call(): pl.pallas_call(kernel, out_shape=outs, in_specs=[VMEM] * count + [pl.Bloc...  11.3 us
    all_to_all x1, blocking collectives, to_members(): lax.all_to_all(parts, 'seq', 0, 0, axis_index_groups=groups, tiled=True)  11.1 us
    ppermute x6, waiting for transfers between devices, z_routed(): lax.ppermute(part, 'seq', [(i, i ^ QUAD * slot[i % 2]) for i in range(siz...  8.07 us
    ppermute x6, starting transfers between devices, z_routed(): lax.ppermute(part, 'seq', [(i, i ^ QUAD * slot[i % 2]) for i in range(siz...  7.09 us
  transfers between devices with their start and end apart: 20, of which 15 were waited for; matrix products, arithmetic and copies ran while one was open for 0% of the time, Pallas kernels for 5%

profile of v9, /device:TPU:0, one launch (start us, length us, event | category | flops | bytes accessed | tf_op | source)
XLA Modules:
  0.0 67.0 jit_solution(7959499349677864516)
XLA Ops:
  1.2 3.0 %collective-permute-start.6 = (bf16[256,512]{1,0:T(8,128)(2,1)S(1)}, bf16[256,512]{1,0:T(8,128)(2,1)S(1)}, u32[]{:S(2)}, u32[]{:S(2)}) collective-permute-start(bf16[256,512]{1,0:T(8,128)(2,1)S(1)} %get-tuple-element.29), channel_id=1, source_target_pairs={{0,2},{1,3},{2,0},{3,1},{4,6},{5,7},{6,4},{7,5},{8,10},{9,11},{10,... | collective-permute-start | bytes 786440 | tf_op jit(solution)/shard_map/ppermute | solution.py:55
  4.2 1.6 %collective-permute-start = (bf16[208,128]{1,0:T(8,128)(2,1)S(1)}, bf16[208,128]{1,0:T(8,128)(2,1)S(1)}, u32[]{:S(2)}, u32[]{:S(2)}) collective-permute-start(bf16[208,128]{1,0:T(8,128)(2,1)S(1)} %get-tuple-element.26), channel_id=1, source_target_pairs={{0,4},{1,5},{2,6},{3,7},{4,0},{5,1},{6,2},{7,3},{8,12},{9,13},{10,... | collective-permute-start | bytes 159752 | tf_op jit(solution)/shard_map/ppermute | solution.py:55
  5.8 2.6 %collective-permute-start.1 = (bf16[208,128]{1,0:T(8,128)(2,1)S(1)}, bf16[208,128]{1,0:T(8,128)(2,1)S(1)}, u32[]{:S(2)}, u32[]{:S(2)}) collective-permute-start(bf16[208,128]{1,0:T(8,128)(2,1)S(1)} %get-tuple-element.27), channel_id=1, source_target_pairs={{0,8},{1,9},{2,10},{3,11},{4,12},{5,13},{6,14},{7,15},{8,0},{9,1},... | collective-permute-start | bytes 159752 | tf_op jit(solution)/shard_map/ppermute | solution.py:55
  8.6 3.0 %collective-permute-done.1.refs_2_ = bf16[208,128]{1,0:T(8,128)(2,1)S(1)} collective-permute-done((bf16[208,128]{1,0:T(8,128)(2,1)S(1)}, bf16[208,128]{1,0:T(8,128)(2,1)S(1)}, u32[]{:S(2)}, u32[]{:S(2)}) %collective-permute-start.1) | collective-permute-done | bytes 53280 | tf_op jit(solution)/shard_map/ppermute | solution.py:55
  11.6 2.7 %collective-permute-done.2.refs_3_ = bf16[208,128]{1,0:T(8,128)(2,1)S(1)} collective-permute-done((bf16[208,128]{1,0:T(8,128)(2,1)S(1)}, bf16[208,128]{1,0:T(8,128)(2,1)S(1)}, u32[]{:S(2)}, u32[]{:S(2)}) %collective-permute-start.2) | collective-permute-done | bytes 53280 | tf_op jit(solution)/shard_map/ppermute | solution.py:55
  15.1 1.8 %collective-permute-start.8 = (bf16[384,128]{1,0:T(8,128)(2,1)S(1)}, bf16[384,128]{1,0:T(8,128)(2,1)S(1)}, u32[]{:S(2)}, u32[]{:S(2)}) collective-permute-start(bf16[384,128]{1,0:T(8,128)(2,1)S(1)} %get-tuple-element.32), channel_id=1, source_target_pairs={{0,12},{1,9},{2,14},{3,11},{4,8},{5,13},{6,10},{7,15},{8,4},{9,1},... | collective-permute-start | bytes 294920 | tf_op jit(solution)/shard_map/ppermute | solution.py:383
  17.0 1.6 %collective-permute-start.9 = (bf16[384,128]{1,0:T(8,128)(2,1)S(1)}, bf16[384,128]{1,0:T(8,128)(2,1)S(1)}, u32[]{:S(2)}, u32[]{:S(2)}) collective-permute-start(bf16[384,128]{1,0:T(8,128)(2,1)S(1)} %get-tuple-element.33), channel_id=1, source_target_pairs={{0,8},{1,5},{2,10},{3,7},{4,12},{5,1},{6,14},{7,3},{8,0},{9,13},{1... | collective-permute-start | bytes 294920 | tf_op jit(solution)/shard_map/ppermute | solution.py:383
  20.2 1.3 %shard_map.103.refs_8_.refs_0_ = bf16[16,512]{1,0:T(8,128)(2,1)S(1)} custom-call(bf16[16,2560]{1,0:T(8,128)(2,1)S(1)} %shard_map.102.refs_0_.refs_2_, bf16[16,2560]{1,0:T(8,128)(2,1)S(1)} %collective-permute-done.3.refs_1_.refs_5_, bf16[16,2560]{1,0:T(8,128)(2,1)S(1)} %collective-permute-done.4.refs_2_.refs_3_, ...), custom_call_target="tpu_custom_call" | custom-call | tf_op jit(solution)/shard_map/pallas_call | solution.py:32
  21.5 1.1 %collective-permute-done.8.refs_6_ = bf16[384,128]{1,0:T(8,128)(2,1)S(1)} collective-permute-done((bf16[384,128]{1,0:T(8,128)(2,1)S(1)}, bf16[384,128]{1,0:T(8,128)(2,1)S(1)}, u32[]{:S(2)}, u32[]{:S(2)}) %collective-permute-start.8) | collective-permute-done | bytes 98336 | tf_op jit(solution)/shard_map/ppermute | solution.py:383
  22.5 1.8 %collective-permute-done.9.refs_7_ = bf16[384,128]{1,0:T(8,128)(2,1)S(1)} collective-permute-done((bf16[384,128]{1,0:T(8,128)(2,1)S(1)}, bf16[384,128]{1,0:T(8,128)(2,1)S(1)}, u32[]{:S(2)}, u32[]{:S(2)}) %collective-permute-start.9) | collective-permute-done | bytes 98336 | tf_op jit(solution)/shard_map/ppermute | solution.py:383
  25.0 1.4 %collective-permute-done.10.refs_4_ = bf16[2048,128]{1,0:T(8,128)(2,1)S(1)} collective-permute-done((bf16[2048,128]{1,0:T(8,128)(2,1)S(1)}, bf16[2048,128]{1,0:T(8,128)(2,1)S(1)}, u32[]{:S(2)}, u32[]{:S(2)}) %collective-permute-start.10) | collective-permute-done | bytes 524320 | tf_op jit(solution)/shard_map/ppermute | solution.py:55
  26.4 1.2 %shard_map.107 = (bf16[16,512]{1,0:T(8,128)(2,1)S(1)}, f32[16,4096]{1,0:T(8,128)S(1)}) custom-call(bf16[16,512]{1,0:T(8,128)(2,1)S(1)} %shard_map.103.refs_8_.refs_0_, f32[64,128]{1,0:T(8,128)S(1)} %get-tuple-element.34.refs_1_, f32[64,128]{1,0:T(8,128)S(1)} %get-tuple-element.35.refs_2_, f32[64,128]{1,0:T(8,128)S(1)} %get-tuple-element.36.refs_3_, ...), custom_call_target="tpu_custom_call" | custom-call | tf_op jit(solution)/shard_map/pallas_call | solution.py:32
  29.4 1.6 %collective-permute-start.12 = (s16[16,2176]{1,0:T(8,128)(2,1)S(1)}, s16[16,2176]{1,0:T(8,128)(2,1)S(1)}, u32[]{:S(2)}, u32[]{:S(2)}) collective-permute-start(s16[16,2176]{1,0:T(8,128)(2,1)S(1)} %get-tuple-element.40), channel_id=1, source_target_pairs={{0,2},{1,3},{2,0},{3,1},{4,6},{5,7},{6,4},{7,5},{8,10},{9,11},{10,... | collective-permute-start | bytes 208904 | tf_op jit(solution)/shard_map/ppermute | solution.py:55
  31.0 2.8 %collective-permute-done.12.refs_1_ = s16[16,2176]{1,0:T(8,128)(2,1)S(1)} collective-permute-done((s16[16,2176]{1,0:T(8,128)(2,1)S(1)}, s16[16,2176]{1,0:T(8,128)(2,1)S(1)}, u32[]{:S(2)}, u32[]{:S(2)}) %collective-permute-start.12) | collective-permute-done | bytes 69664 | tf_op jit(solution)/shard_map/ppermute | solution.py:55
  34.1 1.5 %collective-permute-start.14 = (s16[16,2176]{1,0:T(8,128)(2,1)S(1)}, s16[16,2176]{1,0:T(8,128)(2,1)S(1)}, u32[]{:S(2)}, u32[]{:S(2)}) collective-permute-start(s16[16,2176]{1,0:T(8,128)(2,1)S(1)} %shard_map.110.refs_1_), channel_id=1, source_target_pairs={{0,12},{1,9},{2,14},{3,11},{4,8},{5,13},{6,10},{7,15},{8,4},{9,1},... | collective-permute-start | bytes 208904 | tf_op jit(solution)/shard_map/ppermute | solution.py:383
  35.5 2.0 %collective-permute-start.15 = (s16[16,2176]{1,0:T(8,128)(2,1)S(1)}, s16[16,2176]{1,0:T(8,128)(2,1)S(1)}, u32[]{:S(2)}, u32[]{:S(2)}) collective-permute-start(s16[16,2176]{1,0:T(8,128)(2,1)S(1)} %shard_map.110.refs_1_), channel_id=1, source_target_pairs={{0,8},{1,5},{2,10},{3,7},{4,12},{5,1},{6,14},{7,3},{8,0},{9,13},{1... | collective-permute-start | bytes 208904 | tf_op jit(solution)/shard_map/ppermute | solution.py:383
  37.5 3.5 %collective-permute-done.13.refs_2_ = s16[16,2176]{1,0:T(8,128)(2,1)S(1)} collective-permute-done((s16[16,2176]{1,0:T(8,128)(2,1)S(1)}, s16[16,2176]{1,0:T(8,128)(2,1)S(1)}, u32[]{:S(2)}, u32[]{:S(2)}) %collective-permute-start.13) | collective-permute-done | bytes 69664 | tf_op jit(solution)/shard_map/ppermute | solution.py:383
  41.1 1.6 %collective-permute-done.15.refs_4_ = s16[16,2176]{1,0:T(8,128)(2,1)S(1)} collective-permute-done((s16[16,2176]{1,0:T(8,128)(2,1)S(1)}, s16[16,2176]{1,0:T(8,128)(2,1)S(1)}, u32[]{:S(2)}, u32[]{:S(2)}) %collective-permute-start.15) | collective-permute-done | bytes 69664 | tf_op jit(solution)/shard_map/ppermute | solution.py:383
  42.9 1.6 %collective-permute-start.17 = (bf16[16,2048]{1,0:T(8,128)(2,1)S(1)}, bf16[16,2048]{1,0:T(8,128)(2,1)S(1)}, u32[]{:S(2)}, u32[]{:S(2)}) collective-permute-start(bf16[16,2048]{1,0:T(8,128)(2,1)S(1)} %get-tuple-element.42.refs_0_), channel_id=1, source_target_pairs={{0,2},{1,3},{2,0},{3,1},{4,6},{5,7},{6,4},{7,5},{8,10},{9,11},{10,... | collective-permute-start | bytes 196616 | tf_op jit(solution)/shard_map/ppermute | solution.py:55
  44.4 2.7 %collective-permute-done.17.refs_2_ = bf16[16,2048]{1,0:T(8,128)(2,1)S(1)} collective-permute-done((bf16[16,2048]{1,0:T(8,128)(2,1)S(1)}, bf16[16,2048]{1,0:T(8,128)(2,1)S(1)}, u32[]{:S(2)}, u32[]{:S(2)}) %collective-permute-start.17) | collective-permute-done | bytes 65568 | tf_op jit(solution)/shard_map/ppermute | solution.py:55
  47.2 1.2 %collective-permute-done.18.refs_3_ = bf16[16,2048]{1,0:T(8,128)(2,1)S(1)} collective-permute-done((bf16[16,2048]{1,0:T(8,128)(2,1)S(1)}, bf16[16,2048]{1,0:T(8,128)(2,1)S(1)}, u32[]{:S(2)}, u32[]{:S(2)}) %collective-permute-start.18) | collective-permute-done | bytes 65568 | tf_op jit(solution)/shard_map/ppermute | solution.py:55
  48.6 5.1 %shard_map.112 = (bf16[16,896]{1,0:T(8,128)(2,1)S(1)}, f32[8,16,512]{2,1,0:T(8,128)S(1)}) custom-call(bf16[16,2048]{1,0:T(8,128)(2,1)S(1)} %get-tuple-element.42.refs_0_, bf16[16,2048]{1,0:T(8,128)(2,1)S(1)} %collective-permute-done.16.refs_1_, bf16[16,2048]{1,0:T(8,128)(2,1)S(1)} %collective-permute-done.17.refs_2_, ...), custom_call_target="tpu_custom_call" | custom-call | tf_op jit(solution)/shard_map/pallas_call | solution.py:32
  53.9 1.1 %shard_map.113.refs_0_ = f32[8,16,512]{2,1,0:T(8,128)S(1)} custom-call(bf16[16,896]{1,0:T(8,128)(2,1)S(1)} %get-tuple-element.43.refs_0_, bf16[896,8192]{1,0:T(8,128)(2,1)S(1)} %bitcast.2), custom_call_target="tpu_custom_call" | custom-call | tf_op jit(solution)/shard_map/pallas_call | solution.py:32
  55.3 11.1 %all_to_all.5.refs_1_ = bf16[8,16,512]{2,1,0:T(8,128)(2,1)S(1)} all-to-all(bf16[8,16,512]{2,1,0:T(8,128)(2,1)S(1)} %shard_map.114), channel_id=1, replica_groups={{0,2,4,6,8,10,12,14},{1,3,5,7,9,11,13,15},{16,18,20,22,24,26,28,30},{17..., dimensions={0} | all-to-all | bytes 262144 | tf_op jit(solution)/shard_map/all_to_all | solution.py:159
  (83 shorter events, 7.7 us)
Async XLA Ops:
  1.2 13.8 %collective-permute-start.6 = (bf16[256,512]{1,0:T(8,128)(2,1)S(1)}, bf16[256,512]{1,0:T(8,128)(2,1)S(1)}, u32[]{:S(2)}, u32[]{:S(2)}) collective-permute-start(bf16[256,512]{1,0:T(8,128)(2,1)S(1)} %get-tuple-element.29), channel_id=1, source_target_pairs={{0,2},{1,3},{2,0},{3,1},{4,6},{5,7},{6,4},{7,5},{8,10},{9,11},{10,... | collective-permute-start | bytes 786440 | tf_op jit(solution)/shard_map/ppermute | solution.py:55
  4.2 4.4 %collective-permute-start = (bf16[208,128]{1,0:T(8,128)(2,1)S(1)}, bf16[208,128]{1,0:T(8,128)(2,1)S(1)}, u32[]{:S(2)}, u32[]{:S(2)}) collective-permute-start(bf16[208,128]{1,0:T(8,128)(2,1)S(1)} %get-tuple-element.26), channel_id=1, source_target_pairs={{0,4},{1,5},{2,6},{3,7},{4,0},{5,1},{6,2},{7,3},{8,12},{9,13},{10,... | collective-permute-start | bytes 159752 | tf_op jit(solution)/shard_map/ppermute | solution.py:55
  5.8 5.8 %collective-permute-start.1 = (bf16[208,128]{1,0:T(8,128)(2,1)S(1)}, bf16[208,128]{1,0:T(8,128)(2,1)S(1)}, u32[]{:S(2)}, u32[]{:S(2)}) collective-permute-start(bf16[208,128]{1,0:T(8,128)(2,1)S(1)} %get-tuple-element.27), channel_id=1, source_target_pairs={{0,8},{1,9},{2,10},{3,11},{4,12},{5,13},{6,14},{7,15},{8,0},{9,1},... | collective-permute-start | bytes 159752 | tf_op jit(solution)/shard_map/ppermute | solution.py:55
  8.4 5.9 %collective-permute-start.2 = (bf16[208,128]{1,0:T(8,128)(2,1)S(1)}, bf16[208,128]{1,0:T(8,128)(2,1)S(1)}, u32[]{:S(2)}, u32[]{:S(2)}) collective-permute-start(bf16[208,128]{1,0:T(8,128)(2,1)S(1)} %get-tuple-element.28), channel_id=1, source_target_pairs={{0,12},{1,13},{2,14},{3,15},{4,8},{5,9},{6,10},{7,11},{8,4},{9,5},... | collective-permute-start | bytes 159752 | tf_op jit(solution)/shard_map/ppermute | solution.py:55
  14.4 4.5 %collective-permute-start.4 = (bf16[16,2560]{1,0:T(8,128)(2,1)S(1)}, bf16[16,2560]{1,0:T(8,128)(2,1)S(1)}, u32[]{:S(2)}, u32[]{:S(2)}) collective-permute-start(bf16[16,2560]{1,0:T(8,128)(2,1)S(1)} %shard_map.102.refs_0_.refs_2_), channel_id=1, source_target_pairs={{0,2},{1,3},{2,0},{3,1},{4,6},{5,7},{6,4},{7,5},{8,10},{9,11},{10,... | collective-permute-start | bytes 245768 | tf_op jit(solution)/shard_map/ppermute | solution.py:55
  15.1 6.4 %collective-permute-start.7 = (bf16[384,128]{1,0:T(8,128)(2,1)S(1)}, bf16[384,128]{1,0:T(8,128)(2,1)S(1)}, u32[]{:S(2)}, u32[]{:S(2)}) collective-permute-start(bf16[384,128]{1,0:T(8,128)(2,1)S(1)} %get-tuple-element.31), channel_id=1, source_target_pairs={{0,4},{1,13},{2,6},{3,15},{4,0},{5,9},{6,2},{7,11},{8,12},{9,5},{1... | collective-permute-start | bytes 294920 | tf_op jit(solution)/shard_map/ppermute | solution.py:383
  15.1 7.4 %collective-permute-start.8 = (bf16[384,128]{1,0:T(8,128)(2,1)S(1)}, bf16[384,128]{1,0:T(8,128)(2,1)S(1)}, u32[]{:S(2)}, u32[]{:S(2)}) collective-permute-start(bf16[384,128]{1,0:T(8,128)(2,1)S(1)} %get-tuple-element.32), channel_id=1, source_target_pairs={{0,12},{1,9},{2,14},{3,11},{4,8},{5,13},{6,10},{7,15},{8,4},{9,1},... | collective-permute-start | bytes 294920 | tf_op jit(solution)/shard_map/ppermute | solution.py:383
  17.0 7.4 %collective-permute-start.9 = (bf16[384,128]{1,0:T(8,128)(2,1)S(1)}, bf16[384,128]{1,0:T(8,128)(2,1)S(1)}, u32[]{:S(2)}, u32[]{:S(2)}) collective-permute-start(bf16[384,128]{1,0:T(8,128)(2,1)S(1)} %get-tuple-element.33), channel_id=1, source_target_pairs={{0,8},{1,5},{2,10},{3,7},{4,12},{5,1},{6,14},{7,3},{8,0},{9,13},{1... | collective-permute-start | bytes 294920 | tf_op jit(solution)/shard_map/ppermute | solution.py:383
  18.6 1.3 %collective-permute-start.3 = (bf16[16,2560]{1,0:T(8,128)(2,1)S(1)}, bf16[16,2560]{1,0:T(8,128)(2,1)S(1)}, u32[]{:S(2)}, u32[]{:S(2)}) collective-permute-start(bf16[16,2560]{1,0:T(8,128)(2,1)S(1)} %shard_map.102.refs_0_.refs_2_), channel_id=1, source_target_pairs={{0,1},{1,0},{2,3},{3,2},{4,5},{5,4},{6,7},{7,6},{8,9},{9,8},{10,11... | collective-permute-start | bytes 245768 | tf_op jit(solution)/shard_map/ppermute | solution.py:55
  18.9 1.3 %collective-permute-start.5 = (bf16[16,2560]{1,0:T(8,128)(2,1)S(1)}, bf16[16,2560]{1,0:T(8,128)(2,1)S(1)}, u32[]{:S(2)}, u32[]{:S(2)}) collective-permute-start(bf16[16,2560]{1,0:T(8,128)(2,1)S(1)} %collective-permute-done.4.refs_2_.refs_3_), channel_id=1, source_target_pairs={{0,1},{1,0},{2,3},{3,2},{4,5},{5,4},{6,7},{7,6},{8,9},{9,8},{10,11... | collective-permute-start | bytes 245768 | tf_op jit(solution)/shard_map/ppermute | solution.py:55
  24.4 2.0 %collective-permute-start.10 = (bf16[2048,128]{1,0:T(8,128)(2,1)S(1)}, bf16[2048,128]{1,0:T(8,128)(2,1)S(1)}, u32[]{:S(2)}, u32[]{:S(2)}) collective-permute-start(bf16[2048,128]{1,0:T(8,128)(2,1)S(1)} %shard_map.105.refs_1_), channel_id=1, source_target_pairs={{0,1},{1,0},{2,3},{3,2},{4,5},{5,4},{6,7},{7,6},{8,9},{9,8},{10,11... | collective-permute-start | bytes 1572872 | tf_op jit(solution)/shard_map/ppermute | solution.py:55
  27.6 1.5 %collective-permute-start.11 = (f32[16,4096]{1,0:T(8,128)S(1)}, f32[16,4096]{1,0:T(8,128)S(1)}, u32[]{:S(2)}, u32[]{:S(2)}) collective-permute-start(f32[16,4096]{1,0:T(8,128)S(1)} %get-tuple-element.38), channel_id=1, source_target_pairs={{0,1},{1,0},{2,3},{3,2},{4,5},{5,4},{6,7},{7,6},{8,9},{9,8},{10,11... | collective-permute-start | bytes 786440 | tf_op jit(solution)/shard_map/ppermute | solution.py:55
  29.2 19.3 %slice-start.6 = ((s8[14680064]{0:T(1024)(128)(4,1)}), s8[4194304]{0:T(1024)(128)(4,1)S(1)}, s32[]{:S(2)}) async-start(s8[14680064]{0:T(1024)(128)(4,1)} %bitcast.5), calls=%async_computation.7 | async-start | bytes 8388608
  29.2 19.3 %slice-start.7 = ((s8[14680064]{0:T(1024)(128)(4,1)}), s8[4194304]{0:T(1024)(128)(4,1)S(1)}, s32[]{:S(2)}) async-start(s8[14680064]{0:T(1024)(128)(4,1)} %bitcast.5), calls=%async_computation.8 | async-start | bytes 8388608
  29.2 19.3 %slice-start.10 = ((s8[14680064]{0:T(1024)(128)(4,1)}), s8[4194304]{0:T(1024)(128)(4,1)S(1)}, s32[]{:S(2)}) async-start(s8[14680064]{0:T(1024)(128)(4,1)} %bitcast.7), calls=%async_computation.11 | async-start | bytes 8388608
  29.2 19.3 %slice-start.11 = ((s8[14680064]{0:T(1024)(128)(4,1)}), s8[4194304]{0:T(1024)(128)(4,1)S(1)}, s32[]{:S(2)}) async-start(s8[14680064]{0:T(1024)(128)(4,1)} %bitcast.7), calls=%async_computation.12 | async-start | bytes 8388608
  29.4 4.4 %collective-permute-start.12 = (s16[16,2176]{1,0:T(8,128)(2,1)S(1)}, s16[16,2176]{1,0:T(8,128)(2,1)S(1)}, u32[]{:S(2)}, u32[]{:S(2)}) collective-permute-start(s16[16,2176]{1,0:T(8,128)(2,1)S(1)} %get-tuple-element.40), channel_id=1, source_target_pairs={{0,2},{1,3},{2,0},{3,1},{4,6},{5,7},{6,4},{7,5},{8,10},{9,11},{10,... | collective-permute-start | bytes 208904 | tf_op jit(solution)/shard_map/ppermute | solution.py:55
  34.0 7.1 %collective-permute-start.13 = (s16[16,2176]{1,0:T(8,128)(2,1)S(1)}, s16[16,2176]{1,0:T(8,128)(2,1)S(1)}, u32[]{:S(2)}, u32[]{:S(2)}) collective-permute-start(s16[16,2176]{1,0:T(8,128)(2,1)S(1)} %shard_map.110.refs_1_), channel_id=1, source_target_pairs={{0,4},{1,13},{2,6},{3,15},{4,0},{5,9},{6,2},{7,11},{8,12},{9,5},{1... | collective-permute-start | bytes 208904 | tf_op jit(solution)/shard_map/ppermute | solution.py:383
  34.1 7.0 %collective-permute-start.14 = (s16[16,2176]{1,0:T(8,128)(2,1)S(1)}, s16[16,2176]{1,0:T(8,128)(2,1)S(1)}, u32[]{:S(2)}, u32[]{:S(2)}) collective-permute-start(s16[16,2176]{1,0:T(8,128)(2,1)S(1)} %shard_map.110.refs_1_), channel_id=1, source_target_pairs={{0,12},{1,9},{2,14},{3,11},{4,8},{5,13},{6,10},{7,15},{8,4},{9,1},... | collective-permute-start | bytes 208904 | tf_op jit(solution)/shard_map/ppermute | solution.py:383
  35.5 7.2 %collective-permute-start.15 = (s16[16,2176]{1,0:T(8,128)(2,1)S(1)}, s16[16,2176]{1,0:T(8,128)(2,1)S(1)}, u32[]{:S(2)}, u32[]{:S(2)}) collective-permute-start(s16[16,2176]{1,0:T(8,128)(2,1)S(1)} %shard_map.110.refs_1_), channel_id=1, source_target_pairs={{0,8},{1,5},{2,10},{3,7},{4,12},{5,1},{6,14},{7,3},{8,0},{9,13},{1... | collective-permute-start | bytes 208904 | tf_op jit(solution)/shard_map/ppermute | solution.py:383
  42.9 4.3 %collective-permute-start.17 = (bf16[16,2048]{1,0:T(8,128)(2,1)S(1)}, bf16[16,2048]{1,0:T(8,128)(2,1)S(1)}, u32[]{:S(2)}, u32[]{:S(2)}) collective-permute-start(bf16[16,2048]{1,0:T(8,128)(2,1)S(1)} %get-tuple-element.42.refs_0_), channel_id=1, source_target_pairs={{0,2},{1,3},{2,0},{3,1},{4,6},{5,7},{6,4},{7,5},{8,10},{9,11},{10,... | collective-permute-start | bytes 196616 | tf_op jit(solution)/shard_map/ppermute | solution.py:55
  44.4 2.8 %collective-permute-start.16 = (bf16[16,2048]{1,0:T(8,128)(2,1)S(1)}, bf16[16,2048]{1,0:T(8,128)(2,1)S(1)}, u32[]{:S(2)}, u32[]{:S(2)}) collective-permute-start(bf16[16,2048]{1,0:T(8,128)(2,1)S(1)} %get-tuple-element.42.refs_0_), channel_id=1, source_target_pairs={{0,1},{1,0},{2,3},{3,2},{4,5},{5,4},{6,7},{7,6},{8,9},{9,8},{10,11... | collective-permute-start | bytes 196616 | tf_op jit(solution)/shard_map/ppermute | solution.py:55
  47.2 1.3 %collective-permute-start.18 = (bf16[16,2048]{1,0:T(8,128)(2,1)S(1)}, bf16[16,2048]{1,0:T(8,128)(2,1)S(1)}, u32[]{:S(2)}, u32[]{:S(2)}) collective-permute-start(bf16[16,2048]{1,0:T(8,128)(2,1)S(1)} %collective-permute-done.17.refs_2_), channel_id=1, source_target_pairs={{0,1},{1,0},{2,3},{3,2},{4,5},{5,4},{6,7},{7,6},{8,9},{9,8},{10,11... | collective-permute-start | bytes 196616 | tf_op jit(solution)/shard_map/ppermute | solution.py:55
  53.7 1.5 %collective-permute-start.19 = (f32[8,16,512]{2,1,0:T(8,128)S(1)}, f32[8,16,512]{2,1,0:T(8,128)S(1)}, u32[]{:S(2)}, u32[]{:S(2)}) collective-permute-start(f32[8,16,512]{2,1,0:T(8,128)S(1)} %get-tuple-element.44), channel_id=1, source_target_pairs={{0,1},{1,0},{2,3},{3,2},{4,5},{5,4},{6,7},{7,6},{8,9},{9,8},{10,11... | collective-permute-start | bytes 786440 | tf_op jit(solution)/shard_map/ppermute | solution.py:55
  (17 other events, 183.9 us)

commit v10 on v9

--- a/solution.py
+++ b/solution.py
@@ -14,6 +14,7 @@
 QUAD = 4
 RANGE = 32000.0
 STEPS = 256.0
+Z_ORDER = ((0, 3, 1, 2), (0, 2, 3, 1))
 
 eps = 1e-05
 floor_score = -1e30
@@ -89,20 +90,15 @@
             at += HEAD_DIM
 
 
-def z_slots(outer):
-    order = list(range(outer - 1, 0, -1))
-    return list(zip([0, *order[-1:], *order[:-1]], [0, *order]))
-
-
 def z_distance(slot, core):
-    return jnp.where(core == 0, slot[0], slot[1])
+    return jnp.where(core == 0, Z_ORDER[0][slot], Z_ORDER[1][slot])
 
 
 def route_kernel(outer, kv_ref, other_ref, *outs):
     me = lax.axis_index("seq")
     z, y = me // QUAD, (me // 2) % 2
     keys = kv_ref.shape[1]
-    for slot, out in zip(z_slots(outer), outs):
+    for slot, out in enumerate(outs):
         k = z_distance(slot, me % 2)
         head = 2 * jnp.bitwise_xor(z, k) + y
         cols = pl.ds(pl.multiple_of(head * HEAD_DIM, HEAD_DIM), HEAD_DIM)
@@ -113,13 +109,13 @@
 def cache_kernel(outer, keys, *refs):
     firsts, rests, out_ref = refs[:outer], refs[outer : 2 * outer], refs[2 * outer]
     core = lax.axis_index("seq") % 2
-    for i, slot in enumerate(z_slots(outer)):
+    for i in range(outer):
         at = 4 * i * keys
         for at_core in range(2):
 
             @pl.when(core == at_core)
             def _():
-                out_ref[at : at + keys, :] = firsts[slot[at_core]][0:keys, :]
+                out_ref[at : at + keys, :] = firsts[Z_ORDER[at_core][i]][0:keys, :]
 
         out_ref[at + keys : at + 4 * keys, :] = rests[i][...]
 
@@ -280,7 +276,7 @@
     core = lax.axis_index("seq") % 2
     masks = [
         line_mask(wide, ref, z_distance(slot, core))
-        for slot in z_slots(outer)
+        for slot in range(outer)
         for ref in (line_ref, other_ref)
     ]
     top, total, accum_ref[...] = combined(span_states(q_ref, cache_ref, masks))
@@ -296,7 +292,7 @@
     core = 1 - lax.axis_index("seq") % 2
     masks = [
         line_mask(wide, ref, z_distance(slot, core))
-        for slot in z_slots(outer)
+        for slot in range(outer)
         for ref in (core_ref, far_ref)
     ]
     states = span_states(q_ref, cache_ref, masks)
@@ -380,8 +376,8 @@
 def z_routed(parts):
     size = lax.axis_size("seq")
     return [parts[0]] + [
-        lax.ppermute(part, "seq", [(i, i ^ QUAD * slot[i % 2]) for i in range(size)])
-        for slot, part in list(zip(z_slots(len(parts)), parts))[1:]
+        lax.ppermute(part, "seq", [(i, i ^ QUAD * Z_ORDER[i % 2][slot]) for i in range(size)])
+        for slot, part in list(enumerate(parts))[1:]
     ]
 
 

time: 67.2 us -> 66.1 us (0.984)
  waiting for transfers between devices: 24.3 us -> 21.4 us
  starting transfers between devices: 18.9 us -> 20.9 us
    ppermute x6, waiting for transfers between devices: 8.07 us -> 5.59 us  [z_routed(): lax.ppermute(part, 'seq', [(i, i ^ QUAD * Z_ORDER[i % 2][slot]) for i in...]
    ppermute x6, starting transfers between devices: 7.09 us -> 8.91 us  [z_routed(): lax.ppermute(part, 'seq', [(i, i ^ QUAD * Z_ORDER[i % 2][slot]) for i in...]
  transfers between devices with their start and end apart: 20 -> 20, of which waited for: 15 -> 14; matrix products, arithmetic and copies ran while one was open for 0% -> 0% of each run, Pallas kernels for 5% -> 5%
where the time goes in v10:
time: 66.1 us; the launch traced here: 65.8 us
  waiting for transfers between devices  21.4 us (32%)
  starting transfers between devices  20.9 us (32%)
  Pallas kernels  11.3 us (17%)
  blocking collectives  10.7 us (16%)
  local copies, waits for them, and re-layouts  1.18 us (2%)
    ppermute x14, waiting for transfers between devices, swap(): return lax.ppermute(x, 'seq', [(i, i ^ distance) for i in range(size)])  15.8 us
    ppermute x14, starting transfers between devices, swap(): return lax.ppermute(x, 'seq', [(i, i ^ distance) for i in range(size)])  12 us
    pallas_call x15, Pallas kernels, call(): pl.pallas_call(kernel, out_shape=outs, in_specs=[VMEM] * count + [pl.Bloc...  11.3 us
    all_to_all x1, blocking collectives, to_members(): lax.all_to_all(parts, 'seq', 0, 0, axis_index_groups=groups, tiled=True)  10.7 us
    ppermute x6, starting transfers between devices, z_routed(): lax.ppermute(part, 'seq', [(i, i ^ QUAD * Z_ORDER[i % 2][slot]) for i in...  8.91 us
    ppermute x6, waiting for transfers between devices, z_routed(): lax.ppermute(part, 'seq', [(i, i ^ QUAD * Z_ORDER[i % 2][slot]) for i in...  5.59 us
  transfers between devices with their start and end apart: 20, of which 14 were waited for; matrix products, arithmetic and copies ran while one was open for 0% of the time, Pallas kernels for 5%

profile of v10, /device:TPU:0, one launch (start us, length us, event | category | flops | bytes accessed | tf_op | source)
XLA Modules:
  0.0 65.8 jit_solution(3127298601913534884)
XLA Ops:
  1.2 3.0 %collective-permute-start.6 = (bf16[256,512]{1,0:T(8,128)(2,1)S(1)}, bf16[256,512]{1,0:T(8,128)(2,1)S(1)}, u32[]{:S(2)}, u32[]{:S(2)}) collective-permute-start(bf16[256,512]{1,0:T(8,128)(2,1)S(1)} %get-tuple-element.29), channel_id=1, source_target_pairs={{0,2},{1,3},{2,0},{3,1},{4,6},{5,7},{6,4},{7,5},{8,10},{9,11},{10,... | collective-permute-start | bytes 786440 | tf_op jit(solution)/shard_map/ppermute | solution.py:56
  4.2 1.6 %collective-permute-start = (bf16[208,128]{1,0:T(8,128)(2,1)S(1)}, bf16[208,128]{1,0:T(8,128)(2,1)S(1)}, u32[]{:S(2)}, u32[]{:S(2)}) collective-permute-start(bf16[208,128]{1,0:T(8,128)(2,1)S(1)} %get-tuple-element.26), channel_id=1, source_target_pairs={{0,4},{1,5},{2,6},{3,7},{4,0},{5,1},{6,2},{7,3},{8,12},{9,13},{10,... | collective-permute-start | bytes 159752 | tf_op jit(solution)/shard_map/ppermute | solution.py:56
  5.8 2.6 %collective-permute-start.1 = (bf16[208,128]{1,0:T(8,128)(2,1)S(1)}, bf16[208,128]{1,0:T(8,128)(2,1)S(1)}, u32[]{:S(2)}, u32[]{:S(2)}) collective-permute-start(bf16[208,128]{1,0:T(8,128)(2,1)S(1)} %get-tuple-element.27), channel_id=1, source_target_pairs={{0,8},{1,9},{2,10},{3,11},{4,12},{5,13},{6,14},{7,15},{8,0},{9,1},... | collective-permute-start | bytes 159752 | tf_op jit(solution)/shard_map/ppermute | solution.py:56
  8.6 3.0 %collective-permute-done.1.refs_2_ = bf16[208,128]{1,0:T(8,128)(2,1)S(1)} collective-permute-done((bf16[208,128]{1,0:T(8,128)(2,1)S(1)}, bf16[208,128]{1,0:T(8,128)(2,1)S(1)}, u32[]{:S(2)}, u32[]{:S(2)}) %collective-permute-start.1) | collective-permute-done | bytes 53280 | tf_op jit(solution)/shard_map/ppermute | solution.py:56
  11.6 2.7 %collective-permute-done.2.refs_3_ = bf16[208,128]{1,0:T(8,128)(2,1)S(1)} collective-permute-done((bf16[208,128]{1,0:T(8,128)(2,1)S(1)}, bf16[208,128]{1,0:T(8,128)(2,1)S(1)}, u32[]{:S(2)}, u32[]{:S(2)}) %collective-permute-start.2) | collective-permute-done | bytes 53280 | tf_op jit(solution)/shard_map/ppermute | solution.py:56
  16.1 3.4 %collective-permute-start.9 = (bf16[384,128]{1,0:T(8,128)(2,1)S(1)}, bf16[384,128]{1,0:T(8,128)(2,1)S(1)}, u32[]{:S(2)}, u32[]{:S(2)}) collective-permute-start(bf16[384,128]{1,0:T(8,128)(2,1)S(1)} %get-tuple-element.33), channel_id=1, source_target_pairs={{0,8},{1,5},{2,10},{3,7},{4,12},{5,1},{6,14},{7,3},{8,0},{9,13},{1... | collective-permute-start | bytes 294920 | tf_op jit(solution)/shard_map/ppermute | solution.py:379
  21.0 1.3 %shard_map.103.refs_8_.refs_0_ = bf16[16,512]{1,0:T(8,128)(2,1)S(1)} custom-call(bf16[16,2560]{1,0:T(8,128)(2,1)S(1)} %shard_map.102.refs_0_.refs_2_, bf16[16,2560]{1,0:T(8,128)(2,1)S(1)} %collective-permute-done.3.refs_1_.refs_5_, bf16[16,2560]{1,0:T(8,128)(2,1)S(1)} %collective-permute-done.4.refs_2_.refs_3_, ...), custom_call_target="tpu_custom_call" | custom-call | tf_op jit(solution)/shard_map/pallas_call | solution.py:33
  22.3 1.6 %collective-permute-done.9.refs_7_ = bf16[384,128]{1,0:T(8,128)(2,1)S(1)} collective-permute-done((bf16[384,128]{1,0:T(8,128)(2,1)S(1)}, bf16[384,128]{1,0:T(8,128)(2,1)S(1)}, u32[]{:S(2)}, u32[]{:S(2)}) %collective-permute-start.9) | collective-permute-done | bytes 98336 | tf_op jit(solution)/shard_map/ppermute | solution.py:379
  24.5 1.4 %collective-permute-done.10.refs_4_ = bf16[2048,128]{1,0:T(8,128)(2,1)S(1)} collective-permute-done((bf16[2048,128]{1,0:T(8,128)(2,1)S(1)}, bf16[2048,128]{1,0:T(8,128)(2,1)S(1)}, u32[]{:S(2)}, u32[]{:S(2)}) %collective-permute-start.10) | collective-permute-done | bytes 524320 | tf_op jit(solution)/shard_map/ppermute | solution.py:56
  25.9 1.2 %shard_map.107 = (bf16[16,512]{1,0:T(8,128)(2,1)S(1)}, f32[16,4096]{1,0:T(8,128)S(1)}) custom-call(bf16[16,512]{1,0:T(8,128)(2,1)S(1)} %shard_map.103.refs_8_.refs_0_, f32[64,128]{1,0:T(8,128)S(1)} %get-tuple-element.34.refs_1_, f32[64,128]{1,0:T(8,128)S(1)} %get-tuple-element.35.refs_2_, f32[64,128]{1,0:T(8,128)S(1)} %get-tuple-element.36.refs_3_, ...), custom_call_target="tpu_custom_call" | custom-call | tf_op jit(solution)/shard_map/pallas_call | solution.py:33
  28.8 1.6 %collective-permute-start.12 = (s16[16,2176]{1,0:T(8,128)(2,1)S(1)}, s16[16,2176]{1,0:T(8,128)(2,1)S(1)}, u32[]{:S(2)}, u32[]{:S(2)}) collective-permute-start(s16[16,2176]{1,0:T(8,128)(2,1)S(1)} %get-tuple-element.40), channel_id=1, source_target_pairs={{0,2},{1,3},{2,0},{3,1},{4,6},{5,7},{6,4},{7,5},{8,10},{9,11},{10,... | collective-permute-start | bytes 208904 | tf_op jit(solution)/shard_map/ppermute | solution.py:56
  30.4 2.8 %collective-permute-done.12.refs_1_ = s16[16,2176]{1,0:T(8,128)(2,1)S(1)} collective-permute-done((s16[16,2176]{1,0:T(8,128)(2,1)S(1)}, s16[16,2176]{1,0:T(8,128)(2,1)S(1)}, u32[]{:S(2)}, u32[]{:S(2)}) %collective-permute-start.12) | collective-permute-done | bytes 69664 | tf_op jit(solution)/shard_map/ppermute | solution.py:56
  33.4 0.9 %collective-permute-start.13 = (s16[16,2176]{1,0:T(8,128)(2,1)S(1)}, s16[16,2176]{1,0:T(8,128)(2,1)S(1)}, u32[]{:S(2)}, u32[]{:S(2)}) collective-permute-start(s16[16,2176]{1,0:T(8,128)(2,1)S(1)} %shard_map.110.refs_1_), channel_id=1, source_target_pairs={{0,12},{1,9},{2,14},{3,11},{4,8},{5,13},{6,10},{7,15},{8,4},{9,1},... | collective-permute-start | bytes 208904 | tf_op jit(solution)/shard_map/ppermute | solution.py:379
  34.3 1.0 %collective-permute-start.14 = (s16[16,2176]{1,0:T(8,128)(2,1)S(1)}, s16[16,2176]{1,0:T(8,128)(2,1)S(1)}, u32[]{:S(2)}, u32[]{:S(2)}) collective-permute-start(s16[16,2176]{1,0:T(8,128)(2,1)S(1)} %shard_map.110.refs_1_), channel_id=1, source_target_pairs={{0,4},{1,13},{2,6},{3,15},{4,0},{5,9},{6,2},{7,11},{8,12},{9,5},{1... | collective-permute-start | bytes 208904 | tf_op jit(solution)/shard_map/ppermute | solution.py:379
  35.3 2.6 %collective-permute-start.15 = (s16[16,2176]{1,0:T(8,128)(2,1)S(1)}, s16[16,2176]{1,0:T(8,128)(2,1)S(1)}, u32[]{:S(2)}, u32[]{:S(2)}) collective-permute-start(s16[16,2176]{1,0:T(8,128)(2,1)S(1)} %shard_map.110.refs_1_), channel_id=1, source_target_pairs={{0,8},{1,5},{2,10},{3,7},{4,12},{5,1},{6,14},{7,3},{8,0},{9,13},{1... | collective-permute-start | bytes 208904 | tf_op jit(solution)/shard_map/ppermute | solution.py:379
  37.9 2.2 %collective-permute-done.13.refs_2_ = s16[16,2176]{1,0:T(8,128)(2,1)S(1)} collective-permute-done((s16[16,2176]{1,0:T(8,128)(2,1)S(1)}, s16[16,2176]{1,0:T(8,128)(2,1)S(1)}, u32[]{:S(2)}, u32[]{:S(2)}) %collective-permute-start.13) | collective-permute-done | bytes 69664 | tf_op jit(solution)/shard_map/ppermute | solution.py:379
  40.1 1.0 %collective-permute-done.14.refs_3_ = s16[16,2176]{1,0:T(8,128)(2,1)S(1)} collective-permute-done((s16[16,2176]{1,0:T(8,128)(2,1)S(1)}, s16[16,2176]{1,0:T(8,128)(2,1)S(1)}, u32[]{:S(2)}, u32[]{:S(2)}) %collective-permute-start.14) | collective-permute-done | bytes 69664 | tf_op jit(solution)/shard_map/ppermute | solution.py:379
  41.1 0.8 %collective-permute-done.15.refs_4_ = s16[16,2176]{1,0:T(8,128)(2,1)S(1)} collective-permute-done((s16[16,2176]{1,0:T(8,128)(2,1)S(1)}, s16[16,2176]{1,0:T(8,128)(2,1)S(1)}, u32[]{:S(2)}, u32[]{:S(2)}) %collective-permute-start.15) | collective-permute-done | bytes 69664 | tf_op jit(solution)/shard_map/ppermute | solution.py:379
  42.1 1.6 %collective-permute-start.17 = (bf16[16,2048]{1,0:T(8,128)(2,1)S(1)}, bf16[16,2048]{1,0:T(8,128)(2,1)S(1)}, u32[]{:S(2)}, u32[]{:S(2)}) collective-permute-start(bf16[16,2048]{1,0:T(8,128)(2,1)S(1)} %get-tuple-element.42.refs_0_), channel_id=1, source_target_pairs={{0,2},{1,3},{2,0},{3,1},{4,6},{5,7},{6,4},{7,5},{8,10},{9,11},{10,... | collective-permute-start | bytes 196616 | tf_op jit(solution)/shard_map/ppermute | solution.py:56
  43.7 2.7 %collective-permute-done.17.refs_2_ = bf16[16,2048]{1,0:T(8,128)(2,1)S(1)} collective-permute-done((bf16[16,2048]{1,0:T(8,128)(2,1)S(1)}, bf16[16,2048]{1,0:T(8,128)(2,1)S(1)}, u32[]{:S(2)}, u32[]{:S(2)}) %collective-permute-start.17) | collective-permute-done | bytes 65568 | tf_op jit(solution)/shard_map/ppermute | solution.py:56
  46.4 1.2 %collective-permute-done.18.refs_3_ = bf16[16,2048]{1,0:T(8,128)(2,1)S(1)} collective-permute-done((bf16[16,2048]{1,0:T(8,128)(2,1)S(1)}, bf16[16,2048]{1,0:T(8,128)(2,1)S(1)}, u32[]{:S(2)}, u32[]{:S(2)}) %collective-permute-start.18) | collective-permute-done | bytes 65568 | tf_op jit(solution)/shard_map/ppermute | solution.py:56
  47.8 5.1 %shard_map.112 = (bf16[16,896]{1,0:T(8,128)(2,1)S(1)}, f32[8,16,512]{2,1,0:T(8,128)S(1)}) custom-call(bf16[16,2048]{1,0:T(8,128)(2,1)S(1)} %get-tuple-element.42.refs_0_, bf16[16,2048]{1,0:T(8,128)(2,1)S(1)} %collective-permute-done.16.refs_1_, bf16[16,2048]{1,0:T(8,128)(2,1)S(1)} %collective-permute-done.17.refs_2_, ...), custom_call_target="tpu_custom_call" | custom-call | tf_op jit(solution)/shard_map/pallas_call | solution.py:33
  53.1 1.1 %shard_map.113.refs_0_ = f32[8,16,512]{2,1,0:T(8,128)S(1)} custom-call(bf16[16,896]{1,0:T(8,128)(2,1)S(1)} %get-tuple-element.43.refs_0_, bf16[896,8192]{1,0:T(8,128)(2,1)S(1)} %bitcast.2), custom_call_target="tpu_custom_call" | custom-call | tf_op jit(solution)/shard_map/pallas_call | solution.py:33
  54.5 10.7 %all_to_all.5.refs_1_ = bf16[8,16,512]{2,1,0:T(8,128)(2,1)S(1)} all-to-all(bf16[8,16,512]{2,1,0:T(8,128)(2,1)S(1)} %shard_map.114), channel_id=1, replica_groups={{0,2,4,6,8,10,12,14},{1,3,5,7,9,11,13,15},{16,18,20,22,24,26,28,30},{17..., dimensions={0} | all-to-all | bytes 262144 | tf_op jit(solution)/shard_map/all_to_all | solution.py:155
  (83 shorter events, 8.4 us)
Async XLA Ops:
  1.2 13.8 %collective-permute-start.6 = (bf16[256,512]{1,0:T(8,128)(2,1)S(1)}, bf16[256,512]{1,0:T(8,128)(2,1)S(1)}, u32[]{:S(2)}, u32[]{:S(2)}) collective-permute-start(bf16[256,512]{1,0:T(8,128)(2,1)S(1)} %get-tuple-element.29), channel_id=1, source_target_pairs={{0,2},{1,3},{2,0},{3,1},{4,6},{5,7},{6,4},{7,5},{8,10},{9,11},{10,... | collective-permute-start | bytes 786440 | tf_op jit(solution)/shard_map/ppermute | solution.py:56
  4.2 4.4 %collective-permute-start = (bf16[208,128]{1,0:T(8,128)(2,1)S(1)}, bf16[208,128]{1,0:T(8,128)(2,1)S(1)}, u32[]{:S(2)}, u32[]{:S(2)}) collective-permute-start(bf16[208,128]{1,0:T(8,128)(2,1)S(1)} %get-tuple-element.26), channel_id=1, source_target_pairs={{0,4},{1,5},{2,6},{3,7},{4,0},{5,1},{6,2},{7,3},{8,12},{9,13},{10,... | collective-permute-start | bytes 159752 | tf_op jit(solution)/shard_map/ppermute | solution.py:56
  5.8 5.8 %collective-permute-start.1 = (bf16[208,128]{1,0:T(8,128)(2,1)S(1)}, bf16[208,128]{1,0:T(8,128)(2,1)S(1)}, u32[]{:S(2)}, u32[]{:S(2)}) collective-permute-start(bf16[208,128]{1,0:T(8,128)(2,1)S(1)} %get-tuple-element.27), channel_id=1, source_target_pairs={{0,8},{1,9},{2,10},{3,11},{4,12},{5,13},{6,14},{7,15},{8,0},{9,1},... | collective-permute-start | bytes 159752 | tf_op jit(solution)/shard_map/ppermute | solution.py:56
  8.4 5.9 %collective-permute-start.2 = (bf16[208,128]{1,0:T(8,128)(2,1)S(1)}, bf16[208,128]{1,0:T(8,128)(2,1)S(1)}, u32[]{:S(2)}, u32[]{:S(2)}) collective-permute-start(bf16[208,128]{1,0:T(8,128)(2,1)S(1)} %get-tuple-element.28), channel_id=1, source_target_pairs={{0,12},{1,13},{2,14},{3,15},{4,8},{5,9},{6,10},{7,11},{8,4},{9,5},... | collective-permute-start | bytes 159752 | tf_op jit(solution)/shard_map/ppermute | solution.py:56
  14.4 5.1 %collective-permute-start.4 = (bf16[16,2560]{1,0:T(8,128)(2,1)S(1)}, bf16[16,2560]{1,0:T(8,128)(2,1)S(1)}, u32[]{:S(2)}, u32[]{:S(2)}) collective-permute-start(bf16[16,2560]{1,0:T(8,128)(2,1)S(1)} %shard_map.102.refs_0_.refs_2_), channel_id=1, source_target_pairs={{0,2},{1,3},{2,0},{3,1},{4,6},{5,7},{6,4},{7,5},{8,10},{9,11},{10,... | collective-permute-start | bytes 245768 | tf_op jit(solution)/shard_map/ppermute | solution.py:56
  15.1 7.2 %collective-permute-start.7 = (bf16[384,128]{1,0:T(8,128)(2,1)S(1)}, bf16[384,128]{1,0:T(8,128)(2,1)S(1)}, u32[]{:S(2)}, u32[]{:S(2)}) collective-permute-start(bf16[384,128]{1,0:T(8,128)(2,1)S(1)} %get-tuple-element.31), channel_id=1, source_target_pairs={{0,12},{1,9},{2,14},{3,11},{4,8},{5,13},{6,10},{7,15},{8,4},{9,1},... | collective-permute-start | bytes 294920 | tf_op jit(solution)/shard_map/ppermute | solution.py:379
  15.8 6.4 %collective-permute-start.8 = (bf16[384,128]{1,0:T(8,128)(2,1)S(1)}, bf16[384,128]{1,0:T(8,128)(2,1)S(1)}, u32[]{:S(2)}, u32[]{:S(2)}) collective-permute-start(bf16[384,128]{1,0:T(8,128)(2,1)S(1)} %get-tuple-element.32), channel_id=1, source_target_pairs={{0,4},{1,13},{2,6},{3,15},{4,0},{5,9},{6,2},{7,11},{8,12},{9,5},{1... | collective-permute-start | bytes 294920 | tf_op jit(solution)/shard_map/ppermute | solution.py:379
  16.1 7.7 %collective-permute-start.9 = (bf16[384,128]{1,0:T(8,128)(2,1)S(1)}, bf16[384,128]{1,0:T(8,128)(2,1)S(1)}, u32[]{:S(2)}, u32[]{:S(2)}) collective-permute-start(bf16[384,128]{1,0:T(8,128)(2,1)S(1)} %get-tuple-element.33), channel_id=1, source_target_pairs={{0,8},{1,5},{2,10},{3,7},{4,12},{5,1},{6,14},{7,3},{8,0},{9,13},{1... | collective-permute-start | bytes 294920 | tf_op jit(solution)/shard_map/ppermute | solution.py:379
  19.5 1.3 %collective-permute-start.3 = (bf16[16,2560]{1,0:T(8,128)(2,1)S(1)}, bf16[16,2560]{1,0:T(8,128)(2,1)S(1)}, u32[]{:S(2)}, u32[]{:S(2)}) collective-permute-start(bf16[16,2560]{1,0:T(8,128)(2,1)S(1)} %shard_map.102.refs_0_.refs_2_), channel_id=1, source_target_pairs={{0,1},{1,0},{2,3},{3,2},{4,5},{5,4},{6,7},{7,6},{8,9},{9,8},{10,11... | collective-permute-start | bytes 245768 | tf_op jit(solution)/shard_map/ppermute | solution.py:56
  19.5 1.4 %collective-permute-start.5 = (bf16[16,2560]{1,0:T(8,128)(2,1)S(1)}, bf16[16,2560]{1,0:T(8,128)(2,1)S(1)}, u32[]{:S(2)}, u32[]{:S(2)}) collective-permute-start(bf16[16,2560]{1,0:T(8,128)(2,1)S(1)} %collective-permute-done.4.refs_2_.refs_3_), channel_id=1, source_target_pairs={{0,1},{1,0},{2,3},{3,2},{4,5},{5,4},{6,7},{7,6},{8,9},{9,8},{10,11... | collective-permute-start | bytes 245768 | tf_op jit(solution)/shard_map/ppermute | solution.py:56
  23.9 2.0 %collective-permute-start.10 = (bf16[2048,128]{1,0:T(8,128)(2,1)S(1)}, bf16[2048,128]{1,0:T(8,128)(2,1)S(1)}, u32[]{:S(2)}, u32[]{:S(2)}) collective-permute-start(bf16[2048,128]{1,0:T(8,128)(2,1)S(1)} %shard_map.105.refs_1_), channel_id=1, source_target_pairs={{0,1},{1,0},{2,3},{3,2},{4,5},{5,4},{6,7},{7,6},{8,9},{9,8},{10,11... | collective-permute-start | bytes 1572872 | tf_op jit(solution)/shard_map/ppermute | solution.py:56
  27.1 1.5 %collective-permute-start.11 = (f32[16,4096]{1,0:T(8,128)S(1)}, f32[16,4096]{1,0:T(8,128)S(1)}, u32[]{:S(2)}, u32[]{:S(2)}) collective-permute-start(f32[16,4096]{1,0:T(8,128)S(1)} %get-tuple-element.38), channel_id=1, source_target_pairs={{0,1},{1,0},{2,3},{3,2},{4,5},{5,4},{6,7},{7,6},{8,9},{9,8},{10,11... | collective-permute-start | bytes 786440 | tf_op jit(solution)/shard_map/ppermute | solution.py:56
  28.6 19.0 %slice-start.6 = ((s8[14680064]{0:T(1024)(128)(4,1)}), s8[4194304]{0:T(1024)(128)(4,1)S(1)}, s32[]{:S(2)}) async-start(s8[14680064]{0:T(1024)(128)(4,1)} %bitcast.5), calls=%async_computation.7 | async-start | bytes 8388608
  28.6 19.0 %slice-start.7 = ((s8[14680064]{0:T(1024)(128)(4,1)}), s8[4194304]{0:T(1024)(128)(4,1)S(1)}, s32[]{:S(2)}) async-start(s8[14680064]{0:T(1024)(128)(4,1)} %bitcast.5), calls=%async_computation.8 | async-start | bytes 8388608
  28.7 19.0 %slice-start.10 = ((s8[14680064]{0:T(1024)(128)(4,1)}), s8[4194304]{0:T(1024)(128)(4,1)S(1)}, s32[]{:S(2)}) async-start(s8[14680064]{0:T(1024)(128)(4,1)} %bitcast.7), calls=%async_computation.11 | async-start | bytes 8388608
  28.7 19.0 %slice-start.11 = ((s8[14680064]{0:T(1024)(128)(4,1)}), s8[4194304]{0:T(1024)(128)(4,1)S(1)}, s32[]{:S(2)}) async-start(s8[14680064]{0:T(1024)(128)(4,1)} %bitcast.7), calls=%async_computation.12 | async-start | bytes 8388608
  28.8 4.4 %collective-permute-start.12 = (s16[16,2176]{1,0:T(8,128)(2,1)S(1)}, s16[16,2176]{1,0:T(8,128)(2,1)S(1)}, u32[]{:S(2)}, u32[]{:S(2)}) collective-permute-start(s16[16,2176]{1,0:T(8,128)(2,1)S(1)} %get-tuple-element.40), channel_id=1, source_target_pairs={{0,2},{1,3},{2,0},{3,1},{4,6},{5,7},{6,4},{7,5},{8,10},{9,11},{10,... | collective-permute-start | bytes 208904 | tf_op jit(solution)/shard_map/ppermute | solution.py:56
  33.4 6.6 %collective-permute-start.13 = (s16[16,2176]{1,0:T(8,128)(2,1)S(1)}, s16[16,2176]{1,0:T(8,128)(2,1)S(1)}, u32[]{:S(2)}, u32[]{:S(2)}) collective-permute-start(s16[16,2176]{1,0:T(8,128)(2,1)S(1)} %shard_map.110.refs_1_), channel_id=1, source_target_pairs={{0,12},{1,9},{2,14},{3,11},{4,8},{5,13},{6,10},{7,15},{8,4},{9,1},... | collective-permute-start | bytes 208904 | tf_op jit(solution)/shard_map/ppermute | solution.py:379
  34.3 6.8 %collective-permute-start.14 = (s16[16,2176]{1,0:T(8,128)(2,1)S(1)}, s16[16,2176]{1,0:T(8,128)(2,1)S(1)}, u32[]{:S(2)}, u32[]{:S(2)}) collective-permute-start(s16[16,2176]{1,0:T(8,128)(2,1)S(1)} %shard_map.110.refs_1_), channel_id=1, source_target_pairs={{0,4},{1,13},{2,6},{3,15},{4,0},{5,9},{6,2},{7,11},{8,12},{9,5},{1... | collective-permute-start | bytes 208904 | tf_op jit(solution)/shard_map/ppermute | solution.py:379
  35.3 6.6 %collective-permute-start.15 = (s16[16,2176]{1,0:T(8,128)(2,1)S(1)}, s16[16,2176]{1,0:T(8,128)(2,1)S(1)}, u32[]{:S(2)}, u32[]{:S(2)}) collective-permute-start(s16[16,2176]{1,0:T(8,128)(2,1)S(1)} %shard_map.110.refs_1_), channel_id=1, source_target_pairs={{0,8},{1,5},{2,10},{3,7},{4,12},{5,1},{6,14},{7,3},{8,0},{9,13},{1... | collective-permute-start | bytes 208904 | tf_op jit(solution)/shard_map/ppermute | solution.py:379
  42.1 4.3 %collective-permute-start.17 = (bf16[16,2048]{1,0:T(8,128)(2,1)S(1)}, bf16[16,2048]{1,0:T(8,128)(2,1)S(1)}, u32[]{:S(2)}, u32[]{:S(2)}) collective-permute-start(bf16[16,2048]{1,0:T(8,128)(2,1)S(1)} %get-tuple-element.42.refs_0_), channel_id=1, source_target_pairs={{0,2},{1,3},{2,0},{3,1},{4,6},{5,7},{6,4},{7,5},{8,10},{9,11},{10,... | collective-permute-start | bytes 196616 | tf_op jit(solution)/shard_map/ppermute | solution.py:56
  43.6 2.8 %collective-permute-start.16 = (bf16[16,2048]{1,0:T(8,128)(2,1)S(1)}, bf16[16,2048]{1,0:T(8,128)(2,1)S(1)}, u32[]{:S(2)}, u32[]{:S(2)}) collective-permute-start(bf16[16,2048]{1,0:T(8,128)(2,1)S(1)} %get-tuple-element.42.refs_0_), channel_id=1, source_target_pairs={{0,1},{1,0},{2,3},{3,2},{4,5},{5,4},{6,7},{7,6},{8,9},{9,8},{10,11... | collective-permute-start | bytes 196616 | tf_op jit(solution)/shard_map/ppermute | solution.py:56
  46.4 1.3 %collective-permute-start.18 = (bf16[16,2048]{1,0:T(8,128)(2,1)S(1)}, bf16[16,2048]{1,0:T(8,128)(2,1)S(1)}, u32[]{:S(2)}, u32[]{:S(2)}) collective-permute-start(bf16[16,2048]{1,0:T(8,128)(2,1)S(1)} %collective-permute-done.17.refs_2_), channel_id=1, source_target_pairs={{0,1},{1,0},{2,3},{3,2},{4,5},{5,4},{6,7},{7,6},{8,9},{9,8},{10,11... | collective-permute-start | bytes 196616 | tf_op jit(solution)/shard_map/ppermute | solution.py:56
  52.9 1.5 %collective-permute-start.19 = (f32[8,16,512]{2,1,0:T(8,128)S(1)}, f32[8,16,512]{2,1,0:T(8,128)S(1)}, u32[]{:S(2)}, u32[]{:S(2)}) collective-permute-start(f32[8,16,512]{2,1,0:T(8,128)S(1)} %get-tuple-element.44), channel_id=1, source_target_pairs={{0,1},{1,0},{2,3},{3,2},{4,5},{5,4},{6,7},{7,6},{8,9},{9,8},{10,11... | collective-permute-start | bytes 786440 | tf_op jit(solution)/shard_map/ppermute | solution.py:56
  (17 other events, 182.9 us)

commit v11 on v10

--- a/solution.py
+++ b/solution.py
@@ -223,8 +223,8 @@
     scatter_dot(wide, False, left_ref[...], w_ref, out_ref)
 
 
-def keep_line_kernel(wide, left_ref, w_ref, out_ref):
-    line_dot(wide, (0, 2), left_ref[...], w_ref, out_ref)
+def line_kernel(wide, near, left_ref, w_ref, out_ref):
+    line_dot(wide, (near,), left_ref[...], w_ref, out_ref)
 
 
 def span_states(q_ref, cache_ref, masks):
@@ -301,7 +301,7 @@
     attended = (accum / total).astype(bf16)
     attended = jnp.concatenate([attended[h * rows : (h + 1) * rows] for h in range(heads)], axis=1)
     left_ref[...] = attended
-    line_dot(wide, (1, 3), attended, w_ref, send_ref)
+    line_dot(wide, (3,), attended, w_ref, send_ref)
 
 
 def hidden_kernel(wide, *refs):
@@ -338,14 +338,12 @@
     return ref[:, 0:wide].astype(jnp.int32).astype(f32) * scale
 
 
-def chip_kernel(own_ref, recv_ref, keep_ref, send_ref):
-    half = own_ref.shape[1] // 2
-    keep_ref[...] = own_ref[:, :half] + recv_ref[:, :half]
-    coded(send_ref, own_ref[:, half:] + recv_ref[:, half:])
-
-
-def pair_kernel(keep_ref, recv_ref, out_ref):
-    coded(out_ref, keep_ref[...] + decoded(recv_ref))
+def chip_kernel(own_ref, core_ref, out_ref):
+    coded(out_ref, own_ref[...] + core_ref[...])
+
+
+def pair_kernel(own_ref, core_ref, y_ref, out_ref):
+    coded(out_ref, own_ref[...] + core_ref[...] + decoded(y_ref))
 
 
 def stream_kernel(wide, x_ref, *refs):
@@ -388,13 +386,16 @@
 
 
 def updated(x_line, send, left, weight, wide, beside):
-    rows, columns = send.shape
-    half = columns // 2
+    rows, half = send.shape
+    line = like((rows, half), f32)
     code = like((rows, half + HEAD_DIM), jnp.int16)
     far = swap(send, 1)
-    own = call(functools.partial(keep_line_kernel, wide), like(send.shape, f32), [left, weight])
-    keep, send = call(chip_kernel, [like((rows, half), f32), code], [own, far], beside)
-    sums = call(pair_kernel, code, [keep, swap(send, 2)], beside)
+    second = call(functools.partial(line_kernel, wide, 2), line, [left, weight])
+    second = call(chip_kernel, code, [second, far])
+    arrived = swap(second, 2)
+    core = swap(call(functools.partial(line_kernel, wide, 1), line, [left, weight]), 1)
+    own = call(functools.partial(line_kernel, wide, 0), line, [left, weight], [second])
+    sums = call(pair_kernel, code, [own, core, arrived], beside * 2)
     return call(
         functools.partial(stream_kernel, wide),
         [like((rows, half), bf16), like((rows, wide), bf16)],
@@ -459,7 +460,7 @@
     )
     left, send = call(
         functools.partial(attend_kernel, outer, wide),
-        [like((rows, columns), bf16), like((rows, 2 * outer * wide), f32)],
+        [like((rows, columns), bf16), like((rows, outer * wide), f32)],
         [queries, *early, far_cache, *x_parts[1::2], o_weight],
     )
     line, stream = updated(x_parts[0], send, left, o_weight, wide, beside)

time: 66.1 us -> 65.5 us (level)
  waiting for transfers between devices: 21.4 us -> 20.2 us
    ppermute x14 -> x15, waiting for transfers between devices: 15.8 us -> 14.6 us  [swap(): return lax.ppermute(x, 'seq', [(i, i ^ distance) for i in range(size)])]
    ppermute x14 -> x15, starting transfers between devices: 12 us -> 12.4 us  [swap(): return lax.ppermute(x, 'seq', [(i, i ^ distance) for i in range(size)])]
    pallas_call x15 -> x17, Pallas kernels: 11.3 us -> 11.5 us  [call(): pl.pallas_call(kernel, out_shape=outs, in_specs=[VMEM] * count + [pl.Bloc...]
  transfers between devices with their start and end apart: 20 -> 21, of which waited for: 14 -> 14; matrix products, arithmetic and copies ran while one was open for 0% -> 0% of each run, Pallas kernels for 5% -> 6%
where the time goes in v11:
time: 65.5 us; the launch traced here: 65.3 us
  starting transfers between devices  21.3 us (33%)
  waiting for transfers between devices  20.2 us (31%)
  Pallas kernels  11.5 us (18%)
  blocking collectives  10.7 us (16%)
  local copies, waits for them, and re-layouts  1.2 us (2%)
    ppermute x15, waiting for transfers between devices, swap(): return lax.ppermute(x, 'seq', [(i, i ^ distance) for i in range(size)])  14.6 us
    ppermute x15, starting transfers between devices, swap(): return lax.ppermute(x, 'seq', [(i, i ^ distance) for i in range(size)])  12.4 us
    pallas_call x17, Pallas kernels, call(): pl.pallas_call(kernel, out_shape=outs, in_specs=[VMEM] * count + [pl.Bloc...  11.5 us
    all_to_all x1, blocking collectives, to_members(): lax.all_to_all(parts, 'seq', 0, 0, axis_index_groups=groups, tiled=True)  10.7 us
    ppermute x6, starting transfers between devices, z_routed(): lax.ppermute(part, 'seq', [(i, i ^ QUAD * Z_ORDER[i % 2][slot]) for i in...  8.91 us
    ppermute x6, waiting for transfers between devices, z_routed(): lax.ppermute(part, 'seq', [(i, i ^ QUAD * Z_ORDER[i % 2][slot]) for i in...  5.6 us
  transfers between devices with their start and end apart: 21, of which 14 were waited for; matrix products, arithmetic and copies ran while one was open for 0% of the time, Pallas kernels for 6%

profile of v11, /device:TPU:0, one launch (start us, length us, event | category | flops | bytes accessed | tf_op | source)
XLA Modules:
  0.0 65.3 jit_solution(18146118178932971720)
XLA Ops:
  1.2 3.0 %collective-permute-start.6 = (bf16[256,512]{1,0:T(8,128)(2,1)S(1)}, bf16[256,512]{1,0:T(8,128)(2,1)S(1)}, u32[]{:S(2)}, u32[]{:S(2)}) collective-permute-start(bf16[256,512]{1,0:T(8,128)(2,1)S(1)} %get-tuple-element.27), channel_id=1, source_target_pairs={{0,2},{1,3},{2,0},{3,1},{4,6},{5,7},{6,4},{7,5},{8,10},{9,11},{10,... | collective-permute-start | bytes 786440 | tf_op jit(solution)/shard_map/ppermute | solution.py:56
  4.2 1.6 %collective-permute-start = (bf16[208,128]{1,0:T(8,128)(2,1)S(1)}, bf16[208,128]{1,0:T(8,128)(2,1)S(1)}, u32[]{:S(2)}, u32[]{:S(2)}) collective-permute-start(bf16[208,128]{1,0:T(8,128)(2,1)S(1)} %get-tuple-element.24), channel_id=1, source_target_pairs={{0,4},{1,5},{2,6},{3,7},{4,0},{5,1},{6,2},{7,3},{8,12},{9,13},{10,... | collective-permute-start | bytes 159752 | tf_op jit(solution)/shard_map/ppermute | solution.py:56
  5.8 2.6 %collective-permute-start.1 = (bf16[208,128]{1,0:T(8,128)(2,1)S(1)}, bf16[208,128]{1,0:T(8,128)(2,1)S(1)}, u32[]{:S(2)}, u32[]{:S(2)}) collective-permute-start(bf16[208,128]{1,0:T(8,128)(2,1)S(1)} %get-tuple-element.25), channel_id=1, source_target_pairs={{0,8},{1,9},{2,10},{3,11},{4,12},{5,13},{6,14},{7,15},{8,0},{9,1},... | collective-permute-start | bytes 159752 | tf_op jit(solution)/shard_map/ppermute | solution.py:56
  8.6 3.0 %collective-permute-done.1.refs_2_ = bf16[208,128]{1,0:T(8,128)(2,1)S(1)} collective-permute-done((bf16[208,128]{1,0:T(8,128)(2,1)S(1)}, bf16[208,128]{1,0:T(8,128)(2,1)S(1)}, u32[]{:S(2)}, u32[]{:S(2)}) %collective-permute-start.1) | collective-permute-done | bytes 53280 | tf_op jit(solution)/shard_map/ppermute | solution.py:56
  11.6 2.7 %collective-permute-done.2.refs_3_ = bf16[208,128]{1,0:T(8,128)(2,1)S(1)} collective-permute-done((bf16[208,128]{1,0:T(8,128)(2,1)S(1)}, bf16[208,128]{1,0:T(8,128)(2,1)S(1)}, u32[]{:S(2)}, u32[]{:S(2)}) %collective-permute-start.2) | collective-permute-done | bytes 53280 | tf_op jit(solution)/shard_map/ppermute | solution.py:56
  16.1 3.4 %collective-permute-start.9 = (bf16[384,128]{1,0:T(8,128)(2,1)S(1)}, bf16[384,128]{1,0:T(8,128)(2,1)S(1)}, u32[]{:S(2)}, u32[]{:S(2)}) collective-permute-start(bf16[384,128]{1,0:T(8,128)(2,1)S(1)} %get-tuple-element.31), channel_id=1, source_target_pairs={{0,8},{1,5},{2,10},{3,7},{4,12},{5,1},{6,14},{7,3},{8,0},{9,13},{1... | collective-permute-start | bytes 294920 | tf_op jit(solution)/shard_map/ppermute | solution.py:377
  21.0 1.3 %shard_map.103.refs_8_.refs_0_ = bf16[16,512]{1,0:T(8,128)(2,1)S(1)} custom-call(bf16[16,2560]{1,0:T(8,128)(2,1)S(1)} %shard_map.102.refs_0_.refs_2_, bf16[16,2560]{1,0:T(8,128)(2,1)S(1)} %collective-permute-done.3.refs_1_.refs_5_, bf16[16,2560]{1,0:T(8,128)(2,1)S(1)} %collective-permute-done.4.refs_2_.refs_3_, ...), custom_call_target="tpu_custom_call" | custom-call | tf_op jit(solution)/shard_map/pallas_call | solution.py:33
  22.3 1.6 %collective-permute-done.9.refs_7_ = bf16[384,128]{1,0:T(8,128)(2,1)S(1)} collective-permute-done((bf16[384,128]{1,0:T(8,128)(2,1)S(1)}, bf16[384,128]{1,0:T(8,128)(2,1)S(1)}, u32[]{:S(2)}, u32[]{:S(2)}) %collective-permute-start.9) | collective-permute-done | bytes 98336 | tf_op jit(solution)/shard_map/ppermute | solution.py:377
  24.5 1.4 %collective-permute-done.10.refs_4_ = bf16[2048,128]{1,0:T(8,128)(2,1)S(1)} collective-permute-done((bf16[2048,128]{1,0:T(8,128)(2,1)S(1)}, bf16[2048,128]{1,0:T(8,128)(2,1)S(1)}, u32[]{:S(2)}, u32[]{:S(2)}) %collective-permute-start.10) | collective-permute-done | bytes 524320 | tf_op jit(solution)/shard_map/ppermute | solution.py:56
  25.9 1.0 %shard_map.107 = (bf16[16,512]{1,0:T(8,128)(2,1)S(1)}, f32[16,2048]{1,0:T(8,128)S(1)}) custom-call(bf16[16,512]{1,0:T(8,128)(2,1)S(1)} %shard_map.103.refs_8_.refs_0_, f32[64,128]{1,0:T(8,128)S(1)} %get-tuple-element.32.refs_1_, f32[64,128]{1,0:T(8,128)S(1)} %get-tuple-element.33.refs_2_, f32[64,128]{1,0:T(8,128)S(1)} %get-tuple-element.34.refs_3_, ...), custom_call_target="tpu_custom_call" | custom-call | tf_op jit(solution)/shard_map/pallas_call | solution.py:33
  28.3 1.6 %collective-permute-start.13 = (s16[16,2176]{1,0:T(8,128)(2,1)S(1)}, s16[16,2176]{1,0:T(8,128)(2,1)S(1)}, u32[]{:S(2)}, u32[]{:S(2)}) collective-permute-start(s16[16,2176]{1,0:T(8,128)(2,1)S(1)} %shard_map.109.refs_2_), channel_id=1, source_target_pairs={{0,2},{1,3},{2,0},{3,1},{4,6},{5,7},{6,4},{7,5},{8,10},{9,11},{10,... | collective-permute-start | bytes 208904 | tf_op jit(solution)/shard_map/ppermute | solution.py:56
  30.4 2.3 %collective-permute-done.13.refs_2_ = s16[16,2176]{1,0:T(8,128)(2,1)S(1)} collective-permute-done((s16[16,2176]{1,0:T(8,128)(2,1)S(1)}, s16[16,2176]{1,0:T(8,128)(2,1)S(1)}, u32[]{:S(2)}, u32[]{:S(2)}) %collective-permute-start.13) | collective-permute-done | bytes 69664 | tf_op jit(solution)/shard_map/ppermute | solution.py:56
  32.9 0.9 %collective-permute-start.14 = (s16[16,2176]{1,0:T(8,128)(2,1)S(1)}, s16[16,2176]{1,0:T(8,128)(2,1)S(1)}, u32[]{:S(2)}, u32[]{:S(2)}) collective-permute-start(s16[16,2176]{1,0:T(8,128)(2,1)S(1)} %shard_map.112.refs_1_), channel_id=1, source_target_pairs={{0,12},{1,9},{2,14},{3,11},{4,8},{5,13},{6,10},{7,15},{8,4},{9,1},... | collective-permute-start | bytes 208904 | tf_op jit(solution)/shard_map/ppermute | solution.py:377
  33.8 1.0 %collective-permute-start.15 = (s16[16,2176]{1,0:T(8,128)(2,1)S(1)}, s16[16,2176]{1,0:T(8,128)(2,1)S(1)}, u32[]{:S(2)}, u32[]{:S(2)}) collective-permute-start(s16[16,2176]{1,0:T(8,128)(2,1)S(1)} %shard_map.112.refs_1_), channel_id=1, source_target_pairs={{0,4},{1,13},{2,6},{3,15},{4,0},{5,9},{6,2},{7,11},{8,12},{9,5},{1... | collective-permute-start | bytes 208904 | tf_op jit(solution)/shard_map/ppermute | solution.py:377
  34.7 2.6 %collective-permute-start.16 = (s16[16,2176]{1,0:T(8,128)(2,1)S(1)}, s16[16,2176]{1,0:T(8,128)(2,1)S(1)}, u32[]{:S(2)}, u32[]{:S(2)}) collective-permute-start(s16[16,2176]{1,0:T(8,128)(2,1)S(1)} %shard_map.112.refs_1_), channel_id=1, source_target_pairs={{0,8},{1,5},{2,10},{3,7},{4,12},{5,1},{6,14},{7,3},{8,0},{9,13},{1... | collective-permute-start | bytes 208904 | tf_op jit(solution)/shard_map/ppermute | solution.py:377
  37.3 2.2 %collective-permute-done.14.refs_2_ = s16[16,2176]{1,0:T(8,128)(2,1)S(1)} collective-permute-done((s16[16,2176]{1,0:T(8,128)(2,1)S(1)}, s16[16,2176]{1,0:T(8,128)(2,1)S(1)}, u32[]{:S(2)}, u32[]{:S(2)}) %collective-permute-start.14) | collective-permute-done | bytes 69664 | tf_op jit(solution)/shard_map/ppermute | solution.py:377
  39.5 1.0 %collective-permute-done.15.refs_3_ = s16[16,2176]{1,0:T(8,128)(2,1)S(1)} collective-permute-done((s16[16,2176]{1,0:T(8,128)(2,1)S(1)}, s16[16,2176]{1,0:T(8,128)(2,1)S(1)}, u32[]{:S(2)}, u32[]{:S(2)}) %collective-permute-start.15) | collective-permute-done | bytes 69664 | tf_op jit(solution)/shard_map/ppermute | solution.py:377
  40.5 0.8 %collective-permute-done.16.refs_4_ = s16[16,2176]{1,0:T(8,128)(2,1)S(1)} collective-permute-done((s16[16,2176]{1,0:T(8,128)(2,1)S(1)}, s16[16,2176]{1,0:T(8,128)(2,1)S(1)}, u32[]{:S(2)}, u32[]{:S(2)}) %collective-permute-start.16) | collective-permute-done | bytes 69664 | tf_op jit(solution)/shard_map/ppermute | solution.py:377
  41.5 1.6 %collective-permute-start.18 = (bf16[16,2048]{1,0:T(8,128)(2,1)S(1)}, bf16[16,2048]{1,0:T(8,128)(2,1)S(1)}, u32[]{:S(2)}, u32[]{:S(2)}) collective-permute-start(bf16[16,2048]{1,0:T(8,128)(2,1)S(1)} %get-tuple-element.38.refs_0_), channel_id=1, source_target_pairs={{0,2},{1,3},{2,0},{3,1},{4,6},{5,7},{6,4},{7,5},{8,10},{9,11},{10,... | collective-permute-start | bytes 196616 | tf_op jit(solution)/shard_map/ppermute | solution.py:56
  43.1 2.7 %collective-permute-done.18.refs_2_ = bf16[16,2048]{1,0:T(8,128)(2,1)S(1)} collective-permute-done((bf16[16,2048]{1,0:T(8,128)(2,1)S(1)}, bf16[16,2048]{1,0:T(8,128)(2,1)S(1)}, u32[]{:S(2)}, u32[]{:S(2)}) %collective-permute-start.18) | collective-permute-done | bytes 65568 | tf_op jit(solution)/shard_map/ppermute | solution.py:56
  45.9 1.2 %collective-permute-done.19.refs_3_ = bf16[16,2048]{1,0:T(8,128)(2,1)S(1)} collective-permute-done((bf16[16,2048]{1,0:T(8,128)(2,1)S(1)}, bf16[16,2048]{1,0:T(8,128)(2,1)S(1)}, u32[]{:S(2)}, u32[]{:S(2)}) %collective-permute-start.19) | collective-permute-done | bytes 65568 | tf_op jit(solution)/shard_map/ppermute | solution.py:56
  47.2 5.1 %shard_map.114 = (bf16[16,896]{1,0:T(8,128)(2,1)S(1)}, f32[8,16,512]{2,1,0:T(8,128)S(1)}) custom-call(bf16[16,2048]{1,0:T(8,128)(2,1)S(1)} %get-tuple-element.38.refs_0_, bf16[16,2048]{1,0:T(8,128)(2,1)S(1)} %collective-permute-done.17.refs_1_, bf16[16,2048]{1,0:T(8,128)(2,1)S(1)} %collective-permute-done.18.refs_2_, ...), custom_call_target="tpu_custom_call" | custom-call | tf_op jit(solution)/shard_map/pallas_call | solution.py:33
  52.5 1.1 %shard_map.115.refs_0_ = f32[8,16,512]{2,1,0:T(8,128)S(1)} custom-call(bf16[16,896]{1,0:T(8,128)(2,1)S(1)} %get-tuple-element.39.refs_0_, bf16[896,8192]{1,0:T(8,128)(2,1)S(1)} %bitcast.4), custom_call_target="tpu_custom_call" | custom-call | tf_op jit(solution)/shard_map/pallas_call | solution.py:33
  53.9 10.7 %all_to_all.5.refs_1_ = bf16[8,16,512]{2,1,0:T(8,128)(2,1)S(1)} all-to-all(bf16[8,16,512]{2,1,0:T(8,128)(2,1)S(1)} %shard_map.116), channel_id=1, replica_groups={{0,2,4,6,8,10,12,14},{1,3,5,7,9,11,13,15},{16,18,20,22,24,26,28,30},{17..., dimensions={0} | all-to-all | bytes 262144 | tf_op jit(solution)/shard_map/all_to_all | solution.py:155
  (87 shorter events, 8.6 us)
Async XLA Ops:
  1.2 13.8 %collective-permute-start.6 = (bf16[256,512]{1,0:T(8,128)(2,1)S(1)}, bf16[256,512]{1,0:T(8,128)(2,1)S(1)}, u32[]{:S(2)}, u32[]{:S(2)}) collective-permute-start(bf16[256,512]{1,0:T(8,128)(2,1)S(1)} %get-tuple-element.27), channel_id=1, source_target_pairs={{0,2},{1,3},{2,0},{3,1},{4,6},{5,7},{6,4},{7,5},{8,10},{9,11},{10,... | collective-permute-start | bytes 786440 | tf_op jit(solution)/shard_map/ppermute | solution.py:56
  4.2 4.4 %collective-permute-start = (bf16[208,128]{1,0:T(8,128)(2,1)S(1)}, bf16[208,128]{1,0:T(8,128)(2,1)S(1)}, u32[]{:S(2)}, u32[]{:S(2)}) collective-permute-start(bf16[208,128]{1,0:T(8,128)(2,1)S(1)} %get-tuple-element.24), channel_id=1, source_target_pairs={{0,4},{1,5},{2,6},{3,7},{4,0},{5,1},{6,2},{7,3},{8,12},{9,13},{10,... | collective-permute-start | bytes 159752 | tf_op jit(solution)/shard_map/ppermute | solution.py:56
  5.8 5.8 %collective-permute-start.1 = (bf16[208,128]{1,0:T(8,128)(2,1)S(1)}, bf16[208,128]{1,0:T(8,128)(2,1)S(1)}, u32[]{:S(2)}, u32[]{:S(2)}) collective-permute-start(bf16[208,128]{1,0:T(8,128)(2,1)S(1)} %get-tuple-element.25), channel_id=1, source_target_pairs={{0,8},{1,9},{2,10},{3,11},{4,12},{5,13},{6,14},{7,15},{8,0},{9,1},... | collective-permute-start | bytes 159752 | tf_op jit(solution)/shard_map/ppermute | solution.py:56
  8.4 5.9 %collective-permute-start.2 = (bf16[208,128]{1,0:T(8,128)(2,1)S(1)}, bf16[208,128]{1,0:T(8,128)(2,1)S(1)}, u32[]{:S(2)}, u32[]{:S(2)}) collective-permute-start(bf16[208,128]{1,0:T(8,128)(2,1)S(1)} %get-tuple-element.26), channel_id=1, source_target_pairs={{0,12},{1,13},{2,14},{3,15},{4,8},{5,9},{6,10},{7,11},{8,4},{9,5},... | collective-permute-start | bytes 159752 | tf_op jit(solution)/shard_map/ppermute | solution.py:56
  14.4 5.1 %collective-permute-start.4 = (bf16[16,2560]{1,0:T(8,128)(2,1)S(1)}, bf16[16,2560]{1,0:T(8,128)(2,1)S(1)}, u32[]{:S(2)}, u32[]{:S(2)}) collective-permute-start(bf16[16,2560]{1,0:T(8,128)(2,1)S(1)} %shard_map.102.refs_0_.refs_2_), channel_id=1, source_target_pairs={{0,2},{1,3},{2,0},{3,1},{4,6},{5,7},{6,4},{7,5},{8,10},{9,11},{10,... | collective-permute-start | bytes 245768 | tf_op jit(solution)/shard_map/ppermute | solution.py:56
  15.1 7.2 %collective-permute-start.7 = (bf16[384,128]{1,0:T(8,128)(2,1)S(1)}, bf16[384,128]{1,0:T(8,128)(2,1)S(1)}, u32[]{:S(2)}, u32[]{:S(2)}) collective-permute-start(bf16[384,128]{1,0:T(8,128)(2,1)S(1)} %get-tuple-element.29), channel_id=1, source_target_pairs={{0,12},{1,9},{2,14},{3,11},{4,8},{5,13},{6,10},{7,15},{8,4},{9,1},... | collective-permute-start | bytes 294920 | tf_op jit(solution)/shard_map/ppermute | solution.py:377
  15.8 6.4 %collective-permute-start.8 = (bf16[384,128]{1,0:T(8,128)(2,1)S(1)}, bf16[384,128]{1,0:T(8,128)(2,1)S(1)}, u32[]{:S(2)}, u32[]{:S(2)}) collective-permute-start(bf16[384,128]{1,0:T(8,128)(2,1)S(1)} %get-tuple-element.30), channel_id=1, source_target_pairs={{0,4},{1,13},{2,6},{3,15},{4,0},{5,9},{6,2},{7,11},{8,12},{9,5},{1... | collective-permute-start | bytes 294920 | tf_op jit(solution)/shard_map/ppermute | solution.py:377
  16.1 7.7 %collective-permute-start.9 = (bf16[384,128]{1,0:T(8,128)(2,1)S(1)}, bf16[384,128]{1,0:T(8,128)(2,1)S(1)}, u32[]{:S(2)}, u32[]{:S(2)}) collective-permute-start(bf16[384,128]{1,0:T(8,128)(2,1)S(1)} %get-tuple-element.31), channel_id=1, source_target_pairs={{0,8},{1,5},{2,10},{3,7},{4,12},{5,1},{6,14},{7,3},{8,0},{9,13},{1... | collective-permute-start | bytes 294920 | tf_op jit(solution)/shard_map/ppermute | solution.py:377
  19.5 1.3 %collective-permute-start.3 = (bf16[16,2560]{1,0:T(8,128)(2,1)S(1)}, bf16[16,2560]{1,0:T(8,128)(2,1)S(1)}, u32[]{:S(2)}, u32[]{:S(2)}) collective-permute-start(bf16[16,2560]{1,0:T(8,128)(2,1)S(1)} %shard_map.102.refs_0_.refs_2_), channel_id=1, source_target_pairs={{0,1},{1,0},{2,3},{3,2},{4,5},{5,4},{6,7},{7,6},{8,9},{9,8},{10,11... | collective-permute-start | bytes 245768 | tf_op jit(solution)/shard_map/ppermute | solution.py:56
  19.5 1.4 %collective-permute-start.5 = (bf16[16,2560]{1,0:T(8,128)(2,1)S(1)}, bf16[16,2560]{1,0:T(8,128)(2,1)S(1)}, u32[]{:S(2)}, u32[]{:S(2)}) collective-permute-start(bf16[16,2560]{1,0:T(8,128)(2,1)S(1)} %collective-permute-done.4.refs_2_.refs_3_), channel_id=1, source_target_pairs={{0,1},{1,0},{2,3},{3,2},{4,5},{5,4},{6,7},{7,6},{8,9},{9,8},{10,11... | collective-permute-start | bytes 245768 | tf_op jit(solution)/shard_map/ppermute | solution.py:56
  23.9 2.0 %collective-permute-start.10 = (bf16[2048,128]{1,0:T(8,128)(2,1)S(1)}, bf16[2048,128]{1,0:T(8,128)(2,1)S(1)}, u32[]{:S(2)}, u32[]{:S(2)}) collective-permute-start(bf16[2048,128]{1,0:T(8,128)(2,1)S(1)} %shard_map.105.refs_1_), channel_id=1, source_target_pairs={{0,1},{1,0},{2,3},{3,2},{4,5},{5,4},{6,7},{7,6},{8,9},{9,8},{10,11... | collective-permute-start | bytes 1572872 | tf_op jit(solution)/shard_map/ppermute | solution.py:56
  26.8 1.4 %collective-permute-start.11 = (f32[16,2048]{1,0:T(8,128)S(1)}, f32[16,2048]{1,0:T(8,128)S(1)}, u32[]{:S(2)}, u32[]{:S(2)}) collective-permute-start(f32[16,2048]{1,0:T(8,128)S(1)} %get-tuple-element.36), channel_id=1, source_target_pairs={{0,1},{1,0},{2,3},{3,2},{4,5},{5,4},{6,7},{7,6},{8,9},{9,8},{10,11... | collective-permute-start | bytes 393224 | tf_op jit(solution)/shard_map/ppermute | solution.py:56
  27.3 3.0 %collective-permute-start.12 = (f32[16,2048]{1,0:T(8,128)S(1)}, f32[16,2048]{1,0:T(8,128)S(1)}, u32[]{:S(2)}, u32[]{:S(2)}) collective-permute-start(f32[16,2048]{1,0:T(8,128)S(1)} %shard_map.111), channel_id=1, source_target_pairs={{0,1},{1,0},{2,3},{3,2},{4,5},{5,4},{6,7},{7,6},{8,9},{9,8},{10,11... | collective-permute-start | bytes 393224 | tf_op jit(solution)/shard_map/ppermute | solution.py:56
  28.3 4.4 %collective-permute-start.13 = (s16[16,2176]{1,0:T(8,128)(2,1)S(1)}, s16[16,2176]{1,0:T(8,128)(2,1)S(1)}, u32[]{:S(2)}, u32[]{:S(2)}) collective-permute-start(s16[16,2176]{1,0:T(8,128)(2,1)S(1)} %shard_map.109.refs_2_), channel_id=1, source_target_pairs={{0,2},{1,3},{2,0},{3,1},{4,6},{5,7},{6,4},{7,5},{8,10},{9,11},{10,... | collective-permute-start | bytes 208904 | tf_op jit(solution)/shard_map/ppermute | solution.py:56
  29.9 17.2 %slice-start.2 = ((s8[14680064]{0:T(1024)(128)(4,1)}), s8[4194304]{0:T(1024)(128)(4,1)S(1)}, s32[]{:S(2)}) async-start(s8[14680064]{0:T(1024)(128)(4,1)} %bitcast.3), calls=%async_computation.3 | async-start | bytes 8388608
  29.9 17.2 %slice-start.6 = ((s8[14680064]{0:T(1024)(128)(4,1)}), s8[4194304]{0:T(1024)(128)(4,1)S(1)}, s32[]{:S(2)}) async-start(s8[14680064]{0:T(1024)(128)(4,1)} %bitcast.5), calls=%async_computation.7 | async-start | bytes 8388608
  29.9 17.2 %slice-start.10 = ((s8[14680064]{0:T(1024)(128)(4,1)}), s8[2097152]{0:T(1024)(128)(4,1)S(1)}, s32[]{:S(2)}) async-start(s8[14680064]{0:T(1024)(128)(4,1)} %bitcast.7), calls=%async_computation.11 | async-start | bytes 4194304
  32.9 6.7 %collective-permute-start.14 = (s16[16,2176]{1,0:T(8,128)(2,1)S(1)}, s16[16,2176]{1,0:T(8,128)(2,1)S(1)}, u32[]{:S(2)}, u32[]{:S(2)}) collective-permute-start(s16[16,2176]{1,0:T(8,128)(2,1)S(1)} %shard_map.112.refs_1_), channel_id=1, source_target_pairs={{0,12},{1,9},{2,14},{3,11},{4,8},{5,13},{6,10},{7,15},{8,4},{9,1},... | collective-permute-start | bytes 208904 | tf_op jit(solution)/shard_map/ppermute | solution.py:377
  33.8 6.8 %collective-permute-start.15 = (s16[16,2176]{1,0:T(8,128)(2,1)S(1)}, s16[16,2176]{1,0:T(8,128)(2,1)S(1)}, u32[]{:S(2)}, u32[]{:S(2)}) collective-permute-start(s16[16,2176]{1,0:T(8,128)(2,1)S(1)} %shard_map.112.refs_1_), channel_id=1, source_target_pairs={{0,4},{1,13},{2,6},{3,15},{4,0},{5,9},{6,2},{7,11},{8,12},{9,5},{1... | collective-permute-start | bytes 208904 | tf_op jit(solution)/shard_map/ppermute | solution.py:377
  34.7 6.7 %collective-permute-start.16 = (s16[16,2176]{1,0:T(8,128)(2,1)S(1)}, s16[16,2176]{1,0:T(8,128)(2,1)S(1)}, u32[]{:S(2)}, u32[]{:S(2)}) collective-permute-start(s16[16,2176]{1,0:T(8,128)(2,1)S(1)} %shard_map.112.refs_1_), channel_id=1, source_target_pairs={{0,8},{1,5},{2,10},{3,7},{4,12},{5,1},{6,14},{7,3},{8,0},{9,13},{1... | collective-permute-start | bytes 208904 | tf_op jit(solution)/shard_map/ppermute | solution.py:377
  41.5 4.3 %collective-permute-start.18 = (bf16[16,2048]{1,0:T(8,128)(2,1)S(1)}, bf16[16,2048]{1,0:T(8,128)(2,1)S(1)}, u32[]{:S(2)}, u32[]{:S(2)}) collective-permute-start(bf16[16,2048]{1,0:T(8,128)(2,1)S(1)} %get-tuple-element.38.refs_0_), channel_id=1, source_target_pairs={{0,2},{1,3},{2,0},{3,1},{4,6},{5,7},{6,4},{7,5},{8,10},{9,11},{10,... | collective-permute-start | bytes 196616 | tf_op jit(solution)/shard_map/ppermute | solution.py:56
  43.1 2.8 %collective-permute-start.17 = (bf16[16,2048]{1,0:T(8,128)(2,1)S(1)}, bf16[16,2048]{1,0:T(8,128)(2,1)S(1)}, u32[]{:S(2)}, u32[]{:S(2)}) collective-permute-start(bf16[16,2048]{1,0:T(8,128)(2,1)S(1)} %get-tuple-element.38.refs_0_), channel_id=1, source_target_pairs={{0,1},{1,0},{2,3},{3,2},{4,5},{5,4},{6,7},{7,6},{8,9},{9,8},{10,11... | collective-permute-start | bytes 196616 | tf_op jit(solution)/shard_map/ppermute | solution.py:56
  45.8 1.3 %collective-permute-start.19 = (bf16[16,2048]{1,0:T(8,128)(2,1)S(1)}, bf16[16,2048]{1,0:T(8,128)(2,1)S(1)}, u32[]{:S(2)}, u32[]{:S(2)}) collective-permute-start(bf16[16,2048]{1,0:T(8,128)(2,1)S(1)} %collective-permute-done.18.refs_2_), channel_id=1, source_target_pairs={{0,1},{1,0},{2,3},{3,2},{4,5},{5,4},{6,7},{7,6},{8,9},{9,8},{10,11... | collective-permute-start | bytes 196616 | tf_op jit(solution)/shard_map/ppermute | solution.py:56
  52.4 1.5 %collective-permute-start.20 = (f32[8,16,512]{2,1,0:T(8,128)S(1)}, f32[8,16,512]{2,1,0:T(8,128)S(1)}, u32[]{:S(2)}, u32[]{:S(2)}) collective-permute-start(f32[8,16,512]{2,1,0:T(8,128)S(1)} %get-tuple-element.40), channel_id=1, source_target_pairs={{0,1},{1,0},{2,3},{3,2},{4,5},{5,4},{6,7},{7,6},{8,9},{9,8},{10,11... | collective-permute-start | bytes 786440 | tf_op jit(solution)/shard_map/ppermute | solution.py:56
  (18 other events, 211.8 us)

commit v12 on v11

--- a/solution.py
+++ b/solution.py
@@ -385,6 +385,12 @@
     return [line, core, y, far]
 
 
+def far_gathered(line):
+    far = swap(line, 3)
+    core, y = swap(line, 1), swap(far, 1)
+    return [line, core, y, far]
+
+
 def updated(x_line, send, left, weight, wide, beside):
     rows, half = send.shape
     line = like((rows, half), f32)
@@ -467,7 +473,7 @@
     left, send = call(
         functools.partial(hidden_kernel, wide),
         [like((rows, gate_weight.shape[1]), bf16), partial_sums],
-        [*near_gathered(line), mlp_gain, gate_weight, up_weight, down_weight],
+        [*far_gathered(line), mlp_gain, gate_weight, up_weight, down_weight],
     )
     return scattered(stream, send, left, down_weight, wide)
 

time: 65.5 us -> 65.5 us (level)
  no operation moved by 1% of the time
where the time goes in v12:
time: 65.5 us; the launch traced here: 65.3 us
  starting transfers between devices  21.6 us (33%)
  waiting for transfers between devices  20.1 us (31%)
  Pallas kernels  11.5 us (18%)
  blocking collectives  10.7 us (16%)
  local copies, waits for them, and re-layouts  1.2 us (2%)
    ppermute x15, waiting for transfers between devices, swap(): return lax.ppermute(x, 'seq', [(i, i ^ distance) for i in range(size)])  14.5 us
    ppermute x15, starting transfers between devices, swap(): return lax.ppermute(x, 'seq', [(i, i ^ distance) for i in range(size)])  12.7 us
    pallas_call x17, Pallas kernels, call(): pl.pallas_call(kernel, out_shape=outs, in_specs=[VMEM] * count + [pl.Bloc...  11.5 us
    all_to_all x1, blocking collectives, to_members(): lax.all_to_all(parts, 'seq', 0, 0, axis_index_groups=groups, tiled=True)  10.7 us
    ppermute x6, starting transfers between devices, z_routed(): lax.ppermute(part, 'seq', [(i, i ^ QUAD * Z_ORDER[i % 2][slot]) for i in...  8.91 us
    ppermute x6, waiting for transfers between devices, z_routed(): lax.ppermute(part, 'seq', [(i, i ^ QUAD * Z_ORDER[i % 2][slot]) for i in...  5.6 us
  transfers between devices with their start and end apart: 21, of which 14 were waited for; matrix products, arithmetic and copies ran while one was open for 0% of the time, Pallas kernels for 6%

profile of v12, /device:TPU:0, one launch (start us, length us, event | category | flops | bytes accessed | tf_op | source)
XLA Modules:
  0.0 65.3 jit_solution(15469723363608971816)
XLA Ops:
  1.2 3.0 %collective-permute-start.6 = (bf16[256,512]{1,0:T(8,128)(2,1)S(1)}, bf16[256,512]{1,0:T(8,128)(2,1)S(1)}, u32[]{:S(2)}, u32[]{:S(2)}) collective-permute-start(bf16[256,512]{1,0:T(8,128)(2,1)S(1)} %get-tuple-element.27), channel_id=1, source_target_pairs={{0,2},{1,3},{2,0},{3,1},{4,6},{5,7},{6,4},{7,5},{8,10},{9,11},{10,... | collective-permute-start | bytes 786440 | tf_op jit(solution)/shard_map/ppermute | solution.py:56
  4.2 1.6 %collective-permute-start = (bf16[208,128]{1,0:T(8,128)(2,1)S(1)}, bf16[208,128]{1,0:T(8,128)(2,1)S(1)}, u32[]{:S(2)}, u32[]{:S(2)}) collective-permute-start(bf16[208,128]{1,0:T(8,128)(2,1)S(1)} %get-tuple-element.24), channel_id=1, source_target_pairs={{0,4},{1,5},{2,6},{3,7},{4,0},{5,1},{6,2},{7,3},{8,12},{9,13},{10,... | collective-permute-start | bytes 159752 | tf_op jit(solution)/shard_map/ppermute | solution.py:56
  5.8 2.6 %collective-permute-start.1 = (bf16[208,128]{1,0:T(8,128)(2,1)S(1)}, bf16[208,128]{1,0:T(8,128)(2,1)S(1)}, u32[]{:S(2)}, u32[]{:S(2)}) collective-permute-start(bf16[208,128]{1,0:T(8,128)(2,1)S(1)} %get-tuple-element.25), channel_id=1, source_target_pairs={{0,8},{1,9},{2,10},{3,11},{4,12},{5,13},{6,14},{7,15},{8,0},{9,1},... | collective-permute-start | bytes 159752 | tf_op jit(solution)/shard_map/ppermute | solution.py:56
  8.6 3.0 %collective-permute-done.1.refs_2_ = bf16[208,128]{1,0:T(8,128)(2,1)S(1)} collective-permute-done((bf16[208,128]{1,0:T(8,128)(2,1)S(1)}, bf16[208,128]{1,0:T(8,128)(2,1)S(1)}, u32[]{:S(2)}, u32[]{:S(2)}) %collective-permute-start.1) | collective-permute-done | bytes 53280 | tf_op jit(solution)/shard_map/ppermute | solution.py:56
  11.6 2.7 %collective-permute-done.2.refs_3_ = bf16[208,128]{1,0:T(8,128)(2,1)S(1)} collective-permute-done((bf16[208,128]{1,0:T(8,128)(2,1)S(1)}, bf16[208,128]{1,0:T(8,128)(2,1)S(1)}, u32[]{:S(2)}, u32[]{:S(2)}) %collective-permute-start.2) | collective-permute-done | bytes 53280 | tf_op jit(solution)/shard_map/ppermute | solution.py:56
  16.1 3.4 %collective-permute-start.9 = (bf16[384,128]{1,0:T(8,128)(2,1)S(1)}, bf16[384,128]{1,0:T(8,128)(2,1)S(1)}, u32[]{:S(2)}, u32[]{:S(2)}) collective-permute-start(bf16[384,128]{1,0:T(8,128)(2,1)S(1)} %get-tuple-element.31), channel_id=1, source_target_pairs={{0,8},{1,5},{2,10},{3,7},{4,12},{5,1},{6,14},{7,3},{8,0},{9,13},{1... | collective-permute-start | bytes 294920 | tf_op jit(solution)/shard_map/ppermute | solution.py:377
  21.0 1.3 %shard_map.103.refs_8_.refs_0_ = bf16[16,512]{1,0:T(8,128)(2,1)S(1)} custom-call(bf16[16,2560]{1,0:T(8,128)(2,1)S(1)} %shard_map.102.refs_0_.refs_2_, bf16[16,2560]{1,0:T(8,128)(2,1)S(1)} %collective-permute-done.3.refs_1_.refs_5_, bf16[16,2560]{1,0:T(8,128)(2,1)S(1)} %collective-permute-done.4.refs_2_.refs_3_, ...), custom_call_target="tpu_custom_call" | custom-call | tf_op jit(solution)/shard_map/pallas_call | solution.py:33
  22.3 1.6 %collective-permute-done.9.refs_7_ = bf16[384,128]{1,0:T(8,128)(2,1)S(1)} collective-permute-done((bf16[384,128]{1,0:T(8,128)(2,1)S(1)}, bf16[384,128]{1,0:T(8,128)(2,1)S(1)}, u32[]{:S(2)}, u32[]{:S(2)}) %collective-permute-start.9) | collective-permute-done | bytes 98336 | tf_op jit(solution)/shard_map/ppermute | solution.py:377
  24.5 1.4 %collective-permute-done.10.refs_4_ = bf16[2048,128]{1,0:T(8,128)(2,1)S(1)} collective-permute-done((bf16[2048,128]{1,0:T(8,128)(2,1)S(1)}, bf16[2048,128]{1,0:T(8,128)(2,1)S(1)}, u32[]{:S(2)}, u32[]{:S(2)}) %collective-permute-start.10) | collective-permute-done | bytes 524320 | tf_op jit(solution)/shard_map/ppermute | solution.py:56
  25.9 1.0 %shard_map.107 = (bf16[16,512]{1,0:T(8,128)(2,1)S(1)}, f32[16,2048]{1,0:T(8,128)S(1)}) custom-call(bf16[16,512]{1,0:T(8,128)(2,1)S(1)} %shard_map.103.refs_8_.refs_0_, f32[64,128]{1,0:T(8,128)S(1)} %get-tuple-element.32.refs_1_, f32[64,128]{1,0:T(8,128)S(1)} %get-tuple-element.33.refs_2_, f32[64,128]{1,0:T(8,128)S(1)} %get-tuple-element.34.refs_3_, ...), custom_call_target="tpu_custom_call" | custom-call | tf_op jit(solution)/shard_map/pallas_call | solution.py:33
  28.3 1.6 %collective-permute-start.13 = (s16[16,2176]{1,0:T(8,128)(2,1)S(1)}, s16[16,2176]{1,0:T(8,128)(2,1)S(1)}, u32[]{:S(2)}, u32[]{:S(2)}) collective-permute-start(s16[16,2176]{1,0:T(8,128)(2,1)S(1)} %shard_map.109.refs_2_), channel_id=1, source_target_pairs={{0,2},{1,3},{2,0},{3,1},{4,6},{5,7},{6,4},{7,5},{8,10},{9,11},{10,... | collective-permute-start | bytes 208904 | tf_op jit(solution)/shard_map/ppermute | solution.py:56
  30.4 2.3 %collective-permute-done.13.refs_2_ = s16[16,2176]{1,0:T(8,128)(2,1)S(1)} collective-permute-done((s16[16,2176]{1,0:T(8,128)(2,1)S(1)}, s16[16,2176]{1,0:T(8,128)(2,1)S(1)}, u32[]{:S(2)}, u32[]{:S(2)}) %collective-permute-start.13) | collective-permute-done | bytes 69664 | tf_op jit(solution)/shard_map/ppermute | solution.py:56
  32.9 0.9 %collective-permute-start.14 = (s16[16,2176]{1,0:T(8,128)(2,1)S(1)}, s16[16,2176]{1,0:T(8,128)(2,1)S(1)}, u32[]{:S(2)}, u32[]{:S(2)}) collective-permute-start(s16[16,2176]{1,0:T(8,128)(2,1)S(1)} %shard_map.112.refs_1_), channel_id=1, source_target_pairs={{0,12},{1,9},{2,14},{3,11},{4,8},{5,13},{6,10},{7,15},{8,4},{9,1},... | collective-permute-start | bytes 208904 | tf_op jit(solution)/shard_map/ppermute | solution.py:377
  33.8 1.0 %collective-permute-start.15 = (s16[16,2176]{1,0:T(8,128)(2,1)S(1)}, s16[16,2176]{1,0:T(8,128)(2,1)S(1)}, u32[]{:S(2)}, u32[]{:S(2)}) collective-permute-start(s16[16,2176]{1,0:T(8,128)(2,1)S(1)} %shard_map.112.refs_1_), channel_id=1, source_target_pairs={{0,4},{1,13},{2,6},{3,15},{4,0},{5,9},{6,2},{7,11},{8,12},{9,5},{1... | collective-permute-start | bytes 208904 | tf_op jit(solution)/shard_map/ppermute | solution.py:377
  34.7 2.6 %collective-permute-start.16 = (s16[16,2176]{1,0:T(8,128)(2,1)S(1)}, s16[16,2176]{1,0:T(8,128)(2,1)S(1)}, u32[]{:S(2)}, u32[]{:S(2)}) collective-permute-start(s16[16,2176]{1,0:T(8,128)(2,1)S(1)} %shard_map.112.refs_1_), channel_id=1, source_target_pairs={{0,8},{1,5},{2,10},{3,7},{4,12},{5,1},{6,14},{7,3},{8,0},{9,13},{1... | collective-permute-start | bytes 208904 | tf_op jit(solution)/shard_map/ppermute | solution.py:377
  37.3 2.2 %collective-permute-done.14.refs_2_ = s16[16,2176]{1,0:T(8,128)(2,1)S(1)} collective-permute-done((s16[16,2176]{1,0:T(8,128)(2,1)S(1)}, s16[16,2176]{1,0:T(8,128)(2,1)S(1)}, u32[]{:S(2)}, u32[]{:S(2)}) %collective-permute-start.14) | collective-permute-done | bytes 69664 | tf_op jit(solution)/shard_map/ppermute | solution.py:377
  39.5 1.0 %collective-permute-done.15.refs_3_ = s16[16,2176]{1,0:T(8,128)(2,1)S(1)} collective-permute-done((s16[16,2176]{1,0:T(8,128)(2,1)S(1)}, s16[16,2176]{1,0:T(8,128)(2,1)S(1)}, u32[]{:S(2)}, u32[]{:S(2)}) %collective-permute-start.15) | collective-permute-done | bytes 69664 | tf_op jit(solution)/shard_map/ppermute | solution.py:377
  40.5 0.8 %collective-permute-done.16.refs_4_ = s16[16,2176]{1,0:T(8,128)(2,1)S(1)} collective-permute-done((s16[16,2176]{1,0:T(8,128)(2,1)S(1)}, s16[16,2176]{1,0:T(8,128)(2,1)S(1)}, u32[]{:S(2)}, u32[]{:S(2)}) %collective-permute-start.16) | collective-permute-done | bytes 69664 | tf_op jit(solution)/shard_map/ppermute | solution.py:377
  41.6 1.6 %collective-permute-start.17 = (bf16[16,2048]{1,0:T(8,128)(2,1)S(1)}, bf16[16,2048]{1,0:T(8,128)(2,1)S(1)}, u32[]{:S(2)}, u32[]{:S(2)}) collective-permute-start(bf16[16,2048]{1,0:T(8,128)(2,1)S(1)} %get-tuple-element.38.refs_0_), channel_id=1, source_target_pairs={{0,1},{1,0},{2,3},{3,2},{4,5},{5,4},{6,7},{7,6},{8,9},{9,8},{10,11... | collective-permute-start | bytes 196616 | tf_op jit(solution)/shard_map/ppermute | solution.py:56
  43.2 2.7 %collective-permute-done.18.refs_3_ = bf16[16,2048]{1,0:T(8,128)(2,1)S(1)} collective-permute-done((bf16[16,2048]{1,0:T(8,128)(2,1)S(1)}, bf16[16,2048]{1,0:T(8,128)(2,1)S(1)}, u32[]{:S(2)}, u32[]{:S(2)}) %collective-permute-start.18) | collective-permute-done | bytes 65568 | tf_op jit(solution)/shard_map/ppermute | solution.py:56
  46.0 1.1 %collective-permute-done.19.refs_2_ = bf16[16,2048]{1,0:T(8,128)(2,1)S(1)} collective-permute-done((bf16[16,2048]{1,0:T(8,128)(2,1)S(1)}, bf16[16,2048]{1,0:T(8,128)(2,1)S(1)}, u32[]{:S(2)}, u32[]{:S(2)}) %collective-permute-start.19) | collective-permute-done | bytes 65568 | tf_op jit(solution)/shard_map/ppermute | solution.py:56
  47.3 5.1 %shard_map.114 = (bf16[16,896]{1,0:T(8,128)(2,1)S(1)}, f32[8,16,512]{2,1,0:T(8,128)S(1)}) custom-call(bf16[16,2048]{1,0:T(8,128)(2,1)S(1)} %get-tuple-element.38.refs_0_, bf16[16,2048]{1,0:T(8,128)(2,1)S(1)} %collective-permute-done.17.refs_1_, bf16[16,2048]{1,0:T(8,128)(2,1)S(1)} %collective-permute-done.19.refs_2_, ...), custom_call_target="tpu_custom_call" | custom-call | tf_op jit(solution)/shard_map/pallas_call | solution.py:33
  52.6 1.1 %shard_map.115.refs_0_ = f32[8,16,512]{2,1,0:T(8,128)S(1)} custom-call(bf16[16,896]{1,0:T(8,128)(2,1)S(1)} %get-tuple-element.39.refs_0_, bf16[896,8192]{1,0:T(8,128)(2,1)S(1)} %bitcast.4), custom_call_target="tpu_custom_call" | custom-call | tf_op jit(solution)/shard_map/pallas_call | solution.py:33
  54.0 10.7 %all_to_all.5.refs_1_ = bf16[8,16,512]{2,1,0:T(8,128)(2,1)S(1)} all-to-all(bf16[8,16,512]{2,1,0:T(8,128)(2,1)S(1)} %shard_map.116), channel_id=1, replica_groups={{0,2,4,6,8,10,12,14},{1,3,5,7,9,11,13,15},{16,18,20,22,24,26,28,30},{17..., dimensions={0} | all-to-all | bytes 262144 | tf_op jit(solution)/shard_map/all_to_all | solution.py:155
  (87 shorter events, 8.8 us)
Async XLA Ops:
  1.2 13.8 %collective-permute-start.6 = (bf16[256,512]{1,0:T(8,128)(2,1)S(1)}, bf16[256,512]{1,0:T(8,128)(2,1)S(1)}, u32[]{:S(2)}, u32[]{:S(2)}) collective-permute-start(bf16[256,512]{1,0:T(8,128)(2,1)S(1)} %get-tuple-element.27), channel_id=1, source_target_pairs={{0,2},{1,3},{2,0},{3,1},{4,6},{5,7},{6,4},{7,5},{8,10},{9,11},{10,... | collective-permute-start | bytes 786440 | tf_op jit(solution)/shard_map/ppermute | solution.py:56
  4.2 4.4 %collective-permute-start = (bf16[208,128]{1,0:T(8,128)(2,1)S(1)}, bf16[208,128]{1,0:T(8,128)(2,1)S(1)}, u32[]{:S(2)}, u32[]{:S(2)}) collective-permute-start(bf16[208,128]{1,0:T(8,128)(2,1)S(1)} %get-tuple-element.24), channel_id=1, source_target_pairs={{0,4},{1,5},{2,6},{3,7},{4,0},{5,1},{6,2},{7,3},{8,12},{9,13},{10,... | collective-permute-start | bytes 159752 | tf_op jit(solution)/shard_map/ppermute | solution.py:56
  5.8 5.8 %collective-permute-start.1 = (bf16[208,128]{1,0:T(8,128)(2,1)S(1)}, bf16[208,128]{1,0:T(8,128)(2,1)S(1)}, u32[]{:S(2)}, u32[]{:S(2)}) collective-permute-start(bf16[208,128]{1,0:T(8,128)(2,1)S(1)} %get-tuple-element.25), channel_id=1, source_target_pairs={{0,8},{1,9},{2,10},{3,11},{4,12},{5,13},{6,14},{7,15},{8,0},{9,1},... | collective-permute-start | bytes 159752 | tf_op jit(solution)/shard_map/ppermute | solution.py:56
  8.4 5.9 %collective-permute-start.2 = (bf16[208,128]{1,0:T(8,128)(2,1)S(1)}, bf16[208,128]{1,0:T(8,128)(2,1)S(1)}, u32[]{:S(2)}, u32[]{:S(2)}) collective-permute-start(bf16[208,128]{1,0:T(8,128)(2,1)S(1)} %get-tuple-element.26), channel_id=1, source_target_pairs={{0,12},{1,13},{2,14},{3,15},{4,8},{5,9},{6,10},{7,11},{8,4},{9,5},... | collective-permute-start | bytes 159752 | tf_op jit(solution)/shard_map/ppermute | solution.py:56
  14.4 5.1 %collective-permute-start.4 = (bf16[16,2560]{1,0:T(8,128)(2,1)S(1)}, bf16[16,2560]{1,0:T(8,128)(2,1)S(1)}, u32[]{:S(2)}, u32[]{:S(2)}) collective-permute-start(bf16[16,2560]{1,0:T(8,128)(2,1)S(1)} %shard_map.102.refs_0_.refs_2_), channel_id=1, source_target_pairs={{0,2},{1,3},{2,0},{3,1},{4,6},{5,7},{6,4},{7,5},{8,10},{9,11},{10,... | collective-permute-start | bytes 245768 | tf_op jit(solution)/shard_map/ppermute | solution.py:56
  15.1 7.2 %collective-permute-start.7 = (bf16[384,128]{1,0:T(8,128)(2,1)S(1)}, bf16[384,128]{1,0:T(8,128)(2,1)S(1)}, u32[]{:S(2)}, u32[]{:S(2)}) collective-permute-start(bf16[384,128]{1,0:T(8,128)(2,1)S(1)} %get-tuple-element.29), channel_id=1, source_target_pairs={{0,12},{1,9},{2,14},{3,11},{4,8},{5,13},{6,10},{7,15},{8,4},{9,1},... | collective-permute-start | bytes 294920 | tf_op jit(solution)/shard_map/ppermute | solution.py:377
  15.8 6.4 %collective-permute-start.8 = (bf16[384,128]{1,0:T(8,128)(2,1)S(1)}, bf16[384,128]{1,0:T(8,128)(2,1)S(1)}, u32[]{:S(2)}, u32[]{:S(2)}) collective-permute-start(bf16[384,128]{1,0:T(8,128)(2,1)S(1)} %get-tuple-element.30), channel_id=1, source_target_pairs={{0,4},{1,13},{2,6},{3,15},{4,0},{5,9},{6,2},{7,11},{8,12},{9,5},{1... | collective-permute-start | bytes 294920 | tf_op jit(solution)/shard_map/ppermute | solution.py:377
  16.1 7.7 %collective-permute-start.9 = (bf16[384,128]{1,0:T(8,128)(2,1)S(1)}, bf16[384,128]{1,0:T(8,128)(2,1)S(1)}, u32[]{:S(2)}, u32[]{:S(2)}) collective-permute-start(bf16[384,128]{1,0:T(8,128)(2,1)S(1)} %get-tuple-element.31), channel_id=1, source_target_pairs={{0,8},{1,5},{2,10},{3,7},{4,12},{5,1},{6,14},{7,3},{8,0},{9,13},{1... | collective-permute-start | bytes 294920 | tf_op jit(solution)/shard_map/ppermute | solution.py:377
  19.5 1.3 %collective-permute-start.3 = (bf16[16,2560]{1,0:T(8,128)(2,1)S(1)}, bf16[16,2560]{1,0:T(8,128)(2,1)S(1)}, u32[]{:S(2)}, u32[]{:S(2)}) collective-permute-start(bf16[16,2560]{1,0:T(8,128)(2,1)S(1)} %shard_map.102.refs_0_.refs_2_), channel_id=1, source_target_pairs={{0,1},{1,0},{2,3},{3,2},{4,5},{5,4},{6,7},{7,6},{8,9},{9,8},{10,11... | collective-permute-start | bytes 245768 | tf_op jit(solution)/shard_map/ppermute | solution.py:56
  19.5 1.4 %collective-permute-start.5 = (bf16[16,2560]{1,0:T(8,128)(2,1)S(1)}, bf16[16,2560]{1,0:T(8,128)(2,1)S(1)}, u32[]{:S(2)}, u32[]{:S(2)}) collective-permute-start(bf16[16,2560]{1,0:T(8,128)(2,1)S(1)} %collective-permute-done.4.refs_2_.refs_3_), channel_id=1, source_target_pairs={{0,1},{1,0},{2,3},{3,2},{4,5},{5,4},{6,7},{7,6},{8,9},{9,8},{10,11... | collective-permute-start | bytes 245768 | tf_op jit(solution)/shard_map/ppermute | solution.py:56
  23.9 2.0 %collective-permute-start.10 = (bf16[2048,128]{1,0:T(8,128)(2,1)S(1)}, bf16[2048,128]{1,0:T(8,128)(2,1)S(1)}, u32[]{:S(2)}, u32[]{:S(2)}) collective-permute-start(bf16[2048,128]{1,0:T(8,128)(2,1)S(1)} %shard_map.105.refs_1_), channel_id=1, source_target_pairs={{0,1},{1,0},{2,3},{3,2},{4,5},{5,4},{6,7},{7,6},{8,9},{9,8},{10,11... | collective-permute-start | bytes 1572872 | tf_op jit(solution)/shard_map/ppermute | solution.py:56
  26.8 1.4 %collective-permute-start.11 = (f32[16,2048]{1,0:T(8,128)S(1)}, f32[16,2048]{1,0:T(8,128)S(1)}, u32[]{:S(2)}, u32[]{:S(2)}) collective-permute-start(f32[16,2048]{1,0:T(8,128)S(1)} %get-tuple-element.36), channel_id=1, source_target_pairs={{0,1},{1,0},{2,3},{3,2},{4,5},{5,4},{6,7},{7,6},{8,9},{9,8},{10,11... | collective-permute-start | bytes 393224 | tf_op jit(solution)/shard_map/ppermute | solution.py:56
  27.3 3.0 %collective-permute-start.12 = (f32[16,2048]{1,0:T(8,128)S(1)}, f32[16,2048]{1,0:T(8,128)S(1)}, u32[]{:S(2)}, u32[]{:S(2)}) collective-permute-start(f32[16,2048]{1,0:T(8,128)S(1)} %shard_map.111), channel_id=1, source_target_pairs={{0,1},{1,0},{2,3},{3,2},{4,5},{5,4},{6,7},{7,6},{8,9},{9,8},{10,11... | collective-permute-start | bytes 393224 | tf_op jit(solution)/shard_map/ppermute | solution.py:56
  28.3 4.4 %collective-permute-start.13 = (s16[16,2176]{1,0:T(8,128)(2,1)S(1)}, s16[16,2176]{1,0:T(8,128)(2,1)S(1)}, u32[]{:S(2)}, u32[]{:S(2)}) collective-permute-start(s16[16,2176]{1,0:T(8,128)(2,1)S(1)} %shard_map.109.refs_2_), channel_id=1, source_target_pairs={{0,2},{1,3},{2,0},{3,1},{4,6},{5,7},{6,4},{7,5},{8,10},{9,11},{10,... | collective-permute-start | bytes 208904 | tf_op jit(solution)/shard_map/ppermute | solution.py:56
  29.9 17.3 %slice-start.2 = ((s8[14680064]{0:T(1024)(128)(4,1)}), s8[4194304]{0:T(1024)(128)(4,1)S(1)}, s32[]{:S(2)}) async-start(s8[14680064]{0:T(1024)(128)(4,1)} %bitcast.3), calls=%async_computation.3 | async-start | bytes 8388608
  29.9 17.3 %slice-start.6 = ((s8[14680064]{0:T(1024)(128)(4,1)}), s8[4194304]{0:T(1024)(128)(4,1)S(1)}, s32[]{:S(2)}) async-start(s8[14680064]{0:T(1024)(128)(4,1)} %bitcast.5), calls=%async_computation.7 | async-start | bytes 8388608
  29.9 17.3 %slice-start.10 = ((s8[14680064]{0:T(1024)(128)(4,1)}), s8[2097152]{0:T(1024)(128)(4,1)S(1)}, s32[]{:S(2)}) async-start(s8[14680064]{0:T(1024)(128)(4,1)} %bitcast.7), calls=%async_computation.11 | async-start | bytes 4194304
  32.9 6.7 %collective-permute-start.14 = (s16[16,2176]{1,0:T(8,128)(2,1)S(1)}, s16[16,2176]{1,0:T(8,128)(2,1)S(1)}, u32[]{:S(2)}, u32[]{:S(2)}) collective-permute-start(s16[16,2176]{1,0:T(8,128)(2,1)S(1)} %shard_map.112.refs_1_), channel_id=1, source_target_pairs={{0,12},{1,9},{2,14},{3,11},{4,8},{5,13},{6,10},{7,15},{8,4},{9,1},... | collective-permute-start | bytes 208904 | tf_op jit(solution)/shard_map/ppermute | solution.py:377
  33.8 6.8 %collective-permute-start.15 = (s16[16,2176]{1,0:T(8,128)(2,1)S(1)}, s16[16,2176]{1,0:T(8,128)(2,1)S(1)}, u32[]{:S(2)}, u32[]{:S(2)}) collective-permute-start(s16[16,2176]{1,0:T(8,128)(2,1)S(1)} %shard_map.112.refs_1_), channel_id=1, source_target_pairs={{0,4},{1,13},{2,6},{3,15},{4,0},{5,9},{6,2},{7,11},{8,12},{9,5},{1... | collective-permute-start | bytes 208904 | tf_op jit(solution)/shard_map/ppermute | solution.py:377
  34.7 6.7 %collective-permute-start.16 = (s16[16,2176]{1,0:T(8,128)(2,1)S(1)}, s16[16,2176]{1,0:T(8,128)(2,1)S(1)}, u32[]{:S(2)}, u32[]{:S(2)}) collective-permute-start(s16[16,2176]{1,0:T(8,128)(2,1)S(1)} %shard_map.112.refs_1_), channel_id=1, source_target_pairs={{0,8},{1,5},{2,10},{3,7},{4,12},{5,1},{6,14},{7,3},{8,0},{9,13},{1... | collective-permute-start | bytes 208904 | tf_op jit(solution)/shard_map/ppermute | solution.py:377
  41.5 4.4 %collective-permute-start.18 = (bf16[16,2048]{1,0:T(8,128)(2,1)S(1)}, bf16[16,2048]{1,0:T(8,128)(2,1)S(1)}, u32[]{:S(2)}, u32[]{:S(2)}) collective-permute-start(bf16[16,2048]{1,0:T(8,128)(2,1)S(1)} %get-tuple-element.38.refs_0_), channel_id=1, source_target_pairs={{0,3},{1,2},{2,1},{3,0},{4,7},{5,6},{6,5},{7,4},{8,11},{9,10},{10,... | collective-permute-start | bytes 196616 | tf_op jit(solution)/shard_map/ppermute | solution.py:56
  41.6 4.4 %collective-permute-start.17 = (bf16[16,2048]{1,0:T(8,128)(2,1)S(1)}, bf16[16,2048]{1,0:T(8,128)(2,1)S(1)}, u32[]{:S(2)}, u32[]{:S(2)}) collective-permute-start(bf16[16,2048]{1,0:T(8,128)(2,1)S(1)} %get-tuple-element.38.refs_0_), channel_id=1, source_target_pairs={{0,1},{1,0},{2,3},{3,2},{4,5},{5,4},{6,7},{7,6},{8,9},{9,8},{10,11... | collective-permute-start | bytes 196616 | tf_op jit(solution)/shard_map/ppermute | solution.py:56
  45.9 1.3 %collective-permute-start.19 = (bf16[16,2048]{1,0:T(8,128)(2,1)S(1)}, bf16[16,2048]{1,0:T(8,128)(2,1)S(1)}, u32[]{:S(2)}, u32[]{:S(2)}) collective-permute-start(bf16[16,2048]{1,0:T(8,128)(2,1)S(1)} %collective-permute-done.18.refs_3_), channel_id=1, source_target_pairs={{0,1},{1,0},{2,3},{3,2},{4,5},{5,4},{6,7},{7,6},{8,9},{9,8},{10,11... | collective-permute-start | bytes 196616 | tf_op jit(solution)/shard_map/ppermute | solution.py:56
  52.4 1.5 %collective-permute-start.20 = (f32[8,16,512]{2,1,0:T(8,128)S(1)}, f32[8,16,512]{2,1,0:T(8,128)S(1)}, u32[]{:S(2)}, u32[]{:S(2)}) collective-permute-start(f32[8,16,512]{2,1,0:T(8,128)S(1)} %get-tuple-element.40), channel_id=1, source_target_pairs={{0,1},{1,0},{2,3},{3,2},{4,5},{5,4},{6,7},{7,6},{8,9},{9,8},{10,11... | collective-permute-start | bytes 786440 | tf_op jit(solution)/shard_map/ppermute | solution.py:56
  (18 other events, 212.4 us)
